TPU v7x, 32 devices: a whole 2x2x4 slice. The times are simulated.
32 devices in a mesh: energy: 8 (over y, x, core), slab: 4 (over z).
Axes of the slice: x: 2, y: 2, z: 4, core: 2. Of those that a mesh axis runs over, the one named last changes fastest.
Arguments:
- free_green: float32 [8, 8, 2, 256, 256], P('energy', 'slab'), may hold values from -2 to 2
- self_energy: float32 [8, 8, 2, 256, 256], P('energy', 'slab'), may hold values from -0.375 to 0.375
- coupling: float32 [8, 2, 256, 256], P('slab'), may hold values from -0.375 to 0.375
- pattern: int32 [8, 16, 16], P('slab'), may hold values 0 or 1
- offsets: int32 [4], replicated, may hold values from 1 to 7
- emission: float32 [4], replicated, may hold values from 0.2 to 1
- absorption: float32 [4], replicated, may hold values from 0.1 to 0.6
Outputs:
- retarded: float32 [8, 8, 2, 256, 256], P('energy', 'slab')
- scattering: float32 [8, 8, 2, 256, 256], P('energy', 'slab')
All inputs are finite; a program needn't handle non-finite values. No bound on the sum of `pattern` on one device may be relied on, other than what follows from the above.
Results may differ from a plain program's by a relative error of at most 0.0003.
Values sent between devices are 32-bit elements; how exact they have to be, the bound alone decides.
No kernel may reach another device: no remote copies, remote signals or barrier semaphores. Data moves between devices by JAX's collectives and lax.ppermute only.
A program may use at most 64 MiB of HBM per device.

v0:
```python
import functools

import jax
import jax.numpy as jnp
from jax import lax
from jax.experimental import pallas as pl
from jax.experimental.pallas import tpu as pltpu
from jax.sharding import PartitionSpec as P

F32 = jnp.float32
HALF = jnp.bfloat16
HBM = pl.BlockSpec(memory_space=pltpu.HBM)
VMEM = pl.BlockSpec(memory_space=pltpu.VMEM)


def split(value):
    high = value.astype(HALF)
    return high, (value - high.astype(F32)).astype(HALF)


def dot(left, right, transposed):
    dims = (((1,), (1 if transposed else 0,)), ((), ()))
    return lax.dot_general(left, right, dims, preferred_element_type=F32)


def put(matrix, block):
    size = block.shape[0]
    for level, part in enumerate(split(block)):
        real, imag = part[:, :size], part[:, size:]
        matrix[level, :size, :size] = real
        matrix[level, :size, size:] = imag
        matrix[level, size:, :size] = -imag
        matrix[level, size:, size:] = real


def times_split(high, low, matrix, transposed=False):
    return (
        dot(high, matrix[0], transposed)
        + dot(low, matrix[0], transposed)
        + dot(high, matrix[1], transposed)
    )


def times(block, matrix, transposed=False):
    high, low = split(block)
    return times_split(high, low, matrix, transposed)


def row_form(pair):
    return jnp.concatenate([pair[0], pair[1]], axis=1)


def adjoint_row(pair):
    return jnp.concatenate([jnp.transpose(pair[0]), -jnp.transpose(pair[1])], axis=1)


def expand(pattern, size):
    blocks = pattern.shape[0]
    tile = size // blocks
    rows = lax.broadcasted_iota(jnp.int32, (size, blocks), 0)
    first = lax.broadcasted_iota(jnp.int32, (size, blocks), 1) * tile
    member = jnp.where((rows >= first) & (rows < first + tile), 1.0, 0.0).astype(HALF)
    tall = dot(member, pattern.astype(F32).astype(HALF), False)
    return dot(tall.astype(HALF), member, True)


def couple(coupling, pattern):
    mask = expand(pattern[...], coupling.shape[-1])
    return jnp.concatenate([coupling[0] * mask, coupling[1] * mask], axis=1)


def parity():
    return lax.rem(lax.axis_index("energy"), 2)


def shape(rows, columns, dtype=F32, *lead):
    return jax.ShapeDtypeStruct(lead + (rows, columns), dtype)


def matrices(number, size):
    return [pltpu.VMEM((2, 2 * size, 2 * size), HALF)] * number


def call(kernel, outs, scratch, args, specs=None, flops=0, name=None, limit=40):
    made = pl.pallas_call(
        kernel,
        out_shape=outs,
        in_specs=specs or [VMEM] * len(args),
        out_specs=[VMEM] * len(outs),
        scratch_shapes=scratch,
        compiler_params=pltpu.CompilerParams(vmem_limit_bytes=limit * 2**20),
        cost_estimate=pl.CostEstimate(flops=flops, bytes_accessed=2**20, transcendentals=0),
        name=name,
    )(*args)
    return list(made)


class Loads:
    def __init__(self, args, targets, sems, slabs=(0, 1)):
        order = [(0, 0), (1, 0), (3, 1), (2, 1), (1, 1), (0, 1), (3, 0), (2, 0)]
        self.copies = {
            (which, slab): pltpu.make_async_copy(
                args[which].at[slab], targets[which].at[slab], sems.at[index]
            )
            for index, (which, slab) in enumerate(order)
            if which < 2 or slab in slabs
        }
        self.targets = targets
        for copy in self.copies.values():
            copy.start()

    def get(self, which, slab):
        self.copies[which, slab].wait()
        return self.targets[which].at[slab]

    def green(self, slab):
        return row_form(self.get(0, slab))

    def sigma(self, slab):
        return row_form(self.get(1, slab))

    def coupler(self, slab):
        tiles = self.get(3, slab)
        return couple(self.get(2, slab), tiles)


def load_scratch(size, blocks):
    return [
        pltpu.VMEM((2, 2, size, size), F32),
        pltpu.VMEM((2, 2, size, size), F32),
        pltpu.VMEM((2, 2, size, size), F32),
        pltpu.VMEM((2, blocks, blocks), jnp.int32),
        pltpu.SemaphoreType.DMA((8,)),
    ]


def left_sources(loads, whole, source, coupler_out, m_a, m_b, m_c):
    first = loads.green(0)
    put(m_b, first)
    put(m_a, loads.sigma(0))
    made = first + times(times(first, m_a), m_b)
    if source is not None:
        source[...] = made
    put(m_a, made)
    coupler = loads.coupler(1)
    if coupler_out is not None:
        coupler_out[...] = coupler
    put(m_c, coupler)
    inner = loads.sigma(1) + times(times(coupler, m_a), m_c, True)
    put(m_a, inner)
    second = loads.green(1)
    put(m_b, second)
    whole[...] = second + times(times(second, m_a), m_b)
    return first, second


def source_kernel(green, sigma, coupling, pattern, whole, *scratch):
    @pl.when(lax.axis_index("slab") == 0)
    def _():
        loads = Loads((green, sigma, coupling, pattern), scratch[:4], scratch[4], (1,))
        left_sources(loads, whole, None, None, *scratch[5:])


def map_kernel(
    green, sigma, coupling, pattern,
    whole, source, coupler, opening, lead, tail, forward, backward, *scratch,
):
    m_a, m_b, m_c = scratch[5:]
    loads = Loads((green, sigma, coupling, pattern), scratch[:4], scratch[4])
    first, second = left_sources(loads, whole, source, coupler, m_a, m_b, m_c)
    before = loads.coupler(0)

    @pl.when(lax.axis_index("slab") > 0)
    def _():
        opening[...] = before
        put(m_a, before)
        ahead = times(first, m_a)
        forward[...] = ahead
        put(m_a, ahead)
        lead[0], lead[1] = split(times(times(second, m_c), m_a))
        put(m_a, first)
        size = before.shape[0]
        behind = times(adjoint_row((before[:, :size], before[:, size:])), m_a)
        backward[...] = behind
        put(tail, times(times(behind, m_c, True), m_b))


def right_terms(first, last, coupler, m_coupler, m_first, m_last, m_upper):
    put(m_coupler, coupler)
    put(m_last, last)
    through = times(times(first, m_coupler, True), m_last)
    put(m_first, first)
    put(m_upper, times(coupler, m_first))
    return through, first + times(through, m_upper)


def prepare_kernel(count, *refs):
    arrived, wholes = refs[: count - 1], refs[count - 1 : 2 * count - 2]
    refs = refs[2 * count - 2 :]
    start_whole, source, forward, backward, coupler, following = refs[:6]
    lead, tail, constant, last_lead, last_tail = refs[6:11]
    first_v, last_v, m_a, m_b, m_c, m_d = refs[11:]
    place = lax.axis_index("slab")

    @pl.when(place == 0)
    def _():
        first_v[...] = source[...]
        last_v[...] = start_whole[...]

    for turn in range(count - 1):
        @pl.when((place > 0) & (place == turn + 1 - parity()))
        def _(turn=turn):
            last_v[...] = wholes[turn][...]
            put(m_a, arrived[turn][...])

    @pl.when((place > 0) & (place < count - 1))
    def _():
        put(m_b, backward[...])
        first_v[...] = source[...] + times(times(forward[...], m_a), m_b)

    @pl.when(place < count - 1)
    def _():
        first, last = first_v[...], last_v[...]
        through, joined = right_terms(first, last, coupler[...], m_a, m_b, m_c, m_d)
        constant[...] = joined
        next_coupler = following[...]
        put(m_a, next_coupler)
        lead[0], lead[1] = split(times(through, m_a, True))
        last_lead[0], last_lead[1] = split(times(last, m_a, True))
        behind = times(next_coupler, m_c)
        put(last_tail, behind)
        put(tail, times(behind, m_d))


def apply_map(mapping, m_x):
    lead, tail, constant = mapping
    return constant[...] + times(times_split(lead[0], lead[1], m_x), tail)


def relay_kernel(step, count, lefts, rights, *refs):
    refs = list(refs)
    place = lax.axis_index("slab")
    turn = step - parity()
    is_left = (turn >= 0) & (turn <= count - 2) & (place == turn + 1)
    is_right = (turn >= count - 1) & (place == 2 * count - 3 - turn)
    closing = lefts and step >= count - 2
    arrived = refs.pop(0)
    left_map = [refs.pop(0) for _ in range(3)] if lefts else None
    right_map = [refs.pop(0) for _ in range(3)] if rights else None
    if closing:
        forward, backward, source, coupler = [refs.pop(0) for _ in range(4)]
    out = refs.pop(0)
    if closing:
        end, m_x, m_a, m_b, m_c = refs
    else:
        (m_x,) = refs

    if step == 0:
        @pl.when(place == 0)
        def _():
            out[...] = left_map[2][...]

    if lefts:
        @pl.when(is_left)
        def _():
            put(m_x, arrived[...])
            out[...] = apply_map(left_map, m_x)

    if closing:
        @pl.when(is_left & (place == count - 1))
        def _():
            last = out[...]
            end[...] = last
            put(m_a, backward[...])
            first = source[...] + times(times(forward[...], m_x), m_a)
            _, joined = right_terms(first, last, coupler[...], m_a, m_b, m_c, m_x)
            out[...] = joined

    if rights:
        @pl.when(is_right)
        def _():
            put(m_x, arrived[...])
            out[...] = apply_map(right_map, m_x)


def finish_kernel(count, *refs):
    refs = list(refs)
    arrived = [refs.pop(0) for _ in range(count)]
    outs = [refs.pop(0) for _ in range(count)]
    ends = [refs.pop(0) for _ in range(2)]
    right_map = [refs.pop(0) for _ in range(3)]
    last_lead, last_tail, whole_start = [refs.pop(0) for _ in range(3)]
    wholes = [refs.pop(0) for _ in range(count - 1)]
    retarded, out_v, whole_v, m_x = refs
    place = lax.axis_index("slab")
    core = parity()
    size = out_v.shape[0]
    is_last = place == count - 1
    at = jnp.where(is_last, count - 2 + core, 2 * count - 3 - place + core)
    late = (place == 0) & (core == 1)

    for index in range(count):
        @pl.when(at == count - 1 + index)
        def _(index=index):
            put(m_x, arrived[index][...])

        @pl.when(at == count - 2 + index)
        def _(index=index):
            out_v[...] = outs[index][...]

    for index in range(2):
        @pl.when(is_last & (core == index))
        def _(index=index):
            whole_v[...] = ends[index][...]

    @pl.when(late)
    def _():
        out_v[...] = apply_map(right_map, m_x)

    @pl.when(place == 0)
    def _():
        whole_v[...] = apply_map((last_lead, last_tail, whole_start), m_x)

    for index in range(count - 1):
        @pl.when((place > 0) & jnp.logical_not(is_last) & (place - 1 + core == index))
        def _(index=index):
            whole_v[...] = apply_map((last_lead, last_tail, wholes[index]), m_x)

    for slab, block in enumerate((out_v, whole_v)):
        for part in range(2):
            retarded[slab, part] = block[:, part * size : (part + 1) * size]


def mode_weights(targets, sources, offsets, emission, absorption):
    spacing = sources[None, :, None] - targets[:, None, None]
    emitted = jnp.where(
        spacing == -offsets[None, None, :],
        emission[None, None, :],
        jnp.zeros_like(emission)[None, None, :],
    )
    absorbed = jnp.where(
        spacing == offsets[None, None, :],
        absorption[None, None, :],
        jnp.zeros_like(absorption)[None, None, :],
    )
    return jnp.sum(emitted + absorbed, axis=-1)


def relay_pairs(step, energies, count):
    pairs = []
    for energy in range(energies):
        turn = step - energy % 2
        if 0 <= turn <= count - 2:
            ends = (turn, turn + 1)
        elif count - 1 <= turn <= 2 * count - 3:
            ends = (2 * count - 2 - turn, 2 * count - 3 - turn)
        else:
            continue
        pairs.append(tuple(energy * count + end for end in ends))
    return pairs


def shards(energies, count, free_green, self_energy, coupling, pattern, offsets, emission, absorption):
    size, blocks = free_green.shape[-1], pattern.shape[-1]
    args = (free_green[0], self_energy[0], coupling, pattern)
    row = shape(size, 2 * size)
    lead = shape(size, 2 * size, HALF, 2)
    tail = shape(2 * size, 2 * size, HALF, 2)
    row_v = pltpu.VMEM(row.shape, F32)
    product = 24 * size**3
    loading = load_scratch(size, blocks) + matrices(3, size)

    def relay(step, value):
        return lax.ppermute(value, ("energy", "slab"), relay_pairs(step, energies, count))

    begun = call(
        source_kernel,
        [row],
        loading,
        args,
        [HBM] * 4,
        flops=6 * product,
        name="source",
        limit=58,
    )
    arrived, outs, ends = [relay(0, begun[0])], [], []
    whole, source, coupler, opening, left_lead, left_tail, forward, backward = call(
        map_kernel,
        [row] * 4 + [lead, tail, row, row],
        loading,
        args,
        [HBM] * 4,
        flops=12 * product,
        name="left_maps",
        limit=42,
    )
    left_map = [left_lead, left_tail, whole]
    right_map = following = None
    for step in range(2 * count - 2):
        lefts, rights = step <= count - 1, step >= count - 1
        closing = lefts and step >= count - 2
        args = [arrived[step]]
        if lefts:
            args += left_map
        if rights:
            args += right_map[:3]
        if closing:
            args += [forward, backward, source, coupler]
        made = call(
            functools.partial(relay_kernel, step, count, lefts, rights),
            [row] * (2 if closing else 1),
            matrices(4 if closing else 1, size),
            args,
            flops=2 * product,
            name="relay",
        )
        outs.append(made[0])
        ends += made[1:]
        arrived.append(relay(step + 1, made[0]))
        if step == 0:
            following = lax.ppermute(opening, "slab", [(i, i - 1) for i in range(1, count)])
        if step == count - 2:
            args = arrived[: count - 1] + outs[: count - 1]
            args += [whole, source, forward, backward, coupler, following]
            right_map = call(
                functools.partial(prepare_kernel, count),
                [lead, tail, row, lead, tail],
                [row_v] * 2 + matrices(4, size),
                args,
                flops=10 * product,
                name="right_maps",
            )
    args = arrived[count - 1 :] + outs[count - 2 :] + ends + right_map + [whole] + outs[: count - 1]
    (retarded,) = call(
        functools.partial(finish_kernel, count),
        [shape(size, size, F32, 2, 2)],
        [row_v] * 2 + matrices(1, size),
        args,
        flops=4 * product,
        name="retarded",
    )
    retarded = retarded[None]
    everyone = jnp.arange(energies, dtype=jnp.int32)
    weights = mode_weights(everyone, everyone, offsets, emission, absorption)
    mixed = jnp.einsum(
        "ef,fsxab->esxab",
        weights,
        lax.all_to_all(retarded, "energy", split_axis=3, concat_axis=0, tiled=True),
        precision=lax.Precision.HIGHEST,
    )
    scattering = lax.all_to_all(mixed, "energy", split_axis=0, concat_axis=3, tiled=True)
    return (retarded, scattering)


def solution(mesh):
    blocks = P("energy", "slab", None, None, None)
    in_specs = (blocks, blocks, P("slab", None, None, None), P("slab", None, None), P(), P(), P())
    body = functools.partial(shards, mesh.shape["energy"], mesh.shape["slab"])
    return jax.shard_map(
        body, mesh=mesh, in_specs=in_specs, out_specs=(blocks, blocks), check_vma=False
    )
```

profile of v0, /device:TPU:0, one launch (start us, length us, event | category | flops | bytes accessed | tf_op | source)
XLA Modules:
  0.0 138.1 jit_solution(12532010114523251301)
XLA Ops:
  0.6 0.0 copy-start
  0.6 0.0 copy-start.1
  0.7 0.0 copy-start.2
  0.7 0.0 copy-start.3
  0.7 5.8 %source.1 = f32[256,512]{1,0:T(8,128)} custom-call(f32[2,2,256,256]{3,2,1,0:T(8,128)} %bitcast.19, f32[2,2,256,256]{3,2,1,0:T(8,128)} %bitcast.21, f32[2,2,256,256]{3,2,1,0:T(8,128)} %coupling.3, s32[2,16,16]{2,1,0:T(8,128)} %pattern.3), custom_call_target="tpu_custom_call" | custom-call | flops 2415919104 | bytes 1048576 | tf_op jit(solution)/shard_map/source/pallas_call | solution.py:85
  6.4 1.3 collective-permute-start
  7.8 0.0 copy-done
  7.8 0.0 copy-done.1
  7.8 0.0 copy-done.2
  7.8 0.0 copy-done.3
  7.8 4.4 %left_maps.1 = (f32[256,512]{1,0:T(8,128)S(1)}, f32[256,512]{1,0:T(8,128)S(1)}, f32[256,512]{1,0:T(8,128)S(1)}, f32[256,512]{1,0:T(8,128)S(1)}, bf16[2,256,512]{...) custom-call(f32[2,2,256,256]{3,2,1,0:T(8,128)S(1)} %bitcast.20, ...), custom_call_target="tpu_custom_call" | custom-call | flops 4831838208 | bytes 1048576 | tf_op jit(solution)/shard_map/left_maps/pallas_call | solution.py:85
  12.3 2.5 %collective-permute-done.refs_0_ = f32[256,512]{1,0:T(8,128)S(1)} collective-permute-done((f32[256,512]{1,0:T(8,128)}, f32[256,512]{1,0:T(8,128)S(1)}, u32[]{:S(2)}, u32[]{:S(2)}) %collective-permute-start) | collective-permute-done | bytes 524320 | tf_op jit(solution)/shard_map/ppermute | solution.py:374
  14.8 0.7 collective-permute-start.1
  15.5 0.0 collective-permute-done.1.refs_0_.refs_1_
  15.5 0.7 collective-permute-start.2
  16.2 1.3 collective-permute-start.4
  17.5 0.0 collective-permute-done.2.refs_0_.refs_2_
  17.6 0.7 collective-permute-start.3
  18.3 21.1 %collective-permute-done.4.refs_11_ = f32[256,512]{1,0:T(8,128)S(1)} collective-permute-done((f32[256,512]{1,0:T(8,128)S(1)}, f32[256,512]{1,0:T(8,128)S(1)}, u32[]{:S(2)}, u32[]{:S(2)}) %collective-permute-start.4) | collective-permute-done | bytes 524320 | tf_op jit(solution)/shard_map/ppermute | solution.py:421
  39.4 3.9 %right_maps.1 = (bf16[2,256,512]{2,1,0:T(8,128)(2,1)S(1)}, bf16[2,512,512]{2,1,0:T(8,128)(2,1)S(1)}, f32[256,512]{1,0:T(8,128)S(1)}, bf16[2,256,512]{2,1,0:T(8,128)(2,1)S(1)}, bf16[2,512,512]{2,1,0:T(8,128)(2,1)S(1)}) custom-call(f32[256,512]{1,0:T(8,128)S(1)} %collective-permute-done.refs_0_, f32[256,512]{1,0:T(8,128)S(1)} %collective-permute-done.1.refs_0_.refs_1_, ...), custom_call_target="tpu_custom_call" | custom-call | flops 4026531840 | bytes 1048576 | tf_op jit(solution)/shard_map/right_maps/pallas_call | solution.py:85
  43.4 0.0 collective-permute-done.3.refs_0_
  43.4 0.7 collective-permute-start.5
  44.1 0.0 collective-permute-done.5.refs_0_.refs_1_
  44.2 1.3 collective-permute-start.6
  45.5 35.9 %collective-permute-done.6.refs_0_.refs_2_ = f32[256,512]{1,0:T(8,128)S(1)} collective-permute-done((f32[256,512]{1,0:T(8,128)S(1)}, f32[256,512]{1,0:T(8,128)S(1)}, u32[]{:S(2)}, u32[]{:S(2)}) %collective-permute-start.6) | collective-permute-done | bytes 524320 | tf_op jit(solution)/shard_map/ppermute | solution.py:374
  81.3 1.1 relay.11.refs_7_
  82.4 0.7 collective-permute-start.7
  83.1 0.0 collective-permute-done.7.refs_3_
  83.1 2.6 %retarded.1 = f32[2,2,256,256]{3,2,1,0:T(8,128)} custom-call(f32[256,512]{1,0:T(8,128)S(1)} %collective-permute-done.3.refs_0_, f32[256,512]{1,0:T(8,128)S(1)} %collective-permute-done.5.refs_0_.refs_1_, f32[256,512]{1,0:T(8,128)S(1)} %collective-permute-done.6.refs_0_.refs_2_, f32[256,512]{1,0:T(8,128)S(1)} %collective-permute-done.7.refs_3_, ...), custom_call_target="tpu_custom_call" | custom-call | flops 1610612736 | bytes 1048576 | tf_op jit(solution)/shard_map/retarded/pallas_call | solution.py:85
  85.7 3.0 %copy.20 = f32[1,2,2,256,256]{4,2,1,0,3:T(2,128)} copy(f32[1,2,2,256,256]{4,3,2,1,0:T(8,128)} %bitcast.23) | data formatting | bytes 2097152 | tf_op jit(solution)/shard_map/broadcast_in_dim | solution.py:442
  88.7 0.0 copy-start.6
  88.7 13.3 %all-to-all-start = ((f32[1,2,2,256,256]{4,2,1,0,3:T(2,128)}), f32[1,2,2,256,256]{4,2,1,0,3:T(2,128)S(1)}, u32[]{:S(2)}, u32[]{:S(2)}) async-start(f32[1,2,2,256,256]{4,2,1,0,3:T(2,128)} %copy.20), calls=%async_computation | async-start | bytes 2097152 | tf_op jit(solution)/shard_map/all_to_all | solution.py:448
  102.0 0.0 copy-done.6
  102.0 0.0 copy-start.4
  102.0 0.0 copy-start.5
  102.0 0.6 copy-done.4
  102.6 0.0 copy-done.5
  102.7 0.1 add_reduce_fusion
  102.7 14.6 %all-to-all-done = f32[1,2,2,256,256]{4,2,1,0,3:T(2,128)S(1)} async-done(((f32[1,2,2,256,256]{4,2,1,0,3:T(2,128)}), f32[1,2,2,256,256]{4,2,1,0,3:T(2,128)S(1)}, u32[]{:S(2)}, u32[]{:S(2)}) %all-to-all-start) | async-done | bytes 1048608 | tf_op jit(solution)/shard_map/all_to_all | solution.py:448
  117.4 1.5 %fusion = f32[8,2,2,32,256]{4,0,3,2,1:T(8,128)S(1)} fusion(f32[1,2,2,8,32,256]{5,2,1,4,3,0:T(2,128)S(1)} %bitcast.25, f32[8,8]{1,0:T(8,128)S(1)} %add_reduce_fusion), kind=kOutput, calls=%fused_computation | convolution fusion | flops 25165824 | bytes 2097408 | tf_op jit(solution)/shard_map/ef,fsxab->esxab/dot_general | solution.py:445
  118.9 0.3 copy.23
  119.2 17.8 %all_to_all.36 = f32[8,2,2,32,256]{4,3,2,1,0:T(8,128)S(1)} all-to-all(f32[8,2,2,32,256]{4,3,2,1,0:T(8,128)S(1)} %copy.23), channel_id=1, replica_groups=mesh['energy'=8,'slab'=4] {'energy'}, dimensions={0} | all-to-all | bytes 2097152 | tf_op jit(solution)/shard_map/all_to_all | solution.py:451
  137.0 1.1 copy.24
  (7 shorter events, 0.1 us)
Async XLA Ops:
  0.6 7.1 %copy-start = (f32[1,2,2,256,256]{4,3,2,1,0:T(8,128)S(1)}, f32[1,2,2,256,256]{4,3,2,1,0:T(8,128)}, u32[]{:S(2)}) copy-start(f32[1,2,2,256,256]{4,3,2,1,0:T(8,128)} %param.7) | copy-start | bytes 3145732
  0.6 7.1 %copy-start.1 = (f32[1,2,2,256,256]{4,3,2,1,0:T(8,128)S(1)}, f32[1,2,2,256,256]{4,3,2,1,0:T(8,128)}, u32[]{:S(2)}) copy-start(f32[1,2,2,256,256]{4,3,2,1,0:T(8,128)} %param.8) | copy-start | bytes 3145732
  0.7 7.1 %copy-start.2 = (f32[2,2,256,256]{3,2,1,0:T(8,128)S(1)}, f32[2,2,256,256]{3,2,1,0:T(8,128)}, u32[]{:S(2)}) copy-start(f32[2,2,256,256]{3,2,1,0:T(8,128)} %coupling.3) | copy-start | bytes 3145732
  0.7 7.1 %copy-start.3 = (s32[2,16,16]{2,1,0:T(8,128)S(1)}, s32[2,16,16]{2,1,0:T(8,128)}, u32[]{:S(2)}) copy-start(s32[2,16,16]{2,1,0:T(8,128)} %pattern.3) | copy-start | bytes 6148
  6.4 8.3 %collective-permute-start = (f32[256,512]{1,0:T(8,128)}, f32[256,512]{1,0:T(8,128)S(1)}, u32[]{:S(2)}, u32[]{:S(2)}) collective-permute-start(f32[256,512]{1,0:T(8,128)} %source.1), channel_id=1, source_target_pairs={{0,1},{8,9},{16,17},{24,25}} | collective-permute-start | bytes 1572872 | tf_op jit(solution)/shard_map/ppermute | solution.py:374
  14.8 0.7 collective-permute-start.1
  15.5 2.0 %collective-permute-start.2 = (f32[256,512]{1,0:T(8,128)S(1)}, f32[256,512]{1,0:T(8,128)S(1)}, u32[]{:S(2)}, u32[]{:S(2)}) collective-permute-start(f32[256,512]{1,0:T(8,128)S(1)} %relay.7.refs_4_.refs_17_), channel_id=1, source_target_pairs={{2,3},{5,6},{10,11},{13,14},{18,19},{21,22},{26,27},{29,30}} | collective-permute-start | bytes 1572872 | tf_op jit(solution)/shard_map/ppermute | solution.py:374
  16.2 23.2 %collective-permute-start.4 = (f32[256,512]{1,0:T(8,128)S(1)}, f32[256,512]{1,0:T(8,128)S(1)}, u32[]{:S(2)}, u32[]{:S(2)}) collective-permute-start(f32[256,512]{1,0:T(8,128)S(1)} %get-tuple-element.27), channel_id=1, source_target_pairs={{1,0},{2,1},{3,2},{5,4},{6,5},{7,6},{9,8},{10,9},{11,10},{13,12},{... | collective-permute-start | bytes 1572872 | tf_op jit(solution)/shard_map/ppermute | solution.py:421
  17.6 25.8 %collective-permute-start.3 = (f32[256,512]{1,0:T(8,128)S(1)}, f32[256,512]{1,0:T(8,128)S(1)}, u32[]{:S(2)}, u32[]{:S(2)}) collective-permute-start(f32[256,512]{1,0:T(8,128)S(1)} %get-tuple-element.26.refs_5_.refs_4_.refs_18_), channel_id=1, source_target_pairs={{3,2},{6,7},{11,10},{14,15},{19,18},{22,23},{27,26},{30,31}} | collective-permute-start | bytes 1572872 | tf_op jit(solution)/shard_map/ppermute | solution.py:374
  43.4 0.7 collective-permute-start.5
  44.2 37.2 %collective-permute-start.6 = (f32[256,512]{1,0:T(8,128)S(1)}, f32[256,512]{1,0:T(8,128)S(1)}, u32[]{:S(2)}, u32[]{:S(2)}) collective-permute-start(f32[256,512]{1,0:T(8,128)S(1)} %relay.10.refs_6_), channel_id=1, source_target_pairs={{1,0},{6,5},{9,8},{14,13},{17,16},{22,21},{25,24},{30,29}} | collective-permute-start | bytes 1572872 | tf_op jit(solution)/shard_map/ppermute | solution.py:374
  82.4 0.7 collective-permute-start.7
  88.7 13.3 %copy-start.6 = (s32[4]{0:T(128)S(1)}, s32[4]{0:T(128)}, u32[]{:S(2)}) copy-start(s32[4]{0:T(128)} %param.11) | copy-start | bytes 52
  88.7 28.7 %all-to-all-start = ((f32[1,2,2,256,256]{4,2,1,0,3:T(2,128)}), f32[1,2,2,256,256]{4,2,1,0,3:T(2,128)S(1)}, u32[]{:S(2)}, u32[]{:S(2)}) async-start(f32[1,2,2,256,256]{4,2,1,0,3:T(2,128)} %copy.20), calls=%async_computation | async-start | bytes 2097152 | tf_op jit(solution)/shard_map/all_to_all | solution.py:448
  102.0 0.7 copy-start.4
  102.0 0.7 copy-start.5
where the time goes:
time: 138 us
  waiting for transfers between devices  74.1 us (54%)
  starting transfers between devices  20.7 us (15%)
  Pallas kernels  17.9 us (13%)
  blocking collectives  17.8 us (13%)
  local copies, waits for them, and re-layouts  5.09 us (4%)
  matrix products  1.48 us (1%)
    ppermute x7, waiting for transfers between devices, relay(): lax.ppermute(value, ('energy', 'slab'), relay_pairs(step, energies, count))  38.4 us
    ppermute x1, waiting for transfers between devices, shards(): lax.ppermute(opening, 'slab', [(i, i - 1) for i in range(1, count)])  21.1 us
    pallas_call x10, Pallas kernels, call(): pl.pallas_call(kernel, out_shape=outs, in_specs=specs or [VMEM] * len(arg...  17.9 us
    all_to_all x1, blocking collectives, shards(): lax.all_to_all(mixed, 'energy', split_axis=0, concat_axis=3, tiled=True)  17.8 us
    all_to_all x1, waiting for transfers between devices, shards(): lax.all_to_all(retarded, 'energy', split_axis=3, concat_axis=0, tiled=True)  14.6 us
    all_to_all x1, starting transfers between devices, shards(): lax.all_to_all(retarded, 'energy', split_axis=3, concat_axis=0, tiled=True)  13.3 us
    ppermute x7, starting transfers between devices, relay(): lax.ppermute(value, ('energy', 'slab'), relay_pairs(step, energies, count))  6.09 us
    broadcast_in_dim x1, local copies, waits for them, and re-layouts, shards(): retarded = retarded[None]  3 us
  transfers between devices with their start and end apart: 9, of which 4 were waited for; matrix products, arithmetic and copies ran while one was open for 0% of the time, Pallas kernels for 6%

commit v1 on v0

--- a/solution.py
+++ b/solution.py
@@ -96,14 +96,14 @@
 
 
 class Loads:
-    def __init__(self, args, targets, sems, slabs=(0, 1)):
+    def __init__(self, args, targets, sems, couplers=(0, 1), blocks=True):
         order = [(0, 0), (1, 0), (3, 1), (2, 1), (1, 1), (0, 1), (3, 0), (2, 0)]
         self.copies = {
             (which, slab): pltpu.make_async_copy(
                 args[which].at[slab], targets[which].at[slab], sems.at[index]
             )
             for index, (which, slab) in enumerate(order)
-            if which < 2 or slab in slabs
+            if (blocks if which < 2 else slab in couplers)
         }
         self.targets = targets
         for copy in self.copies.values():
@@ -160,6 +160,11 @@
         loads = Loads((green, sigma, coupling, pattern), scratch[:4], scratch[4], (1,))
         left_sources(loads, whole, None, None, *scratch[5:])
 
+    @pl.when((lax.axis_index("slab") > 0) & (parity() == 1))
+    def _():
+        loads = Loads((green, sigma, coupling, pattern), scratch[:4], scratch[4], (0,), False)
+        whole[...] = loads.coupler(0)
+
 
 def map_kernel(
     green, sigma, coupling, pattern,
@@ -197,9 +202,10 @@
 def prepare_kernel(count, *refs):
     arrived, wholes = refs[: count - 1], refs[count - 1 : 2 * count - 2]
     refs = refs[2 * count - 2 :]
-    start_whole, source, forward, backward, coupler, following = refs[:6]
-    lead, tail, constant, last_lead, last_tail = refs[6:11]
-    first_v, last_v, m_a, m_b, m_c, m_d = refs[11:]
+    start_whole, source, forward, backward, coupler = refs[:5]
+    followings = refs[5:7]
+    lead, tail, constant, last_lead, last_tail = refs[7:12]
+    first_v, last_v, m_a, m_b, m_c, m_d = refs[12:]
     place = lax.axis_index("slab")
 
     @pl.when(place == 0)
@@ -223,7 +229,7 @@
         first, last = first_v[...], last_v[...]
         through, joined = right_terms(first, last, coupler[...], m_a, m_b, m_c, m_d)
         constant[...] = joined
-        next_coupler = following[...]
+        next_coupler = jnp.where(parity() == 0, followings[0][...], followings[1][...])
         put(m_a, next_coupler)
         lead[0], lead[1] = split(times(through, m_a, True))
         last_lead[0], last_lead[1] = split(times(last, m_a, True))
@@ -350,7 +356,10 @@
     pairs = []
     for energy in range(energies):
         turn = step - energy % 2
-        if 0 <= turn <= count - 2:
+        if turn < 0:
+            pairs += [(energy * count + i, energy * count + i - 1) for i in range(1, count)]
+            continue
+        if turn <= count - 2:
             ends = (turn, turn + 1)
         elif count - 1 <= turn <= 2 * count - 3:
             ends = (2 * count - 2 - turn, 2 * count - 3 - turn)
@@ -418,10 +427,15 @@
         ends += made[1:]
         arrived.append(relay(step + 1, made[0]))
         if step == 0:
-            following = lax.ppermute(opening, "slab", [(i, i - 1) for i in range(1, count)])
+            down = [
+                (energy * count + i, energy * count + i - 1)
+                for energy in range(0, energies, 2)
+                for i in range(1, count)
+            ]
+            following = lax.ppermute(opening, ("energy", "slab"), down)
         if step == count - 2:
             args = arrived[: count - 1] + outs[: count - 1]
-            args += [whole, source, forward, backward, coupler, following]
+            args += [whole, source, forward, backward, coupler, following, arrived[0]]
             right_map = call(
                 functools.partial(prepare_kernel, count),
                 [lead, tail, row, lead, tail],

time: 138 us -> 126 us (0.913)
  waiting for transfers between devices: 74.1 us -> 64.4 us
  starting transfers between devices: 20.7 us -> 18 us
    ppermute x7, waiting for transfers between devices: 38.4 us -> 32.3 us  [relay(): lax.ppermute(value, ('energy', 'slab'), relay_pairs(step, energies, count))]
    ppermute x1, waiting for transfers between devices: 21.1 us -> 17.5 us  [shards(): following = lax.ppermute(opening, ('energy', 'slab'), down)]
    all_to_all x1, starting transfers between devices: 13.3 us -> 10.4 us  [shards(): lax.all_to_all(retarded, 'energy', split_axis=3, concat_axis=0, tiled=True)]
  transfers between devices with their start and end apart: 9 -> 9, of which waited for: 4 -> 4; matrix products, arithmetic and copies ran while one was open for 0% -> 0% of each run, Pallas kernels for 6% -> 7%
where the time goes in v1:
time: 126 us
  waiting for transfers between devices  64.4 us (51%)
  starting transfers between devices  18 us (14%)
  Pallas kernels  17.9 us (14%)
  blocking collectives  17.8 us (14%)
  local copies, waits for them, and re-layouts  5.09 us (4%)
  matrix products  1.48 us (1%)
    ppermute x7, waiting for transfers between devices, relay(): lax.ppermute(value, ('energy', 'slab'), relay_pairs(step, energies, count))  32.3 us
    pallas_call x10, Pallas kernels, call(): pl.pallas_call(kernel, out_shape=outs, in_specs=specs or [VMEM] * len(arg...  17.9 us
    all_to_all x1, blocking collectives, shards(): lax.all_to_all(mixed, 'energy', split_axis=0, concat_axis=3, tiled=True)  17.8 us
    ppermute x1, waiting for transfers between devices, shards(): following = lax.ppermute(opening, ('energy', 'slab'), down)  17.5 us
    all_to_all x1, waiting for transfers between devices, shards(): lax.all_to_all(retarded, 'energy', split_axis=3, concat_axis=0, tiled=True)  14.6 us
    all_to_all x1, starting transfers between devices, shards(): lax.all_to_all(retarded, 'energy', split_axis=3, concat_axis=0, tiled=True)  10.4 us
    ppermute x7, starting transfers between devices, relay(): lax.ppermute(value, ('energy', 'slab'), relay_pairs(step, energies, count))  6.27 us
    broadcast_in_dim x1, local copies, waits for them, and re-layouts, shards(): retarded = retarded[None]  3 us
  transfers between devices with their start and end apart: 9, of which 4 were waited for; matrix products, arithmetic and copies ran while one was open for 0% of the time, Pallas kernels for 7%

profile of v1, /device:TPU:0, one launch (start us, length us, event | category | flops | bytes accessed | tf_op | source)
XLA Modules:
  0.0 125.6 jit_solution(16748461538266594526)
XLA Ops:
  0.6 0.0 copy-start
  0.6 0.0 copy-start.1
  0.7 0.0 copy-start.2
  0.7 0.0 copy-start.3
  0.7 5.8 %source.1 = f32[256,512]{1,0:T(8,128)} custom-call(f32[2,2,256,256]{3,2,1,0:T(8,128)} %bitcast.19, f32[2,2,256,256]{3,2,1,0:T(8,128)} %bitcast.21, f32[2,2,256,256]{3,2,1,0:T(8,128)} %coupling.3, s32[2,16,16]{2,1,0:T(8,128)} %pattern.3), custom_call_target="tpu_custom_call" | custom-call | flops 2415919104 | bytes 1048576 | tf_op jit(solution)/shard_map/source/pallas_call | solution.py:85
  6.5 1.3 %collective-permute-start = (f32[256,512]{1,0:T(8,128)}, f32[256,512]{1,0:T(8,128)S(1)}, u32[]{:S(2)}, u32[]{:S(2)}) collective-permute-start(f32[256,512]{1,0:T(8,128)} %source.1), channel_id=1, source_target_pairs={{0,1},{5,4},{6,5},{7,6},{8,9},{13,12},{14,13},{15,14},{16,17},{21,... | collective-permute-start | bytes 1572872 | tf_op jit(solution)/shard_map/ppermute | solution.py:383
  7.8 0.0 copy-done
  7.8 0.0 copy-done.1
  7.8 0.0 copy-done.2
  7.8 0.0 copy-done.3
  7.8 4.4 %left_maps.1 = (f32[256,512]{1,0:T(8,128)S(1)}, f32[256,512]{1,0:T(8,128)S(1)}, f32[256,512]{1,0:T(8,128)S(1)}, f32[256,512]{1,0:T(8,128)S(1)}, bf16[2,256,512]{...) custom-call(f32[2,2,256,256]{3,2,1,0:T(8,128)S(1)} %bitcast.20, ...), custom_call_target="tpu_custom_call" | custom-call | flops 4831838208 | bytes 1048576 | tf_op jit(solution)/shard_map/left_maps/pallas_call | solution.py:85
  12.3 2.5 %collective-permute-done.refs_0_.refs_12_ = f32[256,512]{1,0:T(8,128)S(1)} collective-permute-done((f32[256,512]{1,0:T(8,128)}, f32[256,512]{1,0:T(8,128)S(1)}, u32[]{:S(2)}, u32[]{:S(2)}) %collective-permute-start) | collective-permute-done | bytes 524320 | tf_op jit(solution)/shard_map/ppermute | solution.py:383
  14.8 0.7 collective-permute-start.1
  15.5 0.0 collective-permute-done.1.refs_0_.refs_1_
  15.5 0.7 collective-permute-start.2
  16.2 1.3 %collective-permute-start.4 = (f32[256,512]{1,0:T(8,128)S(1)}, f32[256,512]{1,0:T(8,128)S(1)}, u32[]{:S(2)}, u32[]{:S(2)}) collective-permute-start(f32[256,512]{1,0:T(8,128)S(1)} %get-tuple-element.27), channel_id=1, source_target_pairs={{1,0},{2,1},{3,2},{9,8},{10,9},{11,10},{17,16},{18,17},{19,18},{25... | collective-permute-start | bytes 1572872 | tf_op jit(solution)/shard_map/ppermute | solution.py:435
  17.5 0.0 collective-permute-done.2.refs_0_.refs_2_
  17.6 0.9 collective-permute-start.3
  18.5 17.5 %collective-permute-done.4.refs_11_ = f32[256,512]{1,0:T(8,128)S(1)} collective-permute-done((f32[256,512]{1,0:T(8,128)S(1)}, f32[256,512]{1,0:T(8,128)S(1)}, u32[]{:S(2)}, u32[]{:S(2)}) %collective-permute-start.4) | collective-permute-done | bytes 524320 | tf_op jit(solution)/shard_map/ppermute | solution.py:435
  35.9 4.0 %right_maps.1 = (bf16[2,256,512]{2,1,0:T(8,128)(2,1)S(1)}, bf16[2,512,512]{2,1,0:T(8,128)(2,1)S(1)}, f32[256,512]{1,0:T(8,128)S(1)}, bf16[2,256,512]{2,1,0:T(8,128)(2,1)S(1)}, bf16[2,512,512]{2,1,0:T(8,128)(2,1)S(1)}) custom-call(f32[256,512]{1,0:T(8,128)S(1)} %collective-permute-done.refs_0_.refs_12_, ...), custom_call_target="tpu_custom_call" | custom-call | flops 4026531840 | bytes 1048576 | tf_op jit(solution)/shard_map/right_maps/pallas_call | solution.py:85
  39.9 0.0 collective-permute-done.3.refs_0_
  39.9 0.7 collective-permute-start.5
  40.6 0.0 collective-permute-done.5.refs_0_.refs_1_
  40.7 1.3 %collective-permute-start.6 = (f32[256,512]{1,0:T(8,128)S(1)}, f32[256,512]{1,0:T(8,128)S(1)}, u32[]{:S(2)}, u32[]{:S(2)}) collective-permute-start(f32[256,512]{1,0:T(8,128)S(1)} %relay.10.refs_6_), channel_id=1, source_target_pairs={{1,0},{6,5},{9,8},{14,13},{17,16},{22,21},{25,24},{30,29}} | collective-permute-start | bytes 1572872 | tf_op jit(solution)/shard_map/ppermute | solution.py:383
  42.0 29.8 %collective-permute-done.6.refs_0_.refs_2_ = f32[256,512]{1,0:T(8,128)S(1)} collective-permute-done((f32[256,512]{1,0:T(8,128)S(1)}, f32[256,512]{1,0:T(8,128)S(1)}, u32[]{:S(2)}, u32[]{:S(2)}) %collective-permute-start.6) | collective-permute-done | bytes 524320 | tf_op jit(solution)/shard_map/ppermute | solution.py:383
  71.7 1.1 relay.11.refs_7_
  72.8 0.7 collective-permute-start.7
  73.5 0.0 collective-permute-done.7.refs_3_
  73.5 2.6 %retarded.1 = f32[2,2,256,256]{3,2,1,0:T(8,128)} custom-call(f32[256,512]{1,0:T(8,128)S(1)} %collective-permute-done.3.refs_0_, f32[256,512]{1,0:T(8,128)S(1)} %collective-permute-done.5.refs_0_.refs_1_, f32[256,512]{1,0:T(8,128)S(1)} %collective-permute-done.6.refs_0_.refs_2_, f32[256,512]{1,0:T(8,128)S(1)} %collective-permute-done.7.refs_3_, ...), custom_call_target="tpu_custom_call" | custom-call | flops 1610612736 | bytes 1048576 | tf_op jit(solution)/shard_map/retarded/pallas_call | solution.py:85
  76.1 3.0 %copy.20 = f32[1,2,2,256,256]{4,2,1,0,3:T(2,128)} copy(f32[1,2,2,256,256]{4,3,2,1,0:T(8,128)} %bitcast.23) | data formatting | bytes 2097152 | tf_op jit(solution)/shard_map/broadcast_in_dim | solution.py:456
  79.1 0.0 copy-start.6
  79.1 10.4 %all-to-all-start = ((f32[1,2,2,256,256]{4,2,1,0,3:T(2,128)}), f32[1,2,2,256,256]{4,2,1,0,3:T(2,128)S(1)}, u32[]{:S(2)}, u32[]{:S(2)}) async-start(f32[1,2,2,256,256]{4,2,1,0,3:T(2,128)} %copy.20), calls=%async_computation | async-start | bytes 2097152 | tf_op jit(solution)/shard_map/all_to_all | solution.py:462
  89.5 0.0 copy-done.6
  89.5 0.0 copy-start.4
  89.5 0.0 copy-start.5
  89.5 0.6 copy-done.4
  90.2 0.0 copy-done.5
  90.2 0.1 add_reduce_fusion
  90.3 14.6 %all-to-all-done = f32[1,2,2,256,256]{4,2,1,0,3:T(2,128)S(1)} async-done(((f32[1,2,2,256,256]{4,2,1,0,3:T(2,128)}), f32[1,2,2,256,256]{4,2,1,0,3:T(2,128)S(1)}, u32[]{:S(2)}, u32[]{:S(2)}) %all-to-all-start) | async-done | bytes 1048608 | tf_op jit(solution)/shard_map/all_to_all | solution.py:462
  104.9 1.5 %fusion = f32[8,2,2,32,256]{4,0,3,2,1:T(8,128)S(1)} fusion(f32[1,2,2,8,32,256]{5,2,1,4,3,0:T(2,128)S(1)} %bitcast.25, f32[8,8]{1,0:T(8,128)S(1)} %add_reduce_fusion), kind=kOutput, calls=%fused_computation | convolution fusion | flops 25165824 | bytes 2097408 | tf_op jit(solution)/shard_map/ef,fsxab->esxab/dot_general | solution.py:459
  106.4 0.3 copy.23
  106.7 17.8 %all_to_all.36 = f32[8,2,2,32,256]{4,3,2,1,0:T(8,128)S(1)} all-to-all(f32[8,2,2,32,256]{4,3,2,1,0:T(8,128)S(1)} %copy.23), channel_id=1, replica_groups=mesh['energy'=8,'slab'=4] {'energy'}, dimensions={0} | all-to-all | bytes 2097152 | tf_op jit(solution)/shard_map/all_to_all | solution.py:465
  124.5 1.1 copy.24
  (7 shorter events, 0.1 us)
Async XLA Ops:
  0.6 7.2 %copy-start = (f32[1,2,2,256,256]{4,3,2,1,0:T(8,128)S(1)}, f32[1,2,2,256,256]{4,3,2,1,0:T(8,128)}, u32[]{:S(2)}) copy-start(f32[1,2,2,256,256]{4,3,2,1,0:T(8,128)} %param.7) | copy-start | bytes 3145732
  0.6 7.2 %copy-start.1 = (f32[1,2,2,256,256]{4,3,2,1,0:T(8,128)S(1)}, f32[1,2,2,256,256]{4,3,2,1,0:T(8,128)}, u32[]{:S(2)}) copy-start(f32[1,2,2,256,256]{4,3,2,1,0:T(8,128)} %param.8) | copy-start | bytes 3145732
  0.7 7.2 %copy-start.2 = (f32[2,2,256,256]{3,2,1,0:T(8,128)S(1)}, f32[2,2,256,256]{3,2,1,0:T(8,128)}, u32[]{:S(2)}) copy-start(f32[2,2,256,256]{3,2,1,0:T(8,128)} %coupling.3) | copy-start | bytes 3145732
  0.7 7.2 %copy-start.3 = (s32[2,16,16]{2,1,0:T(8,128)S(1)}, s32[2,16,16]{2,1,0:T(8,128)}, u32[]{:S(2)}) copy-start(s32[2,16,16]{2,1,0:T(8,128)} %pattern.3) | copy-start | bytes 6148
  6.5 8.3 %collective-permute-start = (f32[256,512]{1,0:T(8,128)}, f32[256,512]{1,0:T(8,128)S(1)}, u32[]{:S(2)}, u32[]{:S(2)}) collective-permute-start(f32[256,512]{1,0:T(8,128)} %source.1), channel_id=1, source_target_pairs={{0,1},{5,4},{6,5},{7,6},{8,9},{13,12},{14,13},{15,14},{16,17},{21,... | collective-permute-start | bytes 1572872 | tf_op jit(solution)/shard_map/ppermute | solution.py:383
  14.8 0.7 collective-permute-start.1
  15.5 2.0 %collective-permute-start.2 = (f32[256,512]{1,0:T(8,128)S(1)}, f32[256,512]{1,0:T(8,128)S(1)}, u32[]{:S(2)}, u32[]{:S(2)}) collective-permute-start(f32[256,512]{1,0:T(8,128)S(1)} %relay.7.refs_4_.refs_17_), channel_id=1, source_target_pairs={{2,3},{5,6},{10,11},{13,14},{18,19},{21,22},{26,27},{29,30}} | collective-permute-start | bytes 1572872 | tf_op jit(solution)/shard_map/ppermute | solution.py:383
  16.2 19.7 %collective-permute-start.4 = (f32[256,512]{1,0:T(8,128)S(1)}, f32[256,512]{1,0:T(8,128)S(1)}, u32[]{:S(2)}, u32[]{:S(2)}) collective-permute-start(f32[256,512]{1,0:T(8,128)S(1)} %get-tuple-element.27), channel_id=1, source_target_pairs={{1,0},{2,1},{3,2},{9,8},{10,9},{11,10},{17,16},{18,17},{19,18},{25... | collective-permute-start | bytes 1572872 | tf_op jit(solution)/shard_map/ppermute | solution.py:435
  17.6 22.3 %collective-permute-start.3 = (f32[256,512]{1,0:T(8,128)S(1)}, f32[256,512]{1,0:T(8,128)S(1)}, u32[]{:S(2)}, u32[]{:S(2)}) collective-permute-start(f32[256,512]{1,0:T(8,128)S(1)} %get-tuple-element.26.refs_5_.refs_4_.refs_18_), channel_id=1, source_target_pairs={{3,2},{6,7},{11,10},{14,15},{19,18},{22,23},{27,26},{30,31}} | collective-permute-start | bytes 1572872 | tf_op jit(solution)/shard_map/ppermute | solution.py:383
  39.9 0.7 collective-permute-start.5
  40.7 31.1 %collective-permute-start.6 = (f32[256,512]{1,0:T(8,128)S(1)}, f32[256,512]{1,0:T(8,128)S(1)}, u32[]{:S(2)}, u32[]{:S(2)}) collective-permute-start(f32[256,512]{1,0:T(8,128)S(1)} %relay.10.refs_6_), channel_id=1, source_target_pairs={{1,0},{6,5},{9,8},{14,13},{17,16},{22,21},{25,24},{30,29}} | collective-permute-start | bytes 1572872 | tf_op jit(solution)/shard_map/ppermute | solution.py:383
  72.8 0.7 collective-permute-start.7
  79.1 10.4 %copy-start.6 = (s32[4]{0:T(128)S(1)}, s32[4]{0:T(128)}, u32[]{:S(2)}) copy-start(s32[4]{0:T(128)} %param.11) | copy-start | bytes 52
  79.1 25.8 %all-to-all-start = ((f32[1,2,2,256,256]{4,2,1,0,3:T(2,128)}), f32[1,2,2,256,256]{4,2,1,0,3:T(2,128)S(1)}, u32[]{:S(2)}, u32[]{:S(2)}) async-start(f32[1,2,2,256,256]{4,2,1,0,3:T(2,128)} %copy.20), calls=%async_computation | async-start | bytes 2097152 | tf_op jit(solution)/shard_map/all_to_all | solution.py:462
  89.5 0.7 copy-start.4
  89.5 0.7 copy-start.5

commit v2 on v1

--- a/solution.py
+++ b/solution.py
@@ -11,6 +11,7 @@
 HALF = jnp.bfloat16
 HBM = pl.BlockSpec(memory_space=pltpu.HBM)
 VMEM = pl.BlockSpec(memory_space=pltpu.VMEM)
+SMEM = pl.BlockSpec(memory_space=pltpu.SMEM)
 
 
 def split(value):
@@ -297,7 +298,9 @@
     right_map = [refs.pop(0) for _ in range(3)]
     last_lead, last_tail, whole_start = [refs.pop(0) for _ in range(3)]
     wholes = [refs.pop(0) for _ in range(count - 1)]
-    retarded, out_v, whole_v, m_x = refs
+    retarded = refs.pop(0)
+    out_v, whole_v, m_x = refs[-3:]
+    parcels = refs[:-3]
     place = lax.axis_index("slab")
     core = parity()
     size = out_v.shape[0]
@@ -335,6 +338,44 @@
     for slab, block in enumerate((out_v, whole_v)):
         for part in range(2):
             retarded[slab, part] = block[:, part * size : (part + 1) * size]
+    for mask, parcel in enumerate(parcels):
+        for slab, block in enumerate((out_v, whole_v)):
+            parcel[slab] = block[share(mask, parcel.shape[1]), :]
+
+
+def share(mask, rows):
+    chip = lax.shift_right_logical(lax.axis_index("energy"), 1)
+    return pl.ds(pl.multiple_of(lax.bitwise_xor(chip, mask) * rows, rows), rows)
+
+
+def mix_kernel(chips, weights, *refs):
+    parcels, (mine, other) = refs[:chips], refs[chips:]
+    energy = lax.axis_index("energy")
+    core = lax.rem(energy, 2)
+    sources = [lax.bitwise_xor(energy, 2 * mask) for mask in range(chips)]
+    for mask in range(chips):
+        for target, out in ((sources[mask], mine), (sources[mask] + 1 - 2 * core, other)):
+            total = weights[target, sources[0]] * parcels[0][...]
+            for index in range(1, chips):
+                total += weights[target, sources[index]] * parcels[index][...]
+            out[mask] = total
+
+
+def sum_kernel(chips, mine, other, *outs):
+    for mask in range(chips):
+        outs[mask][...] = mine[mask] + other[mask]
+
+
+def place_kernel(chips, *refs):
+    parcels, scattering = refs[:chips], refs[chips]
+    size = scattering.shape[-1]
+    for mask, parcel in enumerate(parcels):
+        where = share(mask, parcel.shape[1])
+        for slab in range(2):
+            for part in range(2):
+                scattering[slab, part, where, :] = parcel[
+                    slab, :, part * size : (part + 1) * size
+                ]
 
 
 def mode_weights(targets, sources, offsets, emission, absorption):
@@ -445,25 +486,48 @@
                 name="right_maps",
             )
     args = arrived[count - 1 :] + outs[count - 2 :] + ends + right_map + [whole] + outs[: count - 1]
-    (retarded,) = call(
+    chips = energies // 2
+    parcel = shape(size // chips, 2 * size, F32, 2)
+    retarded, *parcels = call(
         functools.partial(finish_kernel, count),
-        [shape(size, size, F32, 2, 2)],
+        [shape(size, size, F32, 2, 2)] + [parcel] * chips,
         [row_v] * 2 + matrices(1, size),
         args,
         flops=4 * product,
         name="retarded",
     )
-    retarded = retarded[None]
+
+    def exchange(values):
+        return values[:1] + [
+            lax.ppermute(value, "energy", [(i, i ^ (2 * mask)) for i in range(energies)])
+            for mask, value in enumerate(values)
+            if mask
+        ]
+
     everyone = jnp.arange(energies, dtype=jnp.int32)
     weights = mode_weights(everyone, everyone, offsets, emission, absorption)
-    mixed = jnp.einsum(
-        "ef,fsxab->esxab",
-        weights,
-        lax.all_to_all(retarded, "energy", split_axis=3, concat_axis=0, tiled=True),
-        precision=lax.Precision.HIGHEST,
-    )
-    scattering = lax.all_to_all(mixed, "energy", split_axis=0, concat_axis=3, tiled=True)
-    return (retarded, scattering)
+    partial = shape(size // chips, 2 * size, F32, chips, 2)
+    mine, other = call(
+        functools.partial(mix_kernel, chips),
+        [partial] * 2,
+        [],
+        [weights] + exchange(parcels),
+        [SMEM] + [VMEM] * chips,
+        flops=product // 4,
+        name="mix",
+    )
+    other = lax.ppermute(other, "energy", [(i, i ^ 1) for i in range(energies)])
+    parcels = call(
+        functools.partial(sum_kernel, chips), [parcel] * chips, [], [mine, other], name="sum"
+    )
+    (scattering,) = call(
+        functools.partial(place_kernel, chips),
+        [shape(size, size, F32, 2, 2)],
+        [],
+        exchange(parcels),
+        name="scattering",
+    )
+    return (retarded[None], scattering[None])
 
 
 def solution(mesh):

time: 126 us -> 114 us (0.905)
  blocking collectives: 17.8 us -> 0 us
  waiting for transfers between devices: 64.4 us -> 72.7 us
  local copies, waits for them, and re-layouts: 5.09 us -> 0.77 us
  Pallas kernels: 17.9 us -> 20.3 us
  matrix products: 1.48 us -> 0 us
    ppermute x0 -> x7, waiting for transfers between devices: none -> 22.9 us  [the longest x6 20.7 us: exchange(): lax.ppermute(value, 'energy', [(i, i ^ 2 * mask) for i in range(energies)])]
    all_to_all x1 -> x0, blocking collectives: 17.8 us -> none  [shards(): lax.all_to_all(mixed, 'energy', split_axis=0, concat_axis=3, tiled=True)]
    all_to_all x1 -> x0, waiting for transfers between devices: 14.6 us -> none  [shards(): lax.all_to_all(retarded, 'energy', split_axis=3, concat_axis=0, tiled=True)]
    ppermute x0 -> x7, starting transfers between devices: none -> 11.1 us  [the longest x6 8.03 us: exchange(): lax.ppermute(value, 'energy', [(i, i ^ 2 * mask) for i in range(energies)])]
    all_to_all x1 -> x0, starting transfers between devices: 10.4 us -> none  [shards(): lax.all_to_all(retarded, 'energy', split_axis=3, concat_axis=0, tiled=True)]
    broadcast_in_dim x1 -> x0, local copies, waits for them, and re-layouts: 3 us -> none  [shards(): retarded = retarded[None]]
    pallas_call x10 -> x13, Pallas kernels: 17.9 us -> 20.3 us  [call(): pl.pallas_call(kernel, out_shape=outs, in_specs=specs or [VMEM] * len(arg...]
    dot_general x1 -> x0, matrix products: 1.48 us -> none  [shards(): jnp.einsum('ef,fsxab->esxab', weights, lax.all_to_all(retarded, 'energy',...]
  transfers between devices with their start and end apart: 9 -> 15, of which waited for: 4 -> 9; matrix products, arithmetic and copies ran while one was open for 0% -> 0% of each run, Pallas kernels for 7% -> 7%
where the time goes in v2:
time: 114 us; the launch traced here: 113 us
  waiting for transfers between devices  72.7 us (64%)
  Pallas kernels  20.3 us (18%)
  starting transfers between devices  18.7 us (16%)
    ppermute x7, waiting for transfers between devices, relay(): lax.ppermute(value, ('energy', 'slab'), relay_pairs(step, energies, count))  32.3 us
    ppermute x6, waiting for transfers between devices, exchange(): lax.ppermute(value, 'energy', [(i, i ^ 2 * mask) for i in range(energies)])  20.7 us
    pallas_call x13, Pallas kernels, call(): pl.pallas_call(kernel, out_shape=outs, in_specs=specs or [VMEM] * len(arg...  20.3 us
    ppermute x1, waiting for transfers between devices, shards(): following = lax.ppermute(opening, ('energy', 'slab'), down)  17.5 us
    ppermute x6, starting transfers between devices, exchange(): lax.ppermute(value, 'energy', [(i, i ^ 2 * mask) for i in range(energies)])  8.03 us
    ppermute x7, starting transfers between devices, relay(): lax.ppermute(value, ('energy', 'slab'), relay_pairs(step, energies, count))  6.27 us
    ppermute x1, starting transfers between devices, shards(): other = lax.ppermute(other, 'energy', [(i, i ^ 1) for i in range(energies)])  3.11 us
    ppermute x1, waiting for transfers between devices, shards(): other = lax.ppermute(other, 'energy', [(i, i ^ 1) for i in range(energies)])  2.29 us
  transfers between devices with their start and end apart: 15, of which 9 were waited for; matrix products, arithmetic and copies ran while one was open for 0% of the time, Pallas kernels for 7%

profile of v2, /device:TPU:0, one launch (start us, length us, event | category | flops | bytes accessed | tf_op | source)
XLA Modules:
  0.0 113.4 jit_solution(3991465227763075564)
XLA Ops:
  0.6 0.0 copy-start
  0.6 0.0 copy-start.1
  0.7 0.0 copy-start.2
  0.7 0.0 copy-start.3
  0.7 5.8 %source.1 = f32[256,512]{1,0:T(8,128)} custom-call(f32[2,2,256,256]{3,2,1,0:T(8,128)} %bitcast.4, f32[2,2,256,256]{3,2,1,0:T(8,128)} %bitcast.6, f32[2,2,256,256]{3,2,1,0:T(8,128)} %coupling.3, s32[2,16,16]{2,1,0:T(8,128)} %pattern.3), custom_call_target="tpu_custom_call" | custom-call | flops 2415919104 | bytes 1048576 | tf_op jit(solution)/shard_map/source/pallas_call | solution.py:86
  6.5 1.3 %collective-permute-start = (f32[256,512]{1,0:T(8,128)}, f32[256,512]{1,0:T(8,128)S(1)}, u32[]{:S(2)}, u32[]{:S(2)}) collective-permute-start(f32[256,512]{1,0:T(8,128)} %source.1), channel_id=1, source_target_pairs={{0,1},{5,4},{6,5},{7,6},{8,9},{13,12},{14,13},{15,14},{16,17},{21,... | collective-permute-start | bytes 1572872 | tf_op jit(solution)/shard_map/ppermute | solution.py:424
  7.8 0.0 copy-done
  7.8 0.0 copy-done.1
  7.8 0.0 copy-done.2
  7.8 0.0 copy-done.3
  7.8 4.4 %left_maps.1 = (f32[256,512]{1,0:T(8,128)S(1)}, f32[256,512]{1,0:T(8,128)S(1)}, f32[256,512]{1,0:T(8,128)S(1)}, f32[256,512]{1,0:T(8,128)S(1)}, bf16[2,256,512]{...) custom-call(f32[2,2,256,256]{3,2,1,0:T(8,128)S(1)} %bitcast.5, ...), custom_call_target="tpu_custom_call" | custom-call | flops 4831838208 | bytes 1048576 | tf_op jit(solution)/shard_map/left_maps/pallas_call | solution.py:86
  12.3 2.5 %collective-permute-done.refs_0_.refs_12_ = f32[256,512]{1,0:T(8,128)S(1)} collective-permute-done((f32[256,512]{1,0:T(8,128)}, f32[256,512]{1,0:T(8,128)S(1)}, u32[]{:S(2)}, u32[]{:S(2)}) %collective-permute-start) | collective-permute-done | bytes 524320 | tf_op jit(solution)/shard_map/ppermute | solution.py:424
  14.8 0.7 collective-permute-start.1
  15.5 0.0 collective-permute-done.1.refs_0_.refs_1_
  15.5 0.7 collective-permute-start.2
  16.2 1.3 %collective-permute-start.4 = (f32[256,512]{1,0:T(8,128)S(1)}, f32[256,512]{1,0:T(8,128)S(1)}, u32[]{:S(2)}, u32[]{:S(2)}) collective-permute-start(f32[256,512]{1,0:T(8,128)S(1)} %get-tuple-element.38), channel_id=1, source_target_pairs={{1,0},{2,1},{3,2},{9,8},{10,9},{11,10},{17,16},{18,17},{19,18},{25... | collective-permute-start | bytes 1572872 | tf_op jit(solution)/shard_map/ppermute | solution.py:476
  17.5 0.0 collective-permute-done.2.refs_0_.refs_2_
  17.6 0.9 collective-permute-start.3
  18.5 17.5 %collective-permute-done.4.refs_11_ = f32[256,512]{1,0:T(8,128)S(1)} collective-permute-done((f32[256,512]{1,0:T(8,128)S(1)}, f32[256,512]{1,0:T(8,128)S(1)}, u32[]{:S(2)}, u32[]{:S(2)}) %collective-permute-start.4) | collective-permute-done | bytes 524320 | tf_op jit(solution)/shard_map/ppermute | solution.py:476
  35.9 4.0 %right_maps.1 = (bf16[2,256,512]{2,1,0:T(8,128)(2,1)S(1)}, bf16[2,512,512]{2,1,0:T(8,128)(2,1)S(1)}, f32[256,512]{1,0:T(8,128)S(1)}, bf16[2,256,512]{2,1,0:T(8,128)(2,1)S(1)}, bf16[2,512,512]{2,1,0:T(8,128)(2,1)S(1)}) custom-call(f32[256,512]{1,0:T(8,128)S(1)} %collective-permute-done.refs_0_.refs_12_, ...), custom_call_target="tpu_custom_call" | custom-call | flops 4026531840 | bytes 1048576 | tf_op jit(solution)/shard_map/right_maps/pallas_call | solution.py:86
  39.9 0.0 collective-permute-done.3.refs_0_
  39.9 0.7 collective-permute-start.5
  40.6 0.0 collective-permute-done.5.refs_0_.refs_1_
  40.7 1.3 %collective-permute-start.6 = (f32[256,512]{1,0:T(8,128)S(1)}, f32[256,512]{1,0:T(8,128)S(1)}, u32[]{:S(2)}, u32[]{:S(2)}) collective-permute-start(f32[256,512]{1,0:T(8,128)S(1)} %relay.10.refs_6_), channel_id=1, source_target_pairs={{1,0},{6,5},{9,8},{14,13},{17,16},{22,21},{25,24},{30,29}} | collective-permute-start | bytes 1572872 | tf_op jit(solution)/shard_map/ppermute | solution.py:424
  42.0 29.8 %collective-permute-done.6.refs_0_.refs_2_ = f32[256,512]{1,0:T(8,128)S(1)} collective-permute-done((f32[256,512]{1,0:T(8,128)S(1)}, f32[256,512]{1,0:T(8,128)S(1)}, u32[]{:S(2)}, u32[]{:S(2)}) %collective-permute-start.6) | collective-permute-done | bytes 524320 | tf_op jit(solution)/shard_map/ppermute | solution.py:424
  71.7 1.1 relay.11.refs_7_
  72.8 0.7 collective-permute-start.7
  73.5 0.0 collective-permute-done.7.refs_3_
  73.5 2.6 %retarded.1 = (f32[2,2,256,256]{3,2,1,0:T(8,128)}, f32[2,64,512]{2,1,0:T(8,128)S(1)}, f32[2,64,512]{2,1,0:T(8,128)S(1)}, f32[2,64,512]{2,1,0:T(8,128)S(1)}, f32[2,64,512]{2,1,0:T(8,128)S(1)}) custom-call(f32[256,512]{1,0:T(8,128)S(1)} %collective-permute-done.3.refs_0_, f32[256,512]{1,0:T(8,128)S(1)} %collective-permute-done.5.refs_0_.refs_1_, ...), custom_call_target="tpu_custom_call" | custom-call | flops 1610612736 | bytes 1048576 | tf_op jit(solution)/shard_map/retarded/pallas_call | solution.py:86
  76.2 3.9 %collective-permute-start.10 = (f32[2,64,512]{2,1,0:T(8,128)S(1)}, f32[2,64,512]{2,1,0:T(8,128)S(1)}, u32[]{:S(2)}, u32[]{:S(2)}) collective-permute-start(f32[2,64,512]{2,1,0:T(8,128)S(1)} %get-tuple-element.51), channel_id=1, source_target_pairs={{0,24},{4,28},{8,16},{12,20},{16,8},{20,12},{24,0},{28,4},{1,25},{... | collective-permute-start | bytes 786440 | tf_op jit(solution)/shard_map/ppermute | solution.py:502
  80.1 0.0 copy-start.6
  80.1 0.5 collective-permute-start.8
  80.6 0.0 collective-permute-start.9
  80.6 0.1 copy-done.6
  80.7 0.0 copy-start.4
  80.7 0.0 copy-start.5
  80.7 0.6 copy-done.4
  81.4 0.0 copy-done.5
  81.4 0.1 add_reduce_fusion.weights
  81.5 3.0 %collective-permute-done.10.refs_3_ = f32[2,64,512]{2,1,0:T(8,128)S(1)} collective-permute-done((f32[2,64,512]{2,1,0:T(8,128)S(1)}, f32[2,64,512]{2,1,0:T(8,128)S(1)}, u32[]{:S(2)}, u32[]{:S(2)}) %collective-permute-start.10) | collective-permute-done | bytes 262176 | tf_op jit(solution)/shard_map/ppermute | solution.py:502
  84.4 4.4 %collective-permute-done.8.refs_1_ = f32[2,64,512]{2,1,0:T(8,128)S(1)} collective-permute-done((f32[2,64,512]{2,1,0:T(8,128)S(1)}, f32[2,64,512]{2,1,0:T(8,128)S(1)}, u32[]{:S(2)}, u32[]{:S(2)}) %collective-permute-start.8) | collective-permute-done | bytes 262176 | tf_op jit(solution)/shard_map/ppermute | solution.py:502
  88.9 1.4 %collective-permute-done.9.refs_2_ = f32[2,64,512]{2,1,0:T(8,128)S(1)} collective-permute-done((f32[2,64,512]{2,1,0:T(8,128)S(1)}, f32[2,64,512]{2,1,0:T(8,128)S(1)}, u32[]{:S(2)}, u32[]{:S(2)}) %collective-permute-start.9) | collective-permute-done | bytes 262176 | tf_op jit(solution)/shard_map/ppermute | solution.py:502
  90.2 1.1 mix.1
  91.3 3.1 %collective-permute-start.11 = (f32[4,2,64,512]{3,2,1,0:T(8,128)S(1)}, f32[4,2,64,512]{3,2,1,0:T(8,128)S(1)}, u32[]{:S(2)}, u32[]{:S(2)}) collective-permute-start(f32[4,2,64,512]{3,2,1,0:T(8,128)S(1)} %get-tuple-element.53), channel_id=1, source_target_pairs={{0,4},{4,0},{8,12},{12,8},{16,20},{20,16},{24,28},{28,24},{1,5},{5... | collective-permute-start | bytes 3145736 | tf_op jit(solution)/shard_map/ppermute | solution.py:519
  94.4 2.3 %collective-permute-done.11.other = f32[4,2,64,512]{3,2,1,0:T(8,128)S(1)} collective-permute-done((f32[4,2,64,512]{3,2,1,0:T(8,128)S(1)}, f32[4,2,64,512]{3,2,1,0:T(8,128)S(1)}, u32[]{:S(2)}, u32[]{:S(2)}) %collective-permute-start.11) | collective-permute-done | bytes 1048608 | tf_op jit(solution)/shard_map/ppermute | solution.py:519
  96.7 0.1 sum.1
  96.8 1.6 %collective-permute-start.12 = (f32[2,64,512]{2,1,0:T(8,128)S(1)}, f32[2,64,512]{2,1,0:T(8,128)S(1)}, u32[]{:S(2)}, u32[]{:S(2)}) collective-permute-start(f32[2,64,512]{2,1,0:T(8,128)S(1)} %get-tuple-element.55), channel_id=1, source_target_pairs={{0,8},{4,12},{8,0},{12,4},{16,24},{20,28},{24,16},{28,20},{1,9},{5... | collective-permute-start | bytes 786440 | tf_op jit(solution)/shard_map/ppermute | solution.py:502
  98.4 1.4 %collective-permute-start.13 = (f32[2,64,512]{2,1,0:T(8,128)S(1)}, f32[2,64,512]{2,1,0:T(8,128)S(1)}, u32[]{:S(2)}, u32[]{:S(2)}) collective-permute-start(f32[2,64,512]{2,1,0:T(8,128)S(1)} %get-tuple-element.56), channel_id=1, source_target_pairs={{0,16},{4,20},{8,24},{12,28},{16,0},{20,4},{24,8},{28,12},{1,17},{... | collective-permute-start | bytes 786440 | tf_op jit(solution)/shard_map/ppermute | solution.py:502
  99.8 0.6 collective-permute-start.14
  100.4 5.6 %collective-permute-done.12.refs_1_ = f32[2,64,512]{2,1,0:T(8,128)S(1)} collective-permute-done((f32[2,64,512]{2,1,0:T(8,128)S(1)}, f32[2,64,512]{2,1,0:T(8,128)S(1)}, u32[]{:S(2)}, u32[]{:S(2)}) %collective-permute-start.12) | collective-permute-done | bytes 262176 | tf_op jit(solution)/shard_map/ppermute | solution.py:502
  106.0 6.3 %collective-permute-done.13.refs_2_ = f32[2,64,512]{2,1,0:T(8,128)S(1)} collective-permute-done((f32[2,64,512]{2,1,0:T(8,128)S(1)}, f32[2,64,512]{2,1,0:T(8,128)S(1)}, u32[]{:S(2)}, u32[]{:S(2)}) %collective-permute-start.13) | collective-permute-done | bytes 262176 | tf_op jit(solution)/shard_map/ppermute | solution.py:502
  112.3 0.0 collective-permute-done.14.refs_3_
  112.3 1.1 scattering.1
  (7 shorter events, 0.1 us)
Async XLA Ops:
  0.6 7.2 %copy-start = (f32[1,2,2,256,256]{4,3,2,1,0:T(8,128)S(1)}, f32[1,2,2,256,256]{4,3,2,1,0:T(8,128)}, u32[]{:S(2)}) copy-start(f32[1,2,2,256,256]{4,3,2,1,0:T(8,128)} %param.7) | copy-start | bytes 3145732
  0.6 7.2 %copy-start.1 = (f32[1,2,2,256,256]{4,3,2,1,0:T(8,128)S(1)}, f32[1,2,2,256,256]{4,3,2,1,0:T(8,128)}, u32[]{:S(2)}) copy-start(f32[1,2,2,256,256]{4,3,2,1,0:T(8,128)} %param.8) | copy-start | bytes 3145732
  0.7 7.2 %copy-start.2 = (f32[2,2,256,256]{3,2,1,0:T(8,128)S(1)}, f32[2,2,256,256]{3,2,1,0:T(8,128)}, u32[]{:S(2)}) copy-start(f32[2,2,256,256]{3,2,1,0:T(8,128)} %coupling.3) | copy-start | bytes 3145732
  0.7 7.2 %copy-start.3 = (s32[2,16,16]{2,1,0:T(8,128)S(1)}, s32[2,16,16]{2,1,0:T(8,128)}, u32[]{:S(2)}) copy-start(s32[2,16,16]{2,1,0:T(8,128)} %pattern.3) | copy-start | bytes 6148
  6.5 8.3 %collective-permute-start = (f32[256,512]{1,0:T(8,128)}, f32[256,512]{1,0:T(8,128)S(1)}, u32[]{:S(2)}, u32[]{:S(2)}) collective-permute-start(f32[256,512]{1,0:T(8,128)} %source.1), channel_id=1, source_target_pairs={{0,1},{5,4},{6,5},{7,6},{8,9},{13,12},{14,13},{15,14},{16,17},{21,... | collective-permute-start | bytes 1572872 | tf_op jit(solution)/shard_map/ppermute | solution.py:424
  14.8 0.7 collective-permute-start.1
  15.5 2.0 %collective-permute-start.2 = (f32[256,512]{1,0:T(8,128)S(1)}, f32[256,512]{1,0:T(8,128)S(1)}, u32[]{:S(2)}, u32[]{:S(2)}) collective-permute-start(f32[256,512]{1,0:T(8,128)S(1)} %relay.7.refs_4_.refs_17_), channel_id=1, source_target_pairs={{2,3},{5,6},{10,11},{13,14},{18,19},{21,22},{26,27},{29,30}} | collective-permute-start | bytes 1572872 | tf_op jit(solution)/shard_map/ppermute | solution.py:424
  16.2 19.7 %collective-permute-start.4 = (f32[256,512]{1,0:T(8,128)S(1)}, f32[256,512]{1,0:T(8,128)S(1)}, u32[]{:S(2)}, u32[]{:S(2)}) collective-permute-start(f32[256,512]{1,0:T(8,128)S(1)} %get-tuple-element.38), channel_id=1, source_target_pairs={{1,0},{2,1},{3,2},{9,8},{10,9},{11,10},{17,16},{18,17},{19,18},{25... | collective-permute-start | bytes 1572872 | tf_op jit(solution)/shard_map/ppermute | solution.py:476
  17.6 22.3 %collective-permute-start.3 = (f32[256,512]{1,0:T(8,128)S(1)}, f32[256,512]{1,0:T(8,128)S(1)}, u32[]{:S(2)}, u32[]{:S(2)}) collective-permute-start(f32[256,512]{1,0:T(8,128)S(1)} %get-tuple-element.37.refs_5_.refs_4_.refs_18_), channel_id=1, source_target_pairs={{3,2},{6,7},{11,10},{14,15},{19,18},{22,23},{27,26},{30,31}} | collective-permute-start | bytes 1572872 | tf_op jit(solution)/shard_map/ppermute | solution.py:424
  39.9 0.7 collective-permute-start.5
  40.7 31.1 %collective-permute-start.6 = (f32[256,512]{1,0:T(8,128)S(1)}, f32[256,512]{1,0:T(8,128)S(1)}, u32[]{:S(2)}, u32[]{:S(2)}) collective-permute-start(f32[256,512]{1,0:T(8,128)S(1)} %relay.10.refs_6_), channel_id=1, source_target_pairs={{1,0},{6,5},{9,8},{14,13},{17,16},{22,21},{25,24},{30,29}} | collective-permute-start | bytes 1572872 | tf_op jit(solution)/shard_map/ppermute | solution.py:424
  72.8 0.7 collective-permute-start.7
  76.2 8.3 %collective-permute-start.10 = (f32[2,64,512]{2,1,0:T(8,128)S(1)}, f32[2,64,512]{2,1,0:T(8,128)S(1)}, u32[]{:S(2)}, u32[]{:S(2)}) collective-permute-start(f32[2,64,512]{2,1,0:T(8,128)S(1)} %get-tuple-element.51), channel_id=1, source_target_pairs={{0,24},{4,28},{8,16},{12,20},{16,8},{20,12},{24,0},{28,4},{1,25},{... | collective-permute-start | bytes 786440 | tf_op jit(solution)/shard_map/ppermute | solution.py:502
  80.1 0.7 copy-start.6
  80.1 8.8 %collective-permute-start.8 = (f32[2,64,512]{2,1,0:T(8,128)S(1)}, f32[2,64,512]{2,1,0:T(8,128)S(1)}, u32[]{:S(2)}, u32[]{:S(2)}) collective-permute-start(f32[2,64,512]{2,1,0:T(8,128)S(1)} %get-tuple-element.49), channel_id=1, source_target_pairs={{0,8},{4,12},{8,0},{12,4},{16,24},{20,28},{24,16},{28,20},{1,9},{5... | collective-permute-start | bytes 786440 | tf_op jit(solution)/shard_map/ppermute | solution.py:502
  80.6 9.6 %collective-permute-start.9 = (f32[2,64,512]{2,1,0:T(8,128)S(1)}, f32[2,64,512]{2,1,0:T(8,128)S(1)}, u32[]{:S(2)}, u32[]{:S(2)}) collective-permute-start(f32[2,64,512]{2,1,0:T(8,128)S(1)} %get-tuple-element.50), channel_id=1, source_target_pairs={{0,16},{4,20},{8,24},{12,28},{16,0},{20,4},{24,8},{28,12},{1,17},{... | collective-permute-start | bytes 786440 | tf_op jit(solution)/shard_map/ppermute | solution.py:502
  80.7 0.7 copy-start.4
  80.7 0.7 copy-start.5
  91.3 5.4 %collective-permute-start.11 = (f32[4,2,64,512]{3,2,1,0:T(8,128)S(1)}, f32[4,2,64,512]{3,2,1,0:T(8,128)S(1)}, u32[]{:S(2)}, u32[]{:S(2)}) collective-permute-start(f32[4,2,64,512]{3,2,1,0:T(8,128)S(1)} %get-tuple-element.53), channel_id=1, source_target_pairs={{0,4},{4,0},{8,12},{12,8},{16,20},{20,16},{24,28},{28,24},{1,5},{5... | collective-permute-start | bytes 3145736 | tf_op jit(solution)/shard_map/ppermute | solution.py:519
  96.8 9.2 %collective-permute-start.12 = (f32[2,64,512]{2,1,0:T(8,128)S(1)}, f32[2,64,512]{2,1,0:T(8,128)S(1)}, u32[]{:S(2)}, u32[]{:S(2)}) collective-permute-start(f32[2,64,512]{2,1,0:T(8,128)S(1)} %get-tuple-element.55), channel_id=1, source_target_pairs={{0,8},{4,12},{8,0},{12,4},{16,24},{20,28},{24,16},{28,20},{1,9},{5... | collective-permute-start | bytes 786440 | tf_op jit(solution)/shard_map/ppermute | solution.py:502
  98.4 13.9 %collective-permute-start.13 = (f32[2,64,512]{2,1,0:T(8,128)S(1)}, f32[2,64,512]{2,1,0:T(8,128)S(1)}, u32[]{:S(2)}, u32[]{:S(2)}) collective-permute-start(f32[2,64,512]{2,1,0:T(8,128)S(1)} %get-tuple-element.56), channel_id=1, source_target_pairs={{0,16},{4,20},{8,24},{12,28},{16,0},{20,4},{24,8},{28,12},{1,17},{... | collective-permute-start | bytes 786440 | tf_op jit(solution)/shard_map/ppermute | solution.py:502
  99.8 12.5 %collective-permute-start.14 = (f32[2,64,512]{2,1,0:T(8,128)S(1)}, f32[2,64,512]{2,1,0:T(8,128)S(1)}, u32[]{:S(2)}, u32[]{:S(2)}) collective-permute-start(f32[2,64,512]{2,1,0:T(8,128)S(1)} %get-tuple-element.57), channel_id=1, source_target_pairs={{0,24},{4,28},{8,16},{12,20},{16,8},{20,12},{24,0},{28,4},{1,25},{... | collective-permute-start | bytes 786440 | tf_op jit(solution)/shard_map/ppermute | solution.py:502

commit v3 on v2

--- a/solution.py
+++ b/solution.py
@@ -24,27 +24,31 @@
     return lax.dot_general(left, right, dims, preferred_element_type=F32)
 
 
-def put(matrix, block):
+def parts_of(block, adjoint=False):
     size = block.shape[0]
-    for level, part in enumerate(split(block)):
-        real, imag = part[:, :size], part[:, size:]
-        matrix[level, :size, :size] = real
-        matrix[level, :size, size:] = imag
-        matrix[level, size:, :size] = -imag
-        matrix[level, size:, size:] = real
-
-
-def times_split(high, low, matrix, transposed=False):
-    return (
-        dot(high, matrix[0], transposed)
-        + dot(low, matrix[0], transposed)
-        + dot(high, matrix[1], transposed)
-    )
+    real, imag = block[:, :size], block[:, size:]
+    return real, imag, (real - imag if adjoint else real + imag)
+
+
+def put(matrix, block, adjoint=False):
+    for index, part in enumerate(parts_of(block, adjoint)):
+        matrix[0, index], matrix[1, index] = split(part)
+
+
+def times_split(left, matrix, transposed=False):
+    products = []
+    for index, (high, low) in enumerate(left):
+        size = high.shape[0]
+        both = dot(jnp.concatenate([high, low], axis=0), matrix[0, index], transposed)
+        products.append(both[:size] + both[size:] + dot(high, matrix[1, index], transposed))
+    first, second, third = products
+    if transposed:
+        return jnp.concatenate([first + second, third - first + second], axis=1)
+    return jnp.concatenate([first - second, third - first - second], axis=1)
 
 
 def times(block, matrix, transposed=False):
-    high, low = split(block)
-    return times_split(high, low, matrix, transposed)
+    return times_split([split(part) for part in parts_of(block)], matrix, transposed)
 
 
 def row_form(pair):
@@ -79,7 +83,7 @@
 
 
 def matrices(number, size):
-    return [pltpu.VMEM((2, 2 * size, 2 * size), HALF)] * number
+    return [pltpu.VMEM((2, 3, size, size), HALF)] * number
 
 
 def call(kernel, outs, scratch, args, specs=None, flops=0, name=None, limit=40):
@@ -146,7 +150,7 @@
     coupler = loads.coupler(1)
     if coupler_out is not None:
         coupler_out[...] = coupler
-    put(m_c, coupler)
+    put(m_c, coupler, True)
     inner = loads.sigma(1) + times(times(coupler, m_a), m_c, True)
     put(m_a, inner)
     second = loads.green(1)
@@ -179,20 +183,21 @@
     @pl.when(lax.axis_index("slab") > 0)
     def _():
         opening[...] = before
-        put(m_a, before)
-        ahead = times(first, m_a)
-        forward[...] = ahead
-        put(m_a, ahead)
-        lead[0], lead[1] = split(times(times(second, m_c), m_a))
         put(m_a, first)
         size = before.shape[0]
         behind = times(adjoint_row((before[:, :size], before[:, size:])), m_a)
         backward[...] = behind
         put(tail, times(times(behind, m_c, True), m_b))
+        put(m_a, before)
+        ahead = times(first, m_a)
+        forward[...] = ahead
+        put(m_a, ahead)
+        put(m_c, coupler[...])
+        put(lead, times(times(second, m_c), m_a))
 
 
 def right_terms(first, last, coupler, m_coupler, m_first, m_last, m_upper):
-    put(m_coupler, coupler)
+    put(m_coupler, coupler, True)
     put(m_last, last)
     through = times(times(first, m_coupler, True), m_last)
     put(m_first, first)
@@ -231,9 +236,9 @@
         through, joined = right_terms(first, last, coupler[...], m_a, m_b, m_c, m_d)
         constant[...] = joined
         next_coupler = jnp.where(parity() == 0, followings[0][...], followings[1][...])
-        put(m_a, next_coupler)
-        lead[0], lead[1] = split(times(through, m_a, True))
-        last_lead[0], last_lead[1] = split(times(last, m_a, True))
+        put(m_a, next_coupler, True)
+        put(lead, times(through, m_a, True))
+        put(last_lead, times(last, m_a, True))
         behind = times(next_coupler, m_c)
         put(last_tail, behind)
         put(tail, times(behind, m_d))
@@ -241,7 +246,8 @@
 
 def apply_map(mapping, m_x):
     lead, tail, constant = mapping
-    return constant[...] + times(times_split(lead[0], lead[1], m_x), tail)
+    ahead = [(lead[0, index], lead[1, index]) for index in range(3)]
+    return constant[...] + times(times_split(ahead, m_x), tail)
 
 
 def relay_kernel(step, count, lefts, rights, *refs):
@@ -414,8 +420,7 @@
     size, blocks = free_green.shape[-1], pattern.shape[-1]
     args = (free_green[0], self_energy[0], coupling, pattern)
     row = shape(size, 2 * size)
-    lead = shape(size, 2 * size, HALF, 2)
-    tail = shape(2 * size, 2 * size, HALF, 2)
+    factor = shape(size, size, HALF, 2, 3)
     row_v = pltpu.VMEM(row.shape, F32)
     product = 24 * size**3
     loading = load_scratch(size, blocks) + matrices(3, size)
@@ -436,7 +441,7 @@
     arrived, outs, ends = [relay(0, begun[0])], [], []
     whole, source, coupler, opening, left_lead, left_tail, forward, backward = call(
         map_kernel,
-        [row] * 4 + [lead, tail, row, row],
+        [row] * 4 + [factor, factor, row, row],
         loading,
         args,
         [HBM] * 4,
@@ -479,7 +484,7 @@
             args += [whole, source, forward, backward, coupler, following, arrived[0]]
             right_map = call(
                 functools.partial(prepare_kernel, count),
-                [lead, tail, row, lead, tail],
+                [factor, factor, row, factor, factor],
                 [row_v] * 2 + matrices(4, size),
                 args,
                 flops=10 * product,

time: 114 us -> 111 us (0.974)
  Pallas kernels: 20.3 us -> 18.3 us
  starting transfers between devices: 18.7 us -> 17.3 us
    pallas_call x13, Pallas kernels: 20.3 us -> 18.3 us  [call(): pl.pallas_call(kernel, out_shape=outs, in_specs=specs or [VMEM] * len(arg...]
    ppermute x1, starting transfers between devices: 3.11 us -> 1.58 us  [shards(): other = lax.ppermute(other, 'energy', [(i, i ^ 1) for i in range(energies)])]
    ppermute x6, waiting for transfers between devices: 20.7 us -> 22.1 us  [exchange(): lax.ppermute(value, 'energy', [(i, i ^ 2 * mask) for i in range(energies)])]
where the time goes in v3:
time: 111 us
  waiting for transfers between devices  73.8 us (66%)
  Pallas kernels  18.3 us (16%)
  starting transfers between devices  17.3 us (16%)
    ppermute x7, waiting for transfers between devices, relay(): lax.ppermute(value, ('energy', 'slab'), relay_pairs(step, energies, count))  32.2 us
    ppermute x6, waiting for transfers between devices, exchange(): lax.ppermute(value, 'energy', [(i, i ^ 2 * mask) for i in range(energies)])  22.1 us
    pallas_call x13, Pallas kernels, call(): pl.pallas_call(kernel, out_shape=outs, in_specs=specs or [VMEM] * len(arg...  18.3 us
    ppermute x1, waiting for transfers between devices, shards(): following = lax.ppermute(opening, ('energy', 'slab'), down)  17.3 us
    ppermute x6, starting transfers between devices, exchange(): lax.ppermute(value, 'energy', [(i, i ^ 2 * mask) for i in range(energies)])  8.3 us
    ppermute x7, starting transfers between devices, relay(): lax.ppermute(value, ('energy', 'slab'), relay_pairs(step, energies, count))  6.09 us
    ppermute x1, waiting for transfers between devices, shards(): other = lax.ppermute(other, 'energy', [(i, i ^ 1) for i in range(energies)])  2.29 us
  transfers between devices with their start and end apart: 15, of which 9 were waited for; matrix products, arithmetic and copies ran while one was open for 0% of the time, Pallas kernels for 7%

profile of v3, /device:TPU:0, one launch (start us, length us, event | category | flops | bytes accessed | tf_op | source)
XLA Modules:
  0.0 111.2 jit_solution(8967239751387566413)
XLA Ops:
  0.6 0.0 copy-start
  0.6 0.0 copy-start.1
  0.7 0.0 copy-start.2
  0.7 0.0 copy-start.3
  0.7 5.3 %source.1 = f32[256,512]{1,0:T(8,128)} custom-call(f32[2,2,256,256]{3,2,1,0:T(8,128)} %bitcast.4, f32[2,2,256,256]{3,2,1,0:T(8,128)} %bitcast.6, f32[2,2,256,256]{3,2,1,0:T(8,128)} %coupling.3, s32[2,16,16]{2,1,0:T(8,128)} %pattern.3), custom_call_target="tpu_custom_call" | custom-call | flops 2415919104 | bytes 1048576 | tf_op jit(solution)/shard_map/source/pallas_call | solution.py:90
  5.9 1.3 %collective-permute-start = (f32[256,512]{1,0:T(8,128)}, f32[256,512]{1,0:T(8,128)S(1)}, u32[]{:S(2)}, u32[]{:S(2)}) collective-permute-start(f32[256,512]{1,0:T(8,128)} %source.1), channel_id=1, source_target_pairs={{0,1},{5,4},{6,5},{7,6},{8,9},{13,12},{14,13},{15,14},{16,17},{21,... | collective-permute-start | bytes 1572872 | tf_op jit(solution)/shard_map/ppermute | solution.py:429
  7.3 0.0 copy-done
  7.3 0.0 copy-done.1
  7.3 0.0 copy-done.2
  7.3 0.0 copy-done.3
  7.3 3.9 %left_maps.1 = (f32[256,512]{1,0:T(8,128)S(1)}, f32[256,512]{1,0:T(8,128)S(1)}, f32[256,512]{1,0:T(8,128)S(1)}, f32[256,512]{1,0:T(8,128)S(1)}, bf16[2,3,256,256...) custom-call(f32[2,2,256,256]{3,2,1,0:T(8,128)S(1)} %bitcast.5, ...), custom_call_target="tpu_custom_call" | custom-call | flops 4831838208 | bytes 1048576 | tf_op jit(solution)/shard_map/left_maps/pallas_call | solution.py:90
  11.2 3.0 %collective-permute-done.refs_0_.refs_12_ = f32[256,512]{1,0:T(8,128)S(1)} collective-permute-done((f32[256,512]{1,0:T(8,128)}, f32[256,512]{1,0:T(8,128)S(1)}, u32[]{:S(2)}, u32[]{:S(2)}) %collective-permute-start) | collective-permute-done | bytes 524320 | tf_op jit(solution)/shard_map/ppermute | solution.py:429
  14.3 0.7 collective-permute-start.1
  15.0 0.0 collective-permute-done.1.refs_0_.refs_1_
  15.0 0.7 collective-permute-start.2
  15.7 1.3 %collective-permute-start.4 = (f32[256,512]{1,0:T(8,128)S(1)}, f32[256,512]{1,0:T(8,128)S(1)}, u32[]{:S(2)}, u32[]{:S(2)}) collective-permute-start(f32[256,512]{1,0:T(8,128)S(1)} %get-tuple-element.38), channel_id=1, source_target_pairs={{1,0},{2,1},{3,2},{9,8},{10,9},{11,10},{17,16},{18,17},{19,18},{25... | collective-permute-start | bytes 1572872 | tf_op jit(solution)/shard_map/ppermute | solution.py:481
  17.0 0.0 collective-permute-done.2.refs_0_.refs_2_
  17.0 0.2 relay.8
  17.2 0.7 collective-permute-start.3
  17.9 17.3 %collective-permute-done.4.refs_11_ = f32[256,512]{1,0:T(8,128)S(1)} collective-permute-done((f32[256,512]{1,0:T(8,128)S(1)}, f32[256,512]{1,0:T(8,128)S(1)}, u32[]{:S(2)}, u32[]{:S(2)}) %collective-permute-start.4) | collective-permute-done | bytes 524320 | tf_op jit(solution)/shard_map/ppermute | solution.py:481
  35.2 3.3 %right_maps.1 = (bf16[2,3,256,256]{3,2,1,0:T(8,128)(2,1)S(1)}, bf16[2,3,256,256]{3,2,1,0:T(8,128)(2,1)S(1)}, f32[256,512]{1,0:T(8,128)S(1)}, bf16[2,3,256,256]{3...) custom-call(f32[256,512]{1,0:T(8,128)S(1)} %collective-permute-done.refs_0_.refs_12_, ...), custom_call_target="tpu_custom_call" | custom-call | flops 4026531840 | bytes 1048576 | tf_op jit(solution)/shard_map/right_maps/pallas_call | solution.py:90
  38.5 0.0 collective-permute-done.3.refs_0_
  38.6 0.7 collective-permute-start.5
  39.3 0.0 collective-permute-done.5.refs_0_.refs_1_
  39.3 1.3 %collective-permute-start.6 = (f32[256,512]{1,0:T(8,128)S(1)}, f32[256,512]{1,0:T(8,128)S(1)}, u32[]{:S(2)}, u32[]{:S(2)}) collective-permute-start(f32[256,512]{1,0:T(8,128)S(1)} %relay.10.refs_6_), channel_id=1, source_target_pairs={{1,0},{6,5},{9,8},{14,13},{17,16},{22,21},{25,24},{30,29}} | collective-permute-start | bytes 1572872 | tf_op jit(solution)/shard_map/ppermute | solution.py:429
  40.6 29.1 %collective-permute-done.6.refs_0_.refs_2_ = f32[256,512]{1,0:T(8,128)S(1)} collective-permute-done((f32[256,512]{1,0:T(8,128)S(1)}, f32[256,512]{1,0:T(8,128)S(1)}, u32[]{:S(2)}, u32[]{:S(2)}) %collective-permute-start.6) | collective-permute-done | bytes 524320 | tf_op jit(solution)/shard_map/ppermute | solution.py:429
  69.7 0.9 relay.11.refs_7_
  70.6 0.7 collective-permute-start.7
  71.3 0.0 collective-permute-done.7.refs_3_
  71.3 2.4 %retarded.1 = (f32[2,2,256,256]{3,2,1,0:T(8,128)}, f32[2,64,512]{2,1,0:T(8,128)S(1)}, f32[2,64,512]{2,1,0:T(8,128)S(1)}, f32[2,64,512]{2,1,0:T(8,128)S(1)}, f32[2,64,512]{2,1,0:T(8,128)S(1)}) custom-call(f32[256,512]{1,0:T(8,128)S(1)} %collective-permute-done.3.refs_0_, f32[256,512]{1,0:T(8,128)S(1)} %collective-permute-done.5.refs_0_.refs_1_, ...), custom_call_target="tpu_custom_call" | custom-call | flops 1610612736 | bytes 1048576 | tf_op jit(solution)/shard_map/retarded/pallas_call | solution.py:90
  73.7 4.2 %collective-permute-start.10 = (f32[2,64,512]{2,1,0:T(8,128)S(1)}, f32[2,64,512]{2,1,0:T(8,128)S(1)}, u32[]{:S(2)}, u32[]{:S(2)}) collective-permute-start(f32[2,64,512]{2,1,0:T(8,128)S(1)} %get-tuple-element.51), channel_id=1, source_target_pairs={{0,24},{4,28},{8,16},{12,20},{16,8},{20,12},{24,0},{28,4},{1,25},{... | collective-permute-start | bytes 786440 | tf_op jit(solution)/shard_map/ppermute | solution.py:507
  77.9 0.0 copy-start.6
  77.9 0.5 collective-permute-start.8
  78.4 0.1 collective-permute-start.9
  78.5 0.1 copy-done.6
  78.6 0.0 copy-start.4
  78.6 0.0 copy-start.5
  78.6 0.6 copy-done.4
  79.2 0.0 copy-done.5
  79.2 0.1 add_reduce_fusion.weights
  79.3 3.0 %collective-permute-done.10.refs_3_ = f32[2,64,512]{2,1,0:T(8,128)S(1)} collective-permute-done((f32[2,64,512]{2,1,0:T(8,128)S(1)}, f32[2,64,512]{2,1,0:T(8,128)S(1)}, u32[]{:S(2)}, u32[]{:S(2)}) %collective-permute-start.10) | collective-permute-done | bytes 262176 | tf_op jit(solution)/shard_map/ppermute | solution.py:507
  82.3 5.7 %collective-permute-done.8.refs_1_ = f32[2,64,512]{2,1,0:T(8,128)S(1)} collective-permute-done((f32[2,64,512]{2,1,0:T(8,128)S(1)}, f32[2,64,512]{2,1,0:T(8,128)S(1)}, u32[]{:S(2)}, u32[]{:S(2)}) %collective-permute-start.8) | collective-permute-done | bytes 262176 | tf_op jit(solution)/shard_map/ppermute | solution.py:507
  88.0 1.5 %collective-permute-done.9.refs_2_ = f32[2,64,512]{2,1,0:T(8,128)S(1)} collective-permute-done((f32[2,64,512]{2,1,0:T(8,128)S(1)}, f32[2,64,512]{2,1,0:T(8,128)S(1)}, u32[]{:S(2)}, u32[]{:S(2)}) %collective-permute-start.9) | collective-permute-done | bytes 262176 | tf_op jit(solution)/shard_map/ppermute | solution.py:507
  89.5 1.1 mix.1
  90.6 1.6 %collective-permute-start.11 = (f32[4,2,64,512]{3,2,1,0:T(8,128)S(1)}, f32[4,2,64,512]{3,2,1,0:T(8,128)S(1)}, u32[]{:S(2)}, u32[]{:S(2)}) collective-permute-start(f32[4,2,64,512]{3,2,1,0:T(8,128)S(1)} %get-tuple-element.53), channel_id=1, source_target_pairs={{0,4},{4,0},{8,12},{12,8},{16,20},{20,16},{24,28},{28,24},{1,5},{5... | collective-permute-start | bytes 3145736 | tf_op jit(solution)/shard_map/ppermute | solution.py:524
  92.2 2.3 %collective-permute-done.11.other = f32[4,2,64,512]{3,2,1,0:T(8,128)S(1)} collective-permute-done((f32[4,2,64,512]{3,2,1,0:T(8,128)S(1)}, f32[4,2,64,512]{3,2,1,0:T(8,128)S(1)}, u32[]{:S(2)}, u32[]{:S(2)}) %collective-permute-start.11) | collective-permute-done | bytes 1048608 | tf_op jit(solution)/shard_map/ppermute | solution.py:524
  94.5 0.1 sum.1
  94.6 1.6 %collective-permute-start.12 = (f32[2,64,512]{2,1,0:T(8,128)S(1)}, f32[2,64,512]{2,1,0:T(8,128)S(1)}, u32[]{:S(2)}, u32[]{:S(2)}) collective-permute-start(f32[2,64,512]{2,1,0:T(8,128)S(1)} %get-tuple-element.55), channel_id=1, source_target_pairs={{0,8},{4,12},{8,0},{12,4},{16,24},{20,28},{24,16},{28,20},{1,9},{5... | collective-permute-start | bytes 786440 | tf_op jit(solution)/shard_map/ppermute | solution.py:507
  96.2 1.4 %collective-permute-start.13 = (f32[2,64,512]{2,1,0:T(8,128)S(1)}, f32[2,64,512]{2,1,0:T(8,128)S(1)}, u32[]{:S(2)}, u32[]{:S(2)}) collective-permute-start(f32[2,64,512]{2,1,0:T(8,128)S(1)} %get-tuple-element.56), channel_id=1, source_target_pairs={{0,16},{4,20},{8,24},{12,28},{16,0},{20,4},{24,8},{28,12},{1,17},{... | collective-permute-start | bytes 786440 | tf_op jit(solution)/shard_map/ppermute | solution.py:507
  97.6 0.6 collective-permute-start.14
  98.2 5.6 %collective-permute-done.12.refs_1_ = f32[2,64,512]{2,1,0:T(8,128)S(1)} collective-permute-done((f32[2,64,512]{2,1,0:T(8,128)S(1)}, f32[2,64,512]{2,1,0:T(8,128)S(1)}, u32[]{:S(2)}, u32[]{:S(2)}) %collective-permute-start.12) | collective-permute-done | bytes 262176 | tf_op jit(solution)/shard_map/ppermute | solution.py:507
  103.8 6.3 %collective-permute-done.13.refs_2_ = f32[2,64,512]{2,1,0:T(8,128)S(1)} collective-permute-done((f32[2,64,512]{2,1,0:T(8,128)S(1)}, f32[2,64,512]{2,1,0:T(8,128)S(1)}, u32[]{:S(2)}, u32[]{:S(2)}) %collective-permute-start.13) | collective-permute-done | bytes 262176 | tf_op jit(solution)/shard_map/ppermute | solution.py:507
  110.1 0.0 collective-permute-done.14.refs_3_
  110.1 1.1 scattering.1
  (6 shorter events, 0.1 us)
Async XLA Ops:
  0.6 6.6 %copy-start = (f32[1,2,2,256,256]{4,3,2,1,0:T(8,128)S(1)}, f32[1,2,2,256,256]{4,3,2,1,0:T(8,128)}, u32[]{:S(2)}) copy-start(f32[1,2,2,256,256]{4,3,2,1,0:T(8,128)} %param.7) | copy-start | bytes 3145732
  0.6 6.6 %copy-start.1 = (f32[1,2,2,256,256]{4,3,2,1,0:T(8,128)S(1)}, f32[1,2,2,256,256]{4,3,2,1,0:T(8,128)}, u32[]{:S(2)}) copy-start(f32[1,2,2,256,256]{4,3,2,1,0:T(8,128)} %param.8) | copy-start | bytes 3145732
  0.7 6.6 %copy-start.2 = (f32[2,2,256,256]{3,2,1,0:T(8,128)S(1)}, f32[2,2,256,256]{3,2,1,0:T(8,128)}, u32[]{:S(2)}) copy-start(f32[2,2,256,256]{3,2,1,0:T(8,128)} %coupling.3) | copy-start | bytes 3145732
  0.7 6.6 %copy-start.3 = (s32[2,16,16]{2,1,0:T(8,128)S(1)}, s32[2,16,16]{2,1,0:T(8,128)}, u32[]{:S(2)}) copy-start(s32[2,16,16]{2,1,0:T(8,128)} %pattern.3) | copy-start | bytes 6148
  5.9 8.3 %collective-permute-start = (f32[256,512]{1,0:T(8,128)}, f32[256,512]{1,0:T(8,128)S(1)}, u32[]{:S(2)}, u32[]{:S(2)}) collective-permute-start(f32[256,512]{1,0:T(8,128)} %source.1), channel_id=1, source_target_pairs={{0,1},{5,4},{6,5},{7,6},{8,9},{13,12},{14,13},{15,14},{16,17},{21,... | collective-permute-start | bytes 1572872 | tf_op jit(solution)/shard_map/ppermute | solution.py:429
  14.3 0.7 collective-permute-start.1
  15.0 2.0 %collective-permute-start.2 = (f32[256,512]{1,0:T(8,128)S(1)}, f32[256,512]{1,0:T(8,128)S(1)}, u32[]{:S(2)}, u32[]{:S(2)}) collective-permute-start(f32[256,512]{1,0:T(8,128)S(1)} %relay.7.refs_4_.refs_17_), channel_id=1, source_target_pairs={{2,3},{5,6},{10,11},{13,14},{18,19},{21,22},{26,27},{29,30}} | collective-permute-start | bytes 1572872 | tf_op jit(solution)/shard_map/ppermute | solution.py:429
  15.7 19.5 %collective-permute-start.4 = (f32[256,512]{1,0:T(8,128)S(1)}, f32[256,512]{1,0:T(8,128)S(1)}, u32[]{:S(2)}, u32[]{:S(2)}) collective-permute-start(f32[256,512]{1,0:T(8,128)S(1)} %get-tuple-element.38), channel_id=1, source_target_pairs={{1,0},{2,1},{3,2},{9,8},{10,9},{11,10},{17,16},{18,17},{19,18},{25... | collective-permute-start | bytes 1572872 | tf_op jit(solution)/shard_map/ppermute | solution.py:481
  17.2 21.3 %collective-permute-start.3 = (f32[256,512]{1,0:T(8,128)S(1)}, f32[256,512]{1,0:T(8,128)S(1)}, u32[]{:S(2)}, u32[]{:S(2)}) collective-permute-start(f32[256,512]{1,0:T(8,128)S(1)} %get-tuple-element.37.refs_5_.refs_4_.refs_18_), channel_id=1, source_target_pairs={{3,2},{6,7},{11,10},{14,15},{19,18},{22,23},{27,26},{30,31}} | collective-permute-start | bytes 1572872 | tf_op jit(solution)/shard_map/ppermute | solution.py:429
  38.6 0.7 collective-permute-start.5
  39.3 30.4 %collective-permute-start.6 = (f32[256,512]{1,0:T(8,128)S(1)}, f32[256,512]{1,0:T(8,128)S(1)}, u32[]{:S(2)}, u32[]{:S(2)}) collective-permute-start(f32[256,512]{1,0:T(8,128)S(1)} %relay.10.refs_6_), channel_id=1, source_target_pairs={{1,0},{6,5},{9,8},{14,13},{17,16},{22,21},{25,24},{30,29}} | collective-permute-start | bytes 1572872 | tf_op jit(solution)/shard_map/ppermute | solution.py:429
  70.6 0.7 collective-permute-start.7
  73.7 8.5 %collective-permute-start.10 = (f32[2,64,512]{2,1,0:T(8,128)S(1)}, f32[2,64,512]{2,1,0:T(8,128)S(1)}, u32[]{:S(2)}, u32[]{:S(2)}) collective-permute-start(f32[2,64,512]{2,1,0:T(8,128)S(1)} %get-tuple-element.51), channel_id=1, source_target_pairs={{0,24},{4,28},{8,16},{12,20},{16,8},{20,12},{24,0},{28,4},{1,25},{... | collective-permute-start | bytes 786440 | tf_op jit(solution)/shard_map/ppermute | solution.py:507
  77.9 0.7 copy-start.6
  77.9 10.1 %collective-permute-start.8 = (f32[2,64,512]{2,1,0:T(8,128)S(1)}, f32[2,64,512]{2,1,0:T(8,128)S(1)}, u32[]{:S(2)}, u32[]{:S(2)}) collective-permute-start(f32[2,64,512]{2,1,0:T(8,128)S(1)} %get-tuple-element.49), channel_id=1, source_target_pairs={{0,8},{4,12},{8,0},{12,4},{16,24},{20,28},{24,16},{28,20},{1,9},{5... | collective-permute-start | bytes 786440 | tf_op jit(solution)/shard_map/ppermute | solution.py:507
  78.4 11.1 %collective-permute-start.9 = (f32[2,64,512]{2,1,0:T(8,128)S(1)}, f32[2,64,512]{2,1,0:T(8,128)S(1)}, u32[]{:S(2)}, u32[]{:S(2)}) collective-permute-start(f32[2,64,512]{2,1,0:T(8,128)S(1)} %get-tuple-element.50), channel_id=1, source_target_pairs={{0,16},{4,20},{8,24},{12,28},{16,0},{20,4},{24,8},{28,12},{1,17},{... | collective-permute-start | bytes 786440 | tf_op jit(solution)/shard_map/ppermute | solution.py:507
  78.6 0.7 copy-start.4
  78.6 0.7 copy-start.5
  90.6 3.9 %collective-permute-start.11 = (f32[4,2,64,512]{3,2,1,0:T(8,128)S(1)}, f32[4,2,64,512]{3,2,1,0:T(8,128)S(1)}, u32[]{:S(2)}, u32[]{:S(2)}) collective-permute-start(f32[4,2,64,512]{3,2,1,0:T(8,128)S(1)} %get-tuple-element.53), channel_id=1, source_target_pairs={{0,4},{4,0},{8,12},{12,8},{16,20},{20,16},{24,28},{28,24},{1,5},{5... | collective-permute-start | bytes 3145736 | tf_op jit(solution)/shard_map/ppermute | solution.py:524
  94.6 9.2 %collective-permute-start.12 = (f32[2,64,512]{2,1,0:T(8,128)S(1)}, f32[2,64,512]{2,1,0:T(8,128)S(1)}, u32[]{:S(2)}, u32[]{:S(2)}) collective-permute-start(f32[2,64,512]{2,1,0:T(8,128)S(1)} %get-tuple-element.55), channel_id=1, source_target_pairs={{0,8},{4,12},{8,0},{12,4},{16,24},{20,28},{24,16},{28,20},{1,9},{5... | collective-permute-start | bytes 786440 | tf_op jit(solution)/shard_map/ppermute | solution.py:507
  96.2 13.9 %collective-permute-start.13 = (f32[2,64,512]{2,1,0:T(8,128)S(1)}, f32[2,64,512]{2,1,0:T(8,128)S(1)}, u32[]{:S(2)}, u32[]{:S(2)}) collective-permute-start(f32[2,64,512]{2,1,0:T(8,128)S(1)} %get-tuple-element.56), channel_id=1, source_target_pairs={{0,16},{4,20},{8,24},{12,28},{16,0},{20,4},{24,8},{28,12},{1,17},{... | collective-permute-start | bytes 786440 | tf_op jit(solution)/shard_map/ppermute | solution.py:507
  97.6 12.5 %collective-permute-start.14 = (f32[2,64,512]{2,1,0:T(8,128)S(1)}, f32[2,64,512]{2,1,0:T(8,128)S(1)}, u32[]{:S(2)}, u32[]{:S(2)}) collective-permute-start(f32[2,64,512]{2,1,0:T(8,128)S(1)} %get-tuple-element.57), channel_id=1, source_target_pairs={{0,24},{4,28},{8,16},{12,20},{16,8},{20,12},{24,0},{28,4},{1,25},{... | collective-permute-start | bytes 786440 | tf_op jit(solution)/shard_map/ppermute | solution.py:507

commit v4 on v3

--- a/solution.py
+++ b/solution.py
@@ -296,57 +296,74 @@
             out[...] = apply_map(right_map, m_x)
 
 
-def finish_kernel(count, *refs):
+def last_kernel(count, *refs):
     refs = list(refs)
     arrived = [refs.pop(0) for _ in range(count)]
-    outs = [refs.pop(0) for _ in range(count)]
     ends = [refs.pop(0) for _ in range(2)]
-    right_map = [refs.pop(0) for _ in range(3)]
     last_lead, last_tail, whole_start = [refs.pop(0) for _ in range(3)]
     wholes = [refs.pop(0) for _ in range(count - 1)]
-    retarded = refs.pop(0)
-    out_v, whole_v, m_x = refs[-3:]
-    parcels = refs[:-3]
+    block, *parcels, m_x = refs
     place = lax.axis_index("slab")
     core = parity()
-    size = out_v.shape[0]
     is_last = place == count - 1
-    at = jnp.where(is_last, count - 2 + core, 2 * count - 3 - place + core)
-    late = (place == 0) & (core == 1)
 
     for index in range(count):
-        @pl.when(at == count - 1 + index)
+        @pl.when(jnp.logical_not(is_last) & (2 * count - 3 - place + core == count - 1 + index))
         def _(index=index):
             put(m_x, arrived[index][...])
-
-        @pl.when(at == count - 2 + index)
-        def _(index=index):
-            out_v[...] = outs[index][...]
 
     for index in range(2):
         @pl.when(is_last & (core == index))
         def _(index=index):
-            whole_v[...] = ends[index][...]
-
-    @pl.when(late)
-    def _():
-        out_v[...] = apply_map(right_map, m_x)
+            block[...] = ends[index][...]
 
     @pl.when(place == 0)
     def _():
-        whole_v[...] = apply_map((last_lead, last_tail, whole_start), m_x)
+        block[...] = apply_map((last_lead, last_tail, whole_start), m_x)
 
     for index in range(count - 1):
         @pl.when((place > 0) & jnp.logical_not(is_last) & (place - 1 + core == index))
         def _(index=index):
-            whole_v[...] = apply_map((last_lead, last_tail, wholes[index]), m_x)
-
-    for slab, block in enumerate((out_v, whole_v)):
+            block[...] = apply_map((last_lead, last_tail, wholes[index]), m_x)
+
+    pack(block, parcels)
+
+
+def first_kernel(count, *refs):
+    refs = list(refs)
+    arrived = refs.pop(0)
+    outs = [refs.pop(0) for _ in range(count)]
+    right_map = [refs.pop(0) for _ in range(3)]
+    refs.pop(0)
+    block, *parcels, m_x = refs
+    place = lax.axis_index("slab")
+    core = parity()
+    at = jnp.where(place == count - 1, count - 2 + core, 2 * count - 3 - place + core)
+
+    for index in range(count):
+        @pl.when(at == count - 2 + index)
+        def _(index=index):
+            block[...] = outs[index][...]
+
+    @pl.when((place == 0) & (core == 1))
+    def _():
+        put(m_x, arrived[...])
+        block[...] = apply_map(right_map, m_x)
+
+    pack(block, parcels)
+
+
+def pack(block, parcels):
+    for mask, parcel in enumerate(parcels):
+        parcel[...] = block[share(mask, parcel.shape[0]), :]
+
+
+def unpack_kernel(*refs):
+    blocks, out = refs[:2], refs[2]
+    size = out.shape[-1]
+    for slab, block in enumerate(blocks):
         for part in range(2):
-            retarded[slab, part] = block[:, part * size : (part + 1) * size]
-    for mask, parcel in enumerate(parcels):
-        for slab, block in enumerate((out_v, whole_v)):
-            parcel[slab] = block[share(mask, parcel.shape[1]), :]
+            out[slab, part] = block[:, part * size : (part + 1) * size]
 
 
 def share(mask, rows):
@@ -373,15 +390,13 @@
 
 
 def place_kernel(chips, *refs):
-    parcels, scattering = refs[:chips], refs[chips]
+    scattering = refs[2 * chips]
     size = scattering.shape[-1]
-    for mask, parcel in enumerate(parcels):
-        where = share(mask, parcel.shape[1])
-        for slab in range(2):
+    for slab in range(2):
+        for mask, parcel in enumerate(refs[slab * chips : (slab + 1) * chips]):
+            where = share(mask, parcel.shape[0])
             for part in range(2):
-                scattering[slab, part, where, :] = parcel[
-                    slab, :, part * size : (part + 1) * size
-                ]
+                scattering[slab, part, where, :] = parcel[:, part * size : (part + 1) * size]
 
 
 def mode_weights(targets, sources, offsets, emission, absorption):
@@ -490,16 +505,29 @@
                 flops=10 * product,
                 name="right_maps",
             )
-    args = arrived[count - 1 :] + outs[count - 2 :] + ends + right_map + [whole] + outs[: count - 1]
     chips = energies // 2
-    parcel = shape(size // chips, 2 * size, F32, 2)
-    retarded, *parcels = call(
-        functools.partial(finish_kernel, count),
-        [shape(size, size, F32, 2, 2)] + [parcel] * chips,
-        [row_v] * 2 + matrices(1, size),
+    parcel = shape(size // chips, 2 * size)
+    blocks, parcels = [None, None], [None, None]
+    args = arrived[count - 1 :] + ends + right_map[3:] + [whole] + outs[: count - 1]
+    blocks[1], *parcels[1] = call(
+        functools.partial(last_kernel, count),
+        [row] + [parcel] * chips,
+        matrices(1, size),
         args,
-        flops=4 * product,
-        name="retarded",
+        flops=2 * product,
+        name="second_slab",
+    )
+    args = arrived[-1:] + outs[count - 2 :] + right_map[:3] + blocks[1:]
+    blocks[0], *parcels[0] = call(
+        functools.partial(first_kernel, count),
+        [row] + [parcel] * chips,
+        matrices(1, size),
+        args,
+        flops=2 * product,
+        name="first_slab",
+    )
+    (retarded,) = call(
+        unpack_kernel, [shape(size, size, F32, 2, 2)], [], blocks, name="retarded"
     )
 
     def exchange(values):
@@ -511,25 +539,28 @@
 
     everyone = jnp.arange(energies, dtype=jnp.int32)
     weights = mode_weights(everyone, everyone, offsets, emission, absorption)
-    partial = shape(size // chips, 2 * size, F32, chips, 2)
-    mine, other = call(
-        functools.partial(mix_kernel, chips),
-        [partial] * 2,
-        [],
-        [weights] + exchange(parcels),
-        [SMEM] + [VMEM] * chips,
-        flops=product // 4,
-        name="mix",
-    )
-    other = lax.ppermute(other, "energy", [(i, i ^ 1) for i in range(energies)])
-    parcels = call(
-        functools.partial(sum_kernel, chips), [parcel] * chips, [], [mine, other], name="sum"
-    )
+    partial = shape(size // chips, 2 * size, F32, chips)
+    sums = [None, None]
+    for slab in (1, 0):
+        mine, other = call(
+            functools.partial(mix_kernel, chips),
+            [partial] * 2,
+            [],
+            [weights] + exchange(parcels[slab]),
+            [SMEM] + [VMEM] * chips,
+            flops=product // 8,
+            name="mix",
+        )
+        other = lax.ppermute(other, "energy", [(i, i ^ 1) for i in range(energies)])
+        sums[slab] = call(
+            functools.partial(sum_kernel, chips), [parcel] * chips, [], [mine, other], name="sum"
+        )
+    returned = [exchange(sums[slab]) for slab in (1, 0)][::-1]
     (scattering,) = call(
         functools.partial(place_kernel, chips),
         [shape(size, size, F32, 2, 2)],
         [],
-        exchange(parcels),
+        returned[0] + returned[1],
         name="scattering",
     )
     return (retarded[None], scattering[None])

time: 111 us -> 109 us (0.982)
  waiting for transfers between devices: 73.8 us -> 61.6 us
  starting transfers between devices: 17.3 us -> 26.8 us
    ppermute x6 -> x12, waiting for transfers between devices: 22.1 us -> 12.2 us  [exchange(): lax.ppermute(value, 'energy', [(i, i ^ 2 * mask) for i in range(energies)])]
    ppermute x6 -> x12, starting transfers between devices: 8.3 us -> 15 us  [exchange(): lax.ppermute(value, 'energy', [(i, i ^ 2 * mask) for i in range(energies)])]
    ppermute x1 -> x2, starting transfers between devices: 1.58 us -> 4.47 us  [shards(): other = lax.ppermute(other, 'energy', [(i, i ^ 1) for i in range(energies)])]
    ppermute x1 -> x2, waiting for transfers between devices: 2.29 us -> 0.01 us  [shards(): other = lax.ppermute(other, 'energy', [(i, i ^ 1) for i in range(energies)])]
    pallas_call x13 -> x17, Pallas kernels: 18.3 us -> 19 us  [call(): pl.pallas_call(kernel, out_shape=outs, in_specs=specs or [VMEM] * len(arg...]
  transfers between devices with their start and end apart: 15 -> 22, of which waited for: 9 -> 11; matrix products, arithmetic and copies ran while one was open for 0% -> 0% of each run, Pallas kernels for 7% -> 10%
where the time goes in v4:
time: 109 us; the launch traced here: 108 us
  waiting for transfers between devices  61.6 us (57%)
  starting transfers between devices  26.8 us (25%)
  Pallas kernels  19 us (17%)
    ppermute x7, waiting for transfers between devices, relay(): lax.ppermute(value, ('energy', 'slab'), relay_pairs(step, energies, count))  32.2 us
    pallas_call x17, Pallas kernels, call(): pl.pallas_call(kernel, out_shape=outs, in_specs=specs or [VMEM] * len(arg...  19 us
    ppermute x1, waiting for transfers between devices, shards(): following = lax.ppermute(opening, ('energy', 'slab'), down)  17.3 us
    ppermute x12, starting transfers between devices, exchange(): lax.ppermute(value, 'energy', [(i, i ^ 2 * mask) for i in range(energies)])  15 us
    ppermute x12, waiting for transfers between devices, exchange(): lax.ppermute(value, 'energy', [(i, i ^ 2 * mask) for i in range(energies)])  12.2 us
    ppermute x7, starting transfers between devices, relay(): lax.ppermute(value, ('energy', 'slab'), relay_pairs(step, energies, count))  6.09 us
    ppermute x2, starting transfers between devices, shards(): other = lax.ppermute(other, 'energy', [(i, i ^ 1) for i in range(energies)])  4.47 us
  transfers between devices with their start and end apart: 22, of which 11 were waited for; matrix products, arithmetic and copies ran while one was open for 0% of the time, Pallas kernels for 10%

profile of v4, /device:TPU:0, one launch (start us, length us, event | category | flops | bytes accessed | tf_op | source)
XLA Modules:
  0.0 108.5 jit_solution(3693313353546166281)
XLA Ops:
  0.6 0.0 copy-start
  0.6 0.0 copy-start.1
  0.7 0.0 copy-start.2
  0.7 0.0 copy-start.3
  0.7 5.3 %source.1 = f32[256,512]{1,0:T(8,128)} custom-call(f32[2,2,256,256]{3,2,1,0:T(8,128)} %bitcast.4, f32[2,2,256,256]{3,2,1,0:T(8,128)} %bitcast.6, f32[2,2,256,256]{3,2,1,0:T(8,128)} %coupling.3, s32[2,16,16]{2,1,0:T(8,128)} %pattern.3), custom_call_target="tpu_custom_call" | custom-call | flops 2415919104 | bytes 1048576 | tf_op jit(solution)/shard_map/source/pallas_call | solution.py:90
  5.9 1.3 %collective-permute-start = (f32[256,512]{1,0:T(8,128)}, f32[256,512]{1,0:T(8,128)S(1)}, u32[]{:S(2)}, u32[]{:S(2)}) collective-permute-start(f32[256,512]{1,0:T(8,128)} %source.1), channel_id=1, source_target_pairs={{0,1},{5,4},{6,5},{7,6},{8,9},{13,12},{14,13},{15,14},{16,17},{21,... | collective-permute-start | bytes 1572872 | tf_op jit(solution)/shard_map/ppermute | solution.py:444
  7.3 0.0 copy-done
  7.3 3.9 %left_maps.1 = (f32[256,512]{1,0:T(8,128)S(1)}, f32[256,512]{1,0:T(8,128)S(1)}, f32[256,512]{1,0:T(8,128)S(1)}, f32[256,512]{1,0:T(8,128)S(1)}, bf16[2,3,256,256...) custom-call(f32[2,2,256,256]{3,2,1,0:T(8,128)S(1)} %bitcast.5, ...), custom_call_target="tpu_custom_call" | custom-call | flops 4831838208 | bytes 1048576 | tf_op jit(solution)/shard_map/left_maps/pallas_call | solution.py:90
  11.2 3.0 %collective-permute-done.refs_0_.refs_12_ = f32[256,512]{1,0:T(8,128)S(1)} collective-permute-done((f32[256,512]{1,0:T(8,128)}, f32[256,512]{1,0:T(8,128)S(1)}, u32[]{:S(2)}, u32[]{:S(2)}) %collective-permute-start) | collective-permute-done | bytes 524320 | tf_op jit(solution)/shard_map/ppermute | solution.py:444
  14.3 0.7 collective-permute-start.1
  15.0 0.0 collective-permute-done.1.refs_0_.refs_1_
  15.0 0.7 collective-permute-start.2
  15.7 1.3 %collective-permute-start.4 = (f32[256,512]{1,0:T(8,128)S(1)}, f32[256,512]{1,0:T(8,128)S(1)}, u32[]{:S(2)}, u32[]{:S(2)}) collective-permute-start(f32[256,512]{1,0:T(8,128)S(1)} %get-tuple-element.49), channel_id=1, source_target_pairs={{1,0},{2,1},{3,2},{9,8},{10,9},{11,10},{17,16},{18,17},{19,18},{25... | collective-permute-start | bytes 1572872 | tf_op jit(solution)/shard_map/ppermute | solution.py:496
  17.0 0.0 collective-permute-done.2.refs_0_.refs_2_
  17.0 0.2 relay.8
  17.2 0.7 collective-permute-start.3
  17.9 17.3 %collective-permute-done.4.refs_11_ = f32[256,512]{1,0:T(8,128)S(1)} collective-permute-done((f32[256,512]{1,0:T(8,128)S(1)}, f32[256,512]{1,0:T(8,128)S(1)}, u32[]{:S(2)}, u32[]{:S(2)}) %collective-permute-start.4) | collective-permute-done | bytes 524320 | tf_op jit(solution)/shard_map/ppermute | solution.py:496
  35.2 3.3 %right_maps.1 = (bf16[2,3,256,256]{3,2,1,0:T(8,128)(2,1)S(1)}, bf16[2,3,256,256]{3,2,1,0:T(8,128)(2,1)S(1)}, f32[256,512]{1,0:T(8,128)S(1)}, bf16[2,3,256,256]{3...) custom-call(f32[256,512]{1,0:T(8,128)S(1)} %collective-permute-done.refs_0_.refs_12_, ...), custom_call_target="tpu_custom_call" | custom-call | flops 4026531840 | bytes 1048576 | tf_op jit(solution)/shard_map/right_maps/pallas_call | solution.py:90
  38.5 0.0 collective-permute-done.3.refs_0_
  38.6 0.7 collective-permute-start.5
  39.3 0.0 collective-permute-done.5.refs_0_.refs_1_
  39.3 1.3 %collective-permute-start.6 = (f32[256,512]{1,0:T(8,128)S(1)}, f32[256,512]{1,0:T(8,128)S(1)}, u32[]{:S(2)}, u32[]{:S(2)}) collective-permute-start(f32[256,512]{1,0:T(8,128)S(1)} %relay.10.refs_3_), channel_id=1, source_target_pairs={{1,0},{6,5},{9,8},{14,13},{17,16},{22,21},{25,24},{30,29}} | collective-permute-start | bytes 1572872 | tf_op jit(solution)/shard_map/ppermute | solution.py:444
  40.6 29.1 %collective-permute-done.6.refs_0_.refs_2_ = f32[256,512]{1,0:T(8,128)S(1)} collective-permute-done((f32[256,512]{1,0:T(8,128)S(1)}, f32[256,512]{1,0:T(8,128)S(1)}, u32[]{:S(2)}, u32[]{:S(2)}) %collective-permute-start.6) | collective-permute-done | bytes 524320 | tf_op jit(solution)/shard_map/ppermute | solution.py:444
  69.7 0.9 relay.11.refs_4_
  70.6 0.7 collective-permute-start.7
  71.3 0.0 collective-permute-done.7.refs_3_.refs_0_
  71.3 1.3 %second_slab.1 = (f32[256,512]{1,0:T(8,128)S(1)}, f32[64,512]{1,0:T(8,128)S(1)}, f32[64,512]{1,0:T(8,128)S(1)}, f32[64,512]{1,0:T(8,128)S(1)}, f32[64,512]{1,0:T(8,128)S(1)}) custom-call(f32[256,512]{1,0:T(8,128)S(1)} %collective-permute-done.3.refs_0_, f32[256,512]{1,0:T(8,128)S(1)} %collective-permute-done.5.refs_0_.refs_1_, ...), custom_call_target="tpu_custom_call" | custom-call | flops 805306368 | bytes 1048576 | tf_op jit(solution)/shard_map/second_slab/pallas_call | solution.py:90
  72.6 0.0 copy-start.6
  72.6 3.3 %collective-permute-start.15 = (f32[64,512]{1,0:T(8,128)S(1)}, f32[64,512]{1,0:T(8,128)S(1)}, u32[]{:S(2)}, u32[]{:S(2)}) collective-permute-start(f32[64,512]{1,0:T(8,128)S(1)} %get-tuple-element.71), channel_id=1, source_target_pairs={{0,8},{4,12},{8,0},{12,4},{16,24},{20,28},{24,16},{28,20},{1,9},{5... | collective-permute-start | bytes 393224 | tf_op jit(solution)/shard_map/ppermute | solution.py:535
  75.9 1.6 %collective-permute-start.16 = (f32[64,512]{1,0:T(8,128)S(1)}, f32[64,512]{1,0:T(8,128)S(1)}, u32[]{:S(2)}, u32[]{:S(2)}) collective-permute-start(f32[64,512]{1,0:T(8,128)S(1)} %get-tuple-element.72), channel_id=1, source_target_pairs={{0,16},{4,20},{8,24},{12,28},{16,0},{20,4},{24,8},{28,12},{1,17},{... | collective-permute-start | bytes 393224 | tf_op jit(solution)/shard_map/ppermute | solution.py:535
  77.5 0.4 collective-permute-start.17
  77.9 0.1 first_slab.1
  78.0 2.6 %collective-permute-start.10 = (f32[64,512]{1,0:T(8,128)S(1)}, f32[64,512]{1,0:T(8,128)S(1)}, u32[]{:S(2)}, u32[]{:S(2)}) collective-permute-start(f32[64,512]{1,0:T(8,128)S(1)} %get-tuple-element.63), channel_id=1, source_target_pairs={{0,24},{4,28},{8,16},{12,20},{16,8},{20,12},{24,0},{28,4},{1,25},{... | collective-permute-start | bytes 393224 | tf_op jit(solution)/shard_map/ppermute | solution.py:535
  80.6 0.5 collective-permute-start.8
  81.1 0.0 collective-permute-done.15.refs_1_
  81.1 0.5 collective-permute-start.9
  81.6 0.1 add_reduce_fusion.weights
  81.7 0.0 collective-permute-done.16.refs_2_
  81.7 2.7 %collective-permute-done.17.refs_3_ = f32[64,512]{1,0:T(8,128)S(1)} collective-permute-done((f32[64,512]{1,0:T(8,128)S(1)}, f32[64,512]{1,0:T(8,128)S(1)}, u32[]{:S(2)}, u32[]{:S(2)}) %collective-permute-start.17) | collective-permute-done | bytes 131104 | tf_op jit(solution)/shard_map/ppermute | solution.py:535
  84.4 0.9 mix.3
  85.3 4.3 %collective-permute-start.18 = (f32[4,64,512]{2,1,0:T(8,128)S(1)}, f32[4,64,512]{2,1,0:T(8,128)S(1)}, u32[]{:S(2)}, u32[]{:S(2)}) collective-permute-start(f32[4,64,512]{2,1,0:T(8,128)S(1)} %get-tuple-element.75), channel_id=1, source_target_pairs={{0,4},{4,0},{8,12},{12,8},{16,20},{20,16},{24,28},{28,24},{1,5},{5... | collective-permute-start | bytes 1572872 | tf_op jit(solution)/shard_map/ppermute | solution.py:554
  89.6 0.0 collective-permute-done.10.refs_3_
  89.6 0.0 collective-permute-done.8.refs_1_
  89.6 1.6 %collective-permute-done.9.refs_2_ = f32[64,512]{1,0:T(8,128)S(1)} collective-permute-done((f32[64,512]{1,0:T(8,128)S(1)}, f32[64,512]{1,0:T(8,128)S(1)}, u32[]{:S(2)}, u32[]{:S(2)}) %collective-permute-start.9) | collective-permute-done | bytes 131104 | tf_op jit(solution)/shard_map/ppermute | solution.py:535
  91.2 0.9 mix.2
  92.1 0.2 collective-permute-start.11
  92.3 0.0 collective-permute-done.18.other
  92.3 0.1 sum.3
  92.4 1.1 collective-permute-start.19
  93.4 0.7 collective-permute-start.20
  94.1 1.8 %collective-permute-start.21 = (f32[64,512]{1,0:T(8,128)S(1)}, f32[64,512]{1,0:T(8,128)S(1)}, u32[]{:S(2)}, u32[]{:S(2)}) collective-permute-start(f32[64,512]{1,0:T(8,128)S(1)} %get-tuple-element.79), channel_id=1, source_target_pairs={{0,24},{4,28},{8,16},{12,20},{16,8},{20,12},{24,0},{28,4},{1,25},{... | collective-permute-start | bytes 393224 | tf_op jit(solution)/shard_map/ppermute | solution.py:535
  96.0 0.0 collective-permute-done.11.other
  96.0 0.1 sum.2
  96.0 1.0 collective-permute-start.12
  97.1 0.7 collective-permute-start.13
  97.8 1.0 collective-permute-done.19.refs_5_
  98.8 0.8 collective-permute-start.14
  99.6 1.0 retarded.1
  100.6 0.9 collective-permute-done.20.refs_6_
  101.5 0.8 collective-permute-done.21.refs_7_
  102.4 2.1 %collective-permute-done.12.refs_1_ = f32[64,512]{1,0:T(8,128)S(1)} collective-permute-done((f32[64,512]{1,0:T(8,128)S(1)}, f32[64,512]{1,0:T(8,128)S(1)}, u32[]{:S(2)}, u32[]{:S(2)}) %collective-permute-start.12) | collective-permute-done | bytes 131104 | tf_op jit(solution)/shard_map/ppermute | solution.py:535
  104.5 0.6 collective-permute-done.13.refs_2_
  105.0 2.4 %collective-permute-done.14.refs_3_ = f32[64,512]{1,0:T(8,128)S(1)} collective-permute-done((f32[64,512]{1,0:T(8,128)S(1)}, f32[64,512]{1,0:T(8,128)S(1)}, u32[]{:S(2)}, u32[]{:S(2)}) %collective-permute-start.14) | collective-permute-done | bytes 131104 | tf_op jit(solution)/shard_map/ppermute | solution.py:535
  107.4 1.0 scattering.1
  (14 shorter events, 0.1 us)
Async XLA Ops:
  0.6 6.6 %copy-start = (f32[1,2,2,256,256]{4,3,2,1,0:T(8,128)S(1)}, f32[1,2,2,256,256]{4,3,2,1,0:T(8,128)}, u32[]{:S(2)}) copy-start(f32[1,2,2,256,256]{4,3,2,1,0:T(8,128)} %param.7) | copy-start | bytes 3145732
  0.6 6.6 %copy-start.1 = (f32[1,2,2,256,256]{4,3,2,1,0:T(8,128)S(1)}, f32[1,2,2,256,256]{4,3,2,1,0:T(8,128)}, u32[]{:S(2)}) copy-start(f32[1,2,2,256,256]{4,3,2,1,0:T(8,128)} %param.8) | copy-start | bytes 3145732
  0.7 6.6 %copy-start.2 = (f32[2,2,256,256]{3,2,1,0:T(8,128)S(1)}, f32[2,2,256,256]{3,2,1,0:T(8,128)}, u32[]{:S(2)}) copy-start(f32[2,2,256,256]{3,2,1,0:T(8,128)} %coupling.3) | copy-start | bytes 3145732
  0.7 6.6 %copy-start.3 = (s32[2,16,16]{2,1,0:T(8,128)S(1)}, s32[2,16,16]{2,1,0:T(8,128)}, u32[]{:S(2)}) copy-start(s32[2,16,16]{2,1,0:T(8,128)} %pattern.3) | copy-start | bytes 6148
  5.9 8.3 %collective-permute-start = (f32[256,512]{1,0:T(8,128)}, f32[256,512]{1,0:T(8,128)S(1)}, u32[]{:S(2)}, u32[]{:S(2)}) collective-permute-start(f32[256,512]{1,0:T(8,128)} %source.1), channel_id=1, source_target_pairs={{0,1},{5,4},{6,5},{7,6},{8,9},{13,12},{14,13},{15,14},{16,17},{21,... | collective-permute-start | bytes 1572872 | tf_op jit(solution)/shard_map/ppermute | solution.py:444
  14.3 0.7 collective-permute-start.1
  15.0 2.0 %collective-permute-start.2 = (f32[256,512]{1,0:T(8,128)S(1)}, f32[256,512]{1,0:T(8,128)S(1)}, u32[]{:S(2)}, u32[]{:S(2)}) collective-permute-start(f32[256,512]{1,0:T(8,128)S(1)} %relay.7.refs_4_.refs_10_), channel_id=1, source_target_pairs={{2,3},{5,6},{10,11},{13,14},{18,19},{21,22},{26,27},{29,30}} | collective-permute-start | bytes 1572872 | tf_op jit(solution)/shard_map/ppermute | solution.py:444
  15.7 19.5 %collective-permute-start.4 = (f32[256,512]{1,0:T(8,128)S(1)}, f32[256,512]{1,0:T(8,128)S(1)}, u32[]{:S(2)}, u32[]{:S(2)}) collective-permute-start(f32[256,512]{1,0:T(8,128)S(1)} %get-tuple-element.49), channel_id=1, source_target_pairs={{1,0},{2,1},{3,2},{9,8},{10,9},{11,10},{17,16},{18,17},{19,18},{25... | collective-permute-start | bytes 1572872 | tf_op jit(solution)/shard_map/ppermute | solution.py:496
  17.2 21.3 %collective-permute-start.3 = (f32[256,512]{1,0:T(8,128)S(1)}, f32[256,512]{1,0:T(8,128)S(1)}, u32[]{:S(2)}, u32[]{:S(2)}) collective-permute-start(f32[256,512]{1,0:T(8,128)S(1)} %get-tuple-element.48.refs_5_.refs_11_.refs_1_), channel_id=1, source_target_pairs={{3,2},{6,7},{11,10},{14,15},{19,18},{22,23},{27,26},{30,31}} | collective-permute-start | bytes 1572872 | tf_op jit(solution)/shard_map/ppermute | solution.py:444
  38.6 0.7 collective-permute-start.5
  39.3 30.4 %collective-permute-start.6 = (f32[256,512]{1,0:T(8,128)S(1)}, f32[256,512]{1,0:T(8,128)S(1)}, u32[]{:S(2)}, u32[]{:S(2)}) collective-permute-start(f32[256,512]{1,0:T(8,128)S(1)} %relay.10.refs_3_), channel_id=1, source_target_pairs={{1,0},{6,5},{9,8},{14,13},{17,16},{22,21},{25,24},{30,29}} | collective-permute-start | bytes 1572872 | tf_op jit(solution)/shard_map/ppermute | solution.py:444
  70.6 0.7 collective-permute-start.7
  72.6 3.3 %copy-start.6 = (s32[4]{0:T(128)S(1)}, s32[4]{0:T(128)}, u32[]{:S(2)}) copy-start(s32[4]{0:T(128)} %param.11) | copy-start | bytes 52
  72.6 8.5 %collective-permute-start.15 = (f32[64,512]{1,0:T(8,128)S(1)}, f32[64,512]{1,0:T(8,128)S(1)}, u32[]{:S(2)}, u32[]{:S(2)}) collective-permute-start(f32[64,512]{1,0:T(8,128)S(1)} %get-tuple-element.71), channel_id=1, source_target_pairs={{0,8},{4,12},{8,0},{12,4},{16,24},{20,28},{24,16},{28,20},{1,9},{5... | collective-permute-start | bytes 393224 | tf_op jit(solution)/shard_map/ppermute | solution.py:535
  75.9 5.8 %collective-permute-start.16 = (f32[64,512]{1,0:T(8,128)S(1)}, f32[64,512]{1,0:T(8,128)S(1)}, u32[]{:S(2)}, u32[]{:S(2)}) collective-permute-start(f32[64,512]{1,0:T(8,128)S(1)} %get-tuple-element.72), channel_id=1, source_target_pairs={{0,16},{4,20},{8,24},{12,28},{16,0},{20,4},{24,8},{28,12},{1,17},{... | collective-permute-start | bytes 393224 | tf_op jit(solution)/shard_map/ppermute | solution.py:535
  77.5 6.9 %collective-permute-start.17 = (f32[64,512]{1,0:T(8,128)S(1)}, f32[64,512]{1,0:T(8,128)S(1)}, u32[]{:S(2)}, u32[]{:S(2)}) collective-permute-start(f32[64,512]{1,0:T(8,128)S(1)} %get-tuple-element.73), channel_id=1, source_target_pairs={{0,24},{4,28},{8,16},{12,20},{16,8},{20,12},{24,0},{28,4},{1,25},{... | collective-permute-start | bytes 393224 | tf_op jit(solution)/shard_map/ppermute | solution.py:535
  78.0 11.6 %collective-permute-start.10 = (f32[64,512]{1,0:T(8,128)S(1)}, f32[64,512]{1,0:T(8,128)S(1)}, u32[]{:S(2)}, u32[]{:S(2)}) collective-permute-start(f32[64,512]{1,0:T(8,128)S(1)} %get-tuple-element.63), channel_id=1, source_target_pairs={{0,24},{4,28},{8,16},{12,20},{16,8},{20,12},{24,0},{28,4},{1,25},{... | collective-permute-start | bytes 393224 | tf_op jit(solution)/shard_map/ppermute | solution.py:535
  80.6 1.0 copy-start.4
  80.6 1.0 copy-start.5
  80.6 9.0 %collective-permute-start.8 = (f32[64,512]{1,0:T(8,128)S(1)}, f32[64,512]{1,0:T(8,128)S(1)}, u32[]{:S(2)}, u32[]{:S(2)}) collective-permute-start(f32[64,512]{1,0:T(8,128)S(1)} %get-tuple-element.61), channel_id=1, source_target_pairs={{0,8},{4,12},{8,0},{12,4},{16,24},{20,28},{24,16},{28,20},{1,9},{5... | collective-permute-start | bytes 393224 | tf_op jit(solution)/shard_map/ppermute | solution.py:535
  81.1 10.2 %collective-permute-start.9 = (f32[64,512]{1,0:T(8,128)S(1)}, f32[64,512]{1,0:T(8,128)S(1)}, u32[]{:S(2)}, u32[]{:S(2)}) collective-permute-start(f32[64,512]{1,0:T(8,128)S(1)} %get-tuple-element.62), channel_id=1, source_target_pairs={{0,16},{4,20},{8,24},{12,28},{16,0},{20,4},{24,8},{28,12},{1,17},{... | collective-permute-start | bytes 393224 | tf_op jit(solution)/shard_map/ppermute | solution.py:535
  85.3 7.0 %collective-permute-start.18 = (f32[4,64,512]{2,1,0:T(8,128)S(1)}, f32[4,64,512]{2,1,0:T(8,128)S(1)}, u32[]{:S(2)}, u32[]{:S(2)}) collective-permute-start(f32[4,64,512]{2,1,0:T(8,128)S(1)} %get-tuple-element.75), channel_id=1, source_target_pairs={{0,4},{4,0},{8,12},{12,8},{16,20},{20,16},{24,28},{28,24},{1,5},{5... | collective-permute-start | bytes 1572872 | tf_op jit(solution)/shard_map/ppermute | solution.py:554
  92.1 3.8 %collective-permute-start.11 = (f32[4,64,512]{2,1,0:T(8,128)S(1)}, f32[4,64,512]{2,1,0:T(8,128)S(1)}, u32[]{:S(2)}, u32[]{:S(2)}) collective-permute-start(f32[4,64,512]{2,1,0:T(8,128)S(1)} %get-tuple-element.65), channel_id=1, source_target_pairs={{0,4},{4,0},{8,12},{12,8},{16,20},{20,16},{24,28},{28,24},{1,5},{5... | collective-permute-start | bytes 1572872 | tf_op jit(solution)/shard_map/ppermute | solution.py:554
  92.4 6.4 %collective-permute-start.19 = (f32[64,512]{1,0:T(8,128)S(1)}, f32[64,512]{1,0:T(8,128)S(1)}, u32[]{:S(2)}, u32[]{:S(2)}) collective-permute-start(f32[64,512]{1,0:T(8,128)S(1)} %get-tuple-element.77), channel_id=1, source_target_pairs={{0,8},{4,12},{8,0},{12,4},{16,24},{20,28},{24,16},{28,20},{1,9},{5... | collective-permute-start | bytes 393224 | tf_op jit(solution)/shard_map/ppermute | solution.py:535
  93.4 8.1 %collective-permute-start.20 = (f32[64,512]{1,0:T(8,128)S(1)}, f32[64,512]{1,0:T(8,128)S(1)}, u32[]{:S(2)}, u32[]{:S(2)}) collective-permute-start(f32[64,512]{1,0:T(8,128)S(1)} %get-tuple-element.78), channel_id=1, source_target_pairs={{0,16},{4,20},{8,24},{12,28},{16,0},{20,4},{24,8},{28,12},{1,17},{... | collective-permute-start | bytes 393224 | tf_op jit(solution)/shard_map/ppermute | solution.py:535
  94.1 8.2 %collective-permute-start.21 = (f32[64,512]{1,0:T(8,128)S(1)}, f32[64,512]{1,0:T(8,128)S(1)}, u32[]{:S(2)}, u32[]{:S(2)}) collective-permute-start(f32[64,512]{1,0:T(8,128)S(1)} %get-tuple-element.79), channel_id=1, source_target_pairs={{0,24},{4,28},{8,16},{12,20},{16,8},{20,12},{24,0},{28,4},{1,25},{... | collective-permute-start | bytes 393224 | tf_op jit(solution)/shard_map/ppermute | solution.py:535
  96.0 8.4 %collective-permute-start.12 = (f32[64,512]{1,0:T(8,128)S(1)}, f32[64,512]{1,0:T(8,128)S(1)}, u32[]{:S(2)}, u32[]{:S(2)}) collective-permute-start(f32[64,512]{1,0:T(8,128)S(1)} %get-tuple-element.67), channel_id=1, source_target_pairs={{0,8},{4,12},{8,0},{12,4},{16,24},{20,28},{24,16},{28,20},{1,9},{5... | collective-permute-start | bytes 393224 | tf_op jit(solution)/shard_map/ppermute | solution.py:535
  97.1 8.0 %collective-permute-start.13 = (f32[64,512]{1,0:T(8,128)S(1)}, f32[64,512]{1,0:T(8,128)S(1)}, u32[]{:S(2)}, u32[]{:S(2)}) collective-permute-start(f32[64,512]{1,0:T(8,128)S(1)} %get-tuple-element.68), channel_id=1, source_target_pairs={{0,16},{4,20},{8,24},{12,28},{16,0},{20,4},{24,8},{28,12},{1,17},{... | collective-permute-start | bytes 393224 | tf_op jit(solution)/shard_map/ppermute | solution.py:535
  98.8 8.6 %collective-permute-start.14 = (f32[64,512]{1,0:T(8,128)S(1)}, f32[64,512]{1,0:T(8,128)S(1)}, u32[]{:S(2)}, u32[]{:S(2)}) collective-permute-start(f32[64,512]{1,0:T(8,128)S(1)} %get-tuple-element.69), channel_id=1, source_target_pairs={{0,24},{4,28},{8,16},{12,20},{16,8},{20,12},{24,0},{28,4},{1,25},{... | collective-permute-start | bytes 393224 | tf_op jit(solution)/shard_map/ppermute | solution.py:535

commit v5 on v4

--- a/solution.py
+++ b/solution.py
@@ -12,6 +12,7 @@
 HBM = pl.BlockSpec(memory_space=pltpu.HBM)
 VMEM = pl.BlockSpec(memory_space=pltpu.VMEM)
 SMEM = pl.BlockSpec(memory_space=pltpu.SMEM)
+LEADING = 0
 
 
 def split(value):
@@ -74,8 +75,8 @@
     return jnp.concatenate([coupling[0] * mask, coupling[1] * mask], axis=1)
 
 
-def parity():
-    return lax.rem(lax.axis_index("energy"), 2)
+def trailing():
+    return lax.rem(lax.axis_index("energy") + LEADING, 2)
 
 
 def shape(rows, columns, dtype=F32, *lead):
@@ -159,21 +160,21 @@
     return first, second
 
 
-def source_kernel(green, sigma, coupling, pattern, whole, *scratch):
+def source_kernel(green, sigma, coupling, pattern, whole, gate, *scratch):
     @pl.when(lax.axis_index("slab") == 0)
     def _():
         loads = Loads((green, sigma, coupling, pattern), scratch[:4], scratch[4], (1,))
         left_sources(loads, whole, None, None, *scratch[5:])
 
-    @pl.when((lax.axis_index("slab") > 0) & (parity() == 1))
+    @pl.when((lax.axis_index("slab") > 0) & (trailing() == 1))
     def _():
         loads = Loads((green, sigma, coupling, pattern), scratch[:4], scratch[4], (0,), False)
-        whole[...] = loads.coupler(0)
+        gate[...] = loads.coupler(0)[: gate.shape[0]]
 
 
 def map_kernel(
     green, sigma, coupling, pattern,
-    whole, source, coupler, opening, lead, tail, forward, backward, *scratch,
+    whole, source, coupler, upper, lower, lead, tail, forward, backward, *scratch,
 ):
     m_a, m_b, m_c = scratch[5:]
     loads = Loads((green, sigma, coupling, pattern), scratch[:4], scratch[4])
@@ -182,7 +183,8 @@
 
     @pl.when(lax.axis_index("slab") > 0)
     def _():
-        opening[...] = before
+        upper[...] = before[: upper.shape[0]]
+        lower[...] = before[upper.shape[0] :]
         put(m_a, first)
         size = before.shape[0]
         behind = times(adjoint_row((before[:, :size], before[:, size:])), m_a)
@@ -209,9 +211,9 @@
     arrived, wholes = refs[: count - 1], refs[count - 1 : 2 * count - 2]
     refs = refs[2 * count - 2 :]
     start_whole, source, forward, backward, coupler = refs[:5]
-    followings = refs[5:7]
-    lead, tail, constant, last_lead, last_tail = refs[7:12]
-    first_v, last_v, m_a, m_b, m_c, m_d = refs[12:]
+    gate, upper, lower = refs[5:8]
+    lead, tail, constant, last_lead, last_tail = refs[8:13]
+    first_v, last_v, m_a, m_b, m_c, m_d = refs[13:]
     place = lax.axis_index("slab")
 
     @pl.when(place == 0)
@@ -220,7 +222,7 @@
         last_v[...] = start_whole[...]
 
     for turn in range(count - 1):
-        @pl.when((place > 0) & (place == turn + 1 - parity()))
+        @pl.when((place > 0) & (place == turn + 1 - trailing()))
         def _(turn=turn):
             last_v[...] = wholes[turn][...]
             put(m_a, arrived[turn][...])
@@ -235,7 +237,8 @@
         first, last = first_v[...], last_v[...]
         through, joined = right_terms(first, last, coupler[...], m_a, m_b, m_c, m_d)
         constant[...] = joined
-        next_coupler = jnp.where(parity() == 0, followings[0][...], followings[1][...])
+        above = jnp.where(trailing() == 0, upper[...], gate[...])
+        next_coupler = jnp.concatenate([above, lower[...]], axis=0)
         put(m_a, next_coupler, True)
         put(lead, times(through, m_a, True))
         put(last_lead, times(last, m_a, True))
@@ -253,7 +256,7 @@
 def relay_kernel(step, count, lefts, rights, *refs):
     refs = list(refs)
     place = lax.axis_index("slab")
-    turn = step - parity()
+    turn = step - trailing()
     is_left = (turn >= 0) & (turn <= count - 2) & (place == turn + 1)
     is_right = (turn >= count - 1) & (place == 2 * count - 3 - turn)
     closing = lefts and step >= count - 2
@@ -262,6 +265,8 @@
     right_map = [refs.pop(0) for _ in range(3)] if rights else None
     if closing:
         forward, backward, source, coupler = [refs.pop(0) for _ in range(4)]
+    if step == 0:
+        refs.pop(0)
     out = refs.pop(0)
     if closing:
         end, m_x, m_a, m_b, m_c = refs
@@ -304,7 +309,7 @@
     wholes = [refs.pop(0) for _ in range(count - 1)]
     block, *parcels, m_x = refs
     place = lax.axis_index("slab")
-    core = parity()
+    core = trailing()
     is_last = place == count - 1
 
     for index in range(count):
@@ -337,7 +342,7 @@
     refs.pop(0)
     block, *parcels, m_x = refs
     place = lax.axis_index("slab")
-    core = parity()
+    core = trailing()
     at = jnp.where(place == count - 1, count - 2 + core, 2 * count - 3 - place + core)
 
     for index in range(count):
@@ -417,11 +422,8 @@
 def relay_pairs(step, energies, count):
     pairs = []
     for energy in range(energies):
-        turn = step - energy % 2
-        if turn < 0:
-            pairs += [(energy * count + i, energy * count + i - 1) for i in range(1, count)]
-            continue
-        if turn <= count - 2:
+        turn = step - (energy + LEADING) % 2
+        if 0 <= turn <= count - 2:
             ends = (turn, turn + 1)
         elif count - 1 <= turn <= 2 * count - 3:
             ends = (2 * count - 2 - turn, 2 * count - 3 - turn)
@@ -435,6 +437,7 @@
     size, blocks = free_green.shape[-1], pattern.shape[-1]
     args = (free_green[0], self_energy[0], coupling, pattern)
     row = shape(size, 2 * size)
+    half = shape(size // 2, 2 * size)
     factor = shape(size, size, HALF, 2, 3)
     row_v = pltpu.VMEM(row.shape, F32)
     product = 24 * size**3
@@ -443,29 +446,39 @@
     def relay(step, value):
         return lax.ppermute(value, ("energy", "slab"), relay_pairs(step, energies, count))
 
+    def lower_place(value, cores):
+        pairs = [
+            (energy * count + i, energy * count + i - 1)
+            for energy in range(energies)
+            for i in range(1, count)
+            if (energy + LEADING) % 2 in cores
+        ]
+        return lax.ppermute(value, ("energy", "slab"), pairs)
+
     begun = call(
         source_kernel,
-        [row],
+        [row, half],
         loading,
         args,
         [HBM] * 4,
         flops=6 * product,
         name="source",
-        limit=58,
+        limit=61,
     )
     arrived, outs, ends = [relay(0, begun[0])], [], []
-    whole, source, coupler, opening, left_lead, left_tail, forward, backward = call(
+    gate = lower_place(begun[1], [1])
+    whole, source, coupler, upper, lower, left_lead, left_tail, forward, backward = call(
         map_kernel,
-        [row] * 4 + [factor, factor, row, row],
+        [row] * 3 + [half] * 2 + [factor, factor, row, row],
         loading,
         args,
         [HBM] * 4,
         flops=12 * product,
         name="left_maps",
-        limit=42,
+        limit=49,
     )
     left_map = [left_lead, left_tail, whole]
-    right_map = following = None
+    right_map = None
     for step in range(2 * count - 2):
         lefts, rights = step <= count - 1, step >= count - 1
         closing = lefts and step >= count - 2
@@ -476,6 +489,8 @@
             args += right_map[:3]
         if closing:
             args += [forward, backward, source, coupler]
+        if step == 0:
+            args.append(gate)
         made = call(
             functools.partial(relay_kernel, step, count, lefts, rights),
             [row] * (2 if closing else 1),
@@ -488,15 +503,11 @@
         ends += made[1:]
         arrived.append(relay(step + 1, made[0]))
         if step == 0:
-            down = [
-                (energy * count + i, energy * count + i - 1)
-                for energy in range(0, energies, 2)
-                for i in range(1, count)
-            ]
-            following = lax.ppermute(opening, ("energy", "slab"), down)
+            lower = lower_place(lower, [0, 1])
+            upper = lower_place(upper, [0])
         if step == count - 2:
             args = arrived[: count - 1] + outs[: count - 1]
-            args += [whole, source, forward, backward, coupler, following, arrived[0]]
+            args += [whole, source, forward, backward, coupler, gate, upper, lower]
             right_map = call(
                 functools.partial(prepare_kernel, count),
                 [factor, factor, row, factor, factor],

time: 109 us -> 108 us (level)
  waiting for transfers between devices: 61.6 us -> 55.9 us
  starting transfers between devices: 26.8 us -> 31.4 us
    ppermute x7, waiting for transfers between devices: 32.2 us -> 29 us  [relay(): lax.ppermute(value, ('energy', 'slab'), relay_pairs(step, energies, count))]
    ppermute x12, waiting for transfers between devices: 12.2 us -> 9.19 us  [exchange(): lax.ppermute(value, 'energy', [(i, i ^ 2 * mask) for i in range(energies)])]
    ppermute x2, starting transfers between devices: 4.47 us -> 7.09 us  [shards(): other = lax.ppermute(other, 'energy', [(i, i ^ 1) for i in range(energies)])]
    ppermute x1 -> x3, starting transfers between devices: 1.29 us -> 3.26 us  [lower_place(): return lax.ppermute(value, ('energy', 'slab'), pairs)]
    ppermute x1 -> x3, waiting for transfers between devices: 17.3 us -> 17.6 us  [lower_place(): return lax.ppermute(value, ('energy', 'slab'), pairs)]
  transfers between devices with their start and end apart: 22 -> 24, of which waited for: 11 -> 10; matrix products, arithmetic and copies ran while one was open for 0% -> 0% of each run, Pallas kernels for 10% -> 10%
where the time goes in v5:
time: 108 us
  waiting for transfers between devices  55.9 us (52%)
  starting transfers between devices  31.4 us (29%)
  Pallas kernels  19.8 us (18%)
    ppermute x7, waiting for transfers between devices, relay(): lax.ppermute(value, ('energy', 'slab'), relay_pairs(step, energies, count))  29 us
    pallas_call x17, Pallas kernels, call(): pl.pallas_call(kernel, out_shape=outs, in_specs=specs or [VMEM] * len(arg...  19.8 us
    ppermute x3, waiting for transfers between devices, lower_place(): return lax.ppermute(value, ('energy', 'slab'), pairs)  17.6 us
    ppermute x12, starting transfers between devices, exchange(): lax.ppermute(value, 'energy', [(i, i ^ 2 * mask) for i in range(energies)])  15 us
    ppermute x12, waiting for transfers between devices, exchange(): lax.ppermute(value, 'energy', [(i, i ^ 2 * mask) for i in range(energies)])  9.19 us
    ppermute x2, starting transfers between devices, shards(): other = lax.ppermute(other, 'energy', [(i, i ^ 1) for i in range(energies)])  7.09 us
    ppermute x7, starting transfers between devices, relay(): lax.ppermute(value, ('energy', 'slab'), relay_pairs(step, energies, count))  6.09 us
    ppermute x3, starting transfers between devices, lower_place(): return lax.ppermute(value, ('energy', 'slab'), pairs)  3.26 us
  transfers between devices with their start and end apart: 24, of which 10 were waited for; matrix products, arithmetic and copies ran while one was open for 0% of the time, Pallas kernels for 10%

profile of v5, /device:TPU:0, one launch (start us, length us, event | category | flops | bytes accessed | tf_op | source)
XLA Modules:
  0.0 108.1 jit_solution(10595523385919625083)
XLA Ops:
  0.6 0.0 copy-start
  0.6 5.2 %source.1 = (f32[256,512]{1,0:T(8,128)}, f32[128,512]{1,0:T(8,128)}) custom-call(f32[2,2,256,256]{3,2,1,0:T(8,128)} %bitcast.6, f32[2,2,256,256]{3,2,1,0:T(8,128)} %bitcast.8, f32[2,2,256,256]{3,2,1,0:T(8,128)} %coupling.3, s32[2,16,16]{2,1,0:T(8,128)} %pattern.3), custom_call_target="tpu_custom_call" | custom-call | flops 2415919104 | bytes 1048576 | tf_op jit(solution)/shard_map/source/pallas_call | solution.py:91
  5.8 1.3 %collective-permute-start = (f32[256,512]{1,0:T(8,128)}, f32[256,512]{1,0:T(8,128)S(1)}, u32[]{:S(2)}, u32[]{:S(2)}) collective-permute-start(f32[256,512]{1,0:T(8,128)} %get-tuple-element.44), channel_id=1, source_target_pairs={{0,1},{8,9},{16,17},{24,25}} | collective-permute-start | bytes 1572872 | tf_op jit(solution)/shard_map/ppermute | solution.py:447
  7.2 0.7 collective-permute-start.1
  7.9 4.7 %left_maps.1 = (f32[256,512]{1,0:T(8,128)S(1)}, f32[256,512]{1,0:T(8,128)S(1)}, f32[256,512]{1,0:T(8,128)S(1)}, f32[128,512]{1,0:T(8,128)S(1)}, f32[128,512]{1,0...) custom-call(f32[2,2,256,256]{3,2,1,0:T(8,128)} %bitcast.7, ...), custom_call_target="tpu_custom_call" | custom-call | flops 4831838208 | bytes 1048576 | tf_op jit(solution)/shard_map/left_maps/pallas_call | solution.py:91
  12.6 0.0 collective-permute-done.1.refs_4_.refs_11_
  12.6 1.6 %collective-permute-done.refs_0_ = f32[256,512]{1,0:T(8,128)S(1)} collective-permute-done((f32[256,512]{1,0:T(8,128)}, f32[256,512]{1,0:T(8,128)S(1)}, u32[]{:S(2)}, u32[]{:S(2)}) %collective-permute-start) | collective-permute-done | bytes 524320 | tf_op jit(solution)/shard_map/ppermute | solution.py:447
  14.2 0.7 collective-permute-start.2
  14.9 0.0 collective-permute-done.2.refs_0_.refs_1_
  14.9 0.7 collective-permute-start.3
  15.6 1.3 %collective-permute-start.5 = (f32[128,512]{1,0:T(8,128)S(1)}, f32[128,512]{1,0:T(8,128)S(1)}, u32[]{:S(2)}, u32[]{:S(2)}) collective-permute-start(f32[128,512]{1,0:T(8,128)S(1)} %get-tuple-element.54), channel_id=1, source_target_pairs={{1,0},{2,1},{3,2},{9,8},{10,9},{11,10},{17,16},{18,17},{19,18},{25... | collective-permute-start | bytes 786440 | tf_op jit(solution)/shard_map/ppermute | solution.py:456
  16.9 1.3 %collective-permute-start.6 = (f32[128,512]{1,0:T(8,128)S(1)}, f32[128,512]{1,0:T(8,128)S(1)}, u32[]{:S(2)}, u32[]{:S(2)}) collective-permute-start(f32[128,512]{1,0:T(8,128)S(1)} %get-tuple-element.55), channel_id=1, source_target_pairs={{1,0},{2,1},{3,2},{5,4},{6,5},{7,6},{9,8},{10,9},{11,10},{13,12},{... | collective-permute-start | bytes 786440 | tf_op jit(solution)/shard_map/ppermute | solution.py:456
  18.2 0.0 collective-permute-done.3.refs_0_.refs_2_
  18.2 0.2 relay.8
  18.4 0.7 collective-permute-start.4
  19.2 13.1 %collective-permute-done.5.refs_12_ = f32[128,512]{1,0:T(8,128)S(1)} collective-permute-done((f32[128,512]{1,0:T(8,128)S(1)}, f32[128,512]{1,0:T(8,128)S(1)}, u32[]{:S(2)}, u32[]{:S(2)}) %collective-permute-start.5) | collective-permute-done | bytes 262176 | tf_op jit(solution)/shard_map/ppermute | solution.py:456
  32.3 4.5 %collective-permute-done.6.refs_13_ = f32[128,512]{1,0:T(8,128)S(1)} collective-permute-done((f32[128,512]{1,0:T(8,128)S(1)}, f32[128,512]{1,0:T(8,128)S(1)}, u32[]{:S(2)}, u32[]{:S(2)}) %collective-permute-start.6) | collective-permute-done | bytes 262176 | tf_op jit(solution)/shard_map/ppermute | solution.py:456
  36.8 3.3 %right_maps.1 = (bf16[2,3,256,256]{3,2,1,0:T(8,128)(2,1)S(1)}, bf16[2,3,256,256]{3,2,1,0:T(8,128)(2,1)S(1)}, f32[256,512]{1,0:T(8,128)S(1)}, bf16[2,3,256,256]{3...) custom-call(f32[256,512]{1,0:T(8,128)S(1)} %collective-permute-done.refs_0_, ...), custom_call_target="tpu_custom_call" | custom-call | flops 4026531840 | bytes 1048576 | tf_op jit(solution)/shard_map/right_maps/pallas_call | solution.py:91
  40.1 0.0 collective-permute-done.4.refs_0_
  40.1 0.7 collective-permute-start.7
  40.8 0.0 collective-permute-done.7.refs_0_.refs_1_
  40.9 1.3 %collective-permute-start.8 = (f32[256,512]{1,0:T(8,128)S(1)}, f32[256,512]{1,0:T(8,128)S(1)}, u32[]{:S(2)}, u32[]{:S(2)}) collective-permute-start(f32[256,512]{1,0:T(8,128)S(1)} %relay.10.refs_3_), channel_id=1, source_target_pairs={{1,0},{6,5},{9,8},{14,13},{17,16},{22,21},{25,24},{30,29}} | collective-permute-start | bytes 1572872 | tf_op jit(solution)/shard_map/ppermute | solution.py:447
  42.2 27.5 %collective-permute-done.8.refs_0_.refs_2_ = f32[256,512]{1,0:T(8,128)S(1)} collective-permute-done((f32[256,512]{1,0:T(8,128)S(1)}, f32[256,512]{1,0:T(8,128)S(1)}, u32[]{:S(2)}, u32[]{:S(2)}) %collective-permute-start.8) | collective-permute-done | bytes 524320 | tf_op jit(solution)/shard_map/ppermute | solution.py:447
  69.7 0.9 relay.11.refs_4_
  70.5 0.7 collective-permute-start.9
  71.2 0.0 collective-permute-done.9.refs_3_.refs_0_
  71.2 1.3 %second_slab.1 = (f32[256,512]{1,0:T(8,128)S(1)}, f32[64,512]{1,0:T(8,128)S(1)}, f32[64,512]{1,0:T(8,128)S(1)}, f32[64,512]{1,0:T(8,128)S(1)}, f32[64,512]{1,0:T(8,128)S(1)}) custom-call(f32[256,512]{1,0:T(8,128)S(1)} %collective-permute-done.4.refs_0_, f32[256,512]{1,0:T(8,128)S(1)} %collective-permute-done.7.refs_0_.refs_1_, ...), custom_call_target="tpu_custom_call" | custom-call | flops 805306368 | bytes 1048576 | tf_op jit(solution)/shard_map/second_slab/pallas_call | solution.py:91
  72.5 0.0 copy-start.3
  72.5 3.0 %collective-permute-start.17 = (f32[64,512]{1,0:T(8,128)S(1)}, f32[64,512]{1,0:T(8,128)S(1)}, u32[]{:S(2)}, u32[]{:S(2)}) collective-permute-start(f32[64,512]{1,0:T(8,128)S(1)} %get-tuple-element.77), channel_id=1, source_target_pairs={{0,8},{4,12},{8,0},{12,4},{16,24},{20,28},{24,16},{28,20},{1,9},{5... | collective-permute-start | bytes 393224 | tf_op jit(solution)/shard_map/ppermute | solution.py:546
  75.5 1.6 %collective-permute-start.18 = (f32[64,512]{1,0:T(8,128)S(1)}, f32[64,512]{1,0:T(8,128)S(1)}, u32[]{:S(2)}, u32[]{:S(2)}) collective-permute-start(f32[64,512]{1,0:T(8,128)S(1)} %get-tuple-element.78), channel_id=1, source_target_pairs={{0,16},{4,20},{8,24},{12,28},{16,0},{20,4},{24,8},{28,12},{1,17},{... | collective-permute-start | bytes 393224 | tf_op jit(solution)/shard_map/ppermute | solution.py:546
  77.1 0.5 collective-permute-start.19
  77.6 0.1 first_slab.1
  77.7 1.6 %collective-permute-start.10 = (f32[64,512]{1,0:T(8,128)S(1)}, f32[64,512]{1,0:T(8,128)S(1)}, u32[]{:S(2)}, u32[]{:S(2)}) collective-permute-start(f32[64,512]{1,0:T(8,128)S(1)} %get-tuple-element.67), channel_id=1, source_target_pairs={{0,8},{4,12},{8,0},{12,4},{16,24},{20,28},{24,16},{28,20},{1,9},{5... | collective-permute-start | bytes 393224 | tf_op jit(solution)/shard_map/ppermute | solution.py:546
  79.3 1.5 %collective-permute-start.11 = (f32[64,512]{1,0:T(8,128)S(1)}, f32[64,512]{1,0:T(8,128)S(1)}, u32[]{:S(2)}, u32[]{:S(2)}) collective-permute-start(f32[64,512]{1,0:T(8,128)S(1)} %get-tuple-element.68), channel_id=1, source_target_pairs={{0,16},{4,20},{8,24},{12,28},{16,0},{20,4},{24,8},{28,12},{1,17},{... | collective-permute-start | bytes 393224 | tf_op jit(solution)/shard_map/ppermute | solution.py:546
  80.8 0.0 collective-permute-done.17.refs_1_
  80.8 0.7 collective-permute-start.12
  81.5 0.1 add_reduce_fusion.weights
  81.6 0.0 collective-permute-done.18.refs_2_
  81.6 1.8 %collective-permute-done.19.refs_3_ = f32[64,512]{1,0:T(8,128)S(1)} collective-permute-done((f32[64,512]{1,0:T(8,128)S(1)}, f32[64,512]{1,0:T(8,128)S(1)}, u32[]{:S(2)}, u32[]{:S(2)}) %collective-permute-start.19) | collective-permute-done | bytes 131104 | tf_op jit(solution)/shard_map/ppermute | solution.py:546
  83.4 0.9 mix.3
  84.3 5.1 %collective-permute-start.20 = (f32[4,64,512]{2,1,0:T(8,128)S(1)}, f32[4,64,512]{2,1,0:T(8,128)S(1)}, u32[]{:S(2)}, u32[]{:S(2)}) collective-permute-start(f32[4,64,512]{2,1,0:T(8,128)S(1)} %get-tuple-element.81), channel_id=1, source_target_pairs={{0,4},{4,0},{8,12},{12,8},{16,20},{20,16},{24,28},{28,24},{1,5},{5... | collective-permute-start | bytes 1572872 | tf_op jit(solution)/shard_map/ppermute | solution.py:565
  89.4 0.0 collective-permute-done.10.refs_1_
  89.4 0.0 collective-permute-done.11.refs_2_
  89.4 0.0 collective-permute-done.12.refs_3_
  89.4 0.9 mix.2
  90.3 2.0 %collective-permute-start.13 = (f32[4,64,512]{2,1,0:T(8,128)S(1)}, f32[4,64,512]{2,1,0:T(8,128)S(1)}, u32[]{:S(2)}, u32[]{:S(2)}) collective-permute-start(f32[4,64,512]{2,1,0:T(8,128)S(1)} %get-tuple-element.71), channel_id=1, source_target_pairs={{0,4},{4,0},{8,12},{12,8},{16,20},{20,16},{24,28},{28,24},{1,5},{5... | collective-permute-start | bytes 1572872 | tf_op jit(solution)/shard_map/ppermute | solution.py:565
  92.3 0.0 collective-permute-done.20.other
  92.3 0.1 sum.3
  92.4 0.8 collective-permute-start.21
  93.2 1.1 collective-permute-start.22
  94.2 1.7 %collective-permute-start.23 = (f32[64,512]{1,0:T(8,128)S(1)}, f32[64,512]{1,0:T(8,128)S(1)}, u32[]{:S(2)}, u32[]{:S(2)}) collective-permute-start(f32[64,512]{1,0:T(8,128)S(1)} %get-tuple-element.85), channel_id=1, source_target_pairs={{0,24},{4,28},{8,16},{12,20},{16,8},{20,12},{24,0},{28,4},{1,25},{... | collective-permute-start | bytes 393224 | tf_op jit(solution)/shard_map/ppermute | solution.py:546
  95.9 0.0 collective-permute-done.13.other
  95.9 0.1 sum.2
  96.0 0.8 collective-permute-start.14
  96.8 1.1 collective-permute-start.15
  97.9 1.0 collective-permute-done.21.refs_5_
  98.8 0.7 collective-permute-start.16
  99.6 1.0 retarded.1
  100.6 0.0 collective-permute-done.22.refs_6_
  100.6 1.7 %collective-permute-done.23.refs_7_ = f32[64,512]{1,0:T(8,128)S(1)} collective-permute-done((f32[64,512]{1,0:T(8,128)S(1)}, f32[64,512]{1,0:T(8,128)S(1)}, u32[]{:S(2)}, u32[]{:S(2)}) %collective-permute-start.23) | collective-permute-done | bytes 131104 | tf_op jit(solution)/shard_map/ppermute | solution.py:546
  102.3 2.1 %collective-permute-done.14.refs_1_ = f32[64,512]{1,0:T(8,128)S(1)} collective-permute-done((f32[64,512]{1,0:T(8,128)S(1)}, f32[64,512]{1,0:T(8,128)S(1)}, u32[]{:S(2)}, u32[]{:S(2)}) %collective-permute-start.14) | collective-permute-done | bytes 131104 | tf_op jit(solution)/shard_map/ppermute | solution.py:546
  104.5 0.2 collective-permute-done.15.refs_2_
  104.6 2.4 %collective-permute-done.16.refs_3_ = f32[64,512]{1,0:T(8,128)S(1)} collective-permute-done((f32[64,512]{1,0:T(8,128)S(1)}, f32[64,512]{1,0:T(8,128)S(1)}, u32[]{:S(2)}, u32[]{:S(2)}) %collective-permute-start.16) | collective-permute-done | bytes 131104 | tf_op jit(solution)/shard_map/ppermute | solution.py:546
  107.0 1.0 scattering.1
  (12 shorter events, 0.1 us)
Async XLA Ops:
  0.6 7.2 %copy-start = (s32[2,16,16]{2,1,0:T(8,128)S(1)}, s32[2,16,16]{2,1,0:T(8,128)}, u32[]{:S(2)}) copy-start(s32[2,16,16]{2,1,0:T(8,128)} %pattern.3) | copy-start | bytes 6148
  5.8 8.3 %collective-permute-start = (f32[256,512]{1,0:T(8,128)}, f32[256,512]{1,0:T(8,128)S(1)}, u32[]{:S(2)}, u32[]{:S(2)}) collective-permute-start(f32[256,512]{1,0:T(8,128)} %get-tuple-element.44), channel_id=1, source_target_pairs={{0,1},{8,9},{16,17},{24,25}} | collective-permute-start | bytes 1572872 | tf_op jit(solution)/shard_map/ppermute | solution.py:447
  7.2 5.4 %collective-permute-start.1 = (f32[128,512]{1,0:T(8,128)}, f32[128,512]{1,0:T(8,128)S(1)}, u32[]{:S(2)}, u32[]{:S(2)}) collective-permute-start(f32[128,512]{1,0:T(8,128)} %get-tuple-element.48), channel_id=1, source_target_pairs={{5,4},{6,5},{7,6},{13,12},{14,13},{15,14},{21,20},{22,21},{23,22},... | collective-permute-start | bytes 786440 | tf_op jit(solution)/shard_map/ppermute | solution.py:456
  14.2 0.7 collective-permute-start.2
  14.9 3.3 %collective-permute-start.3 = (f32[256,512]{1,0:T(8,128)S(1)}, f32[256,512]{1,0:T(8,128)S(1)}, u32[]{:S(2)}, u32[]{:S(2)}) collective-permute-start(f32[256,512]{1,0:T(8,128)S(1)} %relay.7.refs_4_.refs_10_), channel_id=1, source_target_pairs={{2,3},{5,6},{10,11},{13,14},{18,19},{21,22},{26,27},{29,30}} | collective-permute-start | bytes 1572872 | tf_op jit(solution)/shard_map/ppermute | solution.py:447
  15.6 16.7 %collective-permute-start.5 = (f32[128,512]{1,0:T(8,128)S(1)}, f32[128,512]{1,0:T(8,128)S(1)}, u32[]{:S(2)}, u32[]{:S(2)}) collective-permute-start(f32[128,512]{1,0:T(8,128)S(1)} %get-tuple-element.54), channel_id=1, source_target_pairs={{1,0},{2,1},{3,2},{9,8},{10,9},{11,10},{17,16},{18,17},{19,18},{25... | collective-permute-start | bytes 786440 | tf_op jit(solution)/shard_map/ppermute | solution.py:456
  16.9 19.9 %collective-permute-start.6 = (f32[128,512]{1,0:T(8,128)S(1)}, f32[128,512]{1,0:T(8,128)S(1)}, u32[]{:S(2)}, u32[]{:S(2)}) collective-permute-start(f32[128,512]{1,0:T(8,128)S(1)} %get-tuple-element.55), channel_id=1, source_target_pairs={{1,0},{2,1},{3,2},{5,4},{6,5},{7,6},{9,8},{10,9},{11,10},{13,12},{... | collective-permute-start | bytes 786440 | tf_op jit(solution)/shard_map/ppermute | solution.py:456
  18.4 21.7 %collective-permute-start.4 = (f32[256,512]{1,0:T(8,128)S(1)}, f32[256,512]{1,0:T(8,128)S(1)}, u32[]{:S(2)}, u32[]{:S(2)}) collective-permute-start(f32[256,512]{1,0:T(8,128)S(1)} %get-tuple-element.53.refs_5_.refs_11_.refs_1_), channel_id=1, source_target_pairs={{3,2},{6,7},{11,10},{14,15},{19,18},{22,23},{27,26},{30,31}} | collective-permute-start | bytes 1572872 | tf_op jit(solution)/shard_map/ppermute | solution.py:447
  40.1 0.7 collective-permute-start.7
  40.9 28.8 %collective-permute-start.8 = (f32[256,512]{1,0:T(8,128)S(1)}, f32[256,512]{1,0:T(8,128)S(1)}, u32[]{:S(2)}, u32[]{:S(2)}) collective-permute-start(f32[256,512]{1,0:T(8,128)S(1)} %relay.10.refs_3_), channel_id=1, source_target_pairs={{1,0},{6,5},{9,8},{14,13},{17,16},{22,21},{25,24},{30,29}} | collective-permute-start | bytes 1572872 | tf_op jit(solution)/shard_map/ppermute | solution.py:447
  70.5 0.7 collective-permute-start.9
  72.5 3.0 %copy-start.3 = (s32[4]{0:T(128)S(1)}, s32[4]{0:T(128)}, u32[]{:S(2)}) copy-start(s32[4]{0:T(128)} %param.11) | copy-start | bytes 52
  72.5 8.2 %collective-permute-start.17 = (f32[64,512]{1,0:T(8,128)S(1)}, f32[64,512]{1,0:T(8,128)S(1)}, u32[]{:S(2)}, u32[]{:S(2)}) collective-permute-start(f32[64,512]{1,0:T(8,128)S(1)} %get-tuple-element.77), channel_id=1, source_target_pairs={{0,8},{4,12},{8,0},{12,4},{16,24},{20,28},{24,16},{28,20},{1,9},{5... | collective-permute-start | bytes 393224 | tf_op jit(solution)/shard_map/ppermute | solution.py:546
  75.5 6.0 %collective-permute-start.18 = (f32[64,512]{1,0:T(8,128)S(1)}, f32[64,512]{1,0:T(8,128)S(1)}, u32[]{:S(2)}, u32[]{:S(2)}) collective-permute-start(f32[64,512]{1,0:T(8,128)S(1)} %get-tuple-element.78), channel_id=1, source_target_pairs={{0,16},{4,20},{8,24},{12,28},{16,0},{20,4},{24,8},{28,12},{1,17},{... | collective-permute-start | bytes 393224 | tf_op jit(solution)/shard_map/ppermute | solution.py:546
  77.1 6.2 %collective-permute-start.19 = (f32[64,512]{1,0:T(8,128)S(1)}, f32[64,512]{1,0:T(8,128)S(1)}, u32[]{:S(2)}, u32[]{:S(2)}) collective-permute-start(f32[64,512]{1,0:T(8,128)S(1)} %get-tuple-element.79), channel_id=1, source_target_pairs={{0,24},{4,28},{8,16},{12,20},{16,8},{20,12},{24,0},{28,4},{1,25},{... | collective-permute-start | bytes 393224 | tf_op jit(solution)/shard_map/ppermute | solution.py:546
  77.7 11.7 %collective-permute-start.10 = (f32[64,512]{1,0:T(8,128)S(1)}, f32[64,512]{1,0:T(8,128)S(1)}, u32[]{:S(2)}, u32[]{:S(2)}) collective-permute-start(f32[64,512]{1,0:T(8,128)S(1)} %get-tuple-element.67), channel_id=1, source_target_pairs={{0,8},{4,12},{8,0},{12,4},{16,24},{20,28},{24,16},{28,20},{1,9},{5... | collective-permute-start | bytes 393224 | tf_op jit(solution)/shard_map/ppermute | solution.py:546
  79.2 2.2 %copy-start.1 = (f32[4]{0:T(128)S(1)}, f32[4]{0:T(128)}, u32[]{:S(2)}) copy-start(f32[4]{0:T(128)} %param.13) | copy-start | bytes 52
  79.3 2.2 %copy-start.2 = (f32[4]{0:T(128)S(1)}, f32[4]{0:T(128)}, u32[]{:S(2)}) copy-start(f32[4]{0:T(128)} %param.12) | copy-start | bytes 52
  79.3 10.1 %collective-permute-start.11 = (f32[64,512]{1,0:T(8,128)S(1)}, f32[64,512]{1,0:T(8,128)S(1)}, u32[]{:S(2)}, u32[]{:S(2)}) collective-permute-start(f32[64,512]{1,0:T(8,128)S(1)} %get-tuple-element.68), channel_id=1, source_target_pairs={{0,16},{4,20},{8,24},{12,28},{16,0},{20,4},{24,8},{28,12},{1,17},{... | collective-permute-start | bytes 393224 | tf_op jit(solution)/shard_map/ppermute | solution.py:546
  80.8 8.6 %collective-permute-start.12 = (f32[64,512]{1,0:T(8,128)S(1)}, f32[64,512]{1,0:T(8,128)S(1)}, u32[]{:S(2)}, u32[]{:S(2)}) collective-permute-start(f32[64,512]{1,0:T(8,128)S(1)} %get-tuple-element.69), channel_id=1, source_target_pairs={{0,24},{4,28},{8,16},{12,20},{16,8},{20,12},{24,0},{28,4},{1,25},{... | collective-permute-start | bytes 393224 | tf_op jit(solution)/shard_map/ppermute | solution.py:546
  84.3 8.0 %collective-permute-start.20 = (f32[4,64,512]{2,1,0:T(8,128)S(1)}, f32[4,64,512]{2,1,0:T(8,128)S(1)}, u32[]{:S(2)}, u32[]{:S(2)}) collective-permute-start(f32[4,64,512]{2,1,0:T(8,128)S(1)} %get-tuple-element.81), channel_id=1, source_target_pairs={{0,4},{4,0},{8,12},{12,8},{16,20},{20,16},{24,28},{28,24},{1,5},{5... | collective-permute-start | bytes 1572872 | tf_op jit(solution)/shard_map/ppermute | solution.py:565
  90.3 5.6 %collective-permute-start.13 = (f32[4,64,512]{2,1,0:T(8,128)S(1)}, f32[4,64,512]{2,1,0:T(8,128)S(1)}, u32[]{:S(2)}, u32[]{:S(2)}) collective-permute-start(f32[4,64,512]{2,1,0:T(8,128)S(1)} %get-tuple-element.71), channel_id=1, source_target_pairs={{0,4},{4,0},{8,12},{12,8},{16,20},{20,16},{24,28},{28,24},{1,5},{5... | collective-permute-start | bytes 1572872 | tf_op jit(solution)/shard_map/ppermute | solution.py:565
  92.4 6.4 %collective-permute-start.21 = (f32[64,512]{1,0:T(8,128)S(1)}, f32[64,512]{1,0:T(8,128)S(1)}, u32[]{:S(2)}, u32[]{:S(2)}) collective-permute-start(f32[64,512]{1,0:T(8,128)S(1)} %get-tuple-element.83), channel_id=1, source_target_pairs={{0,8},{4,12},{8,0},{12,4},{16,24},{20,28},{24,16},{28,20},{1,9},{5... | collective-permute-start | bytes 393224 | tf_op jit(solution)/shard_map/ppermute | solution.py:546
  93.2 7.4 %collective-permute-start.22 = (f32[64,512]{1,0:T(8,128)S(1)}, f32[64,512]{1,0:T(8,128)S(1)}, u32[]{:S(2)}, u32[]{:S(2)}) collective-permute-start(f32[64,512]{1,0:T(8,128)S(1)} %get-tuple-element.84), channel_id=1, source_target_pairs={{0,16},{4,20},{8,24},{12,28},{16,0},{20,4},{24,8},{28,12},{1,17},{... | collective-permute-start | bytes 393224 | tf_op jit(solution)/shard_map/ppermute | solution.py:546
  94.2 8.1 %collective-permute-start.23 = (f32[64,512]{1,0:T(8,128)S(1)}, f32[64,512]{1,0:T(8,128)S(1)}, u32[]{:S(2)}, u32[]{:S(2)}) collective-permute-start(f32[64,512]{1,0:T(8,128)S(1)} %get-tuple-element.85), channel_id=1, source_target_pairs={{0,24},{4,28},{8,16},{12,20},{16,8},{20,12},{24,0},{28,4},{1,25},{... | collective-permute-start | bytes 393224 | tf_op jit(solution)/shard_map/ppermute | solution.py:546
  96.0 8.4 %collective-permute-start.14 = (f32[64,512]{1,0:T(8,128)S(1)}, f32[64,512]{1,0:T(8,128)S(1)}, u32[]{:S(2)}, u32[]{:S(2)}) collective-permute-start(f32[64,512]{1,0:T(8,128)S(1)} %get-tuple-element.73), channel_id=1, source_target_pairs={{0,8},{4,12},{8,0},{12,4},{16,24},{20,28},{24,16},{28,20},{1,9},{5... | collective-permute-start | bytes 393224 | tf_op jit(solution)/shard_map/ppermute | solution.py:546
  96.8 7.8 %collective-permute-start.15 = (f32[64,512]{1,0:T(8,128)S(1)}, f32[64,512]{1,0:T(8,128)S(1)}, u32[]{:S(2)}, u32[]{:S(2)}) collective-permute-start(f32[64,512]{1,0:T(8,128)S(1)} %get-tuple-element.74), channel_id=1, source_target_pairs={{0,16},{4,20},{8,24},{12,28},{16,0},{20,4},{24,8},{28,12},{1,17},{... | collective-permute-start | bytes 393224 | tf_op jit(solution)/shard_map/ppermute | solution.py:546
  98.8 8.2 %collective-permute-start.16 = (f32[64,512]{1,0:T(8,128)S(1)}, f32[64,512]{1,0:T(8,128)S(1)}, u32[]{:S(2)}, u32[]{:S(2)}) collective-permute-start(f32[64,512]{1,0:T(8,128)S(1)} %get-tuple-element.75), channel_id=1, source_target_pairs={{0,24},{4,28},{8,16},{12,20},{16,8},{20,12},{24,0},{28,4},{1,25},{... | collective-permute-start | bytes 393224 | tf_op jit(solution)/shard_map/ppermute | solution.py:546

commit v6 on v5

--- a/solution.py
+++ b/solution.py
@@ -12,7 +12,7 @@
 HBM = pl.BlockSpec(memory_space=pltpu.HBM)
 VMEM = pl.BlockSpec(memory_space=pltpu.VMEM)
 SMEM = pl.BlockSpec(memory_space=pltpu.SMEM)
-LEADING = 0
+LEADING = 1
 
 
 def split(value):
@@ -26,7 +26,7 @@
 
 
 def parts_of(block, adjoint=False):
-    size = block.shape[0]
+    size = block.shape[1] // 2
     real, imag = block[:, :size], block[:, size:]
     return real, imag, (real - imag if adjoint else real + imag)
 
@@ -87,12 +87,12 @@
     return [pltpu.VMEM((2, 3, size, size), HALF)] * number
 
 
-def call(kernel, outs, scratch, args, specs=None, flops=0, name=None, limit=40):
+def call(kernel, outs, scratch, args, specs=None, out_specs=None, flops=0, name=None, limit=40):
     made = pl.pallas_call(
         kernel,
         out_shape=outs,
         in_specs=specs or [VMEM] * len(args),
-        out_specs=[VMEM] * len(outs),
+        out_specs=out_specs or [VMEM] * len(outs),
         scratch_shapes=scratch,
         compiler_params=pltpu.CompilerParams(vmem_limit_bytes=limit * 2**20),
         cost_estimate=pl.CostEstimate(flops=flops, bytes_accessed=2**20, transcendentals=0),
@@ -140,7 +140,7 @@
     ]
 
 
-def left_sources(loads, whole, source, coupler_out, m_a, m_b, m_c):
+def left_sources(loads, source, coupler_out, m_a, m_b, m_c):
     first = loads.green(0)
     put(m_b, first)
     put(m_a, loads.sigma(0))
@@ -156,20 +156,36 @@
     put(m_a, inner)
     second = loads.green(1)
     put(m_b, second)
-    whole[...] = second + times(times(second, m_a), m_b)
-    return first, second
+    return first, second, times(second, m_a)
 
 
 def source_kernel(green, sigma, coupling, pattern, whole, gate, *scratch):
-    @pl.when(lax.axis_index("slab") == 0)
+    *scratch, out_v, out_sems = scratch
+    place, behind = lax.axis_index("slab"), trailing()
+
+    @pl.when((place == 0) & (behind == 0))
     def _():
         loads = Loads((green, sigma, coupling, pattern), scratch[:4], scratch[4], (1,))
-        left_sources(loads, whole, None, None, *scratch[5:])
-
-    @pl.when((lax.axis_index("slab") > 0) & (trailing() == 1))
+        _, second, through = left_sources(loads, None, None, *scratch[5:])
+        rows = second.shape[0] // 2
+        copies = []
+        for index in range(2):
+            where = slice(index * rows, (index + 1) * rows)
+            out_v[where] = second[where] + times(through[where], scratch[6])
+            copies.append(
+                pltpu.make_async_copy(out_v.at[where], whole.at[where], out_sems.at[index])
+            )
+            copies[-1].start()
+        for copy in copies:
+            copy.wait()
+
+    @pl.when((place > 0) & (behind == 1))
     def _():
         loads = Loads((green, sigma, coupling, pattern), scratch[:4], scratch[4], (0,), False)
-        gate[...] = loads.coupler(0)[: gate.shape[0]]
+        out_v[...] = loads.coupler(0)
+        copy = pltpu.make_async_copy(out_v.at[: gate.shape[0]], gate, out_sems.at[0])
+        copy.start()
+        copy.wait()
 
 
 def map_kernel(
@@ -178,7 +194,8 @@
 ):
     m_a, m_b, m_c = scratch[5:]
     loads = Loads((green, sigma, coupling, pattern), scratch[:4], scratch[4])
-    first, second = left_sources(loads, whole, source, coupler, m_a, m_b, m_c)
+    first, second, through = left_sources(loads, source, coupler, m_a, m_b, m_c)
+    whole[...] = second + times(through, m_b)
     before = loads.coupler(0)
 
     @pl.when(lax.axis_index("slab") > 0)
@@ -458,9 +475,10 @@
     begun = call(
         source_kernel,
         [row, half],
-        loading,
+        loading + [row_v, pltpu.SemaphoreType.DMA((2,))],
         args,
         [HBM] * 4,
+        [HBM] * 2,
         flops=6 * product,
         name="source",
         limit=61,

time: 108 us -> 111 us (1.028)
  waiting for transfers between devices: 55.9 us -> 70.4 us
  starting transfers between devices: 31.4 us -> 25.3 us
  Pallas kernels: 19.8 us -> 14.4 us
    ppermute x7, waiting for transfers between devices: 29 us -> 44.2 us  [relay(): lax.ppermute(value, ('energy', 'slab'), relay_pairs(step, energies, count))]
    ppermute x2, starting transfers between devices: 7.09 us -> 0.14 us  [shards(): other = lax.ppermute(other, 'energy', [(i, i ^ 1) for i in range(energies)])]
    pallas_call x17, Pallas kernels: 19.8 us -> 14.4 us  [call(): pl.pallas_call(kernel, out_shape=outs, in_specs=specs or [VMEM] * len(arg...]
    ppermute x3, waiting for transfers between devices: 17.6 us -> 13.9 us  [lower_place(): return lax.ppermute(value, ('energy', 'slab'), pairs)]
    ppermute x7, starting transfers between devices: 6.09 us -> 9.26 us  [relay(): lax.ppermute(value, ('energy', 'slab'), relay_pairs(step, energies, count))]
    ppermute x12, waiting for transfers between devices: 9.19 us -> 12.3 us  [exchange(): lax.ppermute(value, 'energy', [(i, i ^ 2 * mask) for i in range(energies)])]
    ppermute x12, starting transfers between devices: 15 us -> 12.6 us  [exchange(): lax.ppermute(value, 'energy', [(i, i ^ 2 * mask) for i in range(energies)])]
  transfers between devices with their start and end apart: 24 -> 24, of which waited for: 10 -> 11; matrix products, arithmetic and copies ran while one was open for 0% -> 0% of each run, Pallas kernels for 10% -> 11%
where the time goes in v6:
time: 111 us
  waiting for transfers between devices  70.4 us (63%)
  starting transfers between devices  25.3 us (23%)
  Pallas kernels  14.4 us (13%)
    ppermute x7, waiting for transfers between devices, relay(): lax.ppermute(value, ('energy', 'slab'), relay_pairs(step, energies, count))  44.2 us
    pallas_call x17, Pallas kernels, call(): pl.pallas_call(kernel, out_shape=outs, in_specs=specs or [VMEM] * len(arg...  14.4 us
    ppermute x3, waiting for transfers between devices, lower_place(): return lax.ppermute(value, ('energy', 'slab'), pairs)  13.9 us
    ppermute x12, starting transfers between devices, exchange(): lax.ppermute(value, 'energy', [(i, i ^ 2 * mask) for i in range(energies)])  12.6 us
    ppermute x12, waiting for transfers between devices, exchange(): lax.ppermute(value, 'energy', [(i, i ^ 2 * mask) for i in range(energies)])  12.3 us
    ppermute x7, starting transfers between devices, relay(): lax.ppermute(value, ('energy', 'slab'), relay_pairs(step, energies, count))  9.26 us
    ppermute x3, starting transfers between devices, lower_place(): return lax.ppermute(value, ('energy', 'slab'), pairs)  3.26 us
  transfers between devices with their start and end apart: 24, of which 11 were waited for; matrix products, arithmetic and copies ran while one was open for 0% of the time, Pallas kernels for 11%

profile of v6, /device:TPU:0, one launch (start us, length us, event | category | flops | bytes accessed | tf_op | source)
XLA Modules:
  0.0 111.1 jit_solution(7596758358009402129)
XLA Ops:
  0.6 0.0 copy-start
  0.6 0.1 source.1
  0.8 0.7 collective-permute-start
  1.5 1.3 %collective-permute-start.1 = (f32[128,512]{1,0:T(8,128)}, f32[128,512]{1,0:T(8,128)S(1)}, u32[]{:S(2)}, u32[]{:S(2)}) collective-permute-start(f32[128,512]{1,0:T(8,128)} %get-tuple-element.48), channel_id=1, source_target_pairs={{1,0},{2,1},{3,2},{9,8},{10,9},{11,10},{17,16},{18,17},{19,18},{25... | collective-permute-start | bytes 786440 | tf_op jit(solution)/shard_map/ppermute | solution.py:473
  2.8 0.0 copy-done
  2.8 4.7 %left_maps.1 = (f32[256,512]{1,0:T(8,128)S(1)}, f32[256,512]{1,0:T(8,128)S(1)}, f32[256,512]{1,0:T(8,128)S(1)}, f32[128,512]{1,0:T(8,128)S(1)}, f32[128,512]{1,0...) custom-call(f32[2,2,256,256]{3,2,1,0:T(8,128)} %bitcast.7, ...), custom_call_target="tpu_custom_call" | custom-call | flops 4831838208 | bytes 1048576 | tf_op jit(solution)/shard_map/left_maps/pallas_call | solution.py:91
  7.5 5.5 %collective-permute-done.1.refs_4_.refs_11_ = f32[128,512]{1,0:T(8,128)S(1)} collective-permute-done((f32[128,512]{1,0:T(8,128)}, f32[128,512]{1,0:T(8,128)S(1)}, u32[]{:S(2)}, u32[]{:S(2)}) %collective-permute-start.1) | collective-permute-done | bytes 262176 | tf_op jit(solution)/shard_map/ppermute | solution.py:473
  13.0 0.0 collective-permute-done.refs_0_
  13.0 4.5 %collective-permute-start.2 = (f32[256,512]{1,0:T(8,128)S(1)}, f32[256,512]{1,0:T(8,128)S(1)}, u32[]{:S(2)}, u32[]{:S(2)}) collective-permute-start(f32[256,512]{1,0:T(8,128)S(1)} %relay.6.refs_3_.refs_9_), channel_id=1, source_target_pairs={{0,1},{5,6},{8,9},{13,14},{16,17},{21,22},{24,25},{29,30}} | collective-permute-start | bytes 1572872 | tf_op jit(solution)/shard_map/ppermute | solution.py:464
  17.6 6.6 %collective-permute-done.2.refs_0_.refs_1_ = f32[256,512]{1,0:T(8,128)S(1)} collective-permute-done((f32[256,512]{1,0:T(8,128)S(1)}, f32[256,512]{1,0:T(8,128)S(1)}, u32[]{:S(2)}, u32[]{:S(2)}) %collective-permute-start.2) | collective-permute-done | bytes 524320 | tf_op jit(solution)/shard_map/ppermute | solution.py:464
  24.2 0.7 collective-permute-start.3
  24.9 0.7 collective-permute-start.5
  25.6 1.3 %collective-permute-start.6 = (f32[128,512]{1,0:T(8,128)S(1)}, f32[128,512]{1,0:T(8,128)S(1)}, u32[]{:S(2)}, u32[]{:S(2)}) collective-permute-start(f32[128,512]{1,0:T(8,128)S(1)} %get-tuple-element.55), channel_id=1, source_target_pairs={{1,0},{2,1},{3,2},{5,4},{6,5},{7,6},{9,8},{10,9},{11,10},{13,12},{... | collective-permute-start | bytes 786440 | tf_op jit(solution)/shard_map/ppermute | solution.py:473
  26.9 0.0 collective-permute-done.3.refs_0_.refs_2_
  26.9 0.2 relay.8
  27.1 0.7 collective-permute-start.4
  27.8 0.0 collective-permute-done.5.refs_12_
  27.8 8.4 %collective-permute-done.6.refs_13_ = f32[128,512]{1,0:T(8,128)S(1)} collective-permute-done((f32[128,512]{1,0:T(8,128)S(1)}, f32[128,512]{1,0:T(8,128)S(1)}, u32[]{:S(2)}, u32[]{:S(2)}) %collective-permute-start.6) | collective-permute-done | bytes 262176 | tf_op jit(solution)/shard_map/ppermute | solution.py:473
  36.2 3.3 %right_maps.1 = (bf16[2,3,256,256]{3,2,1,0:T(8,128)(2,1)S(1)}, bf16[2,3,256,256]{3,2,1,0:T(8,128)(2,1)S(1)}, f32[256,512]{1,0:T(8,128)S(1)}, bf16[2,3,256,256]{3...) custom-call(f32[256,512]{1,0:T(8,128)S(1)} %collective-permute-done.refs_0_, ...), custom_call_target="tpu_custom_call" | custom-call | flops 4026531840 | bytes 1048576 | tf_op jit(solution)/shard_map/right_maps/pallas_call | solution.py:91
  39.5 0.0 collective-permute-done.4.refs_0_
  39.6 0.7 collective-permute-start.7
  40.3 0.0 collective-permute-done.7.refs_0_.refs_1_
  40.3 0.7 collective-permute-start.8
  41.0 0.0 collective-permute-done.8.refs_0_.refs_2_
  41.1 1.3 %collective-permute-start.9 = (f32[256,512]{1,0:T(8,128)S(1)}, f32[256,512]{1,0:T(8,128)S(1)}, u32[]{:S(2)}, u32[]{:S(2)}) collective-permute-start(f32[256,512]{1,0:T(8,128)S(1)} %relay.11.refs_4_), channel_id=1, source_target_pairs={{1,0},{9,8},{17,16},{25,24}} | collective-permute-start | bytes 1572872 | tf_op jit(solution)/shard_map/ppermute | solution.py:464
  42.4 37.5 %collective-permute-done.9.refs_3_.refs_0_ = f32[256,512]{1,0:T(8,128)S(1)} collective-permute-done((f32[256,512]{1,0:T(8,128)S(1)}, f32[256,512]{1,0:T(8,128)S(1)}, u32[]{:S(2)}, u32[]{:S(2)}) %collective-permute-start.9) | collective-permute-done | bytes 524320 | tf_op jit(solution)/shard_map/ppermute | solution.py:464
  79.8 1.0 second_slab.1
  80.9 0.0 copy-start.3
  80.9 1.6 %collective-permute-start.17 = (f32[64,512]{1,0:T(8,128)S(1)}, f32[64,512]{1,0:T(8,128)S(1)}, u32[]{:S(2)}, u32[]{:S(2)}) collective-permute-start(f32[64,512]{1,0:T(8,128)S(1)} %get-tuple-element.77), channel_id=1, source_target_pairs={{0,8},{4,12},{8,0},{12,4},{16,24},{20,28},{24,16},{28,20},{1,9},{5... | collective-permute-start | bytes 393224 | tf_op jit(solution)/shard_map/ppermute | solution.py:564
  82.5 1.6 %collective-permute-start.18 = (f32[64,512]{1,0:T(8,128)S(1)}, f32[64,512]{1,0:T(8,128)S(1)}, u32[]{:S(2)}, u32[]{:S(2)}) collective-permute-start(f32[64,512]{1,0:T(8,128)S(1)} %get-tuple-element.78), channel_id=1, source_target_pairs={{0,16},{4,20},{8,24},{12,28},{16,0},{20,4},{24,8},{28,12},{1,17},{... | collective-permute-start | bytes 393224 | tf_op jit(solution)/shard_map/ppermute | solution.py:564
  84.1 0.5 collective-permute-start.19
  84.5 0.9 first_slab.1
  85.4 1.6 %collective-permute-start.10 = (f32[64,512]{1,0:T(8,128)S(1)}, f32[64,512]{1,0:T(8,128)S(1)}, u32[]{:S(2)}, u32[]{:S(2)}) collective-permute-start(f32[64,512]{1,0:T(8,128)S(1)} %get-tuple-element.67), channel_id=1, source_target_pairs={{0,8},{4,12},{8,0},{12,4},{16,24},{20,28},{24,16},{28,20},{1,9},{5... | collective-permute-start | bytes 393224 | tf_op jit(solution)/shard_map/ppermute | solution.py:564
  87.0 1.5 %collective-permute-start.11 = (f32[64,512]{1,0:T(8,128)S(1)}, f32[64,512]{1,0:T(8,128)S(1)}, u32[]{:S(2)}, u32[]{:S(2)}) collective-permute-start(f32[64,512]{1,0:T(8,128)S(1)} %get-tuple-element.68), channel_id=1, source_target_pairs={{0,16},{4,20},{8,24},{12,28},{16,0},{20,4},{24,8},{28,12},{1,17},{... | collective-permute-start | bytes 393224 | tf_op jit(solution)/shard_map/ppermute | solution.py:564
  88.5 0.0 collective-permute-done.17.refs_1_
  88.5 0.5 collective-permute-start.12
  89.0 0.1 add_reduce_fusion.weights
  89.1 0.0 collective-permute-done.18.refs_2_
  89.1 0.8 collective-permute-done.19.refs_3_
  89.9 0.9 mix.3
  90.8 0.1 collective-permute-start.20
  90.9 0.0 collective-permute-done.10.refs_1_
  90.9 1.0 collective-permute-done.11.refs_2_
  92.0 2.4 %collective-permute-done.12.refs_3_ = f32[64,512]{1,0:T(8,128)S(1)} collective-permute-done((f32[64,512]{1,0:T(8,128)S(1)}, f32[64,512]{1,0:T(8,128)S(1)}, u32[]{:S(2)}, u32[]{:S(2)}) %collective-permute-start.12) | collective-permute-done | bytes 131104 | tf_op jit(solution)/shard_map/ppermute | solution.py:564
  94.4 0.9 mix.2
  95.3 0.1 collective-permute-start.13
  95.4 0.0 collective-permute-done.20.other
  95.4 0.1 sum.3
  95.4 0.6 collective-permute-start.21
  96.0 0.5 collective-permute-start.22
  96.6 2.5 %collective-permute-start.23 = (f32[64,512]{1,0:T(8,128)S(1)}, f32[64,512]{1,0:T(8,128)S(1)}, u32[]{:S(2)}, u32[]{:S(2)}) collective-permute-start(f32[64,512]{1,0:T(8,128)S(1)} %get-tuple-element.85), channel_id=1, source_target_pairs={{0,24},{4,28},{8,16},{12,20},{16,8},{20,12},{24,0},{28,4},{1,25},{... | collective-permute-start | bytes 393224 | tf_op jit(solution)/shard_map/ppermute | solution.py:564
  99.0 0.0 collective-permute-done.13.other
  99.0 0.1 sum.2
  99.1 0.6 collective-permute-start.14
  99.7 0.5 collective-permute-start.15
  100.2 1.6 %collective-permute-done.21.refs_5_ = f32[64,512]{1,0:T(8,128)S(1)} collective-permute-done((f32[64,512]{1,0:T(8,128)S(1)}, f32[64,512]{1,0:T(8,128)S(1)}, u32[]{:S(2)}, u32[]{:S(2)}) %collective-permute-start.21) | collective-permute-done | bytes 131104 | tf_op jit(solution)/shard_map/ppermute | solution.py:564
  101.8 0.8 collective-permute-start.16
  102.6 1.0 retarded.1
  103.7 1.1 collective-permute-done.22.refs_6_
  104.8 0.0 collective-permute-done.23.refs_7_
  104.8 2.7 %collective-permute-done.14.refs_1_ = f32[64,512]{1,0:T(8,128)S(1)} collective-permute-done((f32[64,512]{1,0:T(8,128)S(1)}, f32[64,512]{1,0:T(8,128)S(1)}, u32[]{:S(2)}, u32[]{:S(2)}) %collective-permute-start.14) | collective-permute-done | bytes 131104 | tf_op jit(solution)/shard_map/ppermute | solution.py:564
  107.5 2.6 %collective-permute-done.15.refs_2_ = f32[64,512]{1,0:T(8,128)S(1)} collective-permute-done((f32[64,512]{1,0:T(8,128)S(1)}, f32[64,512]{1,0:T(8,128)S(1)}, u32[]{:S(2)}, u32[]{:S(2)}) %collective-permute-start.15) | collective-permute-done | bytes 131104 | tf_op jit(solution)/shard_map/ppermute | solution.py:564
  110.1 0.0 collective-permute-done.16.refs_3_
  110.1 1.1 scattering.1
  (12 shorter events, 0.1 us)
Async XLA Ops:
  0.6 2.1 %copy-start = (s32[2,16,16]{2,1,0:T(8,128)S(1)}, s32[2,16,16]{2,1,0:T(8,128)}, u32[]{:S(2)}) copy-start(s32[2,16,16]{2,1,0:T(8,128)} %pattern.3) | copy-start | bytes 6148
  0.8 12.2 %collective-permute-start = (f32[256,512]{1,0:T(8,128)}, f32[256,512]{1,0:T(8,128)S(1)}, u32[]{:S(2)}, u32[]{:S(2)}) collective-permute-start(f32[256,512]{1,0:T(8,128)} %get-tuple-element.44), channel_id=1, source_target_pairs={{4,5},{12,13},{20,21},{28,29}} | collective-permute-start | bytes 1572872 | tf_op jit(solution)/shard_map/ppermute | solution.py:464
  1.5 11.5 %collective-permute-start.1 = (f32[128,512]{1,0:T(8,128)}, f32[128,512]{1,0:T(8,128)S(1)}, u32[]{:S(2)}, u32[]{:S(2)}) collective-permute-start(f32[128,512]{1,0:T(8,128)} %get-tuple-element.48), channel_id=1, source_target_pairs={{1,0},{2,1},{3,2},{9,8},{10,9},{11,10},{17,16},{18,17},{19,18},{25... | collective-permute-start | bytes 786440 | tf_op jit(solution)/shard_map/ppermute | solution.py:473
  13.0 11.2 %collective-permute-start.2 = (f32[256,512]{1,0:T(8,128)S(1)}, f32[256,512]{1,0:T(8,128)S(1)}, u32[]{:S(2)}, u32[]{:S(2)}) collective-permute-start(f32[256,512]{1,0:T(8,128)S(1)} %relay.6.refs_3_.refs_9_), channel_id=1, source_target_pairs={{0,1},{5,6},{8,9},{13,14},{16,17},{21,22},{24,25},{29,30}} | collective-permute-start | bytes 1572872 | tf_op jit(solution)/shard_map/ppermute | solution.py:464
  24.2 2.7 %collective-permute-start.3 = (f32[256,512]{1,0:T(8,128)S(1)}, f32[256,512]{1,0:T(8,128)S(1)}, u32[]{:S(2)}, u32[]{:S(2)}) collective-permute-start(f32[256,512]{1,0:T(8,128)S(1)} %relay.7.refs_4_.refs_10_), channel_id=1, source_target_pairs={{1,2},{6,7},{9,10},{14,15},{17,18},{22,23},{25,26},{30,31}} | collective-permute-start | bytes 1572872 | tf_op jit(solution)/shard_map/ppermute | solution.py:464
  24.9 2.9 %collective-permute-start.5 = (f32[128,512]{1,0:T(8,128)S(1)}, f32[128,512]{1,0:T(8,128)S(1)}, u32[]{:S(2)}, u32[]{:S(2)}) collective-permute-start(f32[128,512]{1,0:T(8,128)S(1)} %get-tuple-element.54), channel_id=1, source_target_pairs={{5,4},{6,5},{7,6},{13,12},{14,13},{15,14},{21,20},{22,21},{23,22},... | collective-permute-start | bytes 786440 | tf_op jit(solution)/shard_map/ppermute | solution.py:473
  25.6 10.6 %collective-permute-start.6 = (f32[128,512]{1,0:T(8,128)S(1)}, f32[128,512]{1,0:T(8,128)S(1)}, u32[]{:S(2)}, u32[]{:S(2)}) collective-permute-start(f32[128,512]{1,0:T(8,128)S(1)} %get-tuple-element.55), channel_id=1, source_target_pairs={{1,0},{2,1},{3,2},{5,4},{6,5},{7,6},{9,8},{10,9},{11,10},{13,12},{... | collective-permute-start | bytes 786440 | tf_op jit(solution)/shard_map/ppermute | solution.py:473
  27.1 12.4 %collective-permute-start.4 = (f32[256,512]{1,0:T(8,128)S(1)}, f32[256,512]{1,0:T(8,128)S(1)}, u32[]{:S(2)}, u32[]{:S(2)}) collective-permute-start(f32[256,512]{1,0:T(8,128)S(1)} %get-tuple-element.53.refs_5_.refs_11_.refs_1_), channel_id=1, source_target_pairs={{2,3},{7,6},{10,11},{15,14},{18,19},{23,22},{26,27},{31,30}} | collective-permute-start | bytes 1572872 | tf_op jit(solution)/shard_map/ppermute | solution.py:464
  39.6 0.7 collective-permute-start.7
  40.3 0.7 collective-permute-start.8
  41.1 38.8 %collective-permute-start.9 = (f32[256,512]{1,0:T(8,128)S(1)}, f32[256,512]{1,0:T(8,128)S(1)}, u32[]{:S(2)}, u32[]{:S(2)}) collective-permute-start(f32[256,512]{1,0:T(8,128)S(1)} %relay.11.refs_4_), channel_id=1, source_target_pairs={{1,0},{9,8},{17,16},{25,24}} | collective-permute-start | bytes 1572872 | tf_op jit(solution)/shard_map/ppermute | solution.py:464
  80.9 1.6 %copy-start.3 = (s32[4]{0:T(128)S(1)}, s32[4]{0:T(128)}, u32[]{:S(2)}) copy-start(s32[4]{0:T(128)} %param.11) | copy-start | bytes 52
  80.9 7.6 %collective-permute-start.17 = (f32[64,512]{1,0:T(8,128)S(1)}, f32[64,512]{1,0:T(8,128)S(1)}, u32[]{:S(2)}, u32[]{:S(2)}) collective-permute-start(f32[64,512]{1,0:T(8,128)S(1)} %get-tuple-element.77), channel_id=1, source_target_pairs={{0,8},{4,12},{8,0},{12,4},{16,24},{20,28},{24,16},{28,20},{1,9},{5... | collective-permute-start | bytes 393224 | tf_op jit(solution)/shard_map/ppermute | solution.py:564
  82.5 6.6 %collective-permute-start.18 = (f32[64,512]{1,0:T(8,128)S(1)}, f32[64,512]{1,0:T(8,128)S(1)}, u32[]{:S(2)}, u32[]{:S(2)}) collective-permute-start(f32[64,512]{1,0:T(8,128)S(1)} %get-tuple-element.78), channel_id=1, source_target_pairs={{0,16},{4,20},{8,24},{12,28},{16,0},{20,4},{24,8},{28,12},{1,17},{... | collective-permute-start | bytes 393224 | tf_op jit(solution)/shard_map/ppermute | solution.py:564
  84.1 5.9 %collective-permute-start.19 = (f32[64,512]{1,0:T(8,128)S(1)}, f32[64,512]{1,0:T(8,128)S(1)}, u32[]{:S(2)}, u32[]{:S(2)}) collective-permute-start(f32[64,512]{1,0:T(8,128)S(1)} %get-tuple-element.79), channel_id=1, source_target_pairs={{0,24},{4,28},{8,16},{12,20},{16,8},{20,12},{24,0},{28,4},{1,25},{... | collective-permute-start | bytes 393224 | tf_op jit(solution)/shard_map/ppermute | solution.py:564
  85.4 5.5 %collective-permute-start.10 = (f32[64,512]{1,0:T(8,128)S(1)}, f32[64,512]{1,0:T(8,128)S(1)}, u32[]{:S(2)}, u32[]{:S(2)}) collective-permute-start(f32[64,512]{1,0:T(8,128)S(1)} %get-tuple-element.67), channel_id=1, source_target_pairs={{0,8},{4,12},{8,0},{12,4},{16,24},{20,28},{24,16},{28,20},{1,9},{5... | collective-permute-start | bytes 393224 | tf_op jit(solution)/shard_map/ppermute | solution.py:564
  87.0 2.0 %copy-start.1 = (f32[4]{0:T(128)S(1)}, f32[4]{0:T(128)}, u32[]{:S(2)}) copy-start(f32[4]{0:T(128)} %param.13) | copy-start | bytes 52
  87.0 2.0 %copy-start.2 = (f32[4]{0:T(128)S(1)}, f32[4]{0:T(128)}, u32[]{:S(2)}) copy-start(f32[4]{0:T(128)} %param.12) | copy-start | bytes 52
  87.0 5.0 %collective-permute-start.11 = (f32[64,512]{1,0:T(8,128)S(1)}, f32[64,512]{1,0:T(8,128)S(1)}, u32[]{:S(2)}, u32[]{:S(2)}) collective-permute-start(f32[64,512]{1,0:T(8,128)S(1)} %get-tuple-element.68), channel_id=1, source_target_pairs={{0,16},{4,20},{8,24},{12,28},{16,0},{20,4},{24,8},{28,12},{1,17},{... | collective-permute-start | bytes 393224 | tf_op jit(solution)/shard_map/ppermute | solution.py:564
  88.5 5.9 %collective-permute-start.12 = (f32[64,512]{1,0:T(8,128)S(1)}, f32[64,512]{1,0:T(8,128)S(1)}, u32[]{:S(2)}, u32[]{:S(2)}) collective-permute-start(f32[64,512]{1,0:T(8,128)S(1)} %get-tuple-element.69), channel_id=1, source_target_pairs={{0,24},{4,28},{8,16},{12,20},{16,8},{20,12},{24,0},{28,4},{1,25},{... | collective-permute-start | bytes 393224 | tf_op jit(solution)/shard_map/ppermute | solution.py:564
  90.8 4.5 %collective-permute-start.20 = (f32[4,64,512]{2,1,0:T(8,128)S(1)}, f32[4,64,512]{2,1,0:T(8,128)S(1)}, u32[]{:S(2)}, u32[]{:S(2)}) collective-permute-start(f32[4,64,512]{2,1,0:T(8,128)S(1)} %get-tuple-element.81), channel_id=1, source_target_pairs={{0,4},{4,0},{8,12},{12,8},{16,20},{20,16},{24,28},{28,24},{1,5},{5... | collective-permute-start | bytes 1572872 | tf_op jit(solution)/shard_map/ppermute | solution.py:583
  95.3 3.7 %collective-permute-start.13 = (f32[4,64,512]{2,1,0:T(8,128)S(1)}, f32[4,64,512]{2,1,0:T(8,128)S(1)}, u32[]{:S(2)}, u32[]{:S(2)}) collective-permute-start(f32[4,64,512]{2,1,0:T(8,128)S(1)} %get-tuple-element.71), channel_id=1, source_target_pairs={{0,4},{4,0},{8,12},{12,8},{16,20},{20,16},{24,28},{28,24},{1,5},{5... | collective-permute-start | bytes 1572872 | tf_op jit(solution)/shard_map/ppermute | solution.py:583
  95.4 6.4 %collective-permute-start.21 = (f32[64,512]{1,0:T(8,128)S(1)}, f32[64,512]{1,0:T(8,128)S(1)}, u32[]{:S(2)}, u32[]{:S(2)}) collective-permute-start(f32[64,512]{1,0:T(8,128)S(1)} %get-tuple-element.83), channel_id=1, source_target_pairs={{0,8},{4,12},{8,0},{12,4},{16,24},{20,28},{24,16},{28,20},{1,9},{5... | collective-permute-start | bytes 393224 | tf_op jit(solution)/shard_map/ppermute | solution.py:564
  96.0 8.7 %collective-permute-start.22 = (f32[64,512]{1,0:T(8,128)S(1)}, f32[64,512]{1,0:T(8,128)S(1)}, u32[]{:S(2)}, u32[]{:S(2)}) collective-permute-start(f32[64,512]{1,0:T(8,128)S(1)} %get-tuple-element.84), channel_id=1, source_target_pairs={{0,16},{4,20},{8,24},{12,28},{16,0},{20,4},{24,8},{28,12},{1,17},{... | collective-permute-start | bytes 393224 | tf_op jit(solution)/shard_map/ppermute | solution.py:564
  96.6 8.2 %collective-permute-start.23 = (f32[64,512]{1,0:T(8,128)S(1)}, f32[64,512]{1,0:T(8,128)S(1)}, u32[]{:S(2)}, u32[]{:S(2)}) collective-permute-start(f32[64,512]{1,0:T(8,128)S(1)} %get-tuple-element.85), channel_id=1, source_target_pairs={{0,24},{4,28},{8,16},{12,20},{16,8},{20,12},{24,0},{28,4},{1,25},{... | collective-permute-start | bytes 393224 | tf_op jit(solution)/shard_map/ppermute | solution.py:564
  99.1 8.4 %collective-permute-start.14 = (f32[64,512]{1,0:T(8,128)S(1)}, f32[64,512]{1,0:T(8,128)S(1)}, u32[]{:S(2)}, u32[]{:S(2)}) collective-permute-start(f32[64,512]{1,0:T(8,128)S(1)} %get-tuple-element.73), channel_id=1, source_target_pairs={{0,8},{4,12},{8,0},{12,4},{16,24},{20,28},{24,16},{28,20},{1,9},{5... | collective-permute-start | bytes 393224 | tf_op jit(solution)/shard_map/ppermute | solution.py:564
  99.7 10.4 %collective-permute-start.15 = (f32[64,512]{1,0:T(8,128)S(1)}, f32[64,512]{1,0:T(8,128)S(1)}, u32[]{:S(2)}, u32[]{:S(2)}) collective-permute-start(f32[64,512]{1,0:T(8,128)S(1)} %get-tuple-element.74), channel_id=1, source_target_pairs={{0,16},{4,20},{8,24},{12,28},{16,0},{20,4},{24,8},{28,12},{1,17},{... | collective-permute-start | bytes 393224 | tf_op jit(solution)/shard_map/ppermute | solution.py:564
  101.8 8.3 %collective-permute-start.16 = (f32[64,512]{1,0:T(8,128)S(1)}, f32[64,512]{1,0:T(8,128)S(1)}, u32[]{:S(2)}, u32[]{:S(2)}) collective-permute-start(f32[64,512]{1,0:T(8,128)S(1)} %get-tuple-element.75), channel_id=1, source_target_pairs={{0,24},{4,28},{8,16},{12,20},{16,8},{20,12},{24,0},{28,4},{1,25},{... | collective-permute-start | bytes 393224 | tf_op jit(solution)/shard_map/ppermute | solution.py:564

commit v7 on v6

--- a/solution.py
+++ b/solution.py
@@ -12,7 +12,7 @@
 HBM = pl.BlockSpec(memory_space=pltpu.HBM)
 VMEM = pl.BlockSpec(memory_space=pltpu.VMEM)
 SMEM = pl.BlockSpec(memory_space=pltpu.SMEM)
-LEADING = 1
+LEADING = 0
 
 
 def split(value):

time: 111 us -> 112 us (level)
  waiting for transfers between devices: 70.4 us -> 60.8 us
  Pallas kernels: 14.4 us -> 19.7 us
  starting transfers between devices: 25.3 us -> 30 us
    ppermute x7, waiting for transfers between devices: 44.2 us -> 28.4 us  [relay(): lax.ppermute(value, ('energy', 'slab'), relay_pairs(step, energies, count))]
    ppermute x12, starting transfers between devices: 12.6 us -> 19.8 us  [exchange(): lax.ppermute(value, 'energy', [(i, i ^ 2 * mask) for i in range(energies)])]
    pallas_call x17, Pallas kernels: 14.4 us -> 19.7 us  [call(): pl.pallas_call(kernel, out_shape=outs, in_specs=specs or [VMEM] * len(arg...]
    ppermute x3, waiting for transfers between devices: 13.9 us -> 18.8 us  [lower_place(): return lax.ppermute(value, ('energy', 'slab'), pairs)]
    ppermute x7, starting transfers between devices: 9.26 us -> 6.09 us  [relay(): lax.ppermute(value, ('energy', 'slab'), relay_pairs(step, energies, count))]
    ppermute x12, waiting for transfers between devices: 12.3 us -> 13.6 us  [exchange(): lax.ppermute(value, 'energy', [(i, i ^ 2 * mask) for i in range(energies)])]
  transfers between devices with their start and end apart: 24 -> 24, of which waited for: 11 -> 11; matrix products, arithmetic and copies ran while one was open for 0% -> 0% of each run, Pallas kernels for 11% -> 10%
where the time goes in v7:
time: 112 us
  waiting for transfers between devices  60.8 us (54%)
  starting transfers between devices  30 us (27%)
  Pallas kernels  19.7 us (18%)
    ppermute x7, waiting for transfers between devices, relay(): lax.ppermute(value, ('energy', 'slab'), relay_pairs(step, energies, count))  28.4 us
    ppermute x12, starting transfers between devices, exchange(): lax.ppermute(value, 'energy', [(i, i ^ 2 * mask) for i in range(energies)])  19.8 us
    pallas_call x17, Pallas kernels, call(): pl.pallas_call(kernel, out_shape=outs, in_specs=specs or [VMEM] * len(arg...  19.7 us
    ppermute x3, waiting for transfers between devices, lower_place(): return lax.ppermute(value, ('energy', 'slab'), pairs)  18.8 us
    ppermute x12, waiting for transfers between devices, exchange(): lax.ppermute(value, 'energy', [(i, i ^ 2 * mask) for i in range(energies)])  13.6 us
    ppermute x7, starting transfers between devices, relay(): lax.ppermute(value, ('energy', 'slab'), relay_pairs(step, energies, count))  6.09 us
    ppermute x3, starting transfers between devices, lower_place(): return lax.ppermute(value, ('energy', 'slab'), pairs)  3.26 us
  transfers between devices with their start and end apart: 24, of which 11 were waited for; matrix products, arithmetic and copies ran while one was open for 0% of the time, Pallas kernels for 10%

profile of v7, /device:TPU:0, one launch (start us, length us, event | category | flops | bytes accessed | tf_op | source)
XLA Modules:
  0.0 111.5 jit_solution(1821325399750414282)
XLA Ops:
  0.6 0.0 copy-start
  0.6 5.2 %source.1 = (f32[256,512]{1,0:T(8,128)}, f32[128,512]{1,0:T(8,128)}) custom-call(f32[2,2,256,256]{3,2,1,0:T(8,128)} %bitcast.6, f32[2,2,256,256]{3,2,1,0:T(8,128)} %bitcast.8, f32[2,2,256,256]{3,2,1,0:T(8,128)} %coupling.3, s32[2,16,16]{2,1,0:T(8,128)} %pattern.3), custom_call_target="tpu_custom_call" | custom-call | flops 2415919104 | bytes 1048576 | tf_op jit(solution)/shard_map/source/pallas_call | solution.py:91
  5.8 1.3 %collective-permute-start = (f32[256,512]{1,0:T(8,128)}, f32[256,512]{1,0:T(8,128)S(1)}, u32[]{:S(2)}, u32[]{:S(2)}) collective-permute-start(f32[256,512]{1,0:T(8,128)} %get-tuple-element.44), channel_id=1, source_target_pairs={{0,1},{8,9},{16,17},{24,25}} | collective-permute-start | bytes 1572872 | tf_op jit(solution)/shard_map/ppermute | solution.py:464
  7.1 0.7 collective-permute-start.1
  7.8 4.7 %left_maps.1 = (f32[256,512]{1,0:T(8,128)S(1)}, f32[256,512]{1,0:T(8,128)S(1)}, f32[256,512]{1,0:T(8,128)S(1)}, f32[128,512]{1,0:T(8,128)S(1)}, f32[128,512]{1,0...) custom-call(f32[2,2,256,256]{3,2,1,0:T(8,128)} %bitcast.7, ...), custom_call_target="tpu_custom_call" | custom-call | flops 4831838208 | bytes 1048576 | tf_op jit(solution)/shard_map/left_maps/pallas_call | solution.py:91
  12.6 0.0 collective-permute-done.1.refs_4_.refs_11_
  12.6 1.6 %collective-permute-done.refs_0_ = f32[256,512]{1,0:T(8,128)S(1)} collective-permute-done((f32[256,512]{1,0:T(8,128)}, f32[256,512]{1,0:T(8,128)S(1)}, u32[]{:S(2)}, u32[]{:S(2)}) %collective-permute-start) | collective-permute-done | bytes 524320 | tf_op jit(solution)/shard_map/ppermute | solution.py:464
  14.2 0.7 collective-permute-start.2
  14.9 0.0 collective-permute-done.2.refs_0_.refs_1_
  14.9 0.7 collective-permute-start.3
  15.6 1.3 %collective-permute-start.5 = (f32[128,512]{1,0:T(8,128)S(1)}, f32[128,512]{1,0:T(8,128)S(1)}, u32[]{:S(2)}, u32[]{:S(2)}) collective-permute-start(f32[128,512]{1,0:T(8,128)S(1)} %get-tuple-element.54), channel_id=1, source_target_pairs={{1,0},{2,1},{3,2},{9,8},{10,9},{11,10},{17,16},{18,17},{19,18},{25... | collective-permute-start | bytes 786440 | tf_op jit(solution)/shard_map/ppermute | solution.py:473
  16.9 1.3 %collective-permute-start.6 = (f32[128,512]{1,0:T(8,128)S(1)}, f32[128,512]{1,0:T(8,128)S(1)}, u32[]{:S(2)}, u32[]{:S(2)}) collective-permute-start(f32[128,512]{1,0:T(8,128)S(1)} %get-tuple-element.55), channel_id=1, source_target_pairs={{1,0},{2,1},{3,2},{5,4},{6,5},{7,6},{9,8},{10,9},{11,10},{13,12},{... | collective-permute-start | bytes 786440 | tf_op jit(solution)/shard_map/ppermute | solution.py:473
  18.2 0.0 collective-permute-done.3.refs_0_.refs_2_
  18.2 0.2 relay.8
  18.4 0.7 collective-permute-start.4
  19.1 14.3 %collective-permute-done.5.refs_12_ = f32[128,512]{1,0:T(8,128)S(1)} collective-permute-done((f32[128,512]{1,0:T(8,128)S(1)}, f32[128,512]{1,0:T(8,128)S(1)}, u32[]{:S(2)}, u32[]{:S(2)}) %collective-permute-start.5) | collective-permute-done | bytes 262176 | tf_op jit(solution)/shard_map/ppermute | solution.py:473
  33.5 4.4 %collective-permute-done.6.refs_13_ = f32[128,512]{1,0:T(8,128)S(1)} collective-permute-done((f32[128,512]{1,0:T(8,128)S(1)}, f32[128,512]{1,0:T(8,128)S(1)}, u32[]{:S(2)}, u32[]{:S(2)}) %collective-permute-start.6) | collective-permute-done | bytes 262176 | tf_op jit(solution)/shard_map/ppermute | solution.py:473
  37.9 3.3 %right_maps.1 = (bf16[2,3,256,256]{3,2,1,0:T(8,128)(2,1)S(1)}, bf16[2,3,256,256]{3,2,1,0:T(8,128)(2,1)S(1)}, f32[256,512]{1,0:T(8,128)S(1)}, bf16[2,3,256,256]{3...) custom-call(f32[256,512]{1,0:T(8,128)S(1)} %collective-permute-done.refs_0_, ...), custom_call_target="tpu_custom_call" | custom-call | flops 4026531840 | bytes 1048576 | tf_op jit(solution)/shard_map/right_maps/pallas_call | solution.py:91
  41.2 0.0 collective-permute-done.4.refs_0_
  41.3 0.7 collective-permute-start.7
  42.0 0.0 collective-permute-done.7.refs_0_.refs_1_
  42.0 1.3 %collective-permute-start.8 = (f32[256,512]{1,0:T(8,128)S(1)}, f32[256,512]{1,0:T(8,128)S(1)}, u32[]{:S(2)}, u32[]{:S(2)}) collective-permute-start(f32[256,512]{1,0:T(8,128)S(1)} %relay.10.refs_3_), channel_id=1, source_target_pairs={{1,0},{6,5},{9,8},{14,13},{17,16},{22,21},{25,24},{30,29}} | collective-permute-start | bytes 1572872 | tf_op jit(solution)/shard_map/ppermute | solution.py:464
  43.3 26.8 %collective-permute-done.8.refs_0_.refs_2_ = f32[256,512]{1,0:T(8,128)S(1)} collective-permute-done((f32[256,512]{1,0:T(8,128)S(1)}, f32[256,512]{1,0:T(8,128)S(1)}, u32[]{:S(2)}, u32[]{:S(2)}) %collective-permute-start.8) | collective-permute-done | bytes 524320 | tf_op jit(solution)/shard_map/ppermute | solution.py:464
  70.1 0.9 relay.11.refs_4_
  71.0 0.7 collective-permute-start.9
  71.7 0.0 collective-permute-done.9.refs_3_.refs_0_
  71.7 1.3 %second_slab.1 = (f32[256,512]{1,0:T(8,128)S(1)}, f32[64,512]{1,0:T(8,128)S(1)}, f32[64,512]{1,0:T(8,128)S(1)}, f32[64,512]{1,0:T(8,128)S(1)}, f32[64,512]{1,0:T(8,128)S(1)}) custom-call(f32[256,512]{1,0:T(8,128)S(1)} %collective-permute-done.4.refs_0_, f32[256,512]{1,0:T(8,128)S(1)} %collective-permute-done.7.refs_0_.refs_1_, ...), custom_call_target="tpu_custom_call" | custom-call | flops 805306368 | bytes 1048576 | tf_op jit(solution)/shard_map/second_slab/pallas_call | solution.py:91
  73.0 0.0 copy-start.3
  73.0 6.4 %collective-permute-start.17 = (f32[64,512]{1,0:T(8,128)S(1)}, f32[64,512]{1,0:T(8,128)S(1)}, u32[]{:S(2)}, u32[]{:S(2)}) collective-permute-start(f32[64,512]{1,0:T(8,128)S(1)} %get-tuple-element.77), channel_id=1, source_target_pairs={{0,8},{4,12},{8,0},{12,4},{16,24},{20,28},{24,16},{28,20},{1,9},{5... | collective-permute-start | bytes 393224 | tf_op jit(solution)/shard_map/ppermute | solution.py:564
  79.4 1.6 %collective-permute-start.18 = (f32[64,512]{1,0:T(8,128)S(1)}, f32[64,512]{1,0:T(8,128)S(1)}, u32[]{:S(2)}, u32[]{:S(2)}) collective-permute-start(f32[64,512]{1,0:T(8,128)S(1)} %get-tuple-element.78), channel_id=1, source_target_pairs={{0,16},{4,20},{8,24},{12,28},{16,0},{20,4},{24,8},{28,12},{1,17},{... | collective-permute-start | bytes 393224 | tf_op jit(solution)/shard_map/ppermute | solution.py:564
  81.0 0.5 collective-permute-start.19
  81.5 0.1 first_slab.1
  81.5 1.6 %collective-permute-start.10 = (f32[64,512]{1,0:T(8,128)S(1)}, f32[64,512]{1,0:T(8,128)S(1)}, u32[]{:S(2)}, u32[]{:S(2)}) collective-permute-start(f32[64,512]{1,0:T(8,128)S(1)} %get-tuple-element.67), channel_id=1, source_target_pairs={{0,8},{4,12},{8,0},{12,4},{16,24},{20,28},{24,16},{28,20},{1,9},{5... | collective-permute-start | bytes 393224 | tf_op jit(solution)/shard_map/ppermute | solution.py:564
  83.1 1.5 %collective-permute-start.11 = (f32[64,512]{1,0:T(8,128)S(1)}, f32[64,512]{1,0:T(8,128)S(1)}, u32[]{:S(2)}, u32[]{:S(2)}) collective-permute-start(f32[64,512]{1,0:T(8,128)S(1)} %get-tuple-element.68), channel_id=1, source_target_pairs={{0,16},{4,20},{8,24},{12,28},{16,0},{20,4},{24,8},{28,12},{1,17},{... | collective-permute-start | bytes 393224 | tf_op jit(solution)/shard_map/ppermute | solution.py:564
  84.6 0.0 collective-permute-done.17.refs_1_
  84.6 1.6 %collective-permute-start.12 = (f32[64,512]{1,0:T(8,128)S(1)}, f32[64,512]{1,0:T(8,128)S(1)}, u32[]{:S(2)}, u32[]{:S(2)}) collective-permute-start(f32[64,512]{1,0:T(8,128)S(1)} %get-tuple-element.69), channel_id=1, source_target_pairs={{0,24},{4,28},{8,16},{12,20},{16,8},{20,12},{24,0},{28,4},{1,25},{... | collective-permute-start | bytes 393224 | tf_op jit(solution)/shard_map/ppermute | solution.py:564
  86.3 0.1 add_reduce_fusion.weights
  86.3 2.1 %collective-permute-done.18.refs_2_ = f32[64,512]{1,0:T(8,128)S(1)} collective-permute-done((f32[64,512]{1,0:T(8,128)S(1)}, f32[64,512]{1,0:T(8,128)S(1)}, u32[]{:S(2)}, u32[]{:S(2)}) %collective-permute-start.18) | collective-permute-done | bytes 131104 | tf_op jit(solution)/shard_map/ppermute | solution.py:564
  88.4 0.0 collective-permute-done.19.refs_3_
  88.4 0.9 mix.3
  89.4 0.7 collective-permute-start.20
  90.0 0.2 collective-permute-done.10.refs_1_
  90.2 3.9 %collective-permute-done.11.refs_2_ = f32[64,512]{1,0:T(8,128)S(1)} collective-permute-done((f32[64,512]{1,0:T(8,128)S(1)}, f32[64,512]{1,0:T(8,128)S(1)}, u32[]{:S(2)}, u32[]{:S(2)}) %collective-permute-start.11) | collective-permute-done | bytes 131104 | tf_op jit(solution)/shard_map/ppermute | solution.py:564
  94.0 0.0 collective-permute-done.12.refs_3_
  94.1 0.9 mix.2
  95.0 0.2 collective-permute-start.13
  95.2 0.0 collective-permute-done.20.other
  95.2 0.1 sum.3
  95.2 0.9 collective-permute-start.21
  96.1 1.2 %collective-permute-start.22 = (f32[64,512]{1,0:T(8,128)S(1)}, f32[64,512]{1,0:T(8,128)S(1)}, u32[]{:S(2)}, u32[]{:S(2)}) collective-permute-start(f32[64,512]{1,0:T(8,128)S(1)} %get-tuple-element.84), channel_id=1, source_target_pairs={{0,16},{4,20},{8,24},{12,28},{16,0},{20,4},{24,8},{28,12},{1,17},{... | collective-permute-start | bytes 393224 | tf_op jit(solution)/shard_map/ppermute | solution.py:564
  97.3 1.5 %collective-permute-start.23 = (f32[64,512]{1,0:T(8,128)S(1)}, f32[64,512]{1,0:T(8,128)S(1)}, u32[]{:S(2)}, u32[]{:S(2)}) collective-permute-start(f32[64,512]{1,0:T(8,128)S(1)} %get-tuple-element.85), channel_id=1, source_target_pairs={{0,24},{4,28},{8,16},{12,20},{16,8},{20,12},{24,0},{28,4},{1,25},{... | collective-permute-start | bytes 393224 | tf_op jit(solution)/shard_map/ppermute | solution.py:564
  98.8 0.0 collective-permute-done.13.other
  98.8 0.1 sum.2
  98.9 0.9 collective-permute-start.14
  99.7 1.2 %collective-permute-start.15 = (f32[64,512]{1,0:T(8,128)S(1)}, f32[64,512]{1,0:T(8,128)S(1)}, u32[]{:S(2)}, u32[]{:S(2)}) collective-permute-start(f32[64,512]{1,0:T(8,128)S(1)} %get-tuple-element.74), channel_id=1, source_target_pairs={{0,16},{4,20},{8,24},{12,28},{16,0},{20,4},{24,8},{28,12},{1,17},{... | collective-permute-start | bytes 393224 | tf_op jit(solution)/shard_map/ppermute | solution.py:564
  100.9 0.7 collective-permute-done.21.refs_5_
  101.6 1.0 collective-permute-start.16
  102.6 1.0 retarded.1
  103.7 0.0 collective-permute-done.22.refs_6_
  103.7 1.7 %collective-permute-done.23.refs_7_ = f32[64,512]{1,0:T(8,128)S(1)} collective-permute-done((f32[64,512]{1,0:T(8,128)S(1)}, f32[64,512]{1,0:T(8,128)S(1)}, u32[]{:S(2)}, u32[]{:S(2)}) %collective-permute-start.23) | collective-permute-done | bytes 131104 | tf_op jit(solution)/shard_map/ppermute | solution.py:564
  105.4 1.9 %collective-permute-done.14.refs_1_ = f32[64,512]{1,0:T(8,128)S(1)} collective-permute-done((f32[64,512]{1,0:T(8,128)S(1)}, f32[64,512]{1,0:T(8,128)S(1)}, u32[]{:S(2)}, u32[]{:S(2)}) %collective-permute-start.14) | collective-permute-done | bytes 131104 | tf_op jit(solution)/shard_map/ppermute | solution.py:564
  107.3 0.0 collective-permute-done.15.refs_2_
  107.3 3.2 %collective-permute-done.16.refs_3_ = f32[64,512]{1,0:T(8,128)S(1)} collective-permute-done((f32[64,512]{1,0:T(8,128)S(1)}, f32[64,512]{1,0:T(8,128)S(1)}, u32[]{:S(2)}, u32[]{:S(2)}) %collective-permute-start.16) | collective-permute-done | bytes 131104 | tf_op jit(solution)/shard_map/ppermute | solution.py:564
  110.5 1.0 scattering.1
  (12 shorter events, 0.1 us)
Async XLA Ops:
  0.6 7.2 %copy-start = (s32[2,16,16]{2,1,0:T(8,128)S(1)}, s32[2,16,16]{2,1,0:T(8,128)}, u32[]{:S(2)}) copy-start(s32[2,16,16]{2,1,0:T(8,128)} %pattern.3) | copy-start | bytes 6148
  5.8 8.3 %collective-permute-start = (f32[256,512]{1,0:T(8,128)}, f32[256,512]{1,0:T(8,128)S(1)}, u32[]{:S(2)}, u32[]{:S(2)}) collective-permute-start(f32[256,512]{1,0:T(8,128)} %get-tuple-element.44), channel_id=1, source_target_pairs={{0,1},{8,9},{16,17},{24,25}} | collective-permute-start | bytes 1572872 | tf_op jit(solution)/shard_map/ppermute | solution.py:464
  7.1 5.4 %collective-permute-start.1 = (f32[128,512]{1,0:T(8,128)}, f32[128,512]{1,0:T(8,128)S(1)}, u32[]{:S(2)}, u32[]{:S(2)}) collective-permute-start(f32[128,512]{1,0:T(8,128)} %get-tuple-element.48), channel_id=1, source_target_pairs={{5,4},{6,5},{7,6},{13,12},{14,13},{15,14},{21,20},{22,21},{23,22},... | collective-permute-start | bytes 786440 | tf_op jit(solution)/shard_map/ppermute | solution.py:473
  14.2 0.7 collective-permute-start.2
  14.9 3.3 %collective-permute-start.3 = (f32[256,512]{1,0:T(8,128)S(1)}, f32[256,512]{1,0:T(8,128)S(1)}, u32[]{:S(2)}, u32[]{:S(2)}) collective-permute-start(f32[256,512]{1,0:T(8,128)S(1)} %relay.7.refs_4_.refs_10_), channel_id=1, source_target_pairs={{2,3},{5,6},{10,11},{13,14},{18,19},{21,22},{26,27},{29,30}} | collective-permute-start | bytes 1572872 | tf_op jit(solution)/shard_map/ppermute | solution.py:464
  15.6 17.9 %collective-permute-start.5 = (f32[128,512]{1,0:T(8,128)S(1)}, f32[128,512]{1,0:T(8,128)S(1)}, u32[]{:S(2)}, u32[]{:S(2)}) collective-permute-start(f32[128,512]{1,0:T(8,128)S(1)} %get-tuple-element.54), channel_id=1, source_target_pairs={{1,0},{2,1},{3,2},{9,8},{10,9},{11,10},{17,16},{18,17},{19,18},{25... | collective-permute-start | bytes 786440 | tf_op jit(solution)/shard_map/ppermute | solution.py:473
  16.9 21.0 %collective-permute-start.6 = (f32[128,512]{1,0:T(8,128)S(1)}, f32[128,512]{1,0:T(8,128)S(1)}, u32[]{:S(2)}, u32[]{:S(2)}) collective-permute-start(f32[128,512]{1,0:T(8,128)S(1)} %get-tuple-element.55), channel_id=1, source_target_pairs={{1,0},{2,1},{3,2},{5,4},{6,5},{7,6},{9,8},{10,9},{11,10},{13,12},{... | collective-permute-start | bytes 786440 | tf_op jit(solution)/shard_map/ppermute | solution.py:473
  18.4 22.8 %collective-permute-start.4 = (f32[256,512]{1,0:T(8,128)S(1)}, f32[256,512]{1,0:T(8,128)S(1)}, u32[]{:S(2)}, u32[]{:S(2)}) collective-permute-start(f32[256,512]{1,0:T(8,128)S(1)} %get-tuple-element.53.refs_5_.refs_11_.refs_1_), channel_id=1, source_target_pairs={{3,2},{6,7},{11,10},{14,15},{19,18},{22,23},{27,26},{30,31}} | collective-permute-start | bytes 1572872 | tf_op jit(solution)/shard_map/ppermute | solution.py:464
  41.3 0.7 collective-permute-start.7
  42.0 28.1 %collective-permute-start.8 = (f32[256,512]{1,0:T(8,128)S(1)}, f32[256,512]{1,0:T(8,128)S(1)}, u32[]{:S(2)}, u32[]{:S(2)}) collective-permute-start(f32[256,512]{1,0:T(8,128)S(1)} %relay.10.refs_3_), channel_id=1, source_target_pairs={{1,0},{6,5},{9,8},{14,13},{17,16},{22,21},{25,24},{30,29}} | collective-permute-start | bytes 1572872 | tf_op jit(solution)/shard_map/ppermute | solution.py:464
  71.0 0.7 collective-permute-start.9
  73.0 6.4 %copy-start.3 = (s32[4]{0:T(128)S(1)}, s32[4]{0:T(128)}, u32[]{:S(2)}) copy-start(s32[4]{0:T(128)} %param.11) | copy-start | bytes 52
  73.0 11.6 %collective-permute-start.17 = (f32[64,512]{1,0:T(8,128)S(1)}, f32[64,512]{1,0:T(8,128)S(1)}, u32[]{:S(2)}, u32[]{:S(2)}) collective-permute-start(f32[64,512]{1,0:T(8,128)S(1)} %get-tuple-element.77), channel_id=1, source_target_pairs={{0,8},{4,12},{8,0},{12,4},{16,24},{20,28},{24,16},{28,20},{1,9},{5... | collective-permute-start | bytes 393224 | tf_op jit(solution)/shard_map/ppermute | solution.py:564
  79.4 9.0 %collective-permute-start.18 = (f32[64,512]{1,0:T(8,128)S(1)}, f32[64,512]{1,0:T(8,128)S(1)}, u32[]{:S(2)}, u32[]{:S(2)}) collective-permute-start(f32[64,512]{1,0:T(8,128)S(1)} %get-tuple-element.78), channel_id=1, source_target_pairs={{0,16},{4,20},{8,24},{12,28},{16,0},{20,4},{24,8},{28,12},{1,17},{... | collective-permute-start | bytes 393224 | tf_op jit(solution)/shard_map/ppermute | solution.py:564
  81.0 7.4 %collective-permute-start.19 = (f32[64,512]{1,0:T(8,128)S(1)}, f32[64,512]{1,0:T(8,128)S(1)}, u32[]{:S(2)}, u32[]{:S(2)}) collective-permute-start(f32[64,512]{1,0:T(8,128)S(1)} %get-tuple-element.79), channel_id=1, source_target_pairs={{0,24},{4,28},{8,16},{12,20},{16,8},{20,12},{24,0},{28,4},{1,25},{... | collective-permute-start | bytes 393224 | tf_op jit(solution)/shard_map/ppermute | solution.py:564
  81.5 8.6 %collective-permute-start.10 = (f32[64,512]{1,0:T(8,128)S(1)}, f32[64,512]{1,0:T(8,128)S(1)}, u32[]{:S(2)}, u32[]{:S(2)}) collective-permute-start(f32[64,512]{1,0:T(8,128)S(1)} %get-tuple-element.67), channel_id=1, source_target_pairs={{0,8},{4,12},{8,0},{12,4},{16,24},{20,28},{24,16},{28,20},{1,9},{5... | collective-permute-start | bytes 393224 | tf_op jit(solution)/shard_map/ppermute | solution.py:564
  83.1 3.1 %copy-start.1 = (f32[4]{0:T(128)S(1)}, f32[4]{0:T(128)}, u32[]{:S(2)}) copy-start(f32[4]{0:T(128)} %param.13) | copy-start | bytes 52
  83.1 3.1 %copy-start.2 = (f32[4]{0:T(128)S(1)}, f32[4]{0:T(128)}, u32[]{:S(2)}) copy-start(f32[4]{0:T(128)} %param.12) | copy-start | bytes 52
  83.1 10.9 %collective-permute-start.11 = (f32[64,512]{1,0:T(8,128)S(1)}, f32[64,512]{1,0:T(8,128)S(1)}, u32[]{:S(2)}, u32[]{:S(2)}) collective-permute-start(f32[64,512]{1,0:T(8,128)S(1)} %get-tuple-element.68), channel_id=1, source_target_pairs={{0,16},{4,20},{8,24},{12,28},{16,0},{20,4},{24,8},{28,12},{1,17},{... | collective-permute-start | bytes 393224 | tf_op jit(solution)/shard_map/ppermute | solution.py:564
  84.6 9.4 %collective-permute-start.12 = (f32[64,512]{1,0:T(8,128)S(1)}, f32[64,512]{1,0:T(8,128)S(1)}, u32[]{:S(2)}, u32[]{:S(2)}) collective-permute-start(f32[64,512]{1,0:T(8,128)S(1)} %get-tuple-element.69), channel_id=1, source_target_pairs={{0,24},{4,28},{8,16},{12,20},{16,8},{20,12},{24,0},{28,4},{1,25},{... | collective-permute-start | bytes 393224 | tf_op jit(solution)/shard_map/ppermute | solution.py:564
  89.4 5.8 %collective-permute-start.20 = (f32[4,64,512]{2,1,0:T(8,128)S(1)}, f32[4,64,512]{2,1,0:T(8,128)S(1)}, u32[]{:S(2)}, u32[]{:S(2)}) collective-permute-start(f32[4,64,512]{2,1,0:T(8,128)S(1)} %get-tuple-element.81), channel_id=1, source_target_pairs={{0,4},{4,0},{8,12},{12,8},{16,20},{20,16},{24,28},{28,24},{1,5},{5... | collective-permute-start | bytes 1572872 | tf_op jit(solution)/shard_map/ppermute | solution.py:583
  95.0 3.8 %collective-permute-start.13 = (f32[4,64,512]{2,1,0:T(8,128)S(1)}, f32[4,64,512]{2,1,0:T(8,128)S(1)}, u32[]{:S(2)}, u32[]{:S(2)}) collective-permute-start(f32[4,64,512]{2,1,0:T(8,128)S(1)} %get-tuple-element.71), channel_id=1, source_target_pairs={{0,4},{4,0},{8,12},{12,8},{16,20},{20,16},{24,28},{28,24},{1,5},{5... | collective-permute-start | bytes 1572872 | tf_op jit(solution)/shard_map/ppermute | solution.py:583
  95.2 6.4 %collective-permute-start.21 = (f32[64,512]{1,0:T(8,128)S(1)}, f32[64,512]{1,0:T(8,128)S(1)}, u32[]{:S(2)}, u32[]{:S(2)}) collective-permute-start(f32[64,512]{1,0:T(8,128)S(1)} %get-tuple-element.83), channel_id=1, source_target_pairs={{0,8},{4,12},{8,0},{12,4},{16,24},{20,28},{24,16},{28,20},{1,9},{5... | collective-permute-start | bytes 393224 | tf_op jit(solution)/shard_map/ppermute | solution.py:564
  96.1 7.5 %collective-permute-start.22 = (f32[64,512]{1,0:T(8,128)S(1)}, f32[64,512]{1,0:T(8,128)S(1)}, u32[]{:S(2)}, u32[]{:S(2)}) collective-permute-start(f32[64,512]{1,0:T(8,128)S(1)} %get-tuple-element.84), channel_id=1, source_target_pairs={{0,16},{4,20},{8,24},{12,28},{16,0},{20,4},{24,8},{28,12},{1,17},{... | collective-permute-start | bytes 393224 | tf_op jit(solution)/shard_map/ppermute | solution.py:564
  97.3 8.1 %collective-permute-start.23 = (f32[64,512]{1,0:T(8,128)S(1)}, f32[64,512]{1,0:T(8,128)S(1)}, u32[]{:S(2)}, u32[]{:S(2)}) collective-permute-start(f32[64,512]{1,0:T(8,128)S(1)} %get-tuple-element.85), channel_id=1, source_target_pairs={{0,24},{4,28},{8,16},{12,20},{16,8},{20,12},{24,0},{28,4},{1,25},{... | collective-permute-start | bytes 393224 | tf_op jit(solution)/shard_map/ppermute | solution.py:564
  98.9 8.4 %collective-permute-start.14 = (f32[64,512]{1,0:T(8,128)S(1)}, f32[64,512]{1,0:T(8,128)S(1)}, u32[]{:S(2)}, u32[]{:S(2)}) collective-permute-start(f32[64,512]{1,0:T(8,128)S(1)} %get-tuple-element.73), channel_id=1, source_target_pairs={{0,8},{4,12},{8,0},{12,4},{16,24},{20,28},{24,16},{28,20},{1,9},{5... | collective-permute-start | bytes 393224 | tf_op jit(solution)/shard_map/ppermute | solution.py:564
  99.7 7.5 %collective-permute-start.15 = (f32[64,512]{1,0:T(8,128)S(1)}, f32[64,512]{1,0:T(8,128)S(1)}, u32[]{:S(2)}, u32[]{:S(2)}) collective-permute-start(f32[64,512]{1,0:T(8,128)S(1)} %get-tuple-element.74), channel_id=1, source_target_pairs={{0,16},{4,20},{8,24},{12,28},{16,0},{20,4},{24,8},{28,12},{1,17},{... | collective-permute-start | bytes 393224 | tf_op jit(solution)/shard_map/ppermute | solution.py:564
  101.6 8.8 %collective-permute-start.16 = (f32[64,512]{1,0:T(8,128)S(1)}, f32[64,512]{1,0:T(8,128)S(1)}, u32[]{:S(2)}, u32[]{:S(2)}) collective-permute-start(f32[64,512]{1,0:T(8,128)S(1)} %get-tuple-element.75), channel_id=1, source_target_pairs={{0,24},{4,28},{8,16},{12,20},{16,8},{20,12},{24,0},{28,4},{1,25},{... | collective-permute-start | bytes 393224 | tf_op jit(solution)/shard_map/ppermute | solution.py:564

commit v8 on v7

v8 whole, which is shorter than its diff:
```python
import functools

import jax
import jax.numpy as jnp
from jax import lax
from jax.experimental import pallas as pl
from jax.experimental.pallas import tpu as pltpu
from jax.sharding import PartitionSpec as P

F32 = jnp.float32
HALF = jnp.bfloat16
HBM = pl.BlockSpec(memory_space=pltpu.HBM)
VMEM = pl.BlockSpec(memory_space=pltpu.VMEM)
SMEM = pl.BlockSpec(memory_space=pltpu.SMEM)
LEADING = 0


def split(value):
    high = value.astype(HALF)
    return high, (value - high.astype(F32)).astype(HALF)


def dot(left, right, transposed):
    dims = (((1,), (1 if transposed else 0,)), ((), ()))
    return lax.dot_general(left, right, dims, preferred_element_type=F32)


def parts_of(block, adjoint=False):
    size = block.shape[1] // 2
    real, imag = block[:, :size], block[:, size:]
    return real, imag, (real - imag if adjoint else real + imag)


def put(matrix, block, adjoint=False):
    for index, part in enumerate(parts_of(block, adjoint)):
        matrix[0, index], matrix[1, index] = split(part)


def times_split(left, matrix, transposed=False):
    products = []
    for index, (high, low) in enumerate(left):
        size = high.shape[0]
        both = dot(jnp.concatenate([high, low], axis=0), matrix[0, index], transposed)
        products.append(both[:size] + both[size:] + dot(high, matrix[1, index], transposed))
    first, second, third = products
    if transposed:
        return jnp.concatenate([first + second, third - first + second], axis=1)
    return jnp.concatenate([first - second, third - first - second], axis=1)


def times(block, matrix, transposed=False):
    return times_split([split(part) for part in parts_of(block)], matrix, transposed)


def row_form(pair):
    return jnp.concatenate([pair[0], pair[1]], axis=1)


def adjoint_row(pair):
    return jnp.concatenate([jnp.transpose(pair[0]), -jnp.transpose(pair[1])], axis=1)


def expand(pattern, size):
    blocks = pattern.shape[0]
    tile = size // blocks
    rows = lax.broadcasted_iota(jnp.int32, (size, blocks), 0)
    first = lax.broadcasted_iota(jnp.int32, (size, blocks), 1) * tile
    member = jnp.where((rows >= first) & (rows < first + tile), 1.0, 0.0).astype(HALF)
    tall = dot(member, pattern.astype(F32).astype(HALF), False)
    return dot(tall.astype(HALF), member, True)


def couple(coupling, pattern):
    mask = expand(pattern[...], coupling.shape[-1])
    return jnp.concatenate([coupling[0] * mask, coupling[1] * mask], axis=1)


def trailing():
    return lax.rem(lax.axis_index("energy") + LEADING, 2)


def shape(rows, columns, dtype=F32, *lead):
    return jax.ShapeDtypeStruct(lead + (rows, columns), dtype)


def matrices(number, size):
    return [pltpu.VMEM((2, 3, size, size), HALF)] * number


def call(kernel, outs, scratch, args, specs=None, out_specs=None, flops=0, name=None, limit=40):
    made = pl.pallas_call(
        kernel,
        out_shape=outs,
        in_specs=specs or [VMEM] * len(args),
        out_specs=out_specs or [VMEM] * len(outs),
        scratch_shapes=scratch,
        compiler_params=pltpu.CompilerParams(vmem_limit_bytes=limit * 2**20),
        cost_estimate=pl.CostEstimate(flops=flops, bytes_accessed=2**20, transcendentals=0),
        name=name,
    )(*args)
    return list(made)


class Loads:
    def __init__(self, args, targets, sems):
        order = [(0, 0), (1, 0), (3, 1), (2, 1), (1, 1), (0, 1), (3, 0), (2, 0)]
        self.copies = {}
        for index, (which, slab) in enumerate(order):
            if which == 3:
                pieces = [(args[which].at[slab], targets[which].at[slab])]
            else:
                pieces = [
                    (args[which].at[slab, part], targets[which].at[slab, part]) for part in range(2)
                ]
            self.copies[which, slab] = [
                pltpu.make_async_copy(*piece, sems.at[2 * index + part])
                for part, piece in enumerate(pieces)
            ]
        self.targets = targets
        for copies in self.copies.values():
            for copy in copies:
                copy.start()

    def get(self, which, slab):
        for copy in self.copies[which, slab]:
            copy.wait()
        return self.targets[which].at[slab]

    def green(self, slab):
        return row_form(self.get(0, slab))

    def sigma(self, slab):
        return row_form(self.get(1, slab))

    def coupler(self, slab):
        tiles = self.get(3, slab)
        return couple(self.get(2, slab), tiles)


def load_scratch(size, blocks):
    return [
        pltpu.VMEM((2, 2, size, size), F32),
        pltpu.VMEM((2, 2, size, size), F32),
        pltpu.VMEM((2, 2, size, size), F32),
        pltpu.VMEM((2, blocks, blocks), jnp.int32),
        pltpu.SemaphoreType.DMA((16,)),
    ]


def left_sources(loads, source, coupler_out, m_a, m_b, m_c):
    first = loads.green(0)
    put(m_b, first)
    put(m_a, loads.sigma(0))
    made = first + times(times(first, m_a), m_b)
    if source is not None:
        source[...] = made
    put(m_a, made)
    coupler = loads.coupler(1)
    if coupler_out is not None:
        coupler_out[...] = coupler
    put(m_c, coupler, True)
    inner = loads.sigma(1) + times(times(coupler, m_a), m_c, True)
    put(m_a, inner)
    second = loads.green(1)
    put(m_b, second)
    return first, second, times(second, m_a)


def source_kernel(green, sigma, coupling, pattern, whole, *scratch):
    *scratch, out_v, out_sems = scratch

    @pl.when((lax.axis_index("slab") == 0) & (trailing() == 0))
    def _():
        loads = Loads((green, sigma, coupling, pattern), scratch[:4], scratch[4])
        _, second, through = left_sources(loads, None, None, *scratch[5:])
        rows = second.shape[0] // 2
        copies = []
        for index in range(2):
            where = slice(index * rows, (index + 1) * rows)
            out_v[where] = second[where] + times(through[where], scratch[6])
            copies.append(
                pltpu.make_async_copy(out_v.at[where], whole.at[where], out_sems.at[index])
            )
            copies[-1].start()
        for which in (2, 3):
            loads.get(which, 0)
        for copy in copies:
            copy.wait()


def map_kernel(
    green, sigma, coupling, pattern,
    whole, source, coupler, opening, lead, tail, forward, backward, *scratch,
):
    m_a, m_b, m_c = scratch[5:]
    loads = Loads((green, sigma, coupling, pattern), scratch[:4], scratch[4])
    first, second, through = left_sources(loads, source, coupler, m_a, m_b, m_c)
    whole[...] = second + times(through, m_b)
    before = loads.coupler(0)

    @pl.when(lax.axis_index("slab") > 0)
    def _():
        opening[...] = before
        put(m_a, first)
        size = before.shape[0]
        behind = times(adjoint_row((before[:, :size], before[:, size:])), m_a)
        backward[...] = behind
        put(tail, times(times(behind, m_c, True), m_b))
        put(m_a, before)
        ahead = times(first, m_a)
        forward[...] = ahead
        put(m_a, ahead)
        put(m_c, coupler[...])
        put(lead, times(times(second, m_c), m_a))


def prepare_kernel(count, *refs):
    arrived = refs[: count - 1]
    source, forward, backward, coupler, opening = refs[count - 1 : count + 4]
    lead, tail, constant, first_lead, first_tail, first_constant = refs[count + 4 : count + 10]
    x_v, m_a, m_b, m_c, m_d = refs[count + 10 :]
    place = lax.axis_index("slab")
    inner = (place > 0) & (place < count - 1)

    for turn in range(count - 1):
        @pl.when(inner & (place == turn + 1 - trailing()))
        def _(turn=turn):
            x_v[...] = arrived[turn][...]

    @pl.when(place == 0)
    def _():
        first_constant[...] = source[...]

    @pl.when(inner)
    def _():
        put(m_a, x_v[...])
        put(m_b, backward[...])
        first_constant[...] = source[...] + times(times(forward[...], m_a), m_b)

    @pl.when(place < count - 1)
    def _():
        first = first_constant[...]
        put(m_c, coupler[...], True)
        put(first_lead, times(first, m_c, True))
        put(m_d, first)
        put(first_tail, times(coupler[...], m_d))

    @pl.when(inner)
    def _():
        x, before = x_v[...], opening[...]
        put(m_b, before, True)
        through = times(times(x, m_b, True), m_d)
        put(lead, times(through, m_c, True))
        put(m_b, times(before, m_a))
        constant[...] = x + times(through, m_b)
        behind = times(first_constant[...], m_b)
        put(m_b, behind)
        put(tail, times(coupler[...], m_b))


def apply_map(mapping, m_x):
    lead, tail, constant = mapping
    ahead = [(lead[0, index], lead[1, index]) for index in range(3)]
    return constant[...] + times(times_split(ahead, m_x), tail)


def relay_kernel(step, count, lefts, rights, *refs):
    refs = list(refs)
    place = lax.axis_index("slab")
    turn = step - trailing()
    is_left = (turn >= 0) & (turn <= count - 2) & (place == turn + 1)
    is_right = (turn >= count - 1) & (place == 2 * count - 3 - turn)
    closing = lefts and step >= count - 2
    arrived = refs.pop(0)
    left_map = [refs.pop(0) for _ in range(3)] if lefts else None
    right_map = [refs.pop(0) for _ in range(3)] if rights else None
    if closing:
        forward, backward, source, coupler, opening = [refs.pop(0) for _ in range(5)]
    if step == 0:
        refs.pop(0)
    out = refs.pop(0)
    if closing:
        first_end, last_end, m_x, m_a, m_b = refs
    else:
        (m_x,) = refs

    if step == 0:
        @pl.when(place == 0)
        def _():
            out[...] = left_map[2][...]

    if lefts:
        @pl.when(is_left)
        def _():
            put(m_x, arrived[...])
            out[...] = apply_map(left_map, m_x)

    if closing:
        @pl.when(is_left & (place == count - 1))
        def _():
            last = out[...]
            last_end[...] = last
            put(m_a, backward[...])
            first = source[...] + times(times(forward[...], m_x), m_a)
            put(m_a, coupler[...], True)
            put(m_b, last)
            through = times(times(first, m_a, True), m_b)
            put(m_a, first)
            put(m_b, times(coupler[...], m_a))
            first = first + times(through, m_b)
            first_end[...] = first
            x, before = arrived[...], opening[...]
            put(m_a, before, True)
            put(m_b, first)
            through = times(times(x, m_a, True), m_b)
            put(m_a, times(before, m_x))
            out[...] = x + times(through, m_a)

    if rights:
        @pl.when(is_right & (place > 0))
        def _():
            put(m_x, arrived[...])
            out[...] = apply_map(right_map, m_x)


def pack_kernel(count, chips, *refs):
    outs, ends = refs[:count], refs[count : count + 2]
    parcels, last_parcels = refs[count + 2 : count + 2 + chips], refs[count + 2 + chips :]
    place, core = lax.axis_index("slab"), trailing()
    at = jnp.where(place == count - 1, count - 2 + core, 2 * count - 3 - place + core)

    for index in range(count):
        @pl.when((place > 0) & (at == count - 2 + index))
        def _(index=index):
            pack(outs[index], parcels)

    for index in range(2):
        @pl.when((place == count - 1) & (core == index))
        def _(index=index):
            pack(ends[index], last_parcels)


def first_kernel(count, *refs):
    arrived, ends = refs[:count], refs[count : count + 2]
    mapping = refs[count + 2 : count + 5]
    block, *parcels, m_x = refs[count + 5 :]
    place, core = lax.axis_index("slab"), trailing()

    for index in range(count):
        @pl.when((place < count - 1) & (count - 2 - place + core == index))
        def _(index=index):
            put(m_x, arrived[index][...])

    @pl.when(place < count - 1)
    def _():
        block[...] = apply_map(mapping, m_x)

    for index in range(2):
        @pl.when((place == count - 1) & (core == index))
        def _(index=index):
            block[...] = ends[index][...]

    pack(block, parcels)


def pack(block, parcels):
    for mask, parcel in enumerate(parcels):
        parcel[...] = block[share(mask, parcel.shape[0]), :]


def retarded_kernel(count, *refs):
    block, arrived, ends, out = refs[0], refs[1 : count + 1], refs[count + 1 : count + 3], refs[-1]
    place, core = lax.axis_index("slab"), trailing()
    size = out.shape[-1]

    def write(slab, block):
        for part in range(2):
            out[slab, part] = block[:, part * size : (part + 1) * size]

    write(0, block)
    for index in range(count):
        @pl.when((place < count - 1) & (count - 2 - place + core == index))
        def _(index=index):
            write(1, arrived[index])

    for index in range(2):
        @pl.when((place == count - 1) & (core == index))
        def _(index=index):
            write(1, ends[index])


def share(mask, rows):
    chip = lax.shift_right_logical(lax.axis_index("energy"), 1)
    return pl.ds(pl.multiple_of(lax.bitwise_xor(chip, mask) * rows, rows), rows)


def mix_kernel(chips, lowest, weights, *refs):
    parcels, (mine, other) = refs[:chips], refs[chips : chips + 2]
    energy = lax.axis_index("energy")
    core = lax.rem(energy, 2)

    @pl.when(lax.axis_index("slab") >= lowest)
    def _():
        sources = [lax.bitwise_xor(energy, 2 * mask) for mask in range(chips)]
        for mask in range(chips):
            for target, out in ((sources[mask], mine), (sources[mask] + 1 - 2 * core, other)):
                total = weights[target, sources[0]] * parcels[0][...]
                for index in range(1, chips):
                    total += weights[target, sources[index]] * parcels[index][...]
                out[mask] = total


def sum_kernel(chips, lowest, mine, other, *outs):
    @pl.when(lax.axis_index("slab") >= lowest)
    def _():
        for mask in range(chips):
            outs[mask][...] = mine[mask] + other[mask]


def place_kernel(count, chips, *refs):
    rounds = [refs[index * chips : (index + 1) * chips] for index in range(3)]
    scattering, sems = refs[3 * chips :]
    size = scattering.shape[-1]
    place = lax.axis_index("slab")

    def copies(slab, parcels):
        for mask, parcel in enumerate(parcels):
            for part in range(2):
                yield pltpu.make_async_copy(
                    parcel.at[:, pl.ds(part * size, size)],
                    scattering.at[slab, part, share(mask, parcel.shape[0]), :],
                    sems.at[slab, mask, part],
                )

    def start(slab, parcels):
        for copy in copies(slab, parcels):
            copy.start()

    before, first, last = rounds
    pl.when(place < count - 1)(lambda: start(1, before))
    pl.when(place == count - 1)(lambda: start(1, last))
    start(0, first)
    for slab, parcels in ((1, before), (0, first)):
        for copy in copies(slab, parcels):
            copy.wait()


def mode_weights(targets, sources, offsets, emission, absorption):
    spacing = sources[None, :, None] - targets[:, None, None]
    emitted = jnp.where(
        spacing == -offsets[None, None, :],
        emission[None, None, :],
        jnp.zeros_like(emission)[None, None, :],
    )
    absorbed = jnp.where(
        spacing == offsets[None, None, :],
        absorption[None, None, :],
        jnp.zeros_like(absorption)[None, None, :],
    )
    return jnp.sum(emitted + absorbed, axis=-1)


def relay_pairs(step, energies, count):
    pairs = []
    for energy in range(energies):
        turn = step - (energy + LEADING) % 2
        if 0 <= turn <= count - 2:
            ends = (turn, turn + 1)
        elif count - 1 <= turn <= 2 * count - 3:
            ends = (2 * count - 2 - turn, 2 * count - 3 - turn)
        else:
            continue
        pairs.append(tuple(energy * count + end for end in ends))
    return pairs


def shards(energies, count, free_green, self_energy, coupling, pattern, offsets, emission, absorption):
    size, blocks = free_green.shape[-1], pattern.shape[-1]
    args = (free_green[0], self_energy[0], coupling, pattern)
    row = shape(size, 2 * size)
    factor = shape(size, size, HALF, 2, 3)
    row_v = pltpu.VMEM(row.shape, F32)
    product = 24 * size**3
    loading = load_scratch(size, blocks) + matrices(3, size)

    def relay(step, value):
        return lax.ppermute(value, ("energy", "slab"), relay_pairs(step, energies, count))

    (begun,) = call(
        source_kernel,
        [row],
        loading + [row_v, pltpu.SemaphoreType.DMA((2,))],
        args,
        [HBM] * 4,
        [HBM],
        flops=6 * product,
        name="source",
        limit=61,
    )
    arrived, outs, firsts, lasts = [relay(0, begun)], [], [], []
    whole, source, coupler, opening, left_lead, left_tail, forward, backward = call(
        map_kernel,
        [row] * 4 + [factor, factor, row, row],
        loading,
        args,
        [HBM] * 4,
        flops=12 * product,
        name="left_maps",
        limit=49,
    )
    left_map = [left_lead, left_tail, whole]
    begun, _ = lax.optimization_barrier((arrived[0], whole))
    token = lax.ppermute(
        begun[:8, :128],
        ("energy", "slab"),
        [
            (energy * count, (energy ^ 1) * count)
            for energy in range(energies)
            if (energy + LEADING) % 2 == 0
        ],
    )
    right_map = None
    for step in range(2 * count - 2):
        lefts, rights = step <= count - 1, step >= count - 1
        closing = lefts and step >= count - 2
        args = [arrived[step]]
        if lefts:
            args += left_map
        if rights:
            args += right_map[:3]
        if closing:
            args += [forward, backward, source, coupler, opening]
        if step == 0:
            args.append(token)
        made = call(
            functools.partial(relay_kernel, step, count, lefts, rights),
            [row] * (3 if closing else 1),
            matrices(3 if closing else 1, size),
            args,
            flops=2 * product,
            name="relay",
        )
        outs.append(made[0])
        firsts += made[1:2]
        lasts += made[2:]
        arrived.append(relay(step + 1, made[0]))
        if step == count - 2:
            right_map = call(
                functools.partial(prepare_kernel, count),
                [factor, factor, row, factor, factor, row],
                [row_v] + matrices(4, size),
                arrived[: count - 1] + [source, forward, backward, coupler, opening],
                flops=11 * product,
                name="right_maps",
            )

    chips = energies // 2
    parcel = shape(size // chips, 2 * size)
    partial = shape(size // chips, 2 * size, F32, chips)
    everyone = jnp.arange(energies, dtype=jnp.int32)
    weights = mode_weights(everyone, everyone, offsets, emission, absorption)

    def send(value, flip, places, down=0):
        pairs = [
            (energy * count + i, (energy ^ flip) * count + i - down)
            for energy in range(energies)
            for i in places
        ]
        return lax.ppermute(value, ("energy", "slab"), pairs)

    def exchange(parcels, places):
        return parcels[:1] + [
            send(value, 2 * mask, places) for mask, value in enumerate(parcels) if mask
        ]

    def mix(parcels, places):
        mine, other = call(
            functools.partial(mix_kernel, chips, places[0]),
            [partial] * 2,
            [],
            [weights] + parcels,
            [SMEM] + [VMEM] * chips,
            flops=product // 8,
            name="mix",
        )
        return mine, send(other, 1, places)

    def add(places, mine, other):
        return call(
            functools.partial(sum_kernel, chips, places[0]),
            [parcel] * chips,
            [],
            [mine, other],
            name="sum",
        )

    below, every, end = list(range(1, count)), list(range(count)), [count - 1]
    packed = call(
        functools.partial(pack_kernel, count, chips),
        [parcel] * (2 * chips),
        [],
        outs[count - 2 :] + lasts,
        name="pack",
    )
    halves = mix(exchange(packed[:chips], below), below)
    last_halves = mix(exchange(packed[chips:], end), end)
    final, *_ = lax.optimization_barrier((arrived[-1], halves[0], last_halves[0]))
    arrived = arrived[count - 1 : -1] + [final]
    block, *parcels = call(
        functools.partial(first_kernel, count),
        [row] + [parcel] * chips,
        matrices(1, size),
        arrived + firsts + right_map[3:],
        flops=2 * product,
        name="first_slab",
    )
    received = exchange(parcels, every)
    sums = add(below, *halves)
    returned = [send(value, 2 * mask, below, 1) for mask, value in enumerate(sums)]
    last_returned = exchange(add(end, *last_halves), end)
    *received, _ = lax.optimization_barrier((*received, returned[0]))
    first_returned = exchange(add(every, *mix(received, every)), every)
    (retarded,) = call(
        functools.partial(retarded_kernel, count),
        [shape(size, size, F32, 2, 2)],
        [],
        [block] + arrived + lasts,
        name="retarded",
    )
    (scattering,) = call(
        functools.partial(place_kernel, count, chips),
        [shape(size, size, F32, 2, 2)],
        [pltpu.SemaphoreType.DMA((2, chips, 2))],
        returned + first_returned + last_returned,
        None,
        [HBM],
        name="scattering",
    )
    return (retarded[None], scattering[None])


def solution(mesh):
    blocks = P("energy", "slab", None, None, None)
    in_specs = (blocks, blocks, P("slab", None, None, None), P("slab", None, None), P(), P(), P())
    body = functools.partial(shards, mesh.shape["energy"], mesh.shape["slab"])
    return jax.shard_map(
        body, mesh=mesh, in_specs=in_specs, out_specs=(blocks, blocks), check_vma=False
    )
```

time: 112 us -> 126 us (1.12)
  waiting for transfers between devices: 60.8 us -> 79.3 us
  Pallas kernels: 19.7 us -> 17 us
  starting transfers between devices: 30 us -> 28.1 us
    ppermute x7, waiting for transfers between devices: 28.4 us -> 51.9 us  [relay(): lax.ppermute(value, ('energy', 'slab'), relay_pairs(step, energies, count))]
    ppermute x17 -> x23, waiting for transfers between devices: 32.4 us -> 27.4 us  [the longest x22 26.6 us: send(): return lax.ppermute(value, ('energy', 'slab'), pairs)]
    pallas_call x17 -> x19, Pallas kernels: 19.7 us -> 17 us  [call(): pl.pallas_call(kernel, out_shape=outs, in_specs=specs or [VMEM] * len(arg...]
    ppermute x17 -> x23, starting transfers between devices: 23.9 us -> 22 us  [the longest x22 20.7 us: send(): return lax.ppermute(value, ('energy', 'slab'), pairs)]
  transfers between devices with their start and end apart: 24 -> 30, of which waited for: 11 -> 10; matrix products, arithmetic and copies ran while one was open for 0% -> 0% of each run, Pallas kernels for 10% -> 8%
where the time goes in v8:
time: 126 us
  waiting for transfers between devices  79.3 us (63%)
  starting transfers between devices  28.1 us (22%)
  Pallas kernels  17 us (13%)
  between operations  1.33 us (1%)
    ppermute x7, waiting for transfers between devices, relay(): lax.ppermute(value, ('energy', 'slab'), relay_pairs(step, energies, count))  51.9 us
    ppermute x22, waiting for transfers between devices, send(): return lax.ppermute(value, ('energy', 'slab'), pairs)  26.6 us
    ppermute x22, starting transfers between devices, send(): return lax.ppermute(value, ('energy', 'slab'), pairs)  20.7 us
    pallas_call x19, Pallas kernels, call(): pl.pallas_call(kernel, out_shape=outs, in_specs=specs or [VMEM] * len(arg...  17 us
    ppermute x7, starting transfers between devices, relay(): lax.ppermute(value, ('energy', 'slab'), relay_pairs(step, energies, count))  6.09 us
  transfers between devices with their start and end apart: 30, of which 10 were waited for; matrix products, arithmetic and copies ran while one was open for 0% of the time, Pallas kernels for 8%

profile of v8, /device:TPU:0, one launch (start us, length us, event | category | flops | bytes accessed | tf_op | source)
XLA Modules:
  0.0 125.8 jit_solution(16800521241765733032)
XLA Ops:
  0.6 5.2 %source.1 = f32[256,512]{1,0:T(8,128)} custom-call(f32[2,2,256,256]{3,2,1,0:T(8,128)} %bitcast.6, f32[2,2,256,256]{3,2,1,0:T(8,128)} %bitcast.8, f32[2,2,256,256]{3,2,1,0:T(8,128)} %coupling.3, s32[2,16,16]{2,1,0:T(8,128)} %pattern.3), custom_call_target="tpu_custom_call" | custom-call | flops 2415919104 | bytes 1048576 | tf_op jit(solution)/shard_map/source/pallas_call | solution.py:91
  5.9 1.3 %collective-permute-start = (f32[256,512]{1,0:T(8,128)}, f32[256,512]{1,0:T(8,128)S(1)}, u32[]{:S(2)}, u32[]{:S(2)}) collective-permute-start(f32[256,512]{1,0:T(8,128)} %source.1), channel_id=1, source_target_pairs={{0,1},{8,9},{16,17},{24,25}} | collective-permute-start | bytes 1572872 | tf_op jit(solution)/shard_map/ppermute | solution.py:487
  7.2 4.8 %left_maps.1 = (f32[256,512]{1,0:T(8,128)S(1)}, f32[256,512]{1,0:T(8,128)S(1)}, f32[256,512]{1,0:T(8,128)S(1)}, f32[256,512]{1,0:T(8,128)S(1)}, bf16[2,3,256,256...) custom-call(f32[2,2,256,256]{3,2,1,0:T(8,128)} %bitcast.7, ...), custom_call_target="tpu_custom_call" | custom-call | flops 4831838208 | bytes 1048576 | tf_op jit(solution)/shard_map/left_maps/pallas_call | solution.py:91
  12.0 2.2 %collective-permute-done.refs_0_ = f32[256,512]{1,0:T(8,128)S(1)} collective-permute-done((f32[256,512]{1,0:T(8,128)}, f32[256,512]{1,0:T(8,128)S(1)}, u32[]{:S(2)}, u32[]{:S(2)}) %collective-permute-start) | collective-permute-done | bytes 524320 | tf_op jit(solution)/shard_map/ppermute | solution.py:487
  14.2 1.3 %collective-permute-start.1 = (f32[8,128]{1,0:T(8,128)S(1)}, f32[8,128]{1,0:T(8,128)S(1)}, u32[]{:S(2)}, u32[]{:S(2)}) collective-permute-start(f32[8,128]{1,0:T(8,128)S(1)} %slice.3), channel_id=1, source_target_pairs={{0,4},{8,12},{16,20},{24,28}} | collective-permute-start | bytes 12296 | tf_op jit(solution)/shard_map/ppermute | solution.py:513
  15.5 0.8 collective-permute-done.1.refs_4_
  16.3 0.7 collective-permute-start.2
  17.0 0.0 collective-permute-done.2.refs_0_.refs_1_
  17.1 0.7 collective-permute-start.3
  17.8 0.2 relay.8
  18.0 0.7 collective-permute-start.4
  18.7 1.1 right_maps.1
  19.8 0.3 relay.9
  20.1 0.7 collective-permute-start.5
  20.8 0.0 collective-permute-done.5.refs_0_.refs_1_.refs_2_
  20.8 1.3 %collective-permute-start.6 = (f32[256,512]{1,0:T(8,128)S(1)}, f32[256,512]{1,0:T(8,128)S(1)}, u32[]{:S(2)}, u32[]{:S(2)}) collective-permute-start(f32[256,512]{1,0:T(8,128)S(1)} %relay.10.refs_2_), channel_id=1, source_target_pairs={{1,0},{6,5},{9,8},{14,13},{17,16},{22,21},{25,24},{30,29}} | collective-permute-start | bytes 1572872 | tf_op jit(solution)/shard_map/ppermute | solution.py:487
  22.1 49.7 %collective-permute-done.6.refs_0_.refs_2_.refs_3_ = f32[256,512]{1,0:T(8,128)S(1)} collective-permute-done((f32[256,512]{1,0:T(8,128)S(1)}, f32[256,512]{1,0:T(8,128)S(1)}, u32[]{:S(2)}, u32[]{:S(2)}) %collective-permute-start.6) | collective-permute-done | bytes 524320 | tf_op jit(solution)/shard_map/ppermute | solution.py:487
  71.8 0.7 collective-permute-start.10
  72.4 0.7 collective-permute-start.8
  73.1 0.0 copy-start.3
  73.1 0.7 collective-permute-start.9
  73.8 0.0 copy-start.1
  73.8 0.0 copy-start.2
  73.9 0.7 collective-permute-start.7
  74.6 0.1 add_reduce_fusion.weights
  74.7 0.0 collective-permute-done.10.refs_3_
  74.7 0.0 collective-permute-done.8.refs_1_
  74.7 0.6 mix.3
  75.3 0.7 collective-permute-start.14
  76.0 0.7 collective-permute-start.11
  76.7 0.7 collective-permute-start.12
  77.4 0.7 collective-permute-start.13
  78.1 0.0 collective-permute-done.12.refs_2_
  78.1 0.0 collective-permute-done.13.refs_3_
  78.1 0.6 mix.4
  78.7 1.0 first_slab.1
  79.8 3.0 %collective-permute-start.19 = (f32[64,512]{1,0:T(8,128)S(1)}, f32[64,512]{1,0:T(8,128)S(1)}, u32[]{:S(2)}, u32[]{:S(2)}) collective-permute-start(f32[64,512]{1,0:T(8,128)S(1)} %get-tuple-element.98), channel_id=1, source_target_pairs={{0,8},{1,9},{2,10},{3,11},{4,12},{5,13},{6,14},{7,15},{8,0},{9,1},... | collective-permute-start | bytes 393224 | tf_op jit(solution)/shard_map/ppermute | solution.py:569
  82.8 1.5 %collective-permute-start.20 = (f32[64,512]{1,0:T(8,128)S(1)}, f32[64,512]{1,0:T(8,128)S(1)}, u32[]{:S(2)}, u32[]{:S(2)}) collective-permute-start(f32[64,512]{1,0:T(8,128)S(1)} %get-tuple-element.99), channel_id=1, source_target_pairs={{0,16},{1,17},{2,18},{3,19},{4,20},{5,21},{6,22},{7,23},{8,24},{9,... | collective-permute-start | bytes 393224 | tf_op jit(solution)/shard_map/ppermute | solution.py:569
  84.3 0.0 collective-permute-start.21
  84.3 1.3 %collective-permute-start.15 = (f32[64,512]{1,0:T(8,128)S(1)}, f32[64,512]{1,0:T(8,128)S(1)}, u32[]{:S(2)}, u32[]{:S(2)}) collective-permute-start(f32[64,512]{1,0:T(8,128)S(1)} %get-tuple-element.93), channel_id=1, source_target_pairs={{1,0},{2,1},{3,2},{5,4},{6,5},{7,6},{9,8},{10,9},{11,10},{13,12},{... | collective-permute-start | bytes 393224 | tf_op jit(solution)/shard_map/ppermute | solution.py:569
  85.6 0.7 collective-permute-start.26
  86.3 1.4 %collective-permute-done.20.refs_2_ = f32[64,512]{1,0:T(8,128)S(1)} collective-permute-done((f32[64,512]{1,0:T(8,128)S(1)}, f32[64,512]{1,0:T(8,128)S(1)}, u32[]{:S(2)}, u32[]{:S(2)}) %collective-permute-start.20) | collective-permute-done | bytes 131104 | tf_op jit(solution)/shard_map/ppermute | solution.py:569
  87.8 2.4 %collective-permute-done.21.refs_3_ = f32[64,512]{1,0:T(8,128)S(1)} collective-permute-done((f32[64,512]{1,0:T(8,128)S(1)}, f32[64,512]{1,0:T(8,128)S(1)}, u32[]{:S(2)}, u32[]{:S(2)}) %collective-permute-start.21) | collective-permute-done | bytes 131104 | tf_op jit(solution)/shard_map/ppermute | solution.py:569
  90.2 11.8 %collective-permute-done.15.refs_0_ = f32[64,512]{1,0:T(8,128)S(1)} collective-permute-done((f32[64,512]{1,0:T(8,128)S(1)}, f32[64,512]{1,0:T(8,128)S(1)}, u32[]{:S(2)}, u32[]{:S(2)}) %collective-permute-start.15) | collective-permute-done | bytes 131104 | tf_op jit(solution)/shard_map/ppermute | solution.py:569
  102.0 0.9 mix.5
  102.9 0.1 collective-permute-start.22
  103.0 0.7 collective-permute-start.27
  103.7 0.7 collective-permute-start.28
  104.3 0.7 collective-permute-start.29
  105.0 1.3 %collective-permute-start.16 = (f32[64,512]{1,0:T(8,128)S(1)}, f32[64,512]{1,0:T(8,128)S(1)}, u32[]{:S(2)}, u32[]{:S(2)}) collective-permute-start(f32[64,512]{1,0:T(8,128)S(1)} %get-tuple-element.94), channel_id=1, source_target_pairs={{1,8},{2,9},{3,10},{5,12},{6,13},{7,14},{9,0},{10,1},{11,2},{13,4}... | collective-permute-start | bytes 393224 | tf_op jit(solution)/shard_map/ppermute | solution.py:569
  106.3 1.3 %collective-permute-start.17 = (f32[64,512]{1,0:T(8,128)S(1)}, f32[64,512]{1,0:T(8,128)S(1)}, u32[]{:S(2)}, u32[]{:S(2)}) collective-permute-start(f32[64,512]{1,0:T(8,128)S(1)} %get-tuple-element.95), channel_id=1, source_target_pairs={{1,16},{2,17},{3,18},{5,20},{6,21},{7,22},{9,24},{10,25},{11,26},{... | collective-permute-start | bytes 393224 | tf_op jit(solution)/shard_map/ppermute | solution.py:569
  107.6 0.1 sum.4
  107.7 0.0 collective-permute-done.27.refs_9_
  107.7 1.3 %collective-permute-start.18 = (f32[64,512]{1,0:T(8,128)S(1)}, f32[64,512]{1,0:T(8,128)S(1)}, u32[]{:S(2)}, u32[]{:S(2)}) collective-permute-start(f32[64,512]{1,0:T(8,128)S(1)} %get-tuple-element.96), channel_id=1, source_target_pairs={{1,24},{2,25},{3,26},{5,28},{6,29},{7,30},{9,16},{10,17},{11,18},{... | collective-permute-start | bytes 393224 | tf_op jit(solution)/shard_map/ppermute | solution.py:569
  109.0 1.6 %collective-permute-start.23 = (f32[64,512]{1,0:T(8,128)S(1)}, f32[64,512]{1,0:T(8,128)S(1)}, u32[]{:S(2)}, u32[]{:S(2)}) collective-permute-start(f32[64,512]{1,0:T(8,128)S(1)} %get-tuple-element.108), channel_id=1, source_target_pairs={{0,8},{1,9},{2,10},{3,11},{4,12},{5,13},{6,14},{7,15},{8,0},{9,1},... | collective-permute-start | bytes 393224 | tf_op jit(solution)/shard_map/ppermute | solution.py:569
  110.6 0.5 collective-permute-start.24
  111.1 3.0 %collective-permute-done.16.refs_1_ = f32[64,512]{1,0:T(8,128)S(1)} collective-permute-done((f32[64,512]{1,0:T(8,128)S(1)}, f32[64,512]{1,0:T(8,128)S(1)}, u32[]{:S(2)}, u32[]{:S(2)}) %collective-permute-start.16) | collective-permute-done | bytes 131104 | tf_op jit(solution)/shard_map/ppermute | solution.py:569
  114.1 1.4 %collective-permute-start.25 = (f32[64,512]{1,0:T(8,128)S(1)}, f32[64,512]{1,0:T(8,128)S(1)}, u32[]{:S(2)}, u32[]{:S(2)}) collective-permute-start(f32[64,512]{1,0:T(8,128)S(1)} %get-tuple-element.110), channel_id=1, source_target_pairs={{0,24},{1,25},{2,26},{3,27},{4,28},{5,29},{6,30},{7,31},{8,16},{9,... | collective-permute-start | bytes 393224 | tf_op jit(solution)/shard_map/ppermute | solution.py:569
  115.6 1.1 retarded.1
  116.6 0.4 collective-permute-done.17.refs_2_
  117.1 2.5 %collective-permute-done.18.refs_3_ = f32[64,512]{1,0:T(8,128)S(1)} collective-permute-done((f32[64,512]{1,0:T(8,128)S(1)}, f32[64,512]{1,0:T(8,128)S(1)}, u32[]{:S(2)}, u32[]{:S(2)}) %collective-permute-start.18) | collective-permute-done | bytes 131104 | tf_op jit(solution)/shard_map/ppermute | solution.py:569
  119.5 5.0 %collective-permute-done.24.refs_6_ = f32[64,512]{1,0:T(8,128)S(1)} collective-permute-done((f32[64,512]{1,0:T(8,128)S(1)}, f32[64,512]{1,0:T(8,128)S(1)}, u32[]{:S(2)}, u32[]{:S(2)}) %collective-permute-start.24) | collective-permute-done | bytes 131104 | tf_op jit(solution)/shard_map/ppermute | solution.py:569
  124.5 0.0 collective-permute-done.25.refs_7_
  124.5 1.1 scattering.1
  (27 shorter events, 0.1 us)
Async XLA Ops:
  0.6 6.6 %copy-start = (s32[2,16,16]{2,1,0:T(8,128)S(1)}, s32[2,16,16]{2,1,0:T(8,128)}, u32[]{:S(2)}) copy-start(s32[2,16,16]{2,1,0:T(8,128)} %pattern.3) | copy-start | bytes 6148
  5.9 8.3 %collective-permute-start = (f32[256,512]{1,0:T(8,128)}, f32[256,512]{1,0:T(8,128)S(1)}, u32[]{:S(2)}, u32[]{:S(2)}) collective-permute-start(f32[256,512]{1,0:T(8,128)} %source.1), channel_id=1, source_target_pairs={{0,1},{8,9},{16,17},{24,25}} | collective-permute-start | bytes 1572872 | tf_op jit(solution)/shard_map/ppermute | solution.py:487
  14.2 2.1 %collective-permute-start.1 = (f32[8,128]{1,0:T(8,128)S(1)}, f32[8,128]{1,0:T(8,128)S(1)}, u32[]{:S(2)}, u32[]{:S(2)}) collective-permute-start(f32[8,128]{1,0:T(8,128)S(1)} %slice.3), channel_id=1, source_target_pairs={{0,4},{8,12},{16,20},{24,28}} | collective-permute-start | bytes 12296 | tf_op jit(solution)/shard_map/ppermute | solution.py:513
  16.3 0.7 collective-permute-start.2
  17.1 0.7 collective-permute-start.3
  18.0 1.8 %collective-permute-start.4 = (f32[256,512]{1,0:T(8,128)S(1)}, f32[256,512]{1,0:T(8,128)S(1)}, u32[]{:S(2)}, u32[]{:S(2)}) collective-permute-start(f32[256,512]{1,0:T(8,128)S(1)} %get-tuple-element.68.refs_0_), channel_id=1, source_target_pairs={{3,2},{6,7},{11,10},{14,15},{19,18},{22,23},{27,26},{30,31}} | collective-permute-start | bytes 1572872 | tf_op jit(solution)/shard_map/ppermute | solution.py:487
  20.1 0.7 collective-permute-start.5
  20.8 51.0 %collective-permute-start.6 = (f32[256,512]{1,0:T(8,128)S(1)}, f32[256,512]{1,0:T(8,128)S(1)}, u32[]{:S(2)}, u32[]{:S(2)}) collective-permute-start(f32[256,512]{1,0:T(8,128)S(1)} %relay.10.refs_2_), channel_id=1, source_target_pairs={{1,0},{6,5},{9,8},{14,13},{17,16},{22,21},{25,24},{30,29}} | collective-permute-start | bytes 1572872 | tf_op jit(solution)/shard_map/ppermute | solution.py:487
  71.8 2.9 %collective-permute-start.10 = (f32[64,512]{1,0:T(8,128)S(1)}, f32[64,512]{1,0:T(8,128)S(1)}, u32[]{:S(2)}, u32[]{:S(2)}) collective-permute-start(f32[64,512]{1,0:T(8,128)S(1)} %get-tuple-element.78), channel_id=1, source_target_pairs={{1,25},{2,26},{3,27},{5,29},{6,30},{7,31},{9,17},{10,18},{11,19},{... | collective-permute-start | bytes 393224 | tf_op jit(solution)/shard_map/ppermute | solution.py:569
  72.4 2.2 %collective-permute-start.8 = (f32[64,512]{1,0:T(8,128)S(1)}, f32[64,512]{1,0:T(8,128)S(1)}, u32[]{:S(2)}, u32[]{:S(2)}) collective-permute-start(f32[64,512]{1,0:T(8,128)S(1)} %get-tuple-element.76), channel_id=1, source_target_pairs={{1,9},{2,10},{3,11},{5,13},{6,14},{7,15},{9,1},{10,2},{11,3},{13,5... | collective-permute-start | bytes 393224 | tf_op jit(solution)/shard_map/ppermute | solution.py:569
  73.1 0.7 copy-start.3
  73.1 1.6 %collective-permute-start.9 = (f32[64,512]{1,0:T(8,128)S(1)}, f32[64,512]{1,0:T(8,128)S(1)}, u32[]{:S(2)}, u32[]{:S(2)}) collective-permute-start(f32[64,512]{1,0:T(8,128)S(1)} %get-tuple-element.77), channel_id=1, source_target_pairs={{1,17},{2,18},{3,19},{5,21},{6,22},{7,23},{9,25},{10,26},{11,27},{... | collective-permute-start | bytes 393224 | tf_op jit(solution)/shard_map/ppermute | solution.py:569
  73.8 0.7 copy-start.1
  73.8 0.7 copy-start.2
  73.9 4.9 %collective-permute-start.7 = (f32[256,512]{1,0:T(8,128)S(1)}, f32[256,512]{1,0:T(8,128)S(1)}, u32[]{:S(2)}, u32[]{:S(2)}) collective-permute-start(f32[256,512]{1,0:T(8,128)S(1)} %relay.11.refs_3_), channel_id=1, source_target_pairs={{5,4},{13,12},{21,20},{29,28}} | collective-permute-start | bytes 1572872 | tf_op jit(solution)/shard_map/ppermute | solution.py:487
  75.3 9.0 %collective-permute-start.14 = (f32[4,64,512]{2,1,0:T(8,128)S(1)}, f32[4,64,512]{2,1,0:T(8,128)S(1)}, u32[]{:S(2)}, u32[]{:S(2)}) collective-permute-start(f32[4,64,512]{2,1,0:T(8,128)S(1)} %get-tuple-element.92), channel_id=1, source_target_pairs={{1,5},{2,6},{3,7},{5,1},{6,2},{7,3},{9,13},{10,14},{11,15},{13,9},... | collective-permute-start | bytes 1572872 | tf_op jit(solution)/shard_map/ppermute | solution.py:569
  76.0 2.0 %collective-permute-start.11 = (f32[64,512]{1,0:T(8,128)S(1)}, f32[64,512]{1,0:T(8,128)S(1)}, u32[]{:S(2)}, u32[]{:S(2)}) collective-permute-start(f32[64,512]{1,0:T(8,128)S(1)} %get-tuple-element.81), channel_id=1, source_target_pairs={{3,11},{7,15},{11,3},{15,7},{19,27},{23,31},{27,19},{31,23}} | collective-permute-start | bytes 393224 | tf_op jit(solution)/shard_map/ppermute | solution.py:569
  76.7 1.4 %collective-permute-start.12 = (f32[64,512]{1,0:T(8,128)S(1)}, f32[64,512]{1,0:T(8,128)S(1)}, u32[]{:S(2)}, u32[]{:S(2)}) collective-permute-start(f32[64,512]{1,0:T(8,128)S(1)} %get-tuple-element.82), channel_id=1, source_target_pairs={{3,19},{7,23},{11,27},{15,31},{19,3},{23,7},{27,11},{31,15}} | collective-permute-start | bytes 393224 | tf_op jit(solution)/shard_map/ppermute | solution.py:569
  77.4 0.7 collective-permute-start.13
  79.8 6.6 %collective-permute-start.19 = (f32[64,512]{1,0:T(8,128)S(1)}, f32[64,512]{1,0:T(8,128)S(1)}, u32[]{:S(2)}, u32[]{:S(2)}) collective-permute-start(f32[64,512]{1,0:T(8,128)S(1)} %get-tuple-element.98), channel_id=1, source_target_pairs={{0,8},{1,9},{2,10},{3,11},{4,12},{5,13},{6,14},{7,15},{8,0},{9,1},... | collective-permute-start | bytes 393224 | tf_op jit(solution)/shard_map/ppermute | solution.py:569
  82.8 5.0 %collective-permute-start.20 = (f32[64,512]{1,0:T(8,128)S(1)}, f32[64,512]{1,0:T(8,128)S(1)}, u32[]{:S(2)}, u32[]{:S(2)}) collective-permute-start(f32[64,512]{1,0:T(8,128)S(1)} %get-tuple-element.99), channel_id=1, source_target_pairs={{0,16},{1,17},{2,18},{3,19},{4,20},{5,21},{6,22},{7,23},{8,24},{9,... | collective-permute-start | bytes 393224 | tf_op jit(solution)/shard_map/ppermute | solution.py:569
  84.3 5.9 %collective-permute-start.21 = (f32[64,512]{1,0:T(8,128)S(1)}, f32[64,512]{1,0:T(8,128)S(1)}, u32[]{:S(2)}, u32[]{:S(2)}) collective-permute-start(f32[64,512]{1,0:T(8,128)S(1)} %get-tuple-element.100), channel_id=1, source_target_pairs={{0,24},{1,25},{2,26},{3,27},{4,28},{5,29},{6,30},{7,31},{8,16},{9,... | collective-permute-start | bytes 393224 | tf_op jit(solution)/shard_map/ppermute | solution.py:569
  84.3 17.6 %collective-permute-start.15 = (f32[64,512]{1,0:T(8,128)S(1)}, f32[64,512]{1,0:T(8,128)S(1)}, u32[]{:S(2)}, u32[]{:S(2)}) collective-permute-start(f32[64,512]{1,0:T(8,128)S(1)} %get-tuple-element.93), channel_id=1, source_target_pairs={{1,0},{2,1},{3,2},{5,4},{6,5},{7,6},{9,8},{10,9},{11,10},{13,12},{... | collective-permute-start | bytes 393224 | tf_op jit(solution)/shard_map/ppermute | solution.py:569
  85.6 17.3 %collective-permute-start.26 = (f32[4,64,512]{2,1,0:T(8,128)S(1)}, f32[4,64,512]{2,1,0:T(8,128)S(1)}, u32[]{:S(2)}, u32[]{:S(2)}) collective-permute-start(f32[4,64,512]{2,1,0:T(8,128)S(1)} %get-tuple-element.111), channel_id=1, source_target_pairs={{3,7},{7,3},{11,15},{15,11},{19,23},{23,19},{27,31},{31,27}} | collective-permute-start | bytes 1572872 | tf_op jit(solution)/shard_map/ppermute | solution.py:569
  102.9 3.4 %collective-permute-start.22 = (f32[4,64,512]{2,1,0:T(8,128)S(1)}, f32[4,64,512]{2,1,0:T(8,128)S(1)}, u32[]{:S(2)}, u32[]{:S(2)}) collective-permute-start(f32[4,64,512]{2,1,0:T(8,128)S(1)} %get-tuple-element.106), channel_id=1, source_target_pairs={{0,4},{1,5},{2,6},{3,7},{4,0},{5,1},{6,2},{7,3},{8,12},{9,13},{10,... | collective-permute-start | bytes 1572872 | tf_op jit(solution)/shard_map/ppermute | solution.py:569
  103.0 4.7 %collective-permute-start.27 = (f32[64,512]{1,0:T(8,128)S(1)}, f32[64,512]{1,0:T(8,128)S(1)}, u32[]{:S(2)}, u32[]{:S(2)}) collective-permute-start(f32[64,512]{1,0:T(8,128)S(1)} %get-tuple-element.113), channel_id=1, source_target_pairs={{3,11},{7,15},{11,3},{15,7},{19,27},{23,31},{27,19},{31,23}} | collective-permute-start | bytes 393224 | tf_op jit(solution)/shard_map/ppermute | solution.py:569
  103.7 5.3 %collective-permute-start.28 = (f32[64,512]{1,0:T(8,128)S(1)}, f32[64,512]{1,0:T(8,128)S(1)}, u32[]{:S(2)}, u32[]{:S(2)}) collective-permute-start(f32[64,512]{1,0:T(8,128)S(1)} %get-tuple-element.114), channel_id=1, source_target_pairs={{3,19},{7,23},{11,27},{15,31},{19,3},{23,7},{27,11},{31,15}} | collective-permute-start | bytes 393224 | tf_op jit(solution)/shard_map/ppermute | solution.py:569
  104.3 6.2 %collective-permute-start.29 = (f32[64,512]{1,0:T(8,128)S(1)}, f32[64,512]{1,0:T(8,128)S(1)}, u32[]{:S(2)}, u32[]{:S(2)}) collective-permute-start(f32[64,512]{1,0:T(8,128)S(1)} %get-tuple-element.115), channel_id=1, source_target_pairs={{3,27},{7,31},{11,19},{15,23},{19,11},{23,15},{27,3},{31,7}} | collective-permute-start | bytes 393224 | tf_op jit(solution)/shard_map/ppermute | solution.py:569
  105.0 9.1 %collective-permute-start.16 = (f32[64,512]{1,0:T(8,128)S(1)}, f32[64,512]{1,0:T(8,128)S(1)}, u32[]{:S(2)}, u32[]{:S(2)}) collective-permute-start(f32[64,512]{1,0:T(8,128)S(1)} %get-tuple-element.94), channel_id=1, source_target_pairs={{1,8},{2,9},{3,10},{5,12},{6,13},{7,14},{9,0},{10,1},{11,2},{13,4}... | collective-permute-start | bytes 393224 | tf_op jit(solution)/shard_map/ppermute | solution.py:569
  106.3 10.7 %collective-permute-start.17 = (f32[64,512]{1,0:T(8,128)S(1)}, f32[64,512]{1,0:T(8,128)S(1)}, u32[]{:S(2)}, u32[]{:S(2)}) collective-permute-start(f32[64,512]{1,0:T(8,128)S(1)} %get-tuple-element.95), channel_id=1, source_target_pairs={{1,16},{2,17},{3,18},{5,20},{6,21},{7,22},{9,24},{10,25},{11,26},{... | collective-permute-start | bytes 393224 | tf_op jit(solution)/shard_map/ppermute | solution.py:569
  107.7 11.8 %collective-permute-start.18 = (f32[64,512]{1,0:T(8,128)S(1)}, f32[64,512]{1,0:T(8,128)S(1)}, u32[]{:S(2)}, u32[]{:S(2)}) collective-permute-start(f32[64,512]{1,0:T(8,128)S(1)} %get-tuple-element.96), channel_id=1, source_target_pairs={{1,24},{2,25},{3,26},{5,28},{6,29},{7,30},{9,16},{10,17},{11,18},{... | collective-permute-start | bytes 393224 | tf_op jit(solution)/shard_map/ppermute | solution.py:569
  109.0 10.5 %collective-permute-start.23 = (f32[64,512]{1,0:T(8,128)S(1)}, f32[64,512]{1,0:T(8,128)S(1)}, u32[]{:S(2)}, u32[]{:S(2)}) collective-permute-start(f32[64,512]{1,0:T(8,128)S(1)} %get-tuple-element.108), channel_id=1, source_target_pairs={{0,8},{1,9},{2,10},{3,11},{4,12},{5,13},{6,14},{7,15},{8,0},{9,1},... | collective-permute-start | bytes 393224 | tf_op jit(solution)/shard_map/ppermute | solution.py:569
  110.6 13.9 %collective-permute-start.24 = (f32[64,512]{1,0:T(8,128)S(1)}, f32[64,512]{1,0:T(8,128)S(1)}, u32[]{:S(2)}, u32[]{:S(2)}) collective-permute-start(f32[64,512]{1,0:T(8,128)S(1)} %get-tuple-element.109), channel_id=1, source_target_pairs={{0,16},{1,17},{2,18},{3,19},{4,20},{5,21},{6,22},{7,23},{8,24},{9,... | collective-permute-start | bytes 393224 | tf_op jit(solution)/shard_map/ppermute | solution.py:569
  114.1 10.4 %collective-permute-start.25 = (f32[64,512]{1,0:T(8,128)S(1)}, f32[64,512]{1,0:T(8,128)S(1)}, u32[]{:S(2)}, u32[]{:S(2)}) collective-permute-start(f32[64,512]{1,0:T(8,128)S(1)} %get-tuple-element.110), channel_id=1, source_target_pairs={{0,24},{1,25},{2,26},{3,27},{4,28},{5,29},{6,30},{7,31},{8,16},{9,... | collective-permute-start | bytes 393224 | tf_op jit(solution)/shard_map/ppermute | solution.py:569

commit v9 on v5

--- a/solution.py
+++ b/solution.py
@@ -295,7 +295,7 @@
             out[...] = joined
 
     if rights:
-        @pl.when(is_right)
+        @pl.when(is_right & (place > 0))
         def _():
             put(m_x, arrived[...])
             out[...] = apply_map(right_map, m_x)
@@ -335,24 +335,24 @@
 
 
 def first_kernel(count, *refs):
-    refs = list(refs)
-    arrived = refs.pop(0)
-    outs = [refs.pop(0) for _ in range(count)]
-    right_map = [refs.pop(0) for _ in range(3)]
-    refs.pop(0)
-    block, *parcels, m_x = refs
-    place = lax.axis_index("slab")
-    core = trailing()
+    arrived, outs = refs[:2], refs[2 : count + 2]
+    right_map = refs[count + 2 : count + 5]
+    block, *parcels, m_x = refs[count + 6 :]
+    place, core = lax.axis_index("slab"), trailing()
     at = jnp.where(place == count - 1, count - 2 + core, 2 * count - 3 - place + core)
 
     for index in range(count):
-        @pl.when(at == count - 2 + index)
+        @pl.when((place > 0) & (at == count - 2 + index))
         def _(index=index):
             block[...] = outs[index][...]
 
-    @pl.when((place == 0) & (core == 1))
-    def _():
-        put(m_x, arrived[...])
+    for index in range(2):
+        @pl.when((place == 0) & (core == index))
+        def _(index=index):
+            put(m_x, arrived[index][...])
+
+    @pl.when(place == 0)
+    def _():
         block[...] = apply_map(right_map, m_x)
 
     pack(block, parcels)
@@ -381,12 +381,16 @@
     energy = lax.axis_index("energy")
     core = lax.rem(energy, 2)
     sources = [lax.bitwise_xor(energy, 2 * mask) for mask in range(chips)]
-    for mask in range(chips):
-        for target, out in ((sources[mask], mine), (sources[mask] + 1 - 2 * core, other)):
-            total = weights[target, sources[0]] * parcels[0][...]
-            for index in range(1, chips):
-                total += weights[target, sources[index]] * parcels[index][...]
-            out[mask] = total
+    rows = parcels[0].shape[0]
+    for row in range(0, rows, 8):
+        where = slice(row, row + 8)
+        values = [parcel[where] for parcel in parcels]
+        for mask in range(chips):
+            for target, out in ((sources[mask], mine), (sources[mask] + 1 - 2 * core, other)):
+                total = weights[target, sources[0]] * values[0]
+                for index in range(1, chips):
+                    total += weights[target, sources[index]] * values[index]
+                out[mask, where] = total
 
 
 def sum_kernel(chips, mine, other, *outs):
@@ -528,7 +532,7 @@
         flops=2 * product,
         name="second_slab",
     )
-    args = arrived[-1:] + outs[count - 2 :] + right_map[:3] + blocks[1:]
+    args = arrived[-2:] + outs[count - 2 :] + right_map[:3] + blocks[1:]
     blocks[0], *parcels[0] = call(
         functools.partial(first_kernel, count),
         [row] + [parcel] * chips,

time: 108 us -> 109 us (level)
  starting transfers between devices: 31.4 us -> 32.6 us
  transfers between devices with their start and end apart: 24 -> 24, of which waited for: 10 -> 11; matrix products, arithmetic and copies ran while one was open for 0% -> 0% of each run, Pallas kernels for 10% -> 11%
where the time goes in v9:
time: 109 us
  waiting for transfers between devices  55.2 us (51%)
  starting transfers between devices  32.6 us (30%)
  Pallas kernels  19.8 us (18%)
    ppermute x7, waiting for transfers between devices, relay(): lax.ppermute(value, ('energy', 'slab'), relay_pairs(step, energies, count))  29 us
    pallas_call x17, Pallas kernels, call(): pl.pallas_call(kernel, out_shape=outs, in_specs=specs or [VMEM] * len(arg...  19.8 us
    ppermute x3, waiting for transfers between devices, lower_place(): return lax.ppermute(value, ('energy', 'slab'), pairs)  17.6 us
    ppermute x12, starting transfers between devices, exchange(): lax.ppermute(value, 'energy', [(i, i ^ 2 * mask) for i in range(energies)])  15.2 us
    ppermute x12, waiting for transfers between devices, exchange(): lax.ppermute(value, 'energy', [(i, i ^ 2 * mask) for i in range(energies)])  8.49 us
    ppermute x2, starting transfers between devices, shards(): other = lax.ppermute(other, 'energy', [(i, i ^ 1) for i in range(energies)])  8.13 us
    ppermute x7, starting transfers between devices, relay(): lax.ppermute(value, ('energy', 'slab'), relay_pairs(step, energies, count))  6.07 us
    ppermute x3, starting transfers between devices, lower_place(): return lax.ppermute(value, ('energy', 'slab'), pairs)  3.26 us
  transfers between devices with their start and end apart: 24, of which 11 were waited for; matrix products, arithmetic and copies ran while one was open for 0% of the time, Pallas kernels for 11%

profile of v9, /device:TPU:0, one launch (start us, length us, event | category | flops | bytes accessed | tf_op | source)
XLA Modules:
  0.0 108.6 jit_solution(963473758745114233)
XLA Ops:
  0.6 0.0 copy-start
  0.6 5.2 %source.1 = (f32[256,512]{1,0:T(8,128)}, f32[128,512]{1,0:T(8,128)}) custom-call(f32[2,2,256,256]{3,2,1,0:T(8,128)} %bitcast.6, f32[2,2,256,256]{3,2,1,0:T(8,128)} %bitcast.8, f32[2,2,256,256]{3,2,1,0:T(8,128)} %coupling.3, s32[2,16,16]{2,1,0:T(8,128)} %pattern.3), custom_call_target="tpu_custom_call" | custom-call | flops 2415919104 | bytes 1048576 | tf_op jit(solution)/shard_map/source/pallas_call | solution.py:91
  5.8 1.3 %collective-permute-start = (f32[256,512]{1,0:T(8,128)}, f32[256,512]{1,0:T(8,128)S(1)}, u32[]{:S(2)}, u32[]{:S(2)}) collective-permute-start(f32[256,512]{1,0:T(8,128)} %get-tuple-element.44), channel_id=1, source_target_pairs={{0,1},{8,9},{16,17},{24,25}} | collective-permute-start | bytes 1572872 | tf_op jit(solution)/shard_map/ppermute | solution.py:451
  7.2 0.7 collective-permute-start.1
  7.9 0.0 copy-done
  7.9 4.7 %left_maps.1 = (f32[256,512]{1,0:T(8,128)S(1)}, f32[256,512]{1,0:T(8,128)S(1)}, f32[256,512]{1,0:T(8,128)S(1)}, f32[128,512]{1,0:T(8,128)S(1)}, f32[128,512]{1,0...) custom-call(f32[2,2,256,256]{3,2,1,0:T(8,128)} %bitcast.7, ...), custom_call_target="tpu_custom_call" | custom-call | flops 4831838208 | bytes 1048576 | tf_op jit(solution)/shard_map/left_maps/pallas_call | solution.py:91
  12.6 0.0 collective-permute-done.1.refs_4_.refs_11_
  12.6 1.6 %collective-permute-done.refs_0_ = f32[256,512]{1,0:T(8,128)S(1)} collective-permute-done((f32[256,512]{1,0:T(8,128)}, f32[256,512]{1,0:T(8,128)S(1)}, u32[]{:S(2)}, u32[]{:S(2)}) %collective-permute-start) | collective-permute-done | bytes 524320 | tf_op jit(solution)/shard_map/ppermute | solution.py:451
  14.2 0.7 collective-permute-start.2
  14.9 0.0 collective-permute-done.2.refs_0_.refs_1_
  14.9 0.7 collective-permute-start.3
  15.6 1.3 %collective-permute-start.5 = (f32[128,512]{1,0:T(8,128)S(1)}, f32[128,512]{1,0:T(8,128)S(1)}, u32[]{:S(2)}, u32[]{:S(2)}) collective-permute-start(f32[128,512]{1,0:T(8,128)S(1)} %get-tuple-element.54), channel_id=1, source_target_pairs={{1,0},{2,1},{3,2},{9,8},{10,9},{11,10},{17,16},{18,17},{19,18},{25... | collective-permute-start | bytes 786440 | tf_op jit(solution)/shard_map/ppermute | solution.py:460
  16.9 1.3 %collective-permute-start.6 = (f32[128,512]{1,0:T(8,128)S(1)}, f32[128,512]{1,0:T(8,128)S(1)}, u32[]{:S(2)}, u32[]{:S(2)}) collective-permute-start(f32[128,512]{1,0:T(8,128)S(1)} %get-tuple-element.55), channel_id=1, source_target_pairs={{1,0},{2,1},{3,2},{5,4},{6,5},{7,6},{9,8},{10,9},{11,10},{13,12},{... | collective-permute-start | bytes 786440 | tf_op jit(solution)/shard_map/ppermute | solution.py:460
  18.2 0.0 collective-permute-done.3.refs_0_.refs_2_
  18.2 0.2 relay.8
  18.4 0.7 collective-permute-start.4
  19.2 13.1 %collective-permute-done.5.refs_12_ = f32[128,512]{1,0:T(8,128)S(1)} collective-permute-done((f32[128,512]{1,0:T(8,128)S(1)}, f32[128,512]{1,0:T(8,128)S(1)}, u32[]{:S(2)}, u32[]{:S(2)}) %collective-permute-start.5) | collective-permute-done | bytes 262176 | tf_op jit(solution)/shard_map/ppermute | solution.py:460
  32.3 4.5 %collective-permute-done.6.refs_13_ = f32[128,512]{1,0:T(8,128)S(1)} collective-permute-done((f32[128,512]{1,0:T(8,128)S(1)}, f32[128,512]{1,0:T(8,128)S(1)}, u32[]{:S(2)}, u32[]{:S(2)}) %collective-permute-start.6) | collective-permute-done | bytes 262176 | tf_op jit(solution)/shard_map/ppermute | solution.py:460
  36.8 3.3 %right_maps.1 = (bf16[2,3,256,256]{3,2,1,0:T(8,128)(2,1)S(1)}, bf16[2,3,256,256]{3,2,1,0:T(8,128)(2,1)S(1)}, f32[256,512]{1,0:T(8,128)S(1)}, bf16[2,3,256,256]{3...) custom-call(f32[256,512]{1,0:T(8,128)S(1)} %collective-permute-done.refs_0_, ...), custom_call_target="tpu_custom_call" | custom-call | flops 4026531840 | bytes 1048576 | tf_op jit(solution)/shard_map/right_maps/pallas_call | solution.py:91
  40.1 0.0 collective-permute-done.4.refs_0_
  40.1 0.7 collective-permute-start.7
  40.9 0.0 collective-permute-done.7.refs_0_.refs_1_
  40.9 1.3 %collective-permute-start.8 = (f32[256,512]{1,0:T(8,128)S(1)}, f32[256,512]{1,0:T(8,128)S(1)}, u32[]{:S(2)}, u32[]{:S(2)}) collective-permute-start(f32[256,512]{1,0:T(8,128)S(1)} %relay.10.refs_4_), channel_id=1, source_target_pairs={{1,0},{6,5},{9,8},{14,13},{17,16},{22,21},{25,24},{30,29}} | collective-permute-start | bytes 1572872 | tf_op jit(solution)/shard_map/ppermute | solution.py:451
  42.2 27.5 %collective-permute-done.8.refs_0_.refs_2_ = f32[256,512]{1,0:T(8,128)S(1)} collective-permute-done((f32[256,512]{1,0:T(8,128)S(1)}, f32[256,512]{1,0:T(8,128)S(1)}, u32[]{:S(2)}, u32[]{:S(2)}) %collective-permute-start.8) | collective-permute-done | bytes 524320 | tf_op jit(solution)/shard_map/ppermute | solution.py:451
  69.7 0.7 collective-permute-start.9
  70.3 0.0 collective-permute-done.9.refs_3_.refs_1_
  70.4 1.3 %second_slab.1 = (f32[256,512]{1,0:T(8,128)S(1)}, f32[64,512]{1,0:T(8,128)S(1)}, f32[64,512]{1,0:T(8,128)S(1)}, f32[64,512]{1,0:T(8,128)S(1)}, f32[64,512]{1,0:T(8,128)S(1)}) custom-call(f32[256,512]{1,0:T(8,128)S(1)} %collective-permute-done.4.refs_0_, f32[256,512]{1,0:T(8,128)S(1)} %collective-permute-done.7.refs_0_.refs_1_, ...), custom_call_target="tpu_custom_call" | custom-call | flops 805306368 | bytes 1048576 | tf_op jit(solution)/shard_map/second_slab/pallas_call | solution.py:91
  71.6 0.0 copy-start.3
  71.7 3.0 %collective-permute-start.17 = (f32[64,512]{1,0:T(8,128)S(1)}, f32[64,512]{1,0:T(8,128)S(1)}, u32[]{:S(2)}, u32[]{:S(2)}) collective-permute-start(f32[64,512]{1,0:T(8,128)S(1)} %get-tuple-element.77), channel_id=1, source_target_pairs={{0,8},{4,12},{8,0},{12,4},{16,24},{20,28},{24,16},{28,20},{1,9},{5... | collective-permute-start | bytes 393224 | tf_op jit(solution)/shard_map/ppermute | solution.py:550
  74.7 1.6 %collective-permute-start.18 = (f32[64,512]{1,0:T(8,128)S(1)}, f32[64,512]{1,0:T(8,128)S(1)}, u32[]{:S(2)}, u32[]{:S(2)}) collective-permute-start(f32[64,512]{1,0:T(8,128)S(1)} %get-tuple-element.78), channel_id=1, source_target_pairs={{0,16},{4,20},{8,24},{12,28},{16,0},{20,4},{24,8},{28,12},{1,17},{... | collective-permute-start | bytes 393224 | tf_op jit(solution)/shard_map/ppermute | solution.py:550
  76.3 0.5 collective-permute-start.19
  76.7 1.0 first_slab.1
  77.7 1.6 %collective-permute-start.10 = (f32[64,512]{1,0:T(8,128)S(1)}, f32[64,512]{1,0:T(8,128)S(1)}, u32[]{:S(2)}, u32[]{:S(2)}) collective-permute-start(f32[64,512]{1,0:T(8,128)S(1)} %get-tuple-element.67), channel_id=1, source_target_pairs={{0,8},{4,12},{8,0},{12,4},{16,24},{20,28},{24,16},{28,20},{1,9},{5... | collective-permute-start | bytes 393224 | tf_op jit(solution)/shard_map/ppermute | solution.py:550
  79.3 1.5 %collective-permute-start.11 = (f32[64,512]{1,0:T(8,128)S(1)}, f32[64,512]{1,0:T(8,128)S(1)}, u32[]{:S(2)}, u32[]{:S(2)}) collective-permute-start(f32[64,512]{1,0:T(8,128)S(1)} %get-tuple-element.68), channel_id=1, source_target_pairs={{0,16},{4,20},{8,24},{12,28},{16,0},{20,4},{24,8},{28,12},{1,17},{... | collective-permute-start | bytes 393224 | tf_op jit(solution)/shard_map/ppermute | solution.py:550
  80.8 0.0 collective-permute-done.17.refs_1_
  80.8 0.5 collective-permute-start.12
  81.3 0.1 add_reduce_fusion.weights
  81.4 0.0 collective-permute-done.18.refs_2_
  81.4 0.7 collective-permute-done.19.refs_3_
  82.1 0.9 mix.3
  83.0 6.5 %collective-permute-start.20 = (f32[4,64,512]{2,1,0:T(8,128)S(1)}, f32[4,64,512]{2,1,0:T(8,128)S(1)}, u32[]{:S(2)}, u32[]{:S(2)}) collective-permute-start(f32[4,64,512]{2,1,0:T(8,128)S(1)} %get-tuple-element.81), channel_id=1, source_target_pairs={{0,4},{4,0},{8,12},{12,8},{16,20},{20,16},{24,28},{28,24},{1,5},{5... | collective-permute-start | bytes 1572872 | tf_op jit(solution)/shard_map/ppermute | solution.py:569
  89.5 0.0 collective-permute-done.10.refs_1_
  89.5 0.0 collective-permute-done.11.refs_2_
  89.5 0.0 collective-permute-done.12.refs_3_
  89.5 0.9 mix.2
  90.4 1.7 %collective-permute-start.13 = (f32[4,64,512]{2,1,0:T(8,128)S(1)}, f32[4,64,512]{2,1,0:T(8,128)S(1)}, u32[]{:S(2)}, u32[]{:S(2)}) collective-permute-start(f32[4,64,512]{2,1,0:T(8,128)S(1)} %get-tuple-element.71), channel_id=1, source_target_pairs={{0,4},{4,0},{8,12},{12,8},{16,20},{20,16},{24,28},{28,24},{1,5},{5... | collective-permute-start | bytes 1572872 | tf_op jit(solution)/shard_map/ppermute | solution.py:569
  92.1 0.0 collective-permute-done.20.other
  92.1 0.1 sum.3
  92.2 1.1 collective-permute-start.21
  93.2 1.1 collective-permute-start.22
  94.3 1.4 %collective-permute-start.23 = (f32[64,512]{1,0:T(8,128)S(1)}, f32[64,512]{1,0:T(8,128)S(1)}, u32[]{:S(2)}, u32[]{:S(2)}) collective-permute-start(f32[64,512]{1,0:T(8,128)S(1)} %get-tuple-element.85), channel_id=1, source_target_pairs={{0,24},{4,28},{8,16},{12,20},{16,8},{20,12},{24,0},{28,4},{1,25},{... | collective-permute-start | bytes 393224 | tf_op jit(solution)/shard_map/ppermute | solution.py:550
  95.7 0.0 collective-permute-done.13.other
  95.7 0.1 sum.2
  95.8 1.1 collective-permute-start.14
  96.8 1.1 collective-permute-start.15
  97.9 0.7 collective-permute-done.21.refs_5_
  98.6 0.9 collective-permute-start.16
  99.5 1.0 retarded.1
  100.5 0.1 collective-permute-done.22.refs_6_
  100.6 1.9 %collective-permute-done.23.refs_7_ = f32[64,512]{1,0:T(8,128)S(1)} collective-permute-done((f32[64,512]{1,0:T(8,128)S(1)}, f32[64,512]{1,0:T(8,128)S(1)}, u32[]{:S(2)}, u32[]{:S(2)}) %collective-permute-start.23) | collective-permute-done | bytes 131104 | tf_op jit(solution)/shard_map/ppermute | solution.py:550
  102.5 1.7 %collective-permute-done.14.refs_1_ = f32[64,512]{1,0:T(8,128)S(1)} collective-permute-done((f32[64,512]{1,0:T(8,128)S(1)}, f32[64,512]{1,0:T(8,128)S(1)}, u32[]{:S(2)}, u32[]{:S(2)}) %collective-permute-start.14) | collective-permute-done | bytes 131104 | tf_op jit(solution)/shard_map/ppermute | solution.py:550
  104.2 1.5 %collective-permute-done.15.refs_2_ = f32[64,512]{1,0:T(8,128)S(1)} collective-permute-done((f32[64,512]{1,0:T(8,128)S(1)}, f32[64,512]{1,0:T(8,128)S(1)}, u32[]{:S(2)}, u32[]{:S(2)}) %collective-permute-start.15) | collective-permute-done | bytes 131104 | tf_op jit(solution)/shard_map/ppermute | solution.py:550
  105.7 1.9 %collective-permute-done.16.refs_3_ = f32[64,512]{1,0:T(8,128)S(1)} collective-permute-done((f32[64,512]{1,0:T(8,128)S(1)}, f32[64,512]{1,0:T(8,128)S(1)}, u32[]{:S(2)}, u32[]{:S(2)}) %collective-permute-start.16) | collective-permute-done | bytes 131104 | tf_op jit(solution)/shard_map/ppermute | solution.py:550
  107.6 1.0 scattering.1
  (12 shorter events, 0.1 us)
Async XLA Ops:
  0.6 7.2 %copy-start = (s32[2,16,16]{2,1,0:T(8,128)S(1)}, s32[2,16,16]{2,1,0:T(8,128)}, u32[]{:S(2)}) copy-start(s32[2,16,16]{2,1,0:T(8,128)} %pattern.3) | copy-start | bytes 6148
  5.8 8.3 %collective-permute-start = (f32[256,512]{1,0:T(8,128)}, f32[256,512]{1,0:T(8,128)S(1)}, u32[]{:S(2)}, u32[]{:S(2)}) collective-permute-start(f32[256,512]{1,0:T(8,128)} %get-tuple-element.44), channel_id=1, source_target_pairs={{0,1},{8,9},{16,17},{24,25}} | collective-permute-start | bytes 1572872 | tf_op jit(solution)/shard_map/ppermute | solution.py:451
  7.2 5.4 %collective-permute-start.1 = (f32[128,512]{1,0:T(8,128)}, f32[128,512]{1,0:T(8,128)S(1)}, u32[]{:S(2)}, u32[]{:S(2)}) collective-permute-start(f32[128,512]{1,0:T(8,128)} %get-tuple-element.48), channel_id=1, source_target_pairs={{5,4},{6,5},{7,6},{13,12},{14,13},{15,14},{21,20},{22,21},{23,22},... | collective-permute-start | bytes 786440 | tf_op jit(solution)/shard_map/ppermute | solution.py:460
  14.2 0.7 collective-permute-start.2
  14.9 3.3 %collective-permute-start.3 = (f32[256,512]{1,0:T(8,128)S(1)}, f32[256,512]{1,0:T(8,128)S(1)}, u32[]{:S(2)}, u32[]{:S(2)}) collective-permute-start(f32[256,512]{1,0:T(8,128)S(1)} %relay.7.refs_4_.refs_10_), channel_id=1, source_target_pairs={{2,3},{5,6},{10,11},{13,14},{18,19},{21,22},{26,27},{29,30}} | collective-permute-start | bytes 1572872 | tf_op jit(solution)/shard_map/ppermute | solution.py:451
  15.6 16.7 %collective-permute-start.5 = (f32[128,512]{1,0:T(8,128)S(1)}, f32[128,512]{1,0:T(8,128)S(1)}, u32[]{:S(2)}, u32[]{:S(2)}) collective-permute-start(f32[128,512]{1,0:T(8,128)S(1)} %get-tuple-element.54), channel_id=1, source_target_pairs={{1,0},{2,1},{3,2},{9,8},{10,9},{11,10},{17,16},{18,17},{19,18},{25... | collective-permute-start | bytes 786440 | tf_op jit(solution)/shard_map/ppermute | solution.py:460
  16.9 19.9 %collective-permute-start.6 = (f32[128,512]{1,0:T(8,128)S(1)}, f32[128,512]{1,0:T(8,128)S(1)}, u32[]{:S(2)}, u32[]{:S(2)}) collective-permute-start(f32[128,512]{1,0:T(8,128)S(1)} %get-tuple-element.55), channel_id=1, source_target_pairs={{1,0},{2,1},{3,2},{5,4},{6,5},{7,6},{9,8},{10,9},{11,10},{13,12},{... | collective-permute-start | bytes 786440 | tf_op jit(solution)/shard_map/ppermute | solution.py:460
  18.4 21.7 %collective-permute-start.4 = (f32[256,512]{1,0:T(8,128)S(1)}, f32[256,512]{1,0:T(8,128)S(1)}, u32[]{:S(2)}, u32[]{:S(2)}) collective-permute-start(f32[256,512]{1,0:T(8,128)S(1)} %get-tuple-element.53.refs_5_.refs_11_.refs_2_), channel_id=1, source_target_pairs={{3,2},{6,7},{11,10},{14,15},{19,18},{22,23},{27,26},{30,31}} | collective-permute-start | bytes 1572872 | tf_op jit(solution)/shard_map/ppermute | solution.py:451
  40.1 0.7 collective-permute-start.7
  40.9 28.8 %collective-permute-start.8 = (f32[256,512]{1,0:T(8,128)S(1)}, f32[256,512]{1,0:T(8,128)S(1)}, u32[]{:S(2)}, u32[]{:S(2)}) collective-permute-start(f32[256,512]{1,0:T(8,128)S(1)} %relay.10.refs_4_), channel_id=1, source_target_pairs={{1,0},{6,5},{9,8},{14,13},{17,16},{22,21},{25,24},{30,29}} | collective-permute-start | bytes 1572872 | tf_op jit(solution)/shard_map/ppermute | solution.py:451
  69.7 0.7 collective-permute-start.9
  71.6 3.0 %copy-start.3 = (s32[4]{0:T(128)S(1)}, s32[4]{0:T(128)}, u32[]{:S(2)}) copy-start(s32[4]{0:T(128)} %param.11) | copy-start | bytes 52
  71.7 9.2 %collective-permute-start.17 = (f32[64,512]{1,0:T(8,128)S(1)}, f32[64,512]{1,0:T(8,128)S(1)}, u32[]{:S(2)}, u32[]{:S(2)}) collective-permute-start(f32[64,512]{1,0:T(8,128)S(1)} %get-tuple-element.77), channel_id=1, source_target_pairs={{0,8},{4,12},{8,0},{12,4},{16,24},{20,28},{24,16},{28,20},{1,9},{5... | collective-permute-start | bytes 393224 | tf_op jit(solution)/shard_map/ppermute | solution.py:550
  74.7 6.7 %collective-permute-start.18 = (f32[64,512]{1,0:T(8,128)S(1)}, f32[64,512]{1,0:T(8,128)S(1)}, u32[]{:S(2)}, u32[]{:S(2)}) collective-permute-start(f32[64,512]{1,0:T(8,128)S(1)} %get-tuple-element.78), channel_id=1, source_target_pairs={{0,16},{4,20},{8,24},{12,28},{16,0},{20,4},{24,8},{28,12},{1,17},{... | collective-permute-start | bytes 393224 | tf_op jit(solution)/shard_map/ppermute | solution.py:550
  76.3 5.9 %collective-permute-start.19 = (f32[64,512]{1,0:T(8,128)S(1)}, f32[64,512]{1,0:T(8,128)S(1)}, u32[]{:S(2)}, u32[]{:S(2)}) collective-permute-start(f32[64,512]{1,0:T(8,128)S(1)} %get-tuple-element.79), channel_id=1, source_target_pairs={{0,24},{4,28},{8,16},{12,20},{16,8},{20,12},{24,0},{28,4},{1,25},{... | collective-permute-start | bytes 393224 | tf_op jit(solution)/shard_map/ppermute | solution.py:550
  77.7 11.8 %collective-permute-start.10 = (f32[64,512]{1,0:T(8,128)S(1)}, f32[64,512]{1,0:T(8,128)S(1)}, u32[]{:S(2)}, u32[]{:S(2)}) collective-permute-start(f32[64,512]{1,0:T(8,128)S(1)} %get-tuple-element.67), channel_id=1, source_target_pairs={{0,8},{4,12},{8,0},{12,4},{16,24},{20,28},{24,16},{28,20},{1,9},{5... | collective-permute-start | bytes 393224 | tf_op jit(solution)/shard_map/ppermute | solution.py:550
  79.3 2.0 %copy-start.1 = (f32[4]{0:T(128)S(1)}, f32[4]{0:T(128)}, u32[]{:S(2)}) copy-start(f32[4]{0:T(128)} %param.13) | copy-start | bytes 52
  79.3 2.0 %copy-start.2 = (f32[4]{0:T(128)S(1)}, f32[4]{0:T(128)}, u32[]{:S(2)}) copy-start(f32[4]{0:T(128)} %param.12) | copy-start | bytes 52
  79.3 10.2 %collective-permute-start.11 = (f32[64,512]{1,0:T(8,128)S(1)}, f32[64,512]{1,0:T(8,128)S(1)}, u32[]{:S(2)}, u32[]{:S(2)}) collective-permute-start(f32[64,512]{1,0:T(8,128)S(1)} %get-tuple-element.68), channel_id=1, source_target_pairs={{0,16},{4,20},{8,24},{12,28},{16,0},{20,4},{24,8},{28,12},{1,17},{... | collective-permute-start | bytes 393224 | tf_op jit(solution)/shard_map/ppermute | solution.py:550
  80.8 8.7 %collective-permute-start.12 = (f32[64,512]{1,0:T(8,128)S(1)}, f32[64,512]{1,0:T(8,128)S(1)}, u32[]{:S(2)}, u32[]{:S(2)}) collective-permute-start(f32[64,512]{1,0:T(8,128)S(1)} %get-tuple-element.69), channel_id=1, source_target_pairs={{0,24},{4,28},{8,16},{12,20},{16,8},{20,12},{24,0},{28,4},{1,25},{... | collective-permute-start | bytes 393224 | tf_op jit(solution)/shard_map/ppermute | solution.py:550
  83.0 9.1 %collective-permute-start.20 = (f32[4,64,512]{2,1,0:T(8,128)S(1)}, f32[4,64,512]{2,1,0:T(8,128)S(1)}, u32[]{:S(2)}, u32[]{:S(2)}) collective-permute-start(f32[4,64,512]{2,1,0:T(8,128)S(1)} %get-tuple-element.81), channel_id=1, source_target_pairs={{0,4},{4,0},{8,12},{12,8},{16,20},{20,16},{24,28},{28,24},{1,5},{5... | collective-permute-start | bytes 1572872 | tf_op jit(solution)/shard_map/ppermute | solution.py:569
  90.4 5.3 %collective-permute-start.13 = (f32[4,64,512]{2,1,0:T(8,128)S(1)}, f32[4,64,512]{2,1,0:T(8,128)S(1)}, u32[]{:S(2)}, u32[]{:S(2)}) collective-permute-start(f32[4,64,512]{2,1,0:T(8,128)S(1)} %get-tuple-element.71), channel_id=1, source_target_pairs={{0,4},{4,0},{8,12},{12,8},{16,20},{20,16},{24,28},{28,24},{1,5},{5... | collective-permute-start | bytes 1572872 | tf_op jit(solution)/shard_map/ppermute | solution.py:569
  92.2 6.4 %collective-permute-start.21 = (f32[64,512]{1,0:T(8,128)S(1)}, f32[64,512]{1,0:T(8,128)S(1)}, u32[]{:S(2)}, u32[]{:S(2)}) collective-permute-start(f32[64,512]{1,0:T(8,128)S(1)} %get-tuple-element.83), channel_id=1, source_target_pairs={{0,8},{4,12},{8,0},{12,4},{16,24},{20,28},{24,16},{28,20},{1,9},{5... | collective-permute-start | bytes 393224 | tf_op jit(solution)/shard_map/ppermute | solution.py:550
  93.2 7.4 %collective-permute-start.22 = (f32[64,512]{1,0:T(8,128)S(1)}, f32[64,512]{1,0:T(8,128)S(1)}, u32[]{:S(2)}, u32[]{:S(2)}) collective-permute-start(f32[64,512]{1,0:T(8,128)S(1)} %get-tuple-element.84), channel_id=1, source_target_pairs={{0,16},{4,20},{8,24},{12,28},{16,0},{20,4},{24,8},{28,12},{1,17},{... | collective-permute-start | bytes 393224 | tf_op jit(solution)/shard_map/ppermute | solution.py:550
  94.3 8.2 %collective-permute-start.23 = (f32[64,512]{1,0:T(8,128)S(1)}, f32[64,512]{1,0:T(8,128)S(1)}, u32[]{:S(2)}, u32[]{:S(2)}) collective-permute-start(f32[64,512]{1,0:T(8,128)S(1)} %get-tuple-element.85), channel_id=1, source_target_pairs={{0,24},{4,28},{8,16},{12,20},{16,8},{20,12},{24,0},{28,4},{1,25},{... | collective-permute-start | bytes 393224 | tf_op jit(solution)/shard_map/ppermute | solution.py:550
  95.8 8.4 %collective-permute-start.14 = (f32[64,512]{1,0:T(8,128)S(1)}, f32[64,512]{1,0:T(8,128)S(1)}, u32[]{:S(2)}, u32[]{:S(2)}) collective-permute-start(f32[64,512]{1,0:T(8,128)S(1)} %get-tuple-element.73), channel_id=1, source_target_pairs={{0,8},{4,12},{8,0},{12,4},{16,24},{20,28},{24,16},{28,20},{1,9},{5... | collective-permute-start | bytes 393224 | tf_op jit(solution)/shard_map/ppermute | solution.py:550
  96.8 8.9 %collective-permute-start.15 = (f32[64,512]{1,0:T(8,128)S(1)}, f32[64,512]{1,0:T(8,128)S(1)}, u32[]{:S(2)}, u32[]{:S(2)}) collective-permute-start(f32[64,512]{1,0:T(8,128)S(1)} %get-tuple-element.74), channel_id=1, source_target_pairs={{0,16},{4,20},{8,24},{12,28},{16,0},{20,4},{24,8},{28,12},{1,17},{... | collective-permute-start | bytes 393224 | tf_op jit(solution)/shard_map/ppermute | solution.py:550
  98.6 9.0 %collective-permute-start.16 = (f32[64,512]{1,0:T(8,128)S(1)}, f32[64,512]{1,0:T(8,128)S(1)}, u32[]{:S(2)}, u32[]{:S(2)}) collective-permute-start(f32[64,512]{1,0:T(8,128)S(1)} %get-tuple-element.75), channel_id=1, source_target_pairs={{0,24},{4,28},{8,16},{12,20},{16,8},{20,12},{24,0},{28,4},{1,25},{... | collective-permute-start | bytes 393224 | tf_op jit(solution)/shard_map/ppermute | solution.py:550

commit v10 on v9

--- a/solution.py
+++ b/solution.py
@@ -94,7 +94,7 @@
         in_specs=specs or [VMEM] * len(args),
         out_specs=[VMEM] * len(outs),
         scratch_shapes=scratch,
-        compiler_params=pltpu.CompilerParams(vmem_limit_bytes=limit * 2**20),
+        compiler_params=pltpu.CompilerParams(vmem_limit_bytes=int(limit * 2**20)),
         cost_estimate=pl.CostEstimate(flops=flops, bytes_accessed=2**20, transcendentals=0),
         name=name,
     )(*args)
@@ -307,6 +307,7 @@
     ends = [refs.pop(0) for _ in range(2)]
     last_lead, last_tail, whole_start = [refs.pop(0) for _ in range(3)]
     wholes = [refs.pop(0) for _ in range(count - 1)]
+    refs.pop(0)
     block, *parcels, m_x = refs
     place = lax.axis_index("slab")
     core = trailing()
@@ -376,20 +377,31 @@
     return pl.ds(pl.multiple_of(lax.bitwise_xor(chip, mask) * rows, rows), rows)
 
 
-def mix_kernel(chips, weights, *refs):
-    parcels, (mine, other) = refs[:chips], refs[chips:]
+def weight_kernel(chips, weights, tiles):
     energy = lax.axis_index("energy")
     core = lax.rem(energy, 2)
     sources = [lax.bitwise_xor(energy, 2 * mask) for mask in range(chips)]
-    rows = parcels[0].shape[0]
-    for row in range(0, rows, 8):
-        where = slice(row, row + 8)
+    for mask in range(chips):
+        for side, target in enumerate((sources[mask], sources[mask] + 1 - 2 * core)):
+            for index in range(chips):
+                weight = weights[target, sources[index]]
+                tiles[side, mask, index] = jnp.full(tiles.shape[3:], weight, F32)
+
+
+def mix_kernel(chips, tiles, *refs):
+    parcels, outs = refs[:chips], refs[chips:]
+    rows, columns = parcels[0].shape
+    step, width = tiles.shape[3:]
+    for row in range(0, rows, step):
+        where = slice(row, row + step)
         values = [parcel[where] for parcel in parcels]
-        for mask in range(chips):
-            for target, out in ((sources[mask], mine), (sources[mask] + 1 - 2 * core, other)):
-                total = weights[target, sources[0]] * values[0]
-                for index in range(1, chips):
-                    total += weights[target, sources[index]] * values[index]
+        for side, out in enumerate(outs):
+            for mask in range(chips):
+                total = None
+                for index in range(chips):
+                    weight = jnp.concatenate([tiles[side, mask, index]] * (columns // width), axis=1)
+                    term = weight * values[index]
+                    total = term if total is None else total + term
                 out[mask, where] = total
 
 
@@ -467,7 +479,7 @@
         [HBM] * 4,
         flops=6 * product,
         name="source",
-        limit=61,
+        limit=53,
     )
     arrived, outs, ends = [relay(0, begun[0])], [], []
     gate = lower_place(begun[1], [1])
@@ -479,7 +491,7 @@
         [HBM] * 4,
         flops=12 * product,
         name="left_maps",
-        limit=49,
+        limit=48.6,
     )
     left_map = [left_lead, left_tail, whole]
     right_map = None
@@ -523,7 +535,17 @@
     chips = energies // 2
     parcel = shape(size // chips, 2 * size)
     blocks, parcels = [None, None], [None, None]
-    args = arrived[count - 1 :] + ends + right_map[3:] + [whole] + outs[: count - 1]
+    everyone = jnp.arange(energies, dtype=jnp.int32)
+    weights = mode_weights(everyone, everyone, offsets, emission, absorption)
+    (tiles,) = call(
+        functools.partial(weight_kernel, chips),
+        [shape(8, 128, F32, 2, chips, chips)],
+        [],
+        [weights],
+        [SMEM],
+        name="weights",
+    )
+    args = arrived[count - 1 :] + ends + right_map[3:] + [whole] + outs[: count - 1] + [tiles]
     blocks[1], *parcels[1] = call(
         functools.partial(last_kernel, count),
         [row] + [parcel] * chips,
@@ -552,8 +574,6 @@
             if mask
         ]
 
-    everyone = jnp.arange(energies, dtype=jnp.int32)
-    weights = mode_weights(everyone, everyone, offsets, emission, absorption)
     partial = shape(size // chips, 2 * size, F32, chips)
     sums = [None, None]
     for slab in (1, 0):
@@ -561,8 +581,7 @@
             functools.partial(mix_kernel, chips),
             [partial] * 2,
             [],
-            [weights] + exchange(parcels[slab]),
-            [SMEM] + [VMEM] * chips,
+            [tiles] + exchange(parcels[slab]),
             flops=product // 8,
             name="mix",
         )

time: 109 us -> 108 us (level)
  starting transfers between devices: 32.6 us -> 29 us
  waiting for transfers between devices: 55.2 us -> 57.9 us
  Pallas kernels: 19.8 us -> 18.3 us
  local copies, waits for them, and re-layouts: 0.02 us -> 1.37 us
    ppermute x12, waiting for transfers between devices: 8.49 us -> 11.3 us  [exchange(): lax.ppermute(value, 'energy', [(i, i ^ 2 * mask) for i in range(energies)])]
    ppermute x2, starting transfers between devices: 8.13 us -> 5.92 us  [shards(): other = lax.ppermute(other, 'energy', [(i, i ^ 1) for i in range(energies)])]
    pallas_call x17 -> x18, Pallas kernels: 19.8 us -> 18.3 us  [call(): pl.pallas_call(kernel, out_shape=outs, in_specs=specs or [VMEM] * len(arg...]
    ppermute x12, starting transfers between devices: 15.2 us -> 13.8 us  [exchange(): lax.ppermute(value, 'energy', [(i, i ^ 2 * mask) for i in range(energies)])]
    unnamed x8 -> x10, local copies, waits for them, and re-layouts: 0.02 us -> 1.37 us
where the time goes in v10:
time: 108 us
  waiting for transfers between devices  57.9 us (54%)
  starting transfers between devices  29 us (27%)
  Pallas kernels  18.3 us (17%)
  local copies, waits for them, and re-layouts  1.37 us (1%)
    ppermute x7, waiting for transfers between devices, relay(): lax.ppermute(value, ('energy', 'slab'), relay_pairs(step, energies, count))  29.2 us
    pallas_call x18, Pallas kernels, call(): pl.pallas_call(kernel, out_shape=outs, in_specs=specs or [VMEM] * len(arg...  18.3 us
    ppermute x3, waiting for transfers between devices, lower_place(): return lax.ppermute(value, ('energy', 'slab'), pairs)  17.5 us
    ppermute x12, starting transfers between devices, exchange(): lax.ppermute(value, 'energy', [(i, i ^ 2 * mask) for i in range(energies)])  13.8 us
    ppermute x12, waiting for transfers between devices, exchange(): lax.ppermute(value, 'energy', [(i, i ^ 2 * mask) for i in range(energies)])  11.3 us
    ppermute x7, starting transfers between devices, relay(): lax.ppermute(value, ('energy', 'slab'), relay_pairs(step, energies, count))  6.07 us
    ppermute x2, starting transfers between devices, shards(): other = lax.ppermute(other, 'energy', [(i, i ^ 1) for i in range(energies)])  5.92 us
    ppermute x3, starting transfers between devices, lower_place(): return lax.ppermute(value, ('energy', 'slab'), pairs)  3.26 us
  transfers between devices with their start and end apart: 24, of which 11 were waited for; matrix products, arithmetic and copies ran while one was open for 0% of the time, Pallas kernels for 11%

profile of v10, /device:TPU:0, one launch (start us, length us, event | category | flops | bytes accessed | tf_op | source)
XLA Modules:
  0.0 107.6 jit_solution(11052645050514127441)
XLA Ops:
  0.6 0.7 copy-done
  1.4 4.3 %source.1 = (f32[256,512]{1,0:T(8,128)S(1)}, f32[128,512]{1,0:T(8,128)S(1)}) custom-call(f32[2,2,256,256]{3,2,1,0:T(8,128)} %bitcast.6, f32[2,2,256,256]{3,2,1,0:T(8,128)} %bitcast.8, f32[2,2,256,256]{3,2,1,0:T(8,128)} %coupling.3, s32[2,16,16]{2,1,0:T(8,128)S(1)} %copy-done), custom_call_target="tpu_custom_call" | custom-call | flops 2415919104 | bytes 1048576 | tf_op jit(solution)/shard_map/source/pallas_call | solution.py:91
  5.7 1.3 %collective-permute-start = (f32[256,512]{1,0:T(8,128)S(1)}, f32[256,512]{1,0:T(8,128)S(1)}, u32[]{:S(2)}, u32[]{:S(2)}) collective-permute-start(f32[256,512]{1,0:T(8,128)S(1)} %get-tuple-element.44), channel_id=1, source_target_pairs={{0,1},{8,9},{16,17},{24,25}} | collective-permute-start | bytes 1572872 | tf_op jit(solution)/shard_map/ppermute | solution.py:463
  7.0 0.7 collective-permute-start.1
  7.7 4.7 %left_maps.1 = (f32[256,512]{1,0:T(8,128)S(1)}, f32[256,512]{1,0:T(8,128)S(1)}, f32[256,512]{1,0:T(8,128)S(1)}, f32[128,512]{1,0:T(8,128)S(1)}, f32[128,512]{1,0...) custom-call(f32[2,2,256,256]{3,2,1,0:T(8,128)} %bitcast.7, ...), custom_call_target="tpu_custom_call" | custom-call | flops 4831838208 | bytes 1048576 | tf_op jit(solution)/shard_map/left_maps/pallas_call | solution.py:91
  12.4 0.0 collective-permute-done.1.refs_4_.refs_11_
  12.4 1.2 %collective-permute-done.refs_0_ = f32[256,512]{1,0:T(8,128)S(1)} collective-permute-done((f32[256,512]{1,0:T(8,128)S(1)}, f32[256,512]{1,0:T(8,128)S(1)}, u32[]{:S(2)}, u32[]{:S(2)}) %collective-permute-start) | collective-permute-done | bytes 524320 | tf_op jit(solution)/shard_map/ppermute | solution.py:463
  13.7 0.7 collective-permute-start.2
  14.4 0.0 collective-permute-done.2.refs_0_.refs_1_
  14.4 0.7 collective-permute-start.3
  15.1 1.3 %collective-permute-start.5 = (f32[128,512]{1,0:T(8,128)S(1)}, f32[128,512]{1,0:T(8,128)S(1)}, u32[]{:S(2)}, u32[]{:S(2)}) collective-permute-start(f32[128,512]{1,0:T(8,128)S(1)} %get-tuple-element.54), channel_id=1, source_target_pairs={{1,0},{2,1},{3,2},{9,8},{10,9},{11,10},{17,16},{18,17},{19,18},{25... | collective-permute-start | bytes 786440 | tf_op jit(solution)/shard_map/ppermute | solution.py:472
  16.4 1.3 %collective-permute-start.6 = (f32[128,512]{1,0:T(8,128)S(1)}, f32[128,512]{1,0:T(8,128)S(1)}, u32[]{:S(2)}, u32[]{:S(2)}) collective-permute-start(f32[128,512]{1,0:T(8,128)S(1)} %get-tuple-element.55), channel_id=1, source_target_pairs={{1,0},{2,1},{3,2},{5,4},{6,5},{7,6},{9,8},{10,9},{11,10},{13,12},{... | collective-permute-start | bytes 786440 | tf_op jit(solution)/shard_map/ppermute | solution.py:472
  17.7 0.0 collective-permute-done.3.refs_0_.refs_2_
  17.8 0.2 relay.8
  18.0 0.7 collective-permute-start.4
  18.7 13.3 %collective-permute-done.5.refs_12_ = f32[128,512]{1,0:T(8,128)S(1)} collective-permute-done((f32[128,512]{1,0:T(8,128)S(1)}, f32[128,512]{1,0:T(8,128)S(1)}, u32[]{:S(2)}, u32[]{:S(2)}) %collective-permute-start.5) | collective-permute-done | bytes 262176 | tf_op jit(solution)/shard_map/ppermute | solution.py:472
  32.0 4.2 %collective-permute-done.6.refs_13_ = f32[128,512]{1,0:T(8,128)S(1)} collective-permute-done((f32[128,512]{1,0:T(8,128)S(1)}, f32[128,512]{1,0:T(8,128)S(1)}, u32[]{:S(2)}, u32[]{:S(2)}) %collective-permute-start.6) | collective-permute-done | bytes 262176 | tf_op jit(solution)/shard_map/ppermute | solution.py:472
  36.1 3.3 %right_maps.1 = (bf16[2,3,256,256]{3,2,1,0:T(8,128)(2,1)S(1)}, bf16[2,3,256,256]{3,2,1,0:T(8,128)(2,1)S(1)}, f32[256,512]{1,0:T(8,128)S(1)}, bf16[2,3,256,256]{3...) custom-call(f32[256,512]{1,0:T(8,128)S(1)} %collective-permute-done.refs_0_, ...), custom_call_target="tpu_custom_call" | custom-call | flops 4026531840 | bytes 1048576 | tf_op jit(solution)/shard_map/right_maps/pallas_call | solution.py:91
  39.5 0.7 collective-permute-start.7
  40.2 0.0 collective-permute-done.7.refs_0_.refs_1_
  40.3 0.0 copy-start.4
  40.3 1.3 %collective-permute-start.8 = (f32[256,512]{1,0:T(8,128)S(1)}, f32[256,512]{1,0:T(8,128)S(1)}, u32[]{:S(2)}, u32[]{:S(2)}) collective-permute-start(f32[256,512]{1,0:T(8,128)S(1)} %relay.10.refs_4_), channel_id=1, source_target_pairs={{1,0},{6,5},{9,8},{14,13},{17,16},{22,21},{25,24},{30,29}} | collective-permute-start | bytes 1572872 | tf_op jit(solution)/shard_map/ppermute | solution.py:463
  41.6 27.9 %collective-permute-done.8.refs_0_.refs_2_ = f32[256,512]{1,0:T(8,128)S(1)} collective-permute-done((f32[256,512]{1,0:T(8,128)S(1)}, f32[256,512]{1,0:T(8,128)S(1)}, u32[]{:S(2)}, u32[]{:S(2)}) %collective-permute-start.8) | collective-permute-done | bytes 524320 | tf_op jit(solution)/shard_map/ppermute | solution.py:463
  69.5 0.7 collective-permute-start.9
  70.2 0.0 copy-start.2
  70.2 0.0 copy-start.3
  70.2 0.6 copy-done.2
  70.9 0.0 copy-done.3
  70.9 0.1 add_reduce_fusion.weights
  71.0 0.7 weights.1.refs_12_.tiles
  71.6 0.0 collective-permute-done.9.refs_3_.refs_1_
  71.6 1.3 %second_slab.1 = (f32[256,512]{1,0:T(8,128)S(1)}, f32[64,512]{1,0:T(8,128)S(1)}, f32[64,512]{1,0:T(8,128)S(1)}, f32[64,512]{1,0:T(8,128)S(1)}, f32[64,512]{1,0:T(8,128)S(1)}) custom-call(f32[256,512]{1,0:T(8,128)S(1)} %collective-permute-done.4.refs_0_, f32[256,512]{1,0:T(8,128)S(1)} %collective-permute-done.7.refs_0_.refs_1_, ...), custom_call_target="tpu_custom_call" | custom-call | flops 805306368 | bytes 1048576 | tf_op jit(solution)/shard_map/second_slab/pallas_call | solution.py:91
  72.9 3.0 %collective-permute-start.17 = (f32[64,512]{1,0:T(8,128)S(1)}, f32[64,512]{1,0:T(8,128)S(1)}, u32[]{:S(2)}, u32[]{:S(2)}) collective-permute-start(f32[64,512]{1,0:T(8,128)S(1)} %get-tuple-element.77), channel_id=1, source_target_pairs={{0,8},{4,12},{8,0},{12,4},{16,24},{20,28},{24,16},{28,20},{1,9},{5... | collective-permute-start | bytes 393224 | tf_op jit(solution)/shard_map/ppermute | solution.py:572
  75.9 1.5 %collective-permute-start.18 = (f32[64,512]{1,0:T(8,128)S(1)}, f32[64,512]{1,0:T(8,128)S(1)}, u32[]{:S(2)}, u32[]{:S(2)}) collective-permute-start(f32[64,512]{1,0:T(8,128)S(1)} %get-tuple-element.78), channel_id=1, source_target_pairs={{0,16},{4,20},{8,24},{12,28},{16,0},{20,4},{24,8},{28,12},{1,17},{... | collective-permute-start | bytes 393224 | tf_op jit(solution)/shard_map/ppermute | solution.py:572
  77.5 0.0 collective-permute-start.19
  77.5 1.0 first_slab.1
  78.5 2.0 %collective-permute-start.10 = (f32[64,512]{1,0:T(8,128)S(1)}, f32[64,512]{1,0:T(8,128)S(1)}, u32[]{:S(2)}, u32[]{:S(2)}) collective-permute-start(f32[64,512]{1,0:T(8,128)S(1)} %get-tuple-element.67), channel_id=1, source_target_pairs={{0,8},{4,12},{8,0},{12,4},{16,24},{20,28},{24,16},{28,20},{1,9},{5... | collective-permute-start | bytes 393224 | tf_op jit(solution)/shard_map/ppermute | solution.py:572
  80.5 1.5 %collective-permute-start.11 = (f32[64,512]{1,0:T(8,128)S(1)}, f32[64,512]{1,0:T(8,128)S(1)}, u32[]{:S(2)}, u32[]{:S(2)}) collective-permute-start(f32[64,512]{1,0:T(8,128)S(1)} %get-tuple-element.68), channel_id=1, source_target_pairs={{0,16},{4,20},{8,24},{12,28},{16,0},{20,4},{24,8},{28,12},{1,17},{... | collective-permute-start | bytes 393224 | tf_op jit(solution)/shard_map/ppermute | solution.py:572
  82.0 0.0 collective-permute-done.17.refs_1_
  82.0 0.0 collective-permute-start.12
  82.1 0.0 collective-permute-done.18.refs_2_
  82.1 2.2 %collective-permute-done.19.refs_3_ = f32[64,512]{1,0:T(8,128)S(1)} collective-permute-done((f32[64,512]{1,0:T(8,128)S(1)}, f32[64,512]{1,0:T(8,128)S(1)}, u32[]{:S(2)}, u32[]{:S(2)}) %collective-permute-start.19) | collective-permute-done | bytes 131104 | tf_op jit(solution)/shard_map/ppermute | solution.py:572
  84.2 0.2 mix.3
  84.5 4.0 %collective-permute-start.20 = (f32[4,64,512]{2,1,0:T(8,128)S(1)}, f32[4,64,512]{2,1,0:T(8,128)S(1)}, u32[]{:S(2)}, u32[]{:S(2)}) collective-permute-start(f32[4,64,512]{2,1,0:T(8,128)S(1)} %get-tuple-element.81), channel_id=1, source_target_pairs={{0,4},{4,0},{8,12},{12,8},{16,20},{20,16},{24,28},{28,24},{1,5},{5... | collective-permute-start | bytes 1572872 | tf_op jit(solution)/shard_map/ppermute | solution.py:588
  88.5 0.6 collective-permute-done.11.refs_2_
  89.1 0.8 collective-permute-done.12.refs_3_
  89.9 0.2 mix.2
  90.2 1.9 %collective-permute-start.13 = (f32[4,64,512]{2,1,0:T(8,128)S(1)}, f32[4,64,512]{2,1,0:T(8,128)S(1)}, u32[]{:S(2)}, u32[]{:S(2)}) collective-permute-start(f32[4,64,512]{2,1,0:T(8,128)S(1)} %get-tuple-element.71), channel_id=1, source_target_pairs={{0,4},{4,0},{8,12},{12,8},{16,20},{20,16},{24,28},{28,24},{1,5},{5... | collective-permute-start | bytes 1572872 | tf_op jit(solution)/shard_map/ppermute | solution.py:588
  92.1 0.0 collective-permute-done.20.other
  92.1 0.1 sum.3
  92.1 0.5 collective-permute-start.21
  92.7 0.8 collective-permute-start.22
  93.5 2.2 %collective-permute-start.23 = (f32[64,512]{1,0:T(8,128)S(1)}, f32[64,512]{1,0:T(8,128)S(1)}, u32[]{:S(2)}, u32[]{:S(2)}) collective-permute-start(f32[64,512]{1,0:T(8,128)S(1)} %get-tuple-element.85), channel_id=1, source_target_pairs={{0,24},{4,28},{8,16},{12,20},{16,8},{20,12},{24,0},{28,4},{1,25},{... | collective-permute-start | bytes 393224 | tf_op jit(solution)/shard_map/ppermute | solution.py:572
  95.7 0.0 collective-permute-done.13.other
  95.7 0.1 sum.2
  95.7 0.5 collective-permute-start.14
  96.3 0.8 collective-permute-start.15
  97.1 1.4 %collective-permute-done.21.refs_5_ = f32[64,512]{1,0:T(8,128)S(1)} collective-permute-done((f32[64,512]{1,0:T(8,128)S(1)}, f32[64,512]{1,0:T(8,128)S(1)}, u32[]{:S(2)}, u32[]{:S(2)}) %collective-permute-start.21) | collective-permute-done | bytes 131104 | tf_op jit(solution)/shard_map/ppermute | solution.py:572
  98.5 0.7 collective-permute-start.16
  99.3 1.0 retarded.1
  100.3 1.6 %collective-permute-done.23.refs_7_ = f32[64,512]{1,0:T(8,128)S(1)} collective-permute-done((f32[64,512]{1,0:T(8,128)S(1)}, f32[64,512]{1,0:T(8,128)S(1)}, u32[]{:S(2)}, u32[]{:S(2)}) %collective-permute-start.23) | collective-permute-done | bytes 131104 | tf_op jit(solution)/shard_map/ppermute | solution.py:572
  101.9 2.3 %collective-permute-done.14.refs_1_ = f32[64,512]{1,0:T(8,128)S(1)} collective-permute-done((f32[64,512]{1,0:T(8,128)S(1)}, f32[64,512]{1,0:T(8,128)S(1)}, u32[]{:S(2)}, u32[]{:S(2)}) %collective-permute-start.14) | collective-permute-done | bytes 131104 | tf_op jit(solution)/shard_map/ppermute | solution.py:572
  104.2 2.4 %collective-permute-done.16.refs_3_ = f32[64,512]{1,0:T(8,128)S(1)} collective-permute-done((f32[64,512]{1,0:T(8,128)S(1)}, f32[64,512]{1,0:T(8,128)S(1)}, u32[]{:S(2)}, u32[]{:S(2)}) %collective-permute-start.16) | collective-permute-done | bytes 131104 | tf_op jit(solution)/shard_map/ppermute | solution.py:572
  106.6 1.0 scattering.1
  (15 shorter events, 0.1 us)
Async XLA Ops:
  0.6 0.7 copy-start
  1.3 6.3 %copy-start.1 = (s32[2,16,16]{2,1,0:T(8,128)S(1)}, s32[2,16,16]{2,1,0:T(8,128)}, u32[]{:S(2)}) copy-start(s32[2,16,16]{2,1,0:T(8,128)} %pattern.3) | copy-start | bytes 6148
  5.7 8.0 %collective-permute-start = (f32[256,512]{1,0:T(8,128)S(1)}, f32[256,512]{1,0:T(8,128)S(1)}, u32[]{:S(2)}, u32[]{:S(2)}) collective-permute-start(f32[256,512]{1,0:T(8,128)S(1)} %get-tuple-element.44), channel_id=1, source_target_pairs={{0,1},{8,9},{16,17},{24,25}} | collective-permute-start | bytes 1572872 | tf_op jit(solution)/shard_map/ppermute | solution.py:463
  7.0 5.4 %collective-permute-start.1 = (f32[128,512]{1,0:T(8,128)S(1)}, f32[128,512]{1,0:T(8,128)S(1)}, u32[]{:S(2)}, u32[]{:S(2)}) collective-permute-start(f32[128,512]{1,0:T(8,128)S(1)} %get-tuple-element.48), channel_id=1, source_target_pairs={{5,4},{6,5},{7,6},{13,12},{14,13},{15,14},{21,20},{22,21},{23,22},... | collective-permute-start | bytes 786440 | tf_op jit(solution)/shard_map/ppermute | solution.py:472
  13.7 0.7 collective-permute-start.2
  14.4 3.3 %collective-permute-start.3 = (f32[256,512]{1,0:T(8,128)S(1)}, f32[256,512]{1,0:T(8,128)S(1)}, u32[]{:S(2)}, u32[]{:S(2)}) collective-permute-start(f32[256,512]{1,0:T(8,128)S(1)} %relay.7.refs_4_.refs_10_), channel_id=1, source_target_pairs={{2,3},{5,6},{10,11},{13,14},{18,19},{21,22},{26,27},{29,30}} | collective-permute-start | bytes 1572872 | tf_op jit(solution)/shard_map/ppermute | solution.py:463
  15.1 16.8 %collective-permute-start.5 = (f32[128,512]{1,0:T(8,128)S(1)}, f32[128,512]{1,0:T(8,128)S(1)}, u32[]{:S(2)}, u32[]{:S(2)}) collective-permute-start(f32[128,512]{1,0:T(8,128)S(1)} %get-tuple-element.54), channel_id=1, source_target_pairs={{1,0},{2,1},{3,2},{9,8},{10,9},{11,10},{17,16},{18,17},{19,18},{25... | collective-permute-start | bytes 786440 | tf_op jit(solution)/shard_map/ppermute | solution.py:472
  16.4 19.7 %collective-permute-start.6 = (f32[128,512]{1,0:T(8,128)S(1)}, f32[128,512]{1,0:T(8,128)S(1)}, u32[]{:S(2)}, u32[]{:S(2)}) collective-permute-start(f32[128,512]{1,0:T(8,128)S(1)} %get-tuple-element.55), channel_id=1, source_target_pairs={{1,0},{2,1},{3,2},{5,4},{6,5},{7,6},{9,8},{10,9},{11,10},{13,12},{... | collective-permute-start | bytes 786440 | tf_op jit(solution)/shard_map/ppermute | solution.py:472
  18.0 21.5 %collective-permute-start.4 = (f32[256,512]{1,0:T(8,128)S(1)}, f32[256,512]{1,0:T(8,128)S(1)}, u32[]{:S(2)}, u32[]{:S(2)}) collective-permute-start(f32[256,512]{1,0:T(8,128)S(1)} %get-tuple-element.53.refs_5_.refs_11_.refs_2_), channel_id=1, source_target_pairs={{3,2},{6,7},{11,10},{14,15},{19,18},{22,23},{27,26},{30,31}} | collective-permute-start | bytes 1572872 | tf_op jit(solution)/shard_map/ppermute | solution.py:463
  39.5 0.7 collective-permute-start.7
  40.3 29.9 %copy-start.4 = (s32[4]{0:T(128)S(1)}, s32[4]{0:T(128)}, u32[]{:S(2)}) copy-start(s32[4]{0:T(128)} %param.11) | copy-start | bytes 52
  40.3 29.2 %collective-permute-start.8 = (f32[256,512]{1,0:T(8,128)S(1)}, f32[256,512]{1,0:T(8,128)S(1)}, u32[]{:S(2)}, u32[]{:S(2)}) collective-permute-start(f32[256,512]{1,0:T(8,128)S(1)} %relay.10.refs_4_), channel_id=1, source_target_pairs={{1,0},{6,5},{9,8},{14,13},{17,16},{22,21},{25,24},{30,29}} | collective-permute-start | bytes 1572872 | tf_op jit(solution)/shard_map/ppermute | solution.py:463
  69.5 2.1 %collective-permute-start.9 = (f32[256,512]{1,0:T(8,128)S(1)}, f32[256,512]{1,0:T(8,128)S(1)}, u32[]{:S(2)}, u32[]{:S(2)}) collective-permute-start(f32[256,512]{1,0:T(8,128)S(1)} %relay.11.refs_5_), channel_id=1, source_target_pairs={{5,4},{13,12},{21,20},{29,28}} | collective-permute-start | bytes 1572872 | tf_op jit(solution)/shard_map/ppermute | solution.py:463
  70.2 0.7 copy-start.2
  70.2 0.7 copy-start.3
  72.9 9.1 %collective-permute-start.17 = (f32[64,512]{1,0:T(8,128)S(1)}, f32[64,512]{1,0:T(8,128)S(1)}, u32[]{:S(2)}, u32[]{:S(2)}) collective-permute-start(f32[64,512]{1,0:T(8,128)S(1)} %get-tuple-element.77), channel_id=1, source_target_pairs={{0,8},{4,12},{8,0},{12,4},{16,24},{20,28},{24,16},{28,20},{1,9},{5... | collective-permute-start | bytes 393224 | tf_op jit(solution)/shard_map/ppermute | solution.py:572
  75.9 6.1 %collective-permute-start.18 = (f32[64,512]{1,0:T(8,128)S(1)}, f32[64,512]{1,0:T(8,128)S(1)}, u32[]{:S(2)}, u32[]{:S(2)}) collective-permute-start(f32[64,512]{1,0:T(8,128)S(1)} %get-tuple-element.78), channel_id=1, source_target_pairs={{0,16},{4,20},{8,24},{12,28},{16,0},{20,4},{24,8},{28,12},{1,17},{... | collective-permute-start | bytes 393224 | tf_op jit(solution)/shard_map/ppermute | solution.py:572
  77.5 6.8 %collective-permute-start.19 = (f32[64,512]{1,0:T(8,128)S(1)}, f32[64,512]{1,0:T(8,128)S(1)}, u32[]{:S(2)}, u32[]{:S(2)}) collective-permute-start(f32[64,512]{1,0:T(8,128)S(1)} %get-tuple-element.79), channel_id=1, source_target_pairs={{0,24},{4,28},{8,16},{12,20},{16,8},{20,12},{24,0},{28,4},{1,25},{... | collective-permute-start | bytes 393224 | tf_op jit(solution)/shard_map/ppermute | solution.py:572
  78.5 10.0 %collective-permute-start.10 = (f32[64,512]{1,0:T(8,128)S(1)}, f32[64,512]{1,0:T(8,128)S(1)}, u32[]{:S(2)}, u32[]{:S(2)}) collective-permute-start(f32[64,512]{1,0:T(8,128)S(1)} %get-tuple-element.67), channel_id=1, source_target_pairs={{0,8},{4,12},{8,0},{12,4},{16,24},{20,28},{24,16},{28,20},{1,9},{5... | collective-permute-start | bytes 393224 | tf_op jit(solution)/shard_map/ppermute | solution.py:572
  80.5 8.5 %collective-permute-start.11 = (f32[64,512]{1,0:T(8,128)S(1)}, f32[64,512]{1,0:T(8,128)S(1)}, u32[]{:S(2)}, u32[]{:S(2)}) collective-permute-start(f32[64,512]{1,0:T(8,128)S(1)} %get-tuple-element.68), channel_id=1, source_target_pairs={{0,16},{4,20},{8,24},{12,28},{16,0},{20,4},{24,8},{28,12},{1,17},{... | collective-permute-start | bytes 393224 | tf_op jit(solution)/shard_map/ppermute | solution.py:572
  82.0 7.9 %collective-permute-start.12 = (f32[64,512]{1,0:T(8,128)S(1)}, f32[64,512]{1,0:T(8,128)S(1)}, u32[]{:S(2)}, u32[]{:S(2)}) collective-permute-start(f32[64,512]{1,0:T(8,128)S(1)} %get-tuple-element.69), channel_id=1, source_target_pairs={{0,24},{4,28},{8,16},{12,20},{16,8},{20,12},{24,0},{28,4},{1,25},{... | collective-permute-start | bytes 393224 | tf_op jit(solution)/shard_map/ppermute | solution.py:572
  84.5 7.6 %collective-permute-start.20 = (f32[4,64,512]{2,1,0:T(8,128)S(1)}, f32[4,64,512]{2,1,0:T(8,128)S(1)}, u32[]{:S(2)}, u32[]{:S(2)}) collective-permute-start(f32[4,64,512]{2,1,0:T(8,128)S(1)} %get-tuple-element.81), channel_id=1, source_target_pairs={{0,4},{4,0},{8,12},{12,8},{16,20},{20,16},{24,28},{28,24},{1,5},{5... | collective-permute-start | bytes 1572872 | tf_op jit(solution)/shard_map/ppermute | solution.py:588
  90.2 5.5 %collective-permute-start.13 = (f32[4,64,512]{2,1,0:T(8,128)S(1)}, f32[4,64,512]{2,1,0:T(8,128)S(1)}, u32[]{:S(2)}, u32[]{:S(2)}) collective-permute-start(f32[4,64,512]{2,1,0:T(8,128)S(1)} %get-tuple-element.71), channel_id=1, source_target_pairs={{0,4},{4,0},{8,12},{12,8},{16,20},{20,16},{24,28},{28,24},{1,5},{5... | collective-permute-start | bytes 1572872 | tf_op jit(solution)/shard_map/ppermute | solution.py:588
  92.1 6.4 %collective-permute-start.21 = (f32[64,512]{1,0:T(8,128)S(1)}, f32[64,512]{1,0:T(8,128)S(1)}, u32[]{:S(2)}, u32[]{:S(2)}) collective-permute-start(f32[64,512]{1,0:T(8,128)S(1)} %get-tuple-element.83), channel_id=1, source_target_pairs={{0,8},{4,12},{8,0},{12,4},{16,24},{20,28},{24,16},{28,20},{1,9},{5... | collective-permute-start | bytes 393224 | tf_op jit(solution)/shard_map/ppermute | solution.py:572
  92.7 7.7 %collective-permute-start.22 = (f32[64,512]{1,0:T(8,128)S(1)}, f32[64,512]{1,0:T(8,128)S(1)}, u32[]{:S(2)}, u32[]{:S(2)}) collective-permute-start(f32[64,512]{1,0:T(8,128)S(1)} %get-tuple-element.84), channel_id=1, source_target_pairs={{0,16},{4,20},{8,24},{12,28},{16,0},{20,4},{24,8},{28,12},{1,17},{... | collective-permute-start | bytes 393224 | tf_op jit(solution)/shard_map/ppermute | solution.py:572
  93.5 8.4 %collective-permute-start.23 = (f32[64,512]{1,0:T(8,128)S(1)}, f32[64,512]{1,0:T(8,128)S(1)}, u32[]{:S(2)}, u32[]{:S(2)}) collective-permute-start(f32[64,512]{1,0:T(8,128)S(1)} %get-tuple-element.85), channel_id=1, source_target_pairs={{0,24},{4,28},{8,16},{12,20},{16,8},{20,12},{24,0},{28,4},{1,25},{... | collective-permute-start | bytes 393224 | tf_op jit(solution)/shard_map/ppermute | solution.py:572
  95.7 8.4 %collective-permute-start.14 = (f32[64,512]{1,0:T(8,128)S(1)}, f32[64,512]{1,0:T(8,128)S(1)}, u32[]{:S(2)}, u32[]{:S(2)}) collective-permute-start(f32[64,512]{1,0:T(8,128)S(1)} %get-tuple-element.73), channel_id=1, source_target_pairs={{0,8},{4,12},{8,0},{12,4},{16,24},{20,28},{24,16},{28,20},{1,9},{5... | collective-permute-start | bytes 393224 | tf_op jit(solution)/shard_map/ppermute | solution.py:572
  96.3 7.9 %collective-permute-start.15 = (f32[64,512]{1,0:T(8,128)S(1)}, f32[64,512]{1,0:T(8,128)S(1)}, u32[]{:S(2)}, u32[]{:S(2)}) collective-permute-start(f32[64,512]{1,0:T(8,128)S(1)} %get-tuple-element.74), channel_id=1, source_target_pairs={{0,16},{4,20},{8,24},{12,28},{16,0},{20,4},{24,8},{28,12},{1,17},{... | collective-permute-start | bytes 393224 | tf_op jit(solution)/shard_map/ppermute | solution.py:572
  98.5 8.0 %collective-permute-start.16 = (f32[64,512]{1,0:T(8,128)S(1)}, f32[64,512]{1,0:T(8,128)S(1)}, u32[]{:S(2)}, u32[]{:S(2)}) collective-permute-start(f32[64,512]{1,0:T(8,128)S(1)} %get-tuple-element.75), channel_id=1, source_target_pairs={{0,24},{4,28},{8,16},{12,20},{16,8},{20,12},{24,0},{28,4},{1,25},{... | collective-permute-start | bytes 393224 | tf_op jit(solution)/shard_map/ppermute | solution.py:572

commit v11 on v10

--- a/solution.py
+++ b/solution.py
@@ -212,8 +212,8 @@
     refs = refs[2 * count - 2 :]
     start_whole, source, forward, backward, coupler = refs[:5]
     gate, upper, lower = refs[5:8]
-    lead, tail, constant, last_lead, last_tail = refs[8:13]
-    first_v, last_v, m_a, m_b, m_c, m_d = refs[13:]
+    lead, tail, constant, last_lead, last_tail = refs[9:14]
+    first_v, last_v, m_a, m_b, m_c, m_d = refs[14:]
     place = lax.axis_index("slab")
 
     @pl.when(place == 0)
@@ -307,7 +307,6 @@
     ends = [refs.pop(0) for _ in range(2)]
     last_lead, last_tail, whole_start = [refs.pop(0) for _ in range(3)]
     wholes = [refs.pop(0) for _ in range(count - 1)]
-    refs.pop(0)
     block, *parcels, m_x = refs
     place = lax.axis_index("slab")
     core = trailing()
@@ -375,6 +374,10 @@
 def share(mask, rows):
     chip = lax.shift_right_logical(lax.axis_index("energy"), 1)
     return pl.ds(pl.multiple_of(lax.bitwise_xor(chip, mask) * rows, rows), rows)
+
+
+def far_first(chips):
+    return sorted(range(chips), key=lambda mask: -bin(mask).count("1"))
 
 
 def weight_kernel(chips, weights, tiles):
@@ -389,12 +392,12 @@
 
 
 def mix_kernel(chips, tiles, *refs):
-    parcels, outs = refs[:chips], refs[chips:]
+    parcels, outs = dict(zip(far_first(chips), refs[:chips])), refs[chips:]
     rows, columns = parcels[0].shape
     step, width = tiles.shape[3:]
     for row in range(0, rows, step):
         where = slice(row, row + step)
-        values = [parcel[where] for parcel in parcels]
+        values = [parcels[mask][where] for mask in range(chips)]
         for side, out in enumerate(outs):
             for mask in range(chips):
                 total = None
@@ -414,7 +417,8 @@
     scattering = refs[2 * chips]
     size = scattering.shape[-1]
     for slab in range(2):
-        for mask, parcel in enumerate(refs[slab * chips : (slab + 1) * chips]):
+        parcels = refs[slab * chips : (slab + 1) * chips]
+        for mask, parcel in zip(far_first(chips), parcels):
             where = share(mask, parcel.shape[0])
             for part in range(2):
                 scattering[slab, part, where, :] = parcel[:, part * size : (part + 1) * size]
@@ -494,6 +498,17 @@
         limit=48.6,
     )
     left_map = [left_lead, left_tail, whole]
+    chips = energies // 2
+    everyone = jnp.arange(energies, dtype=jnp.int32)
+    weights = mode_weights(everyone, everyone, offsets, emission, absorption)
+    (tiles,) = call(
+        functools.partial(weight_kernel, chips),
+        [shape(8, 128, F32, 2, chips, chips)],
+        [],
+        [weights],
+        [SMEM],
+        name="weights",
+    )
     right_map = None
     for step in range(2 * count - 2):
         lefts, rights = step <= count - 1, step >= count - 1
@@ -523,7 +538,7 @@
             upper = lower_place(upper, [0])
         if step == count - 2:
             args = arrived[: count - 1] + outs[: count - 1]
-            args += [whole, source, forward, backward, coupler, gate, upper, lower]
+            args += [whole, source, forward, backward, coupler, gate, upper, lower, tiles]
             right_map = call(
                 functools.partial(prepare_kernel, count),
                 [factor, factor, row, factor, factor],
@@ -532,20 +547,9 @@
                 flops=10 * product,
                 name="right_maps",
             )
-    chips = energies // 2
     parcel = shape(size // chips, 2 * size)
     blocks, parcels = [None, None], [None, None]
-    everyone = jnp.arange(energies, dtype=jnp.int32)
-    weights = mode_weights(everyone, everyone, offsets, emission, absorption)
-    (tiles,) = call(
-        functools.partial(weight_kernel, chips),
-        [shape(8, 128, F32, 2, chips, chips)],
-        [],
-        [weights],
-        [SMEM],
-        name="weights",
-    )
-    args = arrived[count - 1 :] + ends + right_map[3:] + [whole] + outs[: count - 1] + [tiles]
+    args = arrived[count - 1 :] + ends + right_map[3:] + [whole] + outs[: count - 1]
     blocks[1], *parcels[1] = call(
         functools.partial(last_kernel, count),
         [row] + [parcel] * chips,
@@ -567,12 +571,14 @@
         unpack_kernel, [shape(size, size, F32, 2, 2)], [], blocks, name="retarded"
     )
 
+    masks = far_first(chips)
+
     def exchange(values):
-        return values[:1] + [
-            lax.ppermute(value, "energy", [(i, i ^ (2 * mask)) for i in range(energies)])
-            for mask, value in enumerate(values)
-            if mask
-        ]
+        sent = list(values)
+        for mask in masks[:-1]:
+            pairs = [(i, i ^ (2 * mask)) for i in range(energies)]
+            sent[mask] = lax.ppermute(values[mask], "energy", pairs)
+        return [sent[mask] for mask in masks]
 
     partial = shape(size // chips, 2 * size, F32, chips)
     sums = [None, None]

time: 108 us -> 108 us (level)
  waiting for transfers between devices: 57.9 us -> 52 us
  starting transfers between devices: 29 us -> 34.4 us
    ppermute x12, waiting for transfers between devices: 11.3 us -> 6.65 us  [exchange(): sent[mask] = lax.ppermute(values[mask], 'energy', pairs)]
    ppermute x2, starting transfers between devices: 5.92 us -> 9.21 us  [shards(): other = lax.ppermute(other, 'energy', [(i, i ^ 1) for i in range(energies)])]
    ppermute x12, starting transfers between devices: 13.8 us -> 15.8 us  [exchange(): sent[mask] = lax.ppermute(values[mask], 'energy', pairs)]
    ppermute x3, waiting for transfers between devices: 17.5 us -> 16 us  [lower_place(): return lax.ppermute(value, ('energy', 'slab'), pairs)]
  transfers between devices with their start and end apart: 24 -> 24, of which waited for: 11 -> 12; matrix products, arithmetic and copies ran while one was open for 0% -> 0% of each run, Pallas kernels for 11% -> 11%
where the time goes in v11:
time: 108 us; the launch traced here: 107 us
  waiting for transfers between devices  52 us (48%)
  starting transfers between devices  34.4 us (32%)
  Pallas kernels  18.3 us (17%)
  local copies, waits for them, and re-layouts  1.37 us (1%)
    ppermute x7, waiting for transfers between devices, relay(): lax.ppermute(value, ('energy', 'slab'), relay_pairs(step, energies, count))  29.2 us
    pallas_call x18, Pallas kernels, call(): pl.pallas_call(kernel, out_shape=outs, in_specs=specs or [VMEM] * len(arg...  18.3 us
    ppermute x3, waiting for transfers between devices, lower_place(): return lax.ppermute(value, ('energy', 'slab'), pairs)  16 us
    ppermute x12, starting transfers between devices, exchange(): sent[mask] = lax.ppermute(values[mask], 'energy', pairs)  15.8 us
    ppermute x2, starting transfers between devices, shards(): other = lax.ppermute(other, 'energy', [(i, i ^ 1) for i in range(energies)])  9.21 us
    ppermute x12, waiting for transfers between devices, exchange(): sent[mask] = lax.ppermute(values[mask], 'energy', pairs)  6.65 us
    ppermute x7, starting transfers between devices, relay(): lax.ppermute(value, ('energy', 'slab'), relay_pairs(step, energies, count))  6.07 us
    ppermute x3, starting transfers between devices, lower_place(): return lax.ppermute(value, ('energy', 'slab'), pairs)  3.26 us
  transfers between devices with their start and end apart: 24, of which 12 were waited for; matrix products, arithmetic and copies ran while one was open for 0% of the time, Pallas kernels for 11%

profile of v11, /device:TPU:0, one launch (start us, length us, event | category | flops | bytes accessed | tf_op | source)
XLA Modules:
  0.0 107.2 jit_solution(4975584743311708396)
XLA Ops:
  0.6 0.7 copy-done
  1.4 4.3 %source.1 = (f32[256,512]{1,0:T(8,128)S(1)}, f32[128,512]{1,0:T(8,128)S(1)}) custom-call(f32[2,2,256,256]{3,2,1,0:T(8,128)} %bitcast.6, f32[2,2,256,256]{3,2,1,0:T(8,128)} %bitcast.8, f32[2,2,256,256]{3,2,1,0:T(8,128)} %coupling.3, s32[2,16,16]{2,1,0:T(8,128)S(1)} %copy-done), custom_call_target="tpu_custom_call" | custom-call | flops 2415919104 | bytes 1048576 | tf_op jit(solution)/shard_map/source/pallas_call | solution.py:91
  5.7 1.3 %collective-permute-start = (f32[256,512]{1,0:T(8,128)S(1)}, f32[256,512]{1,0:T(8,128)S(1)}, u32[]{:S(2)}, u32[]{:S(2)}) collective-permute-start(f32[256,512]{1,0:T(8,128)S(1)} %get-tuple-element.44), channel_id=1, source_target_pairs={{0,1},{8,9},{16,17},{24,25}} | collective-permute-start | bytes 1572872 | tf_op jit(solution)/shard_map/ppermute | solution.py:467
  7.0 0.7 collective-permute-start.1
  7.7 4.7 %left_maps.1 = (f32[256,512]{1,0:T(8,128)S(1)}, f32[256,512]{1,0:T(8,128)S(1)}, f32[256,512]{1,0:T(8,128)S(1)}, f32[128,512]{1,0:T(8,128)S(1)}, f32[128,512]{1,0...) custom-call(f32[2,2,256,256]{3,2,1,0:T(8,128)} %bitcast.7, ...), custom_call_target="tpu_custom_call" | custom-call | flops 4831838208 | bytes 1048576 | tf_op jit(solution)/shard_map/left_maps/pallas_call | solution.py:91
  12.4 0.0 collective-permute-done.1.refs_4_.refs_11_
  12.4 1.2 %collective-permute-done.refs_0_ = f32[256,512]{1,0:T(8,128)S(1)} collective-permute-done((f32[256,512]{1,0:T(8,128)S(1)}, f32[256,512]{1,0:T(8,128)S(1)}, u32[]{:S(2)}, u32[]{:S(2)}) %collective-permute-start) | collective-permute-done | bytes 524320 | tf_op jit(solution)/shard_map/ppermute | solution.py:467
  13.7 0.7 collective-permute-start.2
  14.4 0.0 collective-permute-done.2.refs_0_.refs_1_
  14.4 0.7 collective-permute-start.3
  15.1 1.3 %collective-permute-start.5 = (f32[128,512]{1,0:T(8,128)S(1)}, f32[128,512]{1,0:T(8,128)S(1)}, u32[]{:S(2)}, u32[]{:S(2)}) collective-permute-start(f32[128,512]{1,0:T(8,128)S(1)} %get-tuple-element.54), channel_id=1, source_target_pairs={{1,0},{2,1},{3,2},{9,8},{10,9},{11,10},{17,16},{18,17},{19,18},{25... | collective-permute-start | bytes 786440 | tf_op jit(solution)/shard_map/ppermute | solution.py:476
  16.4 1.3 %collective-permute-start.6 = (f32[128,512]{1,0:T(8,128)S(1)}, f32[128,512]{1,0:T(8,128)S(1)}, u32[]{:S(2)}, u32[]{:S(2)}) collective-permute-start(f32[128,512]{1,0:T(8,128)S(1)} %get-tuple-element.55), channel_id=1, source_target_pairs={{1,0},{2,1},{3,2},{5,4},{6,5},{7,6},{9,8},{10,9},{11,10},{13,12},{... | collective-permute-start | bytes 786440 | tf_op jit(solution)/shard_map/ppermute | solution.py:476
  17.7 0.0 collective-permute-done.3.refs_0_.refs_2_
  17.8 0.2 relay.8
  18.0 0.0 copy-start.4
  18.0 0.7 collective-permute-start.4
  18.7 0.0 copy-start.2
  18.7 0.0 copy-start.3
  18.7 0.6 copy-done.2
  19.4 0.0 copy-done.3
  19.4 0.1 add_reduce_fusion.weights
  19.5 0.7 weights.1.refs_14_.tiles
  20.1 11.8 %collective-permute-done.5.refs_12_ = f32[128,512]{1,0:T(8,128)S(1)} collective-permute-done((f32[128,512]{1,0:T(8,128)S(1)}, f32[128,512]{1,0:T(8,128)S(1)}, u32[]{:S(2)}, u32[]{:S(2)}) %collective-permute-start.5) | collective-permute-done | bytes 262176 | tf_op jit(solution)/shard_map/ppermute | solution.py:476
  32.0 4.2 %collective-permute-done.6.refs_13_ = f32[128,512]{1,0:T(8,128)S(1)} collective-permute-done((f32[128,512]{1,0:T(8,128)S(1)}, f32[128,512]{1,0:T(8,128)S(1)}, u32[]{:S(2)}, u32[]{:S(2)}) %collective-permute-start.6) | collective-permute-done | bytes 262176 | tf_op jit(solution)/shard_map/ppermute | solution.py:476
  36.1 3.3 %right_maps.1 = (bf16[2,3,256,256]{3,2,1,0:T(8,128)(2,1)S(1)}, bf16[2,3,256,256]{3,2,1,0:T(8,128)(2,1)S(1)}, f32[256,512]{1,0:T(8,128)S(1)}, bf16[2,3,256,256]{3...) custom-call(f32[256,512]{1,0:T(8,128)S(1)} %collective-permute-done.refs_0_, ...), custom_call_target="tpu_custom_call" | custom-call | flops 4026531840 | bytes 1048576 | tf_op jit(solution)/shard_map/right_maps/pallas_call | solution.py:91
  39.5 0.0 collective-permute-done.4.refs_0_
  39.5 0.7 collective-permute-start.7
  40.2 0.0 collective-permute-done.7.refs_0_.refs_1_
  40.3 1.3 %collective-permute-start.8 = (f32[256,512]{1,0:T(8,128)S(1)}, f32[256,512]{1,0:T(8,128)S(1)}, u32[]{:S(2)}, u32[]{:S(2)}) collective-permute-start(f32[256,512]{1,0:T(8,128)S(1)} %relay.10.refs_4_), channel_id=1, source_target_pairs={{1,0},{6,5},{9,8},{14,13},{17,16},{22,21},{25,24},{30,29}} | collective-permute-start | bytes 1572872 | tf_op jit(solution)/shard_map/ppermute | solution.py:467
  41.6 28.0 %collective-permute-done.8.refs_0_.refs_2_ = f32[256,512]{1,0:T(8,128)S(1)} collective-permute-done((f32[256,512]{1,0:T(8,128)S(1)}, f32[256,512]{1,0:T(8,128)S(1)}, u32[]{:S(2)}, u32[]{:S(2)}) %collective-permute-start.8) | collective-permute-done | bytes 524320 | tf_op jit(solution)/shard_map/ppermute | solution.py:467
  69.5 0.7 collective-permute-start.9
  70.2 0.0 collective-permute-done.9.refs_3_.refs_1_
  70.2 1.3 %second_slab.1 = (f32[256,512]{1,0:T(8,128)S(1)}, f32[64,512]{1,0:T(8,128)S(1)}, f32[64,512]{1,0:T(8,128)S(1)}, f32[64,512]{1,0:T(8,128)S(1)}, f32[64,512]{1,0:T(8,128)S(1)}) custom-call(f32[256,512]{1,0:T(8,128)S(1)} %collective-permute-done.4.refs_0_, f32[256,512]{1,0:T(8,128)S(1)} %collective-permute-done.7.refs_0_.refs_1_, ...), custom_call_target="tpu_custom_call" | custom-call | flops 805306368 | bytes 1048576 | tf_op jit(solution)/shard_map/second_slab/pallas_call | solution.py:91
  71.5 4.0 %collective-permute-start.17 = (f32[64,512]{1,0:T(8,128)S(1)}, f32[64,512]{1,0:T(8,128)S(1)}, u32[]{:S(2)}, u32[]{:S(2)}) collective-permute-start(f32[64,512]{1,0:T(8,128)S(1)} %get-tuple-element.76), channel_id=1, source_target_pairs={{0,24},{4,28},{8,16},{12,20},{16,8},{20,12},{24,0},{28,4},{1,25},{... | collective-permute-start | bytes 393224 | tf_op jit(solution)/shard_map/ppermute | solution.py:580
  75.5 0.5 collective-permute-start.18
  76.0 0.1 collective-permute-start.19
  76.1 1.0 first_slab.1
  77.2 2.9 %collective-permute-start.10 = (f32[64,512]{1,0:T(8,128)S(1)}, f32[64,512]{1,0:T(8,128)S(1)}, u32[]{:S(2)}, u32[]{:S(2)}) collective-permute-start(f32[64,512]{1,0:T(8,128)S(1)} %get-tuple-element.66), channel_id=1, source_target_pairs={{0,24},{4,28},{8,16},{12,20},{16,8},{20,12},{24,0},{28,4},{1,25},{... | collective-permute-start | bytes 393224 | tf_op jit(solution)/shard_map/ppermute | solution.py:580
  80.1 0.5 collective-permute-start.11
  80.6 0.0 collective-permute-done.17.refs_0_
  80.6 0.1 collective-permute-start.12
  80.7 0.0 collective-permute-done.18.refs_1_
  80.7 0.3 collective-permute-done.19.refs_2_
  81.0 0.2 mix.3
  81.2 8.1 %collective-permute-start.20 = (f32[4,64,512]{2,1,0:T(8,128)S(1)}, f32[4,64,512]{2,1,0:T(8,128)S(1)}, u32[]{:S(2)}, u32[]{:S(2)}) collective-permute-start(f32[4,64,512]{2,1,0:T(8,128)S(1)} %get-tuple-element.81), channel_id=1, source_target_pairs={{0,4},{4,0},{8,12},{12,8},{16,20},{20,16},{24,28},{28,24},{1,5},{5... | collective-permute-start | bytes 1572872 | tf_op jit(solution)/shard_map/ppermute | solution.py:594
  89.4 0.2 mix.2
  89.6 1.1 %collective-permute-start.13 = (f32[4,64,512]{2,1,0:T(8,128)S(1)}, f32[4,64,512]{2,1,0:T(8,128)S(1)}, u32[]{:S(2)}, u32[]{:S(2)}) collective-permute-start(f32[4,64,512]{2,1,0:T(8,128)S(1)} %get-tuple-element.71), channel_id=1, source_target_pairs={{0,4},{4,0},{8,12},{12,8},{16,20},{20,16},{24,28},{28,24},{1,5},{5... | collective-permute-start | bytes 1572872 | tf_op jit(solution)/shard_map/ppermute | solution.py:594
  90.7 0.2 collective-permute-done.20.other
  90.9 0.1 sum.3
  90.9 2.3 %collective-permute-start.21 = (f32[64,512]{1,0:T(8,128)S(1)}, f32[64,512]{1,0:T(8,128)S(1)}, u32[]{:S(2)}, u32[]{:S(2)}) collective-permute-start(f32[64,512]{1,0:T(8,128)S(1)} %get-tuple-element.82), channel_id=1, source_target_pairs={{0,24},{4,28},{8,16},{12,20},{16,8},{20,12},{24,0},{28,4},{1,25},{... | collective-permute-start | bytes 393224 | tf_op jit(solution)/shard_map/ppermute | solution.py:580
  93.2 0.5 collective-permute-start.22
  93.8 0.8 collective-permute-start.23
  94.5 0.1 sum.2
  94.6 2.3 %collective-permute-start.14 = (f32[64,512]{1,0:T(8,128)S(1)}, f32[64,512]{1,0:T(8,128)S(1)}, u32[]{:S(2)}, u32[]{:S(2)}) collective-permute-start(f32[64,512]{1,0:T(8,128)S(1)} %get-tuple-element.72), channel_id=1, source_target_pairs={{0,24},{4,28},{8,16},{12,20},{16,8},{20,12},{24,0},{28,4},{1,25},{... | collective-permute-start | bytes 393224 | tf_op jit(solution)/shard_map/ppermute | solution.py:580
  96.8 0.5 collective-permute-start.15
  97.4 0.9 collective-permute-done.21.refs_4_
  98.2 1.3 %collective-permute-start.16 = (f32[64,512]{1,0:T(8,128)S(1)}, f32[64,512]{1,0:T(8,128)S(1)}, u32[]{:S(2)}, u32[]{:S(2)}) collective-permute-start(f32[64,512]{1,0:T(8,128)S(1)} %get-tuple-element.74), channel_id=1, source_target_pairs={{0,16},{4,20},{8,24},{12,28},{16,0},{20,4},{24,8},{28,12},{1,17},{... | collective-permute-start | bytes 393224 | tf_op jit(solution)/shard_map/ppermute | solution.py:580
  99.5 1.0 retarded.1
  100.6 0.3 collective-permute-done.22.refs_5_
  100.9 1.9 %collective-permute-done.23.refs_6_ = f32[64,512]{1,0:T(8,128)S(1)} collective-permute-done((f32[64,512]{1,0:T(8,128)S(1)}, f32[64,512]{1,0:T(8,128)S(1)}, u32[]{:S(2)}, u32[]{:S(2)}) %collective-permute-start.23) | collective-permute-done | bytes 131104 | tf_op jit(solution)/shard_map/ppermute | solution.py:580
  102.8 1.0 collective-permute-done.14.refs_0_
  103.9 1.7 %collective-permute-done.15.refs_1_ = f32[64,512]{1,0:T(8,128)S(1)} collective-permute-done((f32[64,512]{1,0:T(8,128)S(1)}, f32[64,512]{1,0:T(8,128)S(1)}, u32[]{:S(2)}, u32[]{:S(2)}) %collective-permute-start.15) | collective-permute-done | bytes 131104 | tf_op jit(solution)/shard_map/ppermute | solution.py:580
  105.6 0.5 collective-permute-done.16.refs_2_
  106.1 1.0 scattering.1
  (15 shorter events, 0.1 us)
Async XLA Ops:
  0.6 0.7 copy-start
  1.3 6.3 %copy-start.1 = (s32[2,16,16]{2,1,0:T(8,128)S(1)}, s32[2,16,16]{2,1,0:T(8,128)}, u32[]{:S(2)}) copy-start(s32[2,16,16]{2,1,0:T(8,128)} %pattern.3) | copy-start | bytes 6148
  5.7 8.0 %collective-permute-start = (f32[256,512]{1,0:T(8,128)S(1)}, f32[256,512]{1,0:T(8,128)S(1)}, u32[]{:S(2)}, u32[]{:S(2)}) collective-permute-start(f32[256,512]{1,0:T(8,128)S(1)} %get-tuple-element.44), channel_id=1, source_target_pairs={{0,1},{8,9},{16,17},{24,25}} | collective-permute-start | bytes 1572872 | tf_op jit(solution)/shard_map/ppermute | solution.py:467
  7.0 5.4 %collective-permute-start.1 = (f32[128,512]{1,0:T(8,128)S(1)}, f32[128,512]{1,0:T(8,128)S(1)}, u32[]{:S(2)}, u32[]{:S(2)}) collective-permute-start(f32[128,512]{1,0:T(8,128)S(1)} %get-tuple-element.48), channel_id=1, source_target_pairs={{5,4},{6,5},{7,6},{13,12},{14,13},{15,14},{21,20},{22,21},{23,22},... | collective-permute-start | bytes 786440 | tf_op jit(solution)/shard_map/ppermute | solution.py:476
  13.7 0.7 collective-permute-start.2
  14.4 3.3 %collective-permute-start.3 = (f32[256,512]{1,0:T(8,128)S(1)}, f32[256,512]{1,0:T(8,128)S(1)}, u32[]{:S(2)}, u32[]{:S(2)}) collective-permute-start(f32[256,512]{1,0:T(8,128)S(1)} %relay.7.refs_4_.refs_10_), channel_id=1, source_target_pairs={{2,3},{5,6},{10,11},{13,14},{18,19},{21,22},{26,27},{29,30}} | collective-permute-start | bytes 1572872 | tf_op jit(solution)/shard_map/ppermute | solution.py:467
  15.1 16.8 %collective-permute-start.5 = (f32[128,512]{1,0:T(8,128)S(1)}, f32[128,512]{1,0:T(8,128)S(1)}, u32[]{:S(2)}, u32[]{:S(2)}) collective-permute-start(f32[128,512]{1,0:T(8,128)S(1)} %get-tuple-element.54), channel_id=1, source_target_pairs={{1,0},{2,1},{3,2},{9,8},{10,9},{11,10},{17,16},{18,17},{19,18},{25... | collective-permute-start | bytes 786440 | tf_op jit(solution)/shard_map/ppermute | solution.py:476
  16.4 19.7 %collective-permute-start.6 = (f32[128,512]{1,0:T(8,128)S(1)}, f32[128,512]{1,0:T(8,128)S(1)}, u32[]{:S(2)}, u32[]{:S(2)}) collective-permute-start(f32[128,512]{1,0:T(8,128)S(1)} %get-tuple-element.55), channel_id=1, source_target_pairs={{1,0},{2,1},{3,2},{5,4},{6,5},{7,6},{9,8},{10,9},{11,10},{13,12},{... | collective-permute-start | bytes 786440 | tf_op jit(solution)/shard_map/ppermute | solution.py:476
  18.0 0.7 copy-start.4
  18.0 21.5 %collective-permute-start.4 = (f32[256,512]{1,0:T(8,128)S(1)}, f32[256,512]{1,0:T(8,128)S(1)}, u32[]{:S(2)}, u32[]{:S(2)}) collective-permute-start(f32[256,512]{1,0:T(8,128)S(1)} %get-tuple-element.53.refs_5_.refs_11_.refs_2_), channel_id=1, source_target_pairs={{3,2},{6,7},{11,10},{14,15},{19,18},{22,23},{27,26},{30,31}} | collective-permute-start | bytes 1572872 | tf_op jit(solution)/shard_map/ppermute | solution.py:467
  18.7 0.7 copy-start.2
  18.7 0.7 copy-start.3
  39.5 0.7 collective-permute-start.7
  40.3 29.3 %collective-permute-start.8 = (f32[256,512]{1,0:T(8,128)S(1)}, f32[256,512]{1,0:T(8,128)S(1)}, u32[]{:S(2)}, u32[]{:S(2)}) collective-permute-start(f32[256,512]{1,0:T(8,128)S(1)} %relay.10.refs_4_), channel_id=1, source_target_pairs={{1,0},{6,5},{9,8},{14,13},{17,16},{22,21},{25,24},{30,29}} | collective-permute-start | bytes 1572872 | tf_op jit(solution)/shard_map/ppermute | solution.py:467
  69.5 0.7 collective-permute-start.9
  71.5 9.1 %collective-permute-start.17 = (f32[64,512]{1,0:T(8,128)S(1)}, f32[64,512]{1,0:T(8,128)S(1)}, u32[]{:S(2)}, u32[]{:S(2)}) collective-permute-start(f32[64,512]{1,0:T(8,128)S(1)} %get-tuple-element.76), channel_id=1, source_target_pairs={{0,24},{4,28},{8,16},{12,20},{16,8},{20,12},{24,0},{28,4},{1,25},{... | collective-permute-start | bytes 393224 | tf_op jit(solution)/shard_map/ppermute | solution.py:580
  75.5 5.2 %collective-permute-start.18 = (f32[64,512]{1,0:T(8,128)S(1)}, f32[64,512]{1,0:T(8,128)S(1)}, u32[]{:S(2)}, u32[]{:S(2)}) collective-permute-start(f32[64,512]{1,0:T(8,128)S(1)} %get-tuple-element.77), channel_id=1, source_target_pairs={{0,8},{4,12},{8,0},{12,4},{16,24},{20,28},{24,16},{28,20},{1,9},{5... | collective-permute-start | bytes 393224 | tf_op jit(solution)/shard_map/ppermute | solution.py:580
  76.0 5.0 %collective-permute-start.19 = (f32[64,512]{1,0:T(8,128)S(1)}, f32[64,512]{1,0:T(8,128)S(1)}, u32[]{:S(2)}, u32[]{:S(2)}) collective-permute-start(f32[64,512]{1,0:T(8,128)S(1)} %get-tuple-element.78), channel_id=1, source_target_pairs={{0,16},{4,20},{8,24},{12,28},{16,0},{20,4},{24,8},{28,12},{1,17},{... | collective-permute-start | bytes 393224 | tf_op jit(solution)/shard_map/ppermute | solution.py:580
  77.2 12.2 %collective-permute-start.10 = (f32[64,512]{1,0:T(8,128)S(1)}, f32[64,512]{1,0:T(8,128)S(1)}, u32[]{:S(2)}, u32[]{:S(2)}) collective-permute-start(f32[64,512]{1,0:T(8,128)S(1)} %get-tuple-element.66), channel_id=1, source_target_pairs={{0,24},{4,28},{8,16},{12,20},{16,8},{20,12},{24,0},{28,4},{1,25},{... | collective-permute-start | bytes 393224 | tf_op jit(solution)/shard_map/ppermute | solution.py:580
  80.1 9.3 %collective-permute-start.11 = (f32[64,512]{1,0:T(8,128)S(1)}, f32[64,512]{1,0:T(8,128)S(1)}, u32[]{:S(2)}, u32[]{:S(2)}) collective-permute-start(f32[64,512]{1,0:T(8,128)S(1)} %get-tuple-element.67), channel_id=1, source_target_pairs={{0,8},{4,12},{8,0},{12,4},{16,24},{20,28},{24,16},{28,20},{1,9},{5... | collective-permute-start | bytes 393224 | tf_op jit(solution)/shard_map/ppermute | solution.py:580
  80.6 8.7 %collective-permute-start.12 = (f32[64,512]{1,0:T(8,128)S(1)}, f32[64,512]{1,0:T(8,128)S(1)}, u32[]{:S(2)}, u32[]{:S(2)}) collective-permute-start(f32[64,512]{1,0:T(8,128)S(1)} %get-tuple-element.68), channel_id=1, source_target_pairs={{0,16},{4,20},{8,24},{12,28},{16,0},{20,4},{24,8},{28,12},{1,17},{... | collective-permute-start | bytes 393224 | tf_op jit(solution)/shard_map/ppermute | solution.py:580
  81.2 9.6 %collective-permute-start.20 = (f32[4,64,512]{2,1,0:T(8,128)S(1)}, f32[4,64,512]{2,1,0:T(8,128)S(1)}, u32[]{:S(2)}, u32[]{:S(2)}) collective-permute-start(f32[4,64,512]{2,1,0:T(8,128)S(1)} %get-tuple-element.81), channel_id=1, source_target_pairs={{0,4},{4,0},{8,12},{12,8},{16,20},{20,16},{24,28},{28,24},{1,5},{5... | collective-permute-start | bytes 1572872 | tf_op jit(solution)/shard_map/ppermute | solution.py:594
  89.6 4.9 %collective-permute-start.13 = (f32[4,64,512]{2,1,0:T(8,128)S(1)}, f32[4,64,512]{2,1,0:T(8,128)S(1)}, u32[]{:S(2)}, u32[]{:S(2)}) collective-permute-start(f32[4,64,512]{2,1,0:T(8,128)S(1)} %get-tuple-element.71), channel_id=1, source_target_pairs={{0,4},{4,0},{8,12},{12,8},{16,20},{20,16},{24,28},{28,24},{1,5},{5... | collective-permute-start | bytes 1572872 | tf_op jit(solution)/shard_map/ppermute | solution.py:594
  90.9 7.3 %collective-permute-start.21 = (f32[64,512]{1,0:T(8,128)S(1)}, f32[64,512]{1,0:T(8,128)S(1)}, u32[]{:S(2)}, u32[]{:S(2)}) collective-permute-start(f32[64,512]{1,0:T(8,128)S(1)} %get-tuple-element.82), channel_id=1, source_target_pairs={{0,24},{4,28},{8,16},{12,20},{16,8},{20,12},{24,0},{28,4},{1,25},{... | collective-permute-start | bytes 393224 | tf_op jit(solution)/shard_map/ppermute | solution.py:580
  93.2 7.7 %collective-permute-start.22 = (f32[64,512]{1,0:T(8,128)S(1)}, f32[64,512]{1,0:T(8,128)S(1)}, u32[]{:S(2)}, u32[]{:S(2)}) collective-permute-start(f32[64,512]{1,0:T(8,128)S(1)} %get-tuple-element.83), channel_id=1, source_target_pairs={{0,8},{4,12},{8,0},{12,4},{16,24},{20,28},{24,16},{28,20},{1,9},{5... | collective-permute-start | bytes 393224 | tf_op jit(solution)/shard_map/ppermute | solution.py:580
  93.8 9.1 %collective-permute-start.23 = (f32[64,512]{1,0:T(8,128)S(1)}, f32[64,512]{1,0:T(8,128)S(1)}, u32[]{:S(2)}, u32[]{:S(2)}) collective-permute-start(f32[64,512]{1,0:T(8,128)S(1)} %get-tuple-element.84), channel_id=1, source_target_pairs={{0,16},{4,20},{8,24},{12,28},{16,0},{20,4},{24,8},{28,12},{1,17},{... | collective-permute-start | bytes 393224 | tf_op jit(solution)/shard_map/ppermute | solution.py:580
  94.6 9.3 %collective-permute-start.14 = (f32[64,512]{1,0:T(8,128)S(1)}, f32[64,512]{1,0:T(8,128)S(1)}, u32[]{:S(2)}, u32[]{:S(2)}) collective-permute-start(f32[64,512]{1,0:T(8,128)S(1)} %get-tuple-element.72), channel_id=1, source_target_pairs={{0,24},{4,28},{8,16},{12,20},{16,8},{20,12},{24,0},{28,4},{1,25},{... | collective-permute-start | bytes 393224 | tf_op jit(solution)/shard_map/ppermute | solution.py:580
  96.8 8.8 %collective-permute-start.15 = (f32[64,512]{1,0:T(8,128)S(1)}, f32[64,512]{1,0:T(8,128)S(1)}, u32[]{:S(2)}, u32[]{:S(2)}) collective-permute-start(f32[64,512]{1,0:T(8,128)S(1)} %get-tuple-element.73), channel_id=1, source_target_pairs={{0,8},{4,12},{8,0},{12,4},{16,24},{20,28},{24,16},{28,20},{1,9},{5... | collective-permute-start | bytes 393224 | tf_op jit(solution)/shard_map/ppermute | solution.py:580
  98.2 7.9 %collective-permute-start.16 = (f32[64,512]{1,0:T(8,128)S(1)}, f32[64,512]{1,0:T(8,128)S(1)}, u32[]{:S(2)}, u32[]{:S(2)}) collective-permute-start(f32[64,512]{1,0:T(8,128)S(1)} %get-tuple-element.74), channel_id=1, source_target_pairs={{0,16},{4,20},{8,24},{12,28},{16,0},{20,4},{24,8},{28,12},{1,17},{... | collective-permute-start | bytes 393224 | tf_op jit(solution)/shard_map/ppermute | solution.py:580

commit v12 on v11

--- a/solution.py
+++ b/solution.py
@@ -36,11 +36,18 @@
         matrix[0, index], matrix[1, index] = split(part)
 
 
+def put_left(matrix, block):
+    size = block.shape[0]
+    for index, part in enumerate(parts_of(block)):
+        matrix[index, :size], matrix[index, size:] = split(part)
+
+
 def times_split(left, matrix, transposed=False):
     products = []
-    for index, (high, low) in enumerate(left):
-        size = high.shape[0]
-        both = dot(jnp.concatenate([high, low], axis=0), matrix[0, index], transposed)
+    for index, stacked in enumerate(left):
+        size = stacked.shape[0] // 2
+        both = dot(stacked, matrix[0, index], transposed)
+        high = stacked[:size]
         products.append(both[:size] + both[size:] + dot(high, matrix[1, index], transposed))
     first, second, third = products
     if transposed:
@@ -49,7 +56,8 @@
 
 
 def times(block, matrix, transposed=False):
-    return times_split([split(part) for part in parts_of(block)], matrix, transposed)
+    left = [jnp.concatenate(split(part), axis=0) for part in parts_of(block)]
+    return times_split(left, matrix, transposed)
 
 
 def row_form(pair):
@@ -160,7 +168,7 @@
     return first, second
 
 
-def source_kernel(green, sigma, coupling, pattern, whole, gate, *scratch):
+def source_kernel(green, sigma, coupling, pattern, whole, *scratch):
     @pl.when(lax.axis_index("slab") == 0)
     def _():
         loads = Loads((green, sigma, coupling, pattern), scratch[:4], scratch[4], (1,))
@@ -169,12 +177,12 @@
     @pl.when((lax.axis_index("slab") > 0) & (trailing() == 1))
     def _():
         loads = Loads((green, sigma, coupling, pattern), scratch[:4], scratch[4], (0,), False)
-        gate[...] = loads.coupler(0)[: gate.shape[0]]
+        whole[...] = loads.coupler(0)
 
 
 def map_kernel(
     green, sigma, coupling, pattern,
-    whole, source, coupler, upper, lower, lead, tail, forward, backward, *scratch,
+    whole, source, coupler, opening, lead, tail, forward, backward, *scratch,
 ):
     m_a, m_b, m_c = scratch[5:]
     loads = Loads((green, sigma, coupling, pattern), scratch[:4], scratch[4])
@@ -183,8 +191,7 @@
 
     @pl.when(lax.axis_index("slab") > 0)
     def _():
-        upper[...] = before[: upper.shape[0]]
-        lower[...] = before[upper.shape[0] :]
+        opening[...] = before
         put(m_a, first)
         size = before.shape[0]
         behind = times(adjoint_row((before[:, :size], before[:, size:])), m_a)
@@ -195,7 +202,7 @@
         forward[...] = ahead
         put(m_a, ahead)
         put(m_c, coupler[...])
-        put(lead, times(times(second, m_c), m_a))
+        put_left(lead, times(times(second, m_c), m_a))
 
 
 def right_terms(first, last, coupler, m_coupler, m_first, m_last, m_upper):
@@ -211,9 +218,9 @@
     arrived, wholes = refs[: count - 1], refs[count - 1 : 2 * count - 2]
     refs = refs[2 * count - 2 :]
     start_whole, source, forward, backward, coupler = refs[:5]
-    gate, upper, lower = refs[5:8]
-    lead, tail, constant, last_lead, last_tail = refs[9:14]
-    first_v, last_v, m_a, m_b, m_c, m_d = refs[14:]
+    followings = refs[5:7]
+    lead, tail, constant, last_lead, last_tail = refs[8:13]
+    first_v, last_v, m_a, m_b, m_c, m_d = refs[13:]
     place = lax.axis_index("slab")
 
     @pl.when(place == 0)
@@ -237,11 +244,10 @@
         first, last = first_v[...], last_v[...]
         through, joined = right_terms(first, last, coupler[...], m_a, m_b, m_c, m_d)
         constant[...] = joined
-        above = jnp.where(trailing() == 0, upper[...], gate[...])
-        next_coupler = jnp.concatenate([above, lower[...]], axis=0)
+        next_coupler = jnp.where(trailing() == 0, followings[0][...], followings[1][...])
         put(m_a, next_coupler, True)
-        put(lead, times(through, m_a, True))
-        put(last_lead, times(last, m_a, True))
+        put_left(lead, times(through, m_a, True))
+        put_left(last_lead, times(last, m_a, True))
         behind = times(next_coupler, m_c)
         put(last_tail, behind)
         put(tail, times(behind, m_d))
@@ -249,7 +255,7 @@
 
 def apply_map(mapping, m_x):
     lead, tail, constant = mapping
-    ahead = [(lead[0, index], lead[1, index]) for index in range(3)]
+    ahead = [lead[index] for index in range(3)]
     return constant[...] + times(times_split(ahead, m_x), tail)
 
 
@@ -265,8 +271,6 @@
     right_map = [refs.pop(0) for _ in range(3)] if rights else None
     if closing:
         forward, backward, source, coupler = [refs.pop(0) for _ in range(4)]
-    if step == 0:
-        refs.pop(0)
     out = refs.pop(0)
     if closing:
         end, m_x, m_a, m_b, m_c = refs
@@ -443,6 +447,8 @@
     pairs = []
     for energy in range(energies):
         turn = step - (energy + LEADING) % 2
+        if turn < 0:
+            pairs += [(energy * count + i, energy * count + i - 1) for i in range(1, count)]
         if 0 <= turn <= count - 2:
             ends = (turn, turn + 1)
         elif count - 1 <= turn <= 2 * count - 3:
@@ -457,7 +463,7 @@
     size, blocks = free_green.shape[-1], pattern.shape[-1]
     args = (free_green[0], self_energy[0], coupling, pattern)
     row = shape(size, 2 * size)
-    half = shape(size // 2, 2 * size)
+    left_factor = shape(2 * size, size, HALF, 3)
     factor = shape(size, size, HALF, 2, 3)
     row_v = pltpu.VMEM(row.shape, F32)
     product = 24 * size**3
@@ -466,18 +472,9 @@
     def relay(step, value):
         return lax.ppermute(value, ("energy", "slab"), relay_pairs(step, energies, count))
 
-    def lower_place(value, cores):
-        pairs = [
-            (energy * count + i, energy * count + i - 1)
-            for energy in range(energies)
-            for i in range(1, count)
-            if (energy + LEADING) % 2 in cores
-        ]
-        return lax.ppermute(value, ("energy", "slab"), pairs)
-
     begun = call(
         source_kernel,
-        [row, half],
+        [row],
         loading,
         args,
         [HBM] * 4,
@@ -486,10 +483,9 @@
         limit=53,
     )
     arrived, outs, ends = [relay(0, begun[0])], [], []
-    gate = lower_place(begun[1], [1])
-    whole, source, coupler, upper, lower, left_lead, left_tail, forward, backward = call(
+    whole, source, coupler, opening, left_lead, left_tail, forward, backward = call(
         map_kernel,
-        [row] * 3 + [half] * 2 + [factor, factor, row, row],
+        [row] * 4 + [left_factor, factor, row, row],
         loading,
         args,
         [HBM] * 4,
@@ -520,8 +516,6 @@
             args += right_map[:3]
         if closing:
             args += [forward, backward, source, coupler]
-        if step == 0:
-            args.append(gate)
         made = call(
             functools.partial(relay_kernel, step, count, lefts, rights),
             [row] * (2 if closing else 1),
@@ -534,14 +528,19 @@
         ends += made[1:]
         arrived.append(relay(step + 1, made[0]))
         if step == 0:
-            lower = lower_place(lower, [0, 1])
-            upper = lower_place(upper, [0])
+            down = [
+                (energy * count + i, energy * count + i - 1)
+                for energy in range(energies)
+                for i in range(1, count)
+                if (energy + LEADING) % 2 == 0
+            ]
+            following = lax.ppermute(opening, ("energy", "slab"), down)
         if step == count - 2:
             args = arrived[: count - 1] + outs[: count - 1]
-            args += [whole, source, forward, backward, coupler, gate, upper, lower, tiles]
+            args += [whole, source, forward, backward, coupler, following, arrived[0], tiles]
             right_map = call(
                 functools.partial(prepare_kernel, count),
-                [factor, factor, row, factor, factor],
+                [left_factor, factor, row, left_factor, factor],
                 [row_v] * 2 + matrices(4, size),
                 args,
                 flops=10 * product,

time: 108 us -> 107 us (level)
  starting transfers between devices: 34.4 us -> 30.9 us
  waiting for transfers between devices: 52 us -> 54.8 us
    ppermute x7, waiting for transfers between devices: 29.2 us -> 31.2 us  [relay(): lax.ppermute(value, ('energy', 'slab'), relay_pairs(step, energies, count))]
    ppermute x3 -> x1, starting transfers between devices: 3.26 us -> 1.29 us  [shards(): following = lax.ppermute(opening, ('energy', 'slab'), down)]
    ppermute x3 -> x1, waiting for transfers between devices: 16 us -> 15.9 us  [shards(): following = lax.ppermute(opening, ('energy', 'slab'), down)]
  transfers between devices with their start and end apart: 24 -> 22, of which waited for: 12 -> 11; matrix products, arithmetic and copies ran while one was open for 0% -> 0% of each run, Pallas kernels for 11% -> 11%
where the time goes in v12:
time: 107 us; the launch traced here: 106 us
  waiting for transfers between devices  54.8 us (51%)
  starting transfers between devices  30.9 us (29%)
  Pallas kernels  18.3 us (17%)
  local copies, waits for them, and re-layouts  1.36 us (1%)
    ppermute x7, waiting for transfers between devices, relay(): lax.ppermute(value, ('energy', 'slab'), relay_pairs(step, energies, count))  31.2 us
    pallas_call x18, Pallas kernels, call(): pl.pallas_call(kernel, out_shape=outs, in_specs=specs or [VMEM] * len(arg...  18.3 us
    ppermute x1, waiting for transfers between devices, shards(): following = lax.ppermute(opening, ('energy', 'slab'), down)  15.9 us
    ppermute x12, starting transfers between devices, exchange(): sent[mask] = lax.ppermute(values[mask], 'energy', pairs)  14.9 us
    ppermute x2, starting transfers between devices, shards(): other = lax.ppermute(other, 'energy', [(i, i ^ 1) for i in range(energies)])  8.57 us
    ppermute x12, waiting for transfers between devices, exchange(): sent[mask] = lax.ppermute(values[mask], 'energy', pairs)  7.58 us
    ppermute x7, starting transfers between devices, relay(): lax.ppermute(value, ('energy', 'slab'), relay_pairs(step, energies, count))  6.07 us
  transfers between devices with their start and end apart: 22, of which 11 were waited for; matrix products, arithmetic and copies ran while one was open for 0% of the time, Pallas kernels for 11%

profile of v12, /device:TPU:0, one launch (start us, length us, event | category | flops | bytes accessed | tf_op | source)
XLA Modules:
  0.0 106.3 jit_solution(4583867828264859735)
XLA Ops:
  0.6 0.7 copy-done
  1.3 4.3 %source.1 = f32[256,512]{1,0:T(8,128)S(1)} custom-call(f32[2,2,256,256]{3,2,1,0:T(8,128)} %bitcast.6, f32[2,2,256,256]{3,2,1,0:T(8,128)} %bitcast.8, f32[2,2,256,256]{3,2,1,0:T(8,128)} %coupling.3, s32[2,16,16]{2,1,0:T(8,128)S(1)} %copy-done), custom_call_target="tpu_custom_call" | custom-call | flops 2415919104 | bytes 1048576 | tf_op jit(solution)/shard_map/source/pallas_call | solution.py:99
  5.7 1.3 %collective-permute-start = (f32[256,512]{1,0:T(8,128)S(1)}, f32[256,512]{1,0:T(8,128)S(1)}, u32[]{:S(2)}, u32[]{:S(2)}) collective-permute-start(f32[256,512]{1,0:T(8,128)S(1)} %source.1), channel_id=1, source_target_pairs={{0,1},{5,4},{6,5},{7,6},{8,9},{13,12},{14,13},{15,14},{16,17},{21,... | collective-permute-start | bytes 1572872 | tf_op jit(solution)/shard_map/ppermute | solution.py:473
  7.0 4.7 %left_maps.1 = (f32[256,512]{1,0:T(8,128)S(1)}, f32[256,512]{1,0:T(8,128)S(1)}, f32[256,512]{1,0:T(8,128)S(1)}, f32[256,512]{1,0:T(8,128)S(1)}, bf16[3,512,256]{...) custom-call(f32[2,2,256,256]{3,2,1,0:T(8,128)} %bitcast.7, ...), custom_call_target="tpu_custom_call" | custom-call | flops 4831838208 | bytes 1048576 | tf_op jit(solution)/shard_map/left_maps/pallas_call | solution.py:99
  11.7 1.9 %collective-permute-done.refs_0_.refs_12_ = f32[256,512]{1,0:T(8,128)S(1)} collective-permute-done((f32[256,512]{1,0:T(8,128)S(1)}, f32[256,512]{1,0:T(8,128)S(1)}, u32[]{:S(2)}, u32[]{:S(2)}) %collective-permute-start) | collective-permute-done | bytes 524320 | tf_op jit(solution)/shard_map/ppermute | solution.py:473
  13.7 0.7 collective-permute-start.1
  14.4 0.0 collective-permute-done.1.refs_0_.refs_1_
  14.4 0.7 collective-permute-start.2
  15.1 1.3 %collective-permute-start.4 = (f32[256,512]{1,0:T(8,128)S(1)}, f32[256,512]{1,0:T(8,128)S(1)}, u32[]{:S(2)}, u32[]{:S(2)}) collective-permute-start(f32[256,512]{1,0:T(8,128)S(1)} %get-tuple-element.49), channel_id=1, source_target_pairs={{1,0},{2,1},{3,2},{9,8},{10,9},{11,10},{17,16},{18,17},{19,18},{25... | collective-permute-start | bytes 1572872 | tf_op jit(solution)/shard_map/ppermute | solution.py:537
  16.4 0.0 collective-permute-done.2.refs_0_.refs_2_
  16.4 0.2 relay.8
  16.7 0.0 copy-start.3
  16.7 0.7 collective-permute-start.3
  17.4 0.0 copy-start.1
  17.4 0.0 copy-start.2
  17.4 0.6 copy-done.1
  18.1 0.0 copy-done.2
  18.1 0.1 add_reduce_fusion.weights
  18.2 0.7 weights.1.refs_13_.tiles
  18.8 15.9 %collective-permute-done.4.refs_11_ = f32[256,512]{1,0:T(8,128)S(1)} collective-permute-done((f32[256,512]{1,0:T(8,128)S(1)}, f32[256,512]{1,0:T(8,128)S(1)}, u32[]{:S(2)}, u32[]{:S(2)}) %collective-permute-start.4) | collective-permute-done | bytes 524320 | tf_op jit(solution)/shard_map/ppermute | solution.py:537
  34.8 3.3 %right_maps.1 = (bf16[3,512,256]{2,1,0:T(8,128)(2,1)S(1)}, bf16[2,3,256,256]{3,2,1,0:T(8,128)(2,1)S(1)}, f32[256,512]{1,0:T(8,128)S(1)}, bf16[3,512,256]{2,1,0:T(8,128)(2,1)S(1)}, bf16[2,3,256,256]{3,2,1,0:T(8,128)(2,1)S(1)}) custom-call(f32[256,512]{1,0:T(8,128)S(1)} %collective-permute-done.refs_0_.refs_12_, ...), custom_call_target="tpu_custom_call" | custom-call | flops 4026531840 | bytes 1048576 | tf_op jit(solution)/shard_map/right_maps/pallas_call | solution.py:99
  38.1 0.0 collective-permute-done.3.refs_0_
  38.2 0.7 collective-permute-start.5
  38.9 0.0 collective-permute-done.5.refs_0_.refs_1_
  38.9 1.3 %collective-permute-start.6 = (f32[256,512]{1,0:T(8,128)S(1)}, f32[256,512]{1,0:T(8,128)S(1)}, u32[]{:S(2)}, u32[]{:S(2)}) collective-permute-start(f32[256,512]{1,0:T(8,128)S(1)} %relay.10.refs_4_), channel_id=1, source_target_pairs={{1,0},{6,5},{9,8},{14,13},{17,16},{22,21},{25,24},{30,29}} | collective-permute-start | bytes 1572872 | tf_op jit(solution)/shard_map/ppermute | solution.py:473
  40.2 29.3 %collective-permute-done.6.refs_0_.refs_2_ = f32[256,512]{1,0:T(8,128)S(1)} collective-permute-done((f32[256,512]{1,0:T(8,128)S(1)}, f32[256,512]{1,0:T(8,128)S(1)}, u32[]{:S(2)}, u32[]{:S(2)}) %collective-permute-start.6) | collective-permute-done | bytes 524320 | tf_op jit(solution)/shard_map/ppermute | solution.py:473
  69.5 0.7 collective-permute-start.7
  70.2 0.0 collective-permute-done.7.refs_3_.refs_1_
  70.2 1.3 %second_slab.1 = (f32[256,512]{1,0:T(8,128)S(1)}, f32[64,512]{1,0:T(8,128)S(1)}, f32[64,512]{1,0:T(8,128)S(1)}, f32[64,512]{1,0:T(8,128)S(1)}, f32[64,512]{1,0:T(8,128)S(1)}) custom-call(f32[256,512]{1,0:T(8,128)S(1)} %collective-permute-done.3.refs_0_, f32[256,512]{1,0:T(8,128)S(1)} %collective-permute-done.5.refs_0_.refs_1_, ...), custom_call_target="tpu_custom_call" | custom-call | flops 805306368 | bytes 1048576 | tf_op jit(solution)/shard_map/second_slab/pallas_call | solution.py:99
  71.5 4.0 %collective-permute-start.15 = (f32[64,512]{1,0:T(8,128)S(1)}, f32[64,512]{1,0:T(8,128)S(1)}, u32[]{:S(2)}, u32[]{:S(2)}) collective-permute-start(f32[64,512]{1,0:T(8,128)S(1)} %get-tuple-element.70), channel_id=1, source_target_pairs={{0,24},{4,28},{8,16},{12,20},{16,8},{20,12},{24,0},{28,4},{1,25},{... | collective-permute-start | bytes 393224 | tf_op jit(solution)/shard_map/ppermute | solution.py:579
  75.5 0.5 collective-permute-start.16
  76.0 0.1 collective-permute-start.17
  76.1 1.0 first_slab.1
  77.1 2.0 %collective-permute-start.10 = (f32[64,512]{1,0:T(8,128)S(1)}, f32[64,512]{1,0:T(8,128)S(1)}, u32[]{:S(2)}, u32[]{:S(2)}) collective-permute-start(f32[64,512]{1,0:T(8,128)S(1)} %get-tuple-element.62), channel_id=1, source_target_pairs={{0,16},{4,20},{8,24},{12,28},{16,0},{20,4},{24,8},{28,12},{1,17},{... | collective-permute-start | bytes 393224 | tf_op jit(solution)/shard_map/ppermute | solution.py:579
  79.1 1.4 %collective-permute-start.8 = (f32[64,512]{1,0:T(8,128)S(1)}, f32[64,512]{1,0:T(8,128)S(1)}, u32[]{:S(2)}, u32[]{:S(2)}) collective-permute-start(f32[64,512]{1,0:T(8,128)S(1)} %get-tuple-element.60), channel_id=1, source_target_pairs={{0,24},{4,28},{8,16},{12,20},{16,8},{20,12},{24,0},{28,4},{1,25},{... | collective-permute-start | bytes 393224 | tf_op jit(solution)/shard_map/ppermute | solution.py:579
  80.5 0.0 collective-permute-done.15.refs_0_
  80.5 0.1 collective-permute-start.9
  80.7 0.0 collective-permute-done.16.refs_1_
  80.7 0.3 collective-permute-done.17.refs_2_
  81.0 0.2 mix.3
  81.2 6.2 %collective-permute-start.18 = (f32[4,64,512]{2,1,0:T(8,128)S(1)}, f32[4,64,512]{2,1,0:T(8,128)S(1)}, u32[]{:S(2)}, u32[]{:S(2)}) collective-permute-start(f32[4,64,512]{2,1,0:T(8,128)S(1)} %get-tuple-element.75), channel_id=1, source_target_pairs={{0,4},{4,0},{8,12},{12,8},{16,20},{20,16},{24,28},{28,24},{1,5},{5... | collective-permute-start | bytes 1572872 | tf_op jit(solution)/shard_map/ppermute | solution.py:593
  87.4 0.0 collective-permute-done.10.refs_2_
  87.4 0.0 collective-permute-done.8.refs_0_
  87.4 0.4 collective-permute-done.9.refs_1_
  87.8 0.2 mix.2
  88.0 2.3 %collective-permute-start.11 = (f32[4,64,512]{2,1,0:T(8,128)S(1)}, f32[4,64,512]{2,1,0:T(8,128)S(1)}, u32[]{:S(2)}, u32[]{:S(2)}) collective-permute-start(f32[4,64,512]{2,1,0:T(8,128)S(1)} %get-tuple-element.65), channel_id=1, source_target_pairs={{0,4},{4,0},{8,12},{12,8},{16,20},{20,16},{24,28},{28,24},{1,5},{5... | collective-permute-start | bytes 1572872 | tf_op jit(solution)/shard_map/ppermute | solution.py:593
  90.4 0.0 collective-permute-done.18.other
  90.4 0.1 sum.3
  90.4 1.8 %collective-permute-start.19 = (f32[64,512]{1,0:T(8,128)S(1)}, f32[64,512]{1,0:T(8,128)S(1)}, u32[]{:S(2)}, u32[]{:S(2)}) collective-permute-start(f32[64,512]{1,0:T(8,128)S(1)} %get-tuple-element.76), channel_id=1, source_target_pairs={{0,24},{4,28},{8,16},{12,20},{16,8},{20,12},{24,0},{28,4},{1,25},{... | collective-permute-start | bytes 393224 | tf_op jit(solution)/shard_map/ppermute | solution.py:579
  92.3 0.5 collective-permute-start.20
  92.8 1.2 %collective-permute-start.21 = (f32[64,512]{1,0:T(8,128)S(1)}, f32[64,512]{1,0:T(8,128)S(1)}, u32[]{:S(2)}, u32[]{:S(2)}) collective-permute-start(f32[64,512]{1,0:T(8,128)S(1)} %get-tuple-element.78), channel_id=1, source_target_pairs={{0,16},{4,20},{8,24},{12,28},{16,0},{20,4},{24,8},{28,12},{1,17},{... | collective-permute-start | bytes 393224 | tf_op jit(solution)/shard_map/ppermute | solution.py:579
  94.0 0.0 collective-permute-done.11.other
  94.0 0.1 sum.2
  94.1 1.8 %collective-permute-start.12 = (f32[64,512]{1,0:T(8,128)S(1)}, f32[64,512]{1,0:T(8,128)S(1)}, u32[]{:S(2)}, u32[]{:S(2)}) collective-permute-start(f32[64,512]{1,0:T(8,128)S(1)} %get-tuple-element.66), channel_id=1, source_target_pairs={{0,24},{4,28},{8,16},{12,20},{16,8},{20,12},{24,0},{28,4},{1,25},{... | collective-permute-start | bytes 393224 | tf_op jit(solution)/shard_map/ppermute | solution.py:579
  95.9 0.5 collective-permute-start.13
  96.4 1.3 %collective-permute-done.19.refs_4_ = f32[64,512]{1,0:T(8,128)S(1)} collective-permute-done((f32[64,512]{1,0:T(8,128)S(1)}, f32[64,512]{1,0:T(8,128)S(1)}, u32[]{:S(2)}, u32[]{:S(2)}) %collective-permute-start.19) | collective-permute-done | bytes 131104 | tf_op jit(solution)/shard_map/ppermute | solution.py:579
  97.8 0.9 collective-permute-start.14
  98.6 1.0 retarded.1
  99.7 0.3 collective-permute-done.20.refs_5_
  100.0 2.0 %collective-permute-done.21.refs_6_ = f32[64,512]{1,0:T(8,128)S(1)} collective-permute-done((f32[64,512]{1,0:T(8,128)S(1)}, f32[64,512]{1,0:T(8,128)S(1)}, u32[]{:S(2)}, u32[]{:S(2)}) %collective-permute-start.21) | collective-permute-done | bytes 131104 | tf_op jit(solution)/shard_map/ppermute | solution.py:579
  102.0 1.4 %collective-permute-done.12.refs_0_ = f32[64,512]{1,0:T(8,128)S(1)} collective-permute-done((f32[64,512]{1,0:T(8,128)S(1)}, f32[64,512]{1,0:T(8,128)S(1)}, u32[]{:S(2)}, u32[]{:S(2)}) %collective-permute-start.12) | collective-permute-done | bytes 131104 | tf_op jit(solution)/shard_map/ppermute | solution.py:579
  103.4 1.3 %collective-permute-done.13.refs_1_ = f32[64,512]{1,0:T(8,128)S(1)} collective-permute-done((f32[64,512]{1,0:T(8,128)S(1)}, f32[64,512]{1,0:T(8,128)S(1)}, u32[]{:S(2)}, u32[]{:S(2)}) %collective-permute-start.13) | collective-permute-done | bytes 131104 | tf_op jit(solution)/shard_map/ppermute | solution.py:579
  104.7 0.6 collective-permute-done.14.refs_2_
  105.3 1.0 scattering.1
  (9 shorter events, 0.1 us)
Async XLA Ops:
  0.6 0.7 copy-start
  5.7 8.0 %collective-permute-start = (f32[256,512]{1,0:T(8,128)S(1)}, f32[256,512]{1,0:T(8,128)S(1)}, u32[]{:S(2)}, u32[]{:S(2)}) collective-permute-start(f32[256,512]{1,0:T(8,128)S(1)} %source.1), channel_id=1, source_target_pairs={{0,1},{5,4},{6,5},{7,6},{8,9},{13,12},{14,13},{15,14},{16,17},{21,... | collective-permute-start | bytes 1572872 | tf_op jit(solution)/shard_map/ppermute | solution.py:473
  13.7 0.7 collective-permute-start.1
  14.4 2.0 %collective-permute-start.2 = (f32[256,512]{1,0:T(8,128)S(1)}, f32[256,512]{1,0:T(8,128)S(1)}, u32[]{:S(2)}, u32[]{:S(2)}) collective-permute-start(f32[256,512]{1,0:T(8,128)S(1)} %relay.7.refs_4_.refs_10_), channel_id=1, source_target_pairs={{2,3},{5,6},{10,11},{13,14},{18,19},{21,22},{26,27},{29,30}} | collective-permute-start | bytes 1572872 | tf_op jit(solution)/shard_map/ppermute | solution.py:473
  15.1 19.6 %collective-permute-start.4 = (f32[256,512]{1,0:T(8,128)S(1)}, f32[256,512]{1,0:T(8,128)S(1)}, u32[]{:S(2)}, u32[]{:S(2)}) collective-permute-start(f32[256,512]{1,0:T(8,128)S(1)} %get-tuple-element.49), channel_id=1, source_target_pairs={{1,0},{2,1},{3,2},{9,8},{10,9},{11,10},{17,16},{18,17},{19,18},{25... | collective-permute-start | bytes 1572872 | tf_op jit(solution)/shard_map/ppermute | solution.py:537
  16.7 0.7 copy-start.3
  16.7 21.4 %collective-permute-start.3 = (f32[256,512]{1,0:T(8,128)S(1)}, f32[256,512]{1,0:T(8,128)S(1)}, u32[]{:S(2)}, u32[]{:S(2)}) collective-permute-start(f32[256,512]{1,0:T(8,128)S(1)} %get-tuple-element.48.refs_5_.refs_11_.refs_2_), channel_id=1, source_target_pairs={{3,2},{6,7},{11,10},{14,15},{19,18},{22,23},{27,26},{30,31}} | collective-permute-start | bytes 1572872 | tf_op jit(solution)/shard_map/ppermute | solution.py:473
  17.4 0.7 copy-start.1
  17.4 0.7 copy-start.2
  38.2 0.7 collective-permute-start.5
  38.9 30.6 %collective-permute-start.6 = (f32[256,512]{1,0:T(8,128)S(1)}, f32[256,512]{1,0:T(8,128)S(1)}, u32[]{:S(2)}, u32[]{:S(2)}) collective-permute-start(f32[256,512]{1,0:T(8,128)S(1)} %relay.10.refs_4_), channel_id=1, source_target_pairs={{1,0},{6,5},{9,8},{14,13},{17,16},{22,21},{25,24},{30,29}} | collective-permute-start | bytes 1572872 | tf_op jit(solution)/shard_map/ppermute | solution.py:473
  69.5 0.7 collective-permute-start.7
  71.5 9.0 %collective-permute-start.15 = (f32[64,512]{1,0:T(8,128)S(1)}, f32[64,512]{1,0:T(8,128)S(1)}, u32[]{:S(2)}, u32[]{:S(2)}) collective-permute-start(f32[64,512]{1,0:T(8,128)S(1)} %get-tuple-element.70), channel_id=1, source_target_pairs={{0,24},{4,28},{8,16},{12,20},{16,8},{20,12},{24,0},{28,4},{1,25},{... | collective-permute-start | bytes 393224 | tf_op jit(solution)/shard_map/ppermute | solution.py:579
  75.5 5.2 %collective-permute-start.16 = (f32[64,512]{1,0:T(8,128)S(1)}, f32[64,512]{1,0:T(8,128)S(1)}, u32[]{:S(2)}, u32[]{:S(2)}) collective-permute-start(f32[64,512]{1,0:T(8,128)S(1)} %get-tuple-element.71), channel_id=1, source_target_pairs={{0,8},{4,12},{8,0},{12,4},{16,24},{20,28},{24,16},{28,20},{1,9},{5... | collective-permute-start | bytes 393224 | tf_op jit(solution)/shard_map/ppermute | solution.py:579
  76.0 5.0 %collective-permute-start.17 = (f32[64,512]{1,0:T(8,128)S(1)}, f32[64,512]{1,0:T(8,128)S(1)}, u32[]{:S(2)}, u32[]{:S(2)}) collective-permute-start(f32[64,512]{1,0:T(8,128)S(1)} %get-tuple-element.72), channel_id=1, source_target_pairs={{0,16},{4,20},{8,24},{12,28},{16,0},{20,4},{24,8},{28,12},{1,17},{... | collective-permute-start | bytes 393224 | tf_op jit(solution)/shard_map/ppermute | solution.py:579
  77.1 10.3 %collective-permute-start.10 = (f32[64,512]{1,0:T(8,128)S(1)}, f32[64,512]{1,0:T(8,128)S(1)}, u32[]{:S(2)}, u32[]{:S(2)}) collective-permute-start(f32[64,512]{1,0:T(8,128)S(1)} %get-tuple-element.62), channel_id=1, source_target_pairs={{0,16},{4,20},{8,24},{12,28},{16,0},{20,4},{24,8},{28,12},{1,17},{... | collective-permute-start | bytes 393224 | tf_op jit(solution)/shard_map/ppermute | solution.py:579
  79.1 8.3 %collective-permute-start.8 = (f32[64,512]{1,0:T(8,128)S(1)}, f32[64,512]{1,0:T(8,128)S(1)}, u32[]{:S(2)}, u32[]{:S(2)}) collective-permute-start(f32[64,512]{1,0:T(8,128)S(1)} %get-tuple-element.60), channel_id=1, source_target_pairs={{0,24},{4,28},{8,16},{12,20},{16,8},{20,12},{24,0},{28,4},{1,25},{... | collective-permute-start | bytes 393224 | tf_op jit(solution)/shard_map/ppermute | solution.py:579
  80.5 7.3 %collective-permute-start.9 = (f32[64,512]{1,0:T(8,128)S(1)}, f32[64,512]{1,0:T(8,128)S(1)}, u32[]{:S(2)}, u32[]{:S(2)}) collective-permute-start(f32[64,512]{1,0:T(8,128)S(1)} %get-tuple-element.61), channel_id=1, source_target_pairs={{0,8},{4,12},{8,0},{12,4},{16,24},{20,28},{24,16},{28,20},{1,9},{5... | collective-permute-start | bytes 393224 | tf_op jit(solution)/shard_map/ppermute | solution.py:579
  81.2 9.2 %collective-permute-start.18 = (f32[4,64,512]{2,1,0:T(8,128)S(1)}, f32[4,64,512]{2,1,0:T(8,128)S(1)}, u32[]{:S(2)}, u32[]{:S(2)}) collective-permute-start(f32[4,64,512]{2,1,0:T(8,128)S(1)} %get-tuple-element.75), channel_id=1, source_target_pairs={{0,4},{4,0},{8,12},{12,8},{16,20},{20,16},{24,28},{28,24},{1,5},{5... | collective-permute-start | bytes 1572872 | tf_op jit(solution)/shard_map/ppermute | solution.py:593
  88.0 6.0 %collective-permute-start.11 = (f32[4,64,512]{2,1,0:T(8,128)S(1)}, f32[4,64,512]{2,1,0:T(8,128)S(1)}, u32[]{:S(2)}, u32[]{:S(2)}) collective-permute-start(f32[4,64,512]{2,1,0:T(8,128)S(1)} %get-tuple-element.65), channel_id=1, source_target_pairs={{0,4},{4,0},{8,12},{12,8},{16,20},{20,16},{24,28},{28,24},{1,5},{5... | collective-permute-start | bytes 1572872 | tf_op jit(solution)/shard_map/ppermute | solution.py:593
  90.4 7.3 %collective-permute-start.19 = (f32[64,512]{1,0:T(8,128)S(1)}, f32[64,512]{1,0:T(8,128)S(1)}, u32[]{:S(2)}, u32[]{:S(2)}) collective-permute-start(f32[64,512]{1,0:T(8,128)S(1)} %get-tuple-element.76), channel_id=1, source_target_pairs={{0,24},{4,28},{8,16},{12,20},{16,8},{20,12},{24,0},{28,4},{1,25},{... | collective-permute-start | bytes 393224 | tf_op jit(solution)/shard_map/ppermute | solution.py:579
  92.3 7.7 %collective-permute-start.20 = (f32[64,512]{1,0:T(8,128)S(1)}, f32[64,512]{1,0:T(8,128)S(1)}, u32[]{:S(2)}, u32[]{:S(2)}) collective-permute-start(f32[64,512]{1,0:T(8,128)S(1)} %get-tuple-element.77), channel_id=1, source_target_pairs={{0,8},{4,12},{8,0},{12,4},{16,24},{20,28},{24,16},{28,20},{1,9},{5... | collective-permute-start | bytes 393224 | tf_op jit(solution)/shard_map/ppermute | solution.py:579
  92.8 9.2 %collective-permute-start.21 = (f32[64,512]{1,0:T(8,128)S(1)}, f32[64,512]{1,0:T(8,128)S(1)}, u32[]{:S(2)}, u32[]{:S(2)}) collective-permute-start(f32[64,512]{1,0:T(8,128)S(1)} %get-tuple-element.78), channel_id=1, source_target_pairs={{0,16},{4,20},{8,24},{12,28},{16,0},{20,4},{24,8},{28,12},{1,17},{... | collective-permute-start | bytes 393224 | tf_op jit(solution)/shard_map/ppermute | solution.py:579
  94.1 9.3 %collective-permute-start.12 = (f32[64,512]{1,0:T(8,128)S(1)}, f32[64,512]{1,0:T(8,128)S(1)}, u32[]{:S(2)}, u32[]{:S(2)}) collective-permute-start(f32[64,512]{1,0:T(8,128)S(1)} %get-tuple-element.66), channel_id=1, source_target_pairs={{0,24},{4,28},{8,16},{12,20},{16,8},{20,12},{24,0},{28,4},{1,25},{... | collective-permute-start | bytes 393224 | tf_op jit(solution)/shard_map/ppermute | solution.py:579
  95.9 8.8 %collective-permute-start.13 = (f32[64,512]{1,0:T(8,128)S(1)}, f32[64,512]{1,0:T(8,128)S(1)}, u32[]{:S(2)}, u32[]{:S(2)}) collective-permute-start(f32[64,512]{1,0:T(8,128)S(1)} %get-tuple-element.67), channel_id=1, source_target_pairs={{0,8},{4,12},{8,0},{12,4},{16,24},{20,28},{24,16},{28,20},{1,9},{5... | collective-permute-start | bytes 393224 | tf_op jit(solution)/shard_map/ppermute | solution.py:579
  97.8 7.5 %collective-permute-start.14 = (f32[64,512]{1,0:T(8,128)S(1)}, f32[64,512]{1,0:T(8,128)S(1)}, u32[]{:S(2)}, u32[]{:S(2)}) collective-permute-start(f32[64,512]{1,0:T(8,128)S(1)} %get-tuple-element.68), channel_id=1, source_target_pairs={{0,16},{4,20},{8,24},{12,28},{16,0},{20,4},{24,8},{28,12},{1,17},{... | collective-permute-start | bytes 393224 | tf_op jit(solution)/shard_map/ppermute | solution.py:579

commit v13 on v12

--- a/solution.py
+++ b/solution.py
@@ -32,23 +32,23 @@
 
 
 def put(matrix, block, adjoint=False):
+    size = block.shape[0]
     for index, part in enumerate(parts_of(block, adjoint)):
-        matrix[0, index], matrix[1, index] = split(part)
-
-
-def put_left(matrix, block):
-    size = block.shape[0]
-    for index, part in enumerate(parts_of(block)):
         matrix[index, :size], matrix[index, size:] = split(part)
 
 
 def times_split(left, matrix, transposed=False):
     products = []
     for index, stacked in enumerate(left):
-        size = stacked.shape[0] // 2
-        both = dot(stacked, matrix[0, index], transposed)
-        high = stacked[:size]
-        products.append(both[:size] + both[size:] + dot(high, matrix[1, index], transposed))
+        rows, size = stacked.shape[0] // 2, matrix.shape[1] // 2
+        high, low = stacked[:rows], stacked[rows:]
+        if transposed:
+            both = dot(stacked, matrix[index, :size], True)
+            both = both[:rows] + both[rows:] + dot(high, matrix[index, size:], True)
+        else:
+            both = dot(jnp.concatenate([high, high], axis=1), matrix[index], False)
+            both += dot(low, matrix[index, :size], False)
+        products.append(both)
     first, second, third = products
     if transposed:
         return jnp.concatenate([first + second, third - first + second], axis=1)
@@ -92,7 +92,7 @@
 
 
 def matrices(number, size):
-    return [pltpu.VMEM((2, 3, size, size), HALF)] * number
+    return [pltpu.VMEM((3, 2 * size, size), HALF)] * number
 
 
 def call(kernel, outs, scratch, args, specs=None, flops=0, name=None, limit=40):
@@ -202,7 +202,7 @@
         forward[...] = ahead
         put(m_a, ahead)
         put(m_c, coupler[...])
-        put_left(lead, times(times(second, m_c), m_a))
+        put(lead, times(times(second, m_c), m_a))
 
 
 def right_terms(first, last, coupler, m_coupler, m_first, m_last, m_upper):
@@ -246,8 +246,8 @@
         constant[...] = joined
         next_coupler = jnp.where(trailing() == 0, followings[0][...], followings[1][...])
         put(m_a, next_coupler, True)
-        put_left(lead, times(through, m_a, True))
-        put_left(last_lead, times(last, m_a, True))
+        put(lead, times(through, m_a, True))
+        put(last_lead, times(last, m_a, True))
         behind = times(next_coupler, m_c)
         put(last_tail, behind)
         put(tail, times(behind, m_d))
@@ -283,7 +283,7 @@
             out[...] = left_map[2][...]
 
     if lefts:
-        @pl.when(is_left)
+        @pl.when(is_left & (place < count - 1) if closing else is_left)
         def _():
             put(m_x, arrived[...])
             out[...] = apply_map(left_map, m_x)
@@ -291,7 +291,8 @@
     if closing:
         @pl.when(is_left & (place == count - 1))
         def _():
-            last = out[...]
+            put(m_x, arrived[...])
+            last = apply_map(left_map, m_x)
             end[...] = last
             put(m_a, backward[...])
             first = source[...] + times(times(forward[...], m_x), m_a)
@@ -463,8 +464,7 @@
     size, blocks = free_green.shape[-1], pattern.shape[-1]
     args = (free_green[0], self_energy[0], coupling, pattern)
     row = shape(size, 2 * size)
-    left_factor = shape(2 * size, size, HALF, 3)
-    factor = shape(size, size, HALF, 2, 3)
+    factor = shape(2 * size, size, HALF, 3)
     row_v = pltpu.VMEM(row.shape, F32)
     product = 24 * size**3
     loading = load_scratch(size, blocks) + matrices(3, size)
@@ -485,7 +485,7 @@
     arrived, outs, ends = [relay(0, begun[0])], [], []
     whole, source, coupler, opening, left_lead, left_tail, forward, backward = call(
         map_kernel,
-        [row] * 4 + [left_factor, factor, row, row],
+        [row] * 4 + [factor, factor, row, row],
         loading,
         args,
         [HBM] * 4,
@@ -540,7 +540,7 @@
             args += [whole, source, forward, backward, coupler, following, arrived[0], tiles]
             right_map = call(
                 functools.partial(prepare_kernel, count),
-                [left_factor, factor, row, left_factor, factor],
+                [factor, factor, row, factor, factor],
                 [row_v] * 2 + matrices(4, size),
                 args,
                 flops=10 * product,

time: 107 us -> 107 us (level)
  transfers between devices with their start and end apart: 22 -> 22, of which waited for: 11 -> 10; matrix products, arithmetic and copies ran while one was open for 0% -> 0% of each run, Pallas kernels for 11% -> 11%
where the time goes in v13:
time: 107 us; the launch traced here: 106 us
  waiting for transfers between devices  54.6 us (51%)
  starting transfers between devices  31.1 us (29%)
  Pallas kernels  18.3 us (17%)
  local copies, waits for them, and re-layouts  1.36 us (1%)
    ppermute x7, waiting for transfers between devices, relay(): lax.ppermute(value, ('energy', 'slab'), relay_pairs(step, energies, count))  30.8 us
    pallas_call x18, Pallas kernels, call(): pl.pallas_call(kernel, out_shape=outs, in_specs=specs or [VMEM] * len(arg...  18.3 us
    ppermute x1, waiting for transfers between devices, shards(): following = lax.ppermute(opening, ('energy', 'slab'), down)  15.9 us
    ppermute x12, starting transfers between devices, exchange(): sent[mask] = lax.ppermute(values[mask], 'energy', pairs)  14.3 us
    ppermute x2, starting transfers between devices, shards(): other = lax.ppermute(other, 'energy', [(i, i ^ 1) for i in range(energies)])  9.4 us
    ppermute x12, waiting for transfers between devices, exchange(): sent[mask] = lax.ppermute(values[mask], 'energy', pairs)  7.82 us
    ppermute x7, starting transfers between devices, relay(): lax.ppermute(value, ('energy', 'slab'), relay_pairs(step, energies, count))  6.07 us
  transfers between devices with their start and end apart: 22, of which 10 were waited for; matrix products, arithmetic and copies ran while one was open for 0% of the time, Pallas kernels for 11%

profile of v13, /device:TPU:0, one launch (start us, length us, event | category | flops | bytes accessed | tf_op | source)
XLA Modules:
  0.0 106.3 jit_solution(2430355752717415425)
XLA Ops:
  0.6 0.7 copy-done
  1.3 4.3 %source.1 = f32[256,512]{1,0:T(8,128)S(1)} custom-call(f32[2,2,256,256]{3,2,1,0:T(8,128)} %bitcast.6, f32[2,2,256,256]{3,2,1,0:T(8,128)} %bitcast.8, f32[2,2,256,256]{3,2,1,0:T(8,128)} %coupling.3, s32[2,16,16]{2,1,0:T(8,128)S(1)} %copy-done), custom_call_target="tpu_custom_call" | custom-call | flops 2415919104 | bytes 1048576 | tf_op jit(solution)/shard_map/source/pallas_call | solution.py:99
  5.7 1.3 %collective-permute-start = (f32[256,512]{1,0:T(8,128)S(1)}, f32[256,512]{1,0:T(8,128)S(1)}, u32[]{:S(2)}, u32[]{:S(2)}) collective-permute-start(f32[256,512]{1,0:T(8,128)S(1)} %source.1), channel_id=1, source_target_pairs={{0,1},{5,4},{6,5},{7,6},{8,9},{13,12},{14,13},{15,14},{16,17},{21,... | collective-permute-start | bytes 1572872 | tf_op jit(solution)/shard_map/ppermute | solution.py:473
  7.0 4.7 %left_maps.1 = (f32[256,512]{1,0:T(8,128)S(1)}, f32[256,512]{1,0:T(8,128)S(1)}, f32[256,512]{1,0:T(8,128)S(1)}, f32[256,512]{1,0:T(8,128)S(1)}, bf16[3,512,256]{...) custom-call(f32[2,2,256,256]{3,2,1,0:T(8,128)} %bitcast.7, ...), custom_call_target="tpu_custom_call" | custom-call | flops 4831838208 | bytes 1048576 | tf_op jit(solution)/shard_map/left_maps/pallas_call | solution.py:99
  11.8 1.9 %collective-permute-done.refs_0_.refs_12_ = f32[256,512]{1,0:T(8,128)S(1)} collective-permute-done((f32[256,512]{1,0:T(8,128)S(1)}, f32[256,512]{1,0:T(8,128)S(1)}, u32[]{:S(2)}, u32[]{:S(2)}) %collective-permute-start) | collective-permute-done | bytes 524320 | tf_op jit(solution)/shard_map/ppermute | solution.py:473
  13.7 0.7 collective-permute-start.1
  14.4 0.0 collective-permute-done.1.refs_0_.refs_1_
  14.4 0.7 collective-permute-start.2
  15.2 1.3 %collective-permute-start.4 = (f32[256,512]{1,0:T(8,128)S(1)}, f32[256,512]{1,0:T(8,128)S(1)}, u32[]{:S(2)}, u32[]{:S(2)}) collective-permute-start(f32[256,512]{1,0:T(8,128)S(1)} %get-tuple-element.49), channel_id=1, source_target_pairs={{1,0},{2,1},{3,2},{9,8},{10,9},{11,10},{17,16},{18,17},{19,18},{25... | collective-permute-start | bytes 1572872 | tf_op jit(solution)/shard_map/ppermute | solution.py:537
  16.5 0.0 collective-permute-done.2.refs_0_.refs_2_
  16.5 0.2 relay.8
  16.7 0.0 copy-start.3
  16.7 0.7 collective-permute-start.3
  17.4 0.0 copy-start.1
  17.4 0.0 copy-start.2
  17.4 0.6 copy-done.1
  18.1 0.0 copy-done.2
  18.1 0.1 add_reduce_fusion.weights
  18.2 0.7 weights.1.refs_13_.tiles
  18.8 15.9 %collective-permute-done.4.refs_11_ = f32[256,512]{1,0:T(8,128)S(1)} collective-permute-done((f32[256,512]{1,0:T(8,128)S(1)}, f32[256,512]{1,0:T(8,128)S(1)}, u32[]{:S(2)}, u32[]{:S(2)}) %collective-permute-start.4) | collective-permute-done | bytes 524320 | tf_op jit(solution)/shard_map/ppermute | solution.py:537
  34.8 3.3 %right_maps.1 = (bf16[3,512,256]{2,1,0:T(8,128)(2,1)S(1)}, bf16[3,512,256]{2,1,0:T(8,128)(2,1)S(1)}, f32[256,512]{1,0:T(8,128)S(1)}, bf16[3,512,256]{2,1,0:T(8,128)(2,1)S(1)}, bf16[3,512,256]{2,1,0:T(8,128)(2,1)S(1)}) custom-call(f32[256,512]{1,0:T(8,128)S(1)} %collective-permute-done.refs_0_.refs_12_, ...), custom_call_target="tpu_custom_call" | custom-call | flops 4026531840 | bytes 1048576 | tf_op jit(solution)/shard_map/right_maps/pallas_call | solution.py:99
  38.0 0.0 collective-permute-done.3.refs_0_
  38.1 0.7 collective-permute-start.5
  38.8 0.0 collective-permute-done.5.refs_0_.refs_1_
  38.8 0.2 relay.10.refs_4_
  39.1 1.3 %collective-permute-start.6 = (f32[256,512]{1,0:T(8,128)S(1)}, f32[256,512]{1,0:T(8,128)S(1)}, u32[]{:S(2)}, u32[]{:S(2)}) collective-permute-start(f32[256,512]{1,0:T(8,128)S(1)} %relay.10.refs_4_), channel_id=1, source_target_pairs={{1,0},{6,5},{9,8},{14,13},{17,16},{22,21},{25,24},{30,29}} | collective-permute-start | bytes 1572872 | tf_op jit(solution)/shard_map/ppermute | solution.py:473
  40.4 28.9 %collective-permute-done.6.refs_0_.refs_2_ = f32[256,512]{1,0:T(8,128)S(1)} collective-permute-done((f32[256,512]{1,0:T(8,128)S(1)}, f32[256,512]{1,0:T(8,128)S(1)}, u32[]{:S(2)}, u32[]{:S(2)}) %collective-permute-start.6) | collective-permute-done | bytes 524320 | tf_op jit(solution)/shard_map/ppermute | solution.py:473
  69.2 0.7 collective-permute-start.7
  69.9 0.0 collective-permute-done.7.refs_3_.refs_1_
  69.9 1.1 %second_slab.1 = (f32[256,512]{1,0:T(8,128)S(1)}, f32[64,512]{1,0:T(8,128)S(1)}, f32[64,512]{1,0:T(8,128)S(1)}, f32[64,512]{1,0:T(8,128)S(1)}, f32[64,512]{1,0:T(8,128)S(1)}) custom-call(f32[256,512]{1,0:T(8,128)S(1)} %collective-permute-done.3.refs_0_, f32[256,512]{1,0:T(8,128)S(1)} %collective-permute-done.5.refs_0_.refs_1_, ...), custom_call_target="tpu_custom_call" | custom-call | flops 805306368 | bytes 1048576 | tf_op jit(solution)/shard_map/second_slab/pallas_call | solution.py:99
  71.0 4.0 %collective-permute-start.15 = (f32[64,512]{1,0:T(8,128)S(1)}, f32[64,512]{1,0:T(8,128)S(1)}, u32[]{:S(2)}, u32[]{:S(2)}) collective-permute-start(f32[64,512]{1,0:T(8,128)S(1)} %get-tuple-element.70), channel_id=1, source_target_pairs={{0,24},{4,28},{8,16},{12,20},{16,8},{20,12},{24,0},{28,4},{1,25},{... | collective-permute-start | bytes 393224 | tf_op jit(solution)/shard_map/ppermute | solution.py:579
  75.0 0.5 collective-permute-start.16
  75.5 0.1 collective-permute-start.17
  75.6 1.0 first_slab.1
  76.7 2.0 %collective-permute-start.10 = (f32[64,512]{1,0:T(8,128)S(1)}, f32[64,512]{1,0:T(8,128)S(1)}, u32[]{:S(2)}, u32[]{:S(2)}) collective-permute-start(f32[64,512]{1,0:T(8,128)S(1)} %get-tuple-element.62), channel_id=1, source_target_pairs={{0,16},{4,20},{8,24},{12,28},{16,0},{20,4},{24,8},{28,12},{1,17},{... | collective-permute-start | bytes 393224 | tf_op jit(solution)/shard_map/ppermute | solution.py:579
  78.6 1.4 %collective-permute-start.8 = (f32[64,512]{1,0:T(8,128)S(1)}, f32[64,512]{1,0:T(8,128)S(1)}, u32[]{:S(2)}, u32[]{:S(2)}) collective-permute-start(f32[64,512]{1,0:T(8,128)S(1)} %get-tuple-element.60), channel_id=1, source_target_pairs={{0,24},{4,28},{8,16},{12,20},{16,8},{20,12},{24,0},{28,4},{1,25},{... | collective-permute-start | bytes 393224 | tf_op jit(solution)/shard_map/ppermute | solution.py:579
  80.1 0.0 collective-permute-done.15.refs_0_
  80.1 0.1 collective-permute-start.9
  80.2 0.0 collective-permute-done.16.refs_1_
  80.2 0.3 collective-permute-done.17.refs_2_
  80.5 0.2 mix.3
  80.7 6.9 %collective-permute-start.18 = (f32[4,64,512]{2,1,0:T(8,128)S(1)}, f32[4,64,512]{2,1,0:T(8,128)S(1)}, u32[]{:S(2)}, u32[]{:S(2)}) collective-permute-start(f32[4,64,512]{2,1,0:T(8,128)S(1)} %get-tuple-element.75), channel_id=1, source_target_pairs={{0,4},{4,0},{8,12},{12,8},{16,20},{20,16},{24,28},{28,24},{1,5},{5... | collective-permute-start | bytes 1572872 | tf_op jit(solution)/shard_map/ppermute | solution.py:593
  87.6 0.0 collective-permute-done.10.refs_2_
  87.6 0.0 collective-permute-done.8.refs_0_
  87.6 0.0 collective-permute-done.9.refs_1_
  87.6 0.2 mix.2
  87.9 2.5 %collective-permute-start.11 = (f32[4,64,512]{2,1,0:T(8,128)S(1)}, f32[4,64,512]{2,1,0:T(8,128)S(1)}, u32[]{:S(2)}, u32[]{:S(2)}) collective-permute-start(f32[4,64,512]{2,1,0:T(8,128)S(1)} %get-tuple-element.65), channel_id=1, source_target_pairs={{0,4},{4,0},{8,12},{12,8},{16,20},{20,16},{24,28},{28,24},{1,5},{5... | collective-permute-start | bytes 1572872 | tf_op jit(solution)/shard_map/ppermute | solution.py:593
  90.4 0.0 collective-permute-done.18.other
  90.4 0.1 sum.3
  90.5 1.7 %collective-permute-start.19 = (f32[64,512]{1,0:T(8,128)S(1)}, f32[64,512]{1,0:T(8,128)S(1)}, u32[]{:S(2)}, u32[]{:S(2)}) collective-permute-start(f32[64,512]{1,0:T(8,128)S(1)} %get-tuple-element.76), channel_id=1, source_target_pairs={{0,24},{4,28},{8,16},{12,20},{16,8},{20,12},{24,0},{28,4},{1,25},{... | collective-permute-start | bytes 393224 | tf_op jit(solution)/shard_map/ppermute | solution.py:579
  92.1 0.4 collective-permute-start.20
  92.5 1.5 %collective-permute-start.21 = (f32[64,512]{1,0:T(8,128)S(1)}, f32[64,512]{1,0:T(8,128)S(1)}, u32[]{:S(2)}, u32[]{:S(2)}) collective-permute-start(f32[64,512]{1,0:T(8,128)S(1)} %get-tuple-element.78), channel_id=1, source_target_pairs={{0,16},{4,20},{8,24},{12,28},{16,0},{20,4},{24,8},{28,12},{1,17},{... | collective-permute-start | bytes 393224 | tf_op jit(solution)/shard_map/ppermute | solution.py:579
  94.0 0.1 sum.2
  94.1 1.7 %collective-permute-start.12 = (f32[64,512]{1,0:T(8,128)S(1)}, f32[64,512]{1,0:T(8,128)S(1)}, u32[]{:S(2)}, u32[]{:S(2)}) collective-permute-start(f32[64,512]{1,0:T(8,128)S(1)} %get-tuple-element.66), channel_id=1, source_target_pairs={{0,24},{4,28},{8,16},{12,20},{16,8},{20,12},{24,0},{28,4},{1,25},{... | collective-permute-start | bytes 393224 | tf_op jit(solution)/shard_map/ppermute | solution.py:579
  95.8 0.4 collective-permute-start.13
  96.1 1.6 %collective-permute-done.19.refs_4_ = f32[64,512]{1,0:T(8,128)S(1)} collective-permute-done((f32[64,512]{1,0:T(8,128)S(1)}, f32[64,512]{1,0:T(8,128)S(1)}, u32[]{:S(2)}, u32[]{:S(2)}) %collective-permute-start.19) | collective-permute-done | bytes 131104 | tf_op jit(solution)/shard_map/ppermute | solution.py:579
  97.8 0.5 collective-permute-start.14
  98.3 1.0 retarded.1
  99.4 0.3 collective-permute-done.20.refs_5_
  99.7 1.0 collective-permute-done.21.refs_6_
  100.7 2.7 %collective-permute-done.12.refs_0_ = f32[64,512]{1,0:T(8,128)S(1)} collective-permute-done((f32[64,512]{1,0:T(8,128)S(1)}, f32[64,512]{1,0:T(8,128)S(1)}, u32[]{:S(2)}, u32[]{:S(2)}) %collective-permute-start.12) | collective-permute-done | bytes 131104 | tf_op jit(solution)/shard_map/ppermute | solution.py:579
  103.4 1.0 collective-permute-done.13.refs_1_
  104.4 0.9 collective-permute-done.14.refs_2_
  105.3 1.0 scattering.1
  (9 shorter events, 0.1 us)
Async XLA Ops:
  0.6 0.7 copy-start
  5.7 8.0 %collective-permute-start = (f32[256,512]{1,0:T(8,128)S(1)}, f32[256,512]{1,0:T(8,128)S(1)}, u32[]{:S(2)}, u32[]{:S(2)}) collective-permute-start(f32[256,512]{1,0:T(8,128)S(1)} %source.1), channel_id=1, source_target_pairs={{0,1},{5,4},{6,5},{7,6},{8,9},{13,12},{14,13},{15,14},{16,17},{21,... | collective-permute-start | bytes 1572872 | tf_op jit(solution)/shard_map/ppermute | solution.py:473
  13.7 0.7 collective-permute-start.1
  14.4 2.0 %collective-permute-start.2 = (f32[256,512]{1,0:T(8,128)S(1)}, f32[256,512]{1,0:T(8,128)S(1)}, u32[]{:S(2)}, u32[]{:S(2)}) collective-permute-start(f32[256,512]{1,0:T(8,128)S(1)} %relay.7.refs_4_.refs_10_), channel_id=1, source_target_pairs={{2,3},{5,6},{10,11},{13,14},{18,19},{21,22},{26,27},{29,30}} | collective-permute-start | bytes 1572872 | tf_op jit(solution)/shard_map/ppermute | solution.py:473
  15.2 19.6 %collective-permute-start.4 = (f32[256,512]{1,0:T(8,128)S(1)}, f32[256,512]{1,0:T(8,128)S(1)}, u32[]{:S(2)}, u32[]{:S(2)}) collective-permute-start(f32[256,512]{1,0:T(8,128)S(1)} %get-tuple-element.49), channel_id=1, source_target_pairs={{1,0},{2,1},{3,2},{9,8},{10,9},{11,10},{17,16},{18,17},{19,18},{25... | collective-permute-start | bytes 1572872 | tf_op jit(solution)/shard_map/ppermute | solution.py:537
  16.7 0.7 copy-start.3
  16.7 21.4 %collective-permute-start.3 = (f32[256,512]{1,0:T(8,128)S(1)}, f32[256,512]{1,0:T(8,128)S(1)}, u32[]{:S(2)}, u32[]{:S(2)}) collective-permute-start(f32[256,512]{1,0:T(8,128)S(1)} %get-tuple-element.48.refs_5_.refs_11_.refs_2_), channel_id=1, source_target_pairs={{3,2},{6,7},{11,10},{14,15},{19,18},{22,23},{27,26},{30,31}} | collective-permute-start | bytes 1572872 | tf_op jit(solution)/shard_map/ppermute | solution.py:473
  17.4 0.7 copy-start.1
  17.4 0.7 copy-start.2
  38.1 0.7 collective-permute-start.5
  39.1 30.2 %collective-permute-start.6 = (f32[256,512]{1,0:T(8,128)S(1)}, f32[256,512]{1,0:T(8,128)S(1)}, u32[]{:S(2)}, u32[]{:S(2)}) collective-permute-start(f32[256,512]{1,0:T(8,128)S(1)} %relay.10.refs_4_), channel_id=1, source_target_pairs={{1,0},{6,5},{9,8},{14,13},{17,16},{22,21},{25,24},{30,29}} | collective-permute-start | bytes 1572872 | tf_op jit(solution)/shard_map/ppermute | solution.py:473
  69.2 0.7 collective-permute-start.7
  71.0 9.1 %collective-permute-start.15 = (f32[64,512]{1,0:T(8,128)S(1)}, f32[64,512]{1,0:T(8,128)S(1)}, u32[]{:S(2)}, u32[]{:S(2)}) collective-permute-start(f32[64,512]{1,0:T(8,128)S(1)} %get-tuple-element.70), channel_id=1, source_target_pairs={{0,24},{4,28},{8,16},{12,20},{16,8},{20,12},{24,0},{28,4},{1,25},{... | collective-permute-start | bytes 393224 | tf_op jit(solution)/shard_map/ppermute | solution.py:579
  75.0 5.2 %collective-permute-start.16 = (f32[64,512]{1,0:T(8,128)S(1)}, f32[64,512]{1,0:T(8,128)S(1)}, u32[]{:S(2)}, u32[]{:S(2)}) collective-permute-start(f32[64,512]{1,0:T(8,128)S(1)} %get-tuple-element.71), channel_id=1, source_target_pairs={{0,8},{4,12},{8,0},{12,4},{16,24},{20,28},{24,16},{28,20},{1,9},{5... | collective-permute-start | bytes 393224 | tf_op jit(solution)/shard_map/ppermute | solution.py:579
  75.5 5.0 %collective-permute-start.17 = (f32[64,512]{1,0:T(8,128)S(1)}, f32[64,512]{1,0:T(8,128)S(1)}, u32[]{:S(2)}, u32[]{:S(2)}) collective-permute-start(f32[64,512]{1,0:T(8,128)S(1)} %get-tuple-element.72), channel_id=1, source_target_pairs={{0,16},{4,20},{8,24},{12,28},{16,0},{20,4},{24,8},{28,12},{1,17},{... | collective-permute-start | bytes 393224 | tf_op jit(solution)/shard_map/ppermute | solution.py:579
  76.7 10.9 %collective-permute-start.10 = (f32[64,512]{1,0:T(8,128)S(1)}, f32[64,512]{1,0:T(8,128)S(1)}, u32[]{:S(2)}, u32[]{:S(2)}) collective-permute-start(f32[64,512]{1,0:T(8,128)S(1)} %get-tuple-element.62), channel_id=1, source_target_pairs={{0,16},{4,20},{8,24},{12,28},{16,0},{20,4},{24,8},{28,12},{1,17},{... | collective-permute-start | bytes 393224 | tf_op jit(solution)/shard_map/ppermute | solution.py:579
  78.6 9.0 %collective-permute-start.8 = (f32[64,512]{1,0:T(8,128)S(1)}, f32[64,512]{1,0:T(8,128)S(1)}, u32[]{:S(2)}, u32[]{:S(2)}) collective-permute-start(f32[64,512]{1,0:T(8,128)S(1)} %get-tuple-element.60), channel_id=1, source_target_pairs={{0,24},{4,28},{8,16},{12,20},{16,8},{20,12},{24,0},{28,4},{1,25},{... | collective-permute-start | bytes 393224 | tf_op jit(solution)/shard_map/ppermute | solution.py:579
  80.1 7.5 %collective-permute-start.9 = (f32[64,512]{1,0:T(8,128)S(1)}, f32[64,512]{1,0:T(8,128)S(1)}, u32[]{:S(2)}, u32[]{:S(2)}) collective-permute-start(f32[64,512]{1,0:T(8,128)S(1)} %get-tuple-element.61), channel_id=1, source_target_pairs={{0,8},{4,12},{8,0},{12,4},{16,24},{20,28},{24,16},{28,20},{1,9},{5... | collective-permute-start | bytes 393224 | tf_op jit(solution)/shard_map/ppermute | solution.py:579
  80.7 9.7 %collective-permute-start.18 = (f32[4,64,512]{2,1,0:T(8,128)S(1)}, f32[4,64,512]{2,1,0:T(8,128)S(1)}, u32[]{:S(2)}, u32[]{:S(2)}) collective-permute-start(f32[4,64,512]{2,1,0:T(8,128)S(1)} %get-tuple-element.75), channel_id=1, source_target_pairs={{0,4},{4,0},{8,12},{12,8},{16,20},{20,16},{24,28},{28,24},{1,5},{5... | collective-permute-start | bytes 1572872 | tf_op jit(solution)/shard_map/ppermute | solution.py:593
  87.9 6.1 %collective-permute-start.11 = (f32[4,64,512]{2,1,0:T(8,128)S(1)}, f32[4,64,512]{2,1,0:T(8,128)S(1)}, u32[]{:S(2)}, u32[]{:S(2)}) collective-permute-start(f32[4,64,512]{2,1,0:T(8,128)S(1)} %get-tuple-element.65), channel_id=1, source_target_pairs={{0,4},{4,0},{8,12},{12,8},{16,20},{20,16},{24,28},{28,24},{1,5},{5... | collective-permute-start | bytes 1572872 | tf_op jit(solution)/shard_map/ppermute | solution.py:593
  90.5 7.3 %collective-permute-start.19 = (f32[64,512]{1,0:T(8,128)S(1)}, f32[64,512]{1,0:T(8,128)S(1)}, u32[]{:S(2)}, u32[]{:S(2)}) collective-permute-start(f32[64,512]{1,0:T(8,128)S(1)} %get-tuple-element.76), channel_id=1, source_target_pairs={{0,24},{4,28},{8,16},{12,20},{16,8},{20,12},{24,0},{28,4},{1,25},{... | collective-permute-start | bytes 393224 | tf_op jit(solution)/shard_map/ppermute | solution.py:579
  92.1 7.5 %collective-permute-start.20 = (f32[64,512]{1,0:T(8,128)S(1)}, f32[64,512]{1,0:T(8,128)S(1)}, u32[]{:S(2)}, u32[]{:S(2)}) collective-permute-start(f32[64,512]{1,0:T(8,128)S(1)} %get-tuple-element.77), channel_id=1, source_target_pairs={{0,8},{4,12},{8,0},{12,4},{16,24},{20,28},{24,16},{28,20},{1,9},{5... | collective-permute-start | bytes 393224 | tf_op jit(solution)/shard_map/ppermute | solution.py:579
  92.5 8.2 %collective-permute-start.21 = (f32[64,512]{1,0:T(8,128)S(1)}, f32[64,512]{1,0:T(8,128)S(1)}, u32[]{:S(2)}, u32[]{:S(2)}) collective-permute-start(f32[64,512]{1,0:T(8,128)S(1)} %get-tuple-element.78), channel_id=1, source_target_pairs={{0,16},{4,20},{8,24},{12,28},{16,0},{20,4},{24,8},{28,12},{1,17},{... | collective-permute-start | bytes 393224 | tf_op jit(solution)/shard_map/ppermute | solution.py:579
  94.1 9.3 %collective-permute-start.12 = (f32[64,512]{1,0:T(8,128)S(1)}, f32[64,512]{1,0:T(8,128)S(1)}, u32[]{:S(2)}, u32[]{:S(2)}) collective-permute-start(f32[64,512]{1,0:T(8,128)S(1)} %get-tuple-element.66), channel_id=1, source_target_pairs={{0,24},{4,28},{8,16},{12,20},{16,8},{20,12},{24,0},{28,4},{1,25},{... | collective-permute-start | bytes 393224 | tf_op jit(solution)/shard_map/ppermute | solution.py:579
  95.8 8.6 %collective-permute-start.13 = (f32[64,512]{1,0:T(8,128)S(1)}, f32[64,512]{1,0:T(8,128)S(1)}, u32[]{:S(2)}, u32[]{:S(2)}) collective-permute-start(f32[64,512]{1,0:T(8,128)S(1)} %get-tuple-element.67), channel_id=1, source_target_pairs={{0,8},{4,12},{8,0},{12,4},{16,24},{20,28},{24,16},{28,20},{1,9},{5... | collective-permute-start | bytes 393224 | tf_op jit(solution)/shard_map/ppermute | solution.py:579
  97.8 7.5 %collective-permute-start.14 = (f32[64,512]{1,0:T(8,128)S(1)}, f32[64,512]{1,0:T(8,128)S(1)}, u32[]{:S(2)}, u32[]{:S(2)}) collective-permute-start(f32[64,512]{1,0:T(8,128)S(1)} %get-tuple-element.68), channel_id=1, source_target_pairs={{0,16},{4,20},{8,24},{12,28},{16,0},{20,4},{24,8},{28,12},{1,17},{... | collective-permute-start | bytes 393224 | tf_op jit(solution)/shard_map/ppermute | solution.py:579

commit v14 on v13

--- a/solution.py
+++ b/solution.py
@@ -95,12 +95,15 @@
     return [pltpu.VMEM((3, 2 * size, size), HALF)] * number
 
 
-def call(kernel, outs, scratch, args, specs=None, flops=0, name=None, limit=40):
+def call(
+    kernel, outs, scratch, args, specs=None, out_specs=None, aliases=None, flops=0, name=None, limit=40
+):
     made = pl.pallas_call(
         kernel,
         out_shape=outs,
         in_specs=specs or [VMEM] * len(args),
-        out_specs=[VMEM] * len(outs),
+        out_specs=out_specs or [VMEM] * len(outs),
+        input_output_aliases=aliases or {},
         scratch_shapes=scratch,
         compiler_params=pltpu.CompilerParams(vmem_limit_bytes=int(limit * 2**20)),
         cost_estimate=pl.CostEstimate(flops=flops, bytes_accessed=2**20, transcendentals=0),
@@ -418,15 +421,22 @@
         outs[mask][...] = mine[mask] + other[mask]
 
 
-def place_kernel(chips, *refs):
-    scattering = refs[2 * chips]
+def place_kernel(chips, slab, *refs):
+    parcels, scattering, sems = refs[:chips], refs[-2], refs[-1]
     size = scattering.shape[-1]
-    for slab in range(2):
-        parcels = refs[slab * chips : (slab + 1) * chips]
-        for mask, parcel in zip(far_first(chips), parcels):
-            where = share(mask, parcel.shape[0])
-            for part in range(2):
-                scattering[slab, part, where, :] = parcel[:, part * size : (part + 1) * size]
+    copies = []
+    for index, (mask, parcel) in enumerate(zip(far_first(chips), parcels)):
+        for part in range(2):
+            copies.append(
+                pltpu.make_async_copy(
+                    parcel.at[:, pl.ds(part * size, size)],
+                    scattering.at[slab, part, share(mask, parcel.shape[0]), :],
+                    sems.at[index, part],
+                )
+            )
+            copies[-1].start()
+    for copy in copies:
+        copy.wait()
 
 
 def mode_weights(targets, sources, offsets, emission, absorption):
@@ -581,12 +591,17 @@
 
     partial = shape(size // chips, 2 * size, F32, chips)
     sums = [None, None]
+    received = exchange(parcels[1])
     for slab in (1, 0):
+        if slab == 0 and chips > 1:
+            last = masks[-2]
+            parcels[0][last], _ = lax.optimization_barrier((parcels[0][last], received[0]))
+            received = exchange(parcels[0])
         mine, other = call(
             functools.partial(mix_kernel, chips),
             [partial] * 2,
             [],
-            [tiles] + exchange(parcels[slab]),
+            [tiles] + received,
             flops=product // 8,
             name="mix",
         )
@@ -595,13 +610,19 @@
             functools.partial(sum_kernel, chips), [parcel] * chips, [], [mine, other], name="sum"
         )
     returned = [exchange(sums[slab]) for slab in (1, 0)][::-1]
-    (scattering,) = call(
-        functools.partial(place_kernel, chips),
-        [shape(size, size, F32, 2, 2)],
-        [],
-        returned[0] + returned[1],
-        name="scattering",
-    )
+    scattering = []
+    for slab in (1, 0):
+        scattering = call(
+            functools.partial(place_kernel, chips, slab),
+            [shape(size, size, F32, 2, 2)],
+            [pltpu.SemaphoreType.DMA((chips, 2))],
+            returned[slab] + scattering,
+            [VMEM] * chips + [HBM] * len(scattering),
+            [HBM],
+            aliases={chips: 0} if scattering else {},
+            name="scattering",
+        )
+    (scattering,) = scattering
     return (retarded[None], scattering[None])
 
 

time: 107 us -> 107 us (level)
  waiting for transfers between devices: 54.6 us -> 52 us
  starting transfers between devices: 31.1 us -> 32.6 us
    ppermute x12, waiting for transfers between devices: 7.82 us -> 5.31 us  [exchange(): sent[mask] = lax.ppermute(values[mask], 'energy', pairs)]
    ppermute x12, starting transfers between devices: 14.3 us -> 16 us  [exchange(): sent[mask] = lax.ppermute(values[mask], 'energy', pairs)]
    pallas_call x18 -> x19, Pallas kernels: 18.3 us -> 18.9 us  [call(): pl.pallas_call(kernel, out_shape=outs, in_specs=specs or [VMEM] * len(arg...]
  transfers between devices with their start and end apart: 22 -> 22, of which waited for: 10 -> 9; matrix products, arithmetic and copies ran while one was open for 0% -> 0% of each run, Pallas kernels for 11% -> 12%
where the time goes in v14:
time: 107 us; the launch traced here: 106 us
  waiting for transfers between devices  52 us (49%)
  starting transfers between devices  32.6 us (30%)
  Pallas kernels  18.9 us (18%)
  local copies, waits for them, and re-layouts  1.36 us (1%)
  between operations  1.11 us (1%)
    ppermute x7, waiting for transfers between devices, relay(): lax.ppermute(value, ('energy', 'slab'), relay_pairs(step, energies, count))  30.8 us
    pallas_call x19, Pallas kernels, call(): pl.pallas_call(kernel, out_shape=outs, in_specs=specs or [VMEM] * len(arg...  18.9 us
    ppermute x12, starting transfers between devices, exchange(): sent[mask] = lax.ppermute(values[mask], 'energy', pairs)  16 us
    ppermute x1, waiting for transfers between devices, shards(): following = lax.ppermute(opening, ('energy', 'slab'), down)  15.9 us
    ppermute x2, starting transfers between devices, shards(): other = lax.ppermute(other, 'energy', [(i, i ^ 1) for i in range(energies)])  9.29 us
    ppermute x7, starting transfers between devices, relay(): lax.ppermute(value, ('energy', 'slab'), relay_pairs(step, energies, count))  6.07 us
    ppermute x12, waiting for transfers between devices, exchange(): sent[mask] = lax.ppermute(values[mask], 'energy', pairs)  5.31 us
  transfers between devices with their start and end apart: 22, of which 9 were waited for; matrix products, arithmetic and copies ran while one was open for 0% of the time, Pallas kernels for 12%

profile of v14, /device:TPU:0, one launch (start us, length us, event | category | flops | bytes accessed | tf_op | source)
XLA Modules:
  0.0 106.2 jit_solution(13748750529178791785)
XLA Ops:
  0.6 0.7 copy-done
  1.3 4.3 %source.1 = f32[256,512]{1,0:T(8,128)S(1)} custom-call(f32[2,2,256,256]{3,2,1,0:T(8,128)} %bitcast.6, f32[2,2,256,256]{3,2,1,0:T(8,128)} %bitcast.8, f32[2,2,256,256]{3,2,1,0:T(8,128)} %coupling.3, s32[2,16,16]{2,1,0:T(8,128)S(1)} %copy-done), custom_call_target="tpu_custom_call" | custom-call | flops 2415919104 | bytes 1048576 | tf_op jit(solution)/shard_map/source/pallas_call | solution.py:101
  5.7 1.3 %collective-permute-start = (f32[256,512]{1,0:T(8,128)S(1)}, f32[256,512]{1,0:T(8,128)S(1)}, u32[]{:S(2)}, u32[]{:S(2)}) collective-permute-start(f32[256,512]{1,0:T(8,128)S(1)} %source.1), channel_id=1, source_target_pairs={{0,1},{5,4},{6,5},{7,6},{8,9},{13,12},{14,13},{15,14},{16,17},{21,... | collective-permute-start | bytes 1572872 | tf_op jit(solution)/shard_map/ppermute | solution.py:483
  7.0 4.7 %left_maps.1 = (f32[256,512]{1,0:T(8,128)S(1)}, f32[256,512]{1,0:T(8,128)S(1)}, f32[256,512]{1,0:T(8,128)S(1)}, f32[256,512]{1,0:T(8,128)S(1)}, bf16[3,512,256]{...) custom-call(f32[2,2,256,256]{3,2,1,0:T(8,128)} %bitcast.7, ...), custom_call_target="tpu_custom_call" | custom-call | flops 4831838208 | bytes 1048576 | tf_op jit(solution)/shard_map/left_maps/pallas_call | solution.py:101
  11.8 1.9 %collective-permute-done.refs_0_.refs_12_ = f32[256,512]{1,0:T(8,128)S(1)} collective-permute-done((f32[256,512]{1,0:T(8,128)S(1)}, f32[256,512]{1,0:T(8,128)S(1)}, u32[]{:S(2)}, u32[]{:S(2)}) %collective-permute-start) | collective-permute-done | bytes 524320 | tf_op jit(solution)/shard_map/ppermute | solution.py:483
  13.7 0.7 collective-permute-start.1
  14.4 0.0 collective-permute-done.1.refs_0_.refs_1_
  14.4 0.7 collective-permute-start.2
  15.2 1.3 %collective-permute-start.4 = (f32[256,512]{1,0:T(8,128)S(1)}, f32[256,512]{1,0:T(8,128)S(1)}, u32[]{:S(2)}, u32[]{:S(2)}) collective-permute-start(f32[256,512]{1,0:T(8,128)S(1)} %get-tuple-element.50), channel_id=1, source_target_pairs={{1,0},{2,1},{3,2},{9,8},{10,9},{11,10},{17,16},{18,17},{19,18},{25... | collective-permute-start | bytes 1572872 | tf_op jit(solution)/shard_map/ppermute | solution.py:547
  16.5 0.0 collective-permute-done.2.refs_0_.refs_2_
  16.5 0.2 relay.8
  16.7 0.0 copy-start.3
  16.7 0.7 collective-permute-start.3
  17.4 0.0 copy-start.1
  17.4 0.0 copy-start.2
  17.4 0.6 copy-done.1
  18.1 0.0 copy-done.2
  18.1 0.1 add_reduce_fusion.weights
  18.2 0.7 weights.1.refs_13_.tiles
  18.8 15.9 %collective-permute-done.4.refs_11_ = f32[256,512]{1,0:T(8,128)S(1)} collective-permute-done((f32[256,512]{1,0:T(8,128)S(1)}, f32[256,512]{1,0:T(8,128)S(1)}, u32[]{:S(2)}, u32[]{:S(2)}) %collective-permute-start.4) | collective-permute-done | bytes 524320 | tf_op jit(solution)/shard_map/ppermute | solution.py:547
  34.8 3.3 %right_maps.1 = (bf16[3,512,256]{2,1,0:T(8,128)(2,1)S(1)}, bf16[3,512,256]{2,1,0:T(8,128)(2,1)S(1)}, f32[256,512]{1,0:T(8,128)S(1)}, bf16[3,512,256]{2,1,0:T(8,128)(2,1)S(1)}, bf16[3,512,256]{2,1,0:T(8,128)(2,1)S(1)}) custom-call(f32[256,512]{1,0:T(8,128)S(1)} %collective-permute-done.refs_0_.refs_12_, ...), custom_call_target="tpu_custom_call" | custom-call | flops 4026531840 | bytes 1048576 | tf_op jit(solution)/shard_map/right_maps/pallas_call | solution.py:101
  38.0 0.0 collective-permute-done.3.refs_0_
  38.1 0.7 collective-permute-start.5
  38.8 0.0 collective-permute-done.5.refs_0_.refs_1_
  38.8 0.2 relay.10.refs_4_
  39.1 1.3 %collective-permute-start.6 = (f32[256,512]{1,0:T(8,128)S(1)}, f32[256,512]{1,0:T(8,128)S(1)}, u32[]{:S(2)}, u32[]{:S(2)}) collective-permute-start(f32[256,512]{1,0:T(8,128)S(1)} %relay.10.refs_4_), channel_id=1, source_target_pairs={{1,0},{6,5},{9,8},{14,13},{17,16},{22,21},{25,24},{30,29}} | collective-permute-start | bytes 1572872 | tf_op jit(solution)/shard_map/ppermute | solution.py:483
  40.4 28.9 %collective-permute-done.6.refs_0_.refs_2_ = f32[256,512]{1,0:T(8,128)S(1)} collective-permute-done((f32[256,512]{1,0:T(8,128)S(1)}, f32[256,512]{1,0:T(8,128)S(1)}, u32[]{:S(2)}, u32[]{:S(2)}) %collective-permute-start.6) | collective-permute-done | bytes 524320 | tf_op jit(solution)/shard_map/ppermute | solution.py:483
  69.2 0.7 collective-permute-start.7
  69.9 0.0 collective-permute-done.7.refs_3_.refs_1_
  69.9 1.1 %second_slab.1 = (f32[256,512]{1,0:T(8,128)S(1)}, f32[64,512]{1,0:T(8,128)S(1)}, f32[64,512]{1,0:T(8,128)S(1)}, f32[64,512]{1,0:T(8,128)S(1)}, f32[64,512]{1,0:T(8,128)S(1)}) custom-call(f32[256,512]{1,0:T(8,128)S(1)} %collective-permute-done.3.refs_0_, f32[256,512]{1,0:T(8,128)S(1)} %collective-permute-done.5.refs_0_.refs_1_, ...), custom_call_target="tpu_custom_call" | custom-call | flops 805306368 | bytes 1048576 | tf_op jit(solution)/shard_map/second_slab/pallas_call | solution.py:101
  71.0 4.0 %collective-permute-start.10 = (f32[64,512]{1,0:T(8,128)S(1)}, f32[64,512]{1,0:T(8,128)S(1)}, u32[]{:S(2)}, u32[]{:S(2)}) collective-permute-start(f32[64,512]{1,0:T(8,128)S(1)} %get-tuple-element.64), channel_id=1, source_target_pairs={{0,24},{4,28},{8,16},{12,20},{16,8},{20,12},{24,0},{28,4},{1,25},{... | collective-permute-start | bytes 393224 | tf_op jit(solution)/shard_map/ppermute | solution.py:589
  75.0 0.5 collective-permute-start.16
  75.5 0.1 collective-permute-start.17
  75.6 1.0 first_slab.1
  76.7 2.9 %collective-permute-start.8 = (f32[64,512]{1,0:T(8,128)S(1)}, f32[64,512]{1,0:T(8,128)S(1)}, u32[]{:S(2)}, u32[]{:S(2)}) collective-permute-start(f32[64,512]{1,0:T(8,128)S(1)} %get-tuple-element.61), channel_id=1, source_target_pairs={{0,24},{4,28},{8,16},{12,20},{16,8},{20,12},{24,0},{28,4},{1,25},{... | collective-permute-start | bytes 393224 | tf_op jit(solution)/shard_map/ppermute | solution.py:589
  79.6 0.5 collective-permute-start.9
  80.1 0.0 collective-permute-done.10.refs_0_
  80.1 0.1 collective-permute-start.11
  80.2 0.0 collective-permute-done.16.refs_1_
  80.2 0.3 collective-permute-done.17.refs_2_
  80.5 0.2 mix.3
  80.7 6.7 %collective-permute-start.18 = (f32[4,64,512]{2,1,0:T(8,128)S(1)}, f32[4,64,512]{2,1,0:T(8,128)S(1)}, u32[]{:S(2)}, u32[]{:S(2)}) collective-permute-start(f32[4,64,512]{2,1,0:T(8,128)S(1)} %get-tuple-element.77), channel_id=1, source_target_pairs={{0,4},{4,0},{8,12},{12,8},{16,20},{20,16},{24,28},{28,24},{1,5},{5... | collective-permute-start | bytes 1572872 | tf_op jit(solution)/shard_map/ppermute | solution.py:608
  87.5 0.0 collective-permute-done.8.refs_0_
  87.5 0.0 collective-permute-done.9.refs_1_
  87.5 0.0 collective-permute-done.11.refs_2_
  87.5 0.2 mix.2
  87.7 2.6 %collective-permute-start.12 = (f32[4,64,512]{2,1,0:T(8,128)S(1)}, f32[4,64,512]{2,1,0:T(8,128)S(1)}, u32[]{:S(2)}, u32[]{:S(2)}) collective-permute-start(f32[4,64,512]{2,1,0:T(8,128)S(1)} %get-tuple-element.68), channel_id=1, source_target_pairs={{0,4},{4,0},{8,12},{12,8},{16,20},{20,16},{24,28},{28,24},{1,5},{5... | collective-permute-start | bytes 1572872 | tf_op jit(solution)/shard_map/ppermute | solution.py:608
  90.3 0.1 sum.3
  90.3 2.4 %collective-permute-start.19 = (f32[64,512]{1,0:T(8,128)S(1)}, f32[64,512]{1,0:T(8,128)S(1)}, u32[]{:S(2)}, u32[]{:S(2)}) collective-permute-start(f32[64,512]{1,0:T(8,128)S(1)} %get-tuple-element.78), channel_id=1, source_target_pairs={{0,24},{4,28},{8,16},{12,20},{16,8},{20,12},{24,0},{28,4},{1,25},{... | collective-permute-start | bytes 393224 | tf_op jit(solution)/shard_map/ppermute | solution.py:589
  92.7 0.5 collective-permute-start.20
  93.2 0.7 collective-permute-start.21
  93.9 0.0 collective-permute-done.12.other
  93.9 0.1 sum.2
  94.0 2.4 %collective-permute-start.13 = (f32[64,512]{1,0:T(8,128)S(1)}, f32[64,512]{1,0:T(8,128)S(1)}, u32[]{:S(2)}, u32[]{:S(2)}) collective-permute-start(f32[64,512]{1,0:T(8,128)S(1)} %get-tuple-element.69), channel_id=1, source_target_pairs={{0,24},{4,28},{8,16},{12,20},{16,8},{20,12},{24,0},{28,4},{1,25},{... | collective-permute-start | bytes 393224 | tf_op jit(solution)/shard_map/ppermute | solution.py:589
  96.3 0.5 collective-permute-start.14
  96.9 0.8 collective-permute-done.19.refs_0_
  97.7 1.4 %collective-permute-start.15 = (f32[64,512]{1,0:T(8,128)S(1)}, f32[64,512]{1,0:T(8,128)S(1)}, u32[]{:S(2)}, u32[]{:S(2)}) collective-permute-start(f32[64,512]{1,0:T(8,128)S(1)} %get-tuple-element.71), channel_id=1, source_target_pairs={{0,16},{4,20},{8,24},{12,28},{16,0},{20,4},{24,8},{28,12},{1,17},{... | collective-permute-start | bytes 393224 | tf_op jit(solution)/shard_map/ppermute | solution.py:589
  99.0 1.0 retarded.1
  100.1 0.3 collective-permute-done.20.refs_1_
  100.4 2.1 %collective-permute-done.21.refs_2_ = f32[64,512]{1,0:T(8,128)S(1)} collective-permute-done((f32[64,512]{1,0:T(8,128)S(1)}, f32[64,512]{1,0:T(8,128)S(1)}, u32[]{:S(2)}, u32[]{:S(2)}) %collective-permute-start.21) | collective-permute-done | bytes 131104 | tf_op jit(solution)/shard_map/ppermute | solution.py:589
  102.5 0.8 scattering.2.refs_4_
  103.4 1.7 %collective-permute-done.14.refs_1_ = f32[64,512]{1,0:T(8,128)S(1)} collective-permute-done((f32[64,512]{1,0:T(8,128)S(1)}, f32[64,512]{1,0:T(8,128)S(1)}, u32[]{:S(2)}, u32[]{:S(2)}) %collective-permute-start.14) | collective-permute-done | bytes 131104 | tf_op jit(solution)/shard_map/ppermute | solution.py:589
  105.1 0.1 collective-permute-done.15.refs_2_
  105.2 0.8 scattering.3
  (10 shorter events, 0.1 us)
Async XLA Ops:
  0.6 0.7 copy-start
  5.7 8.0 %collective-permute-start = (f32[256,512]{1,0:T(8,128)S(1)}, f32[256,512]{1,0:T(8,128)S(1)}, u32[]{:S(2)}, u32[]{:S(2)}) collective-permute-start(f32[256,512]{1,0:T(8,128)S(1)} %source.1), channel_id=1, source_target_pairs={{0,1},{5,4},{6,5},{7,6},{8,9},{13,12},{14,13},{15,14},{16,17},{21,... | collective-permute-start | bytes 1572872 | tf_op jit(solution)/shard_map/ppermute | solution.py:483
  13.7 0.7 collective-permute-start.1
  14.4 2.0 %collective-permute-start.2 = (f32[256,512]{1,0:T(8,128)S(1)}, f32[256,512]{1,0:T(8,128)S(1)}, u32[]{:S(2)}, u32[]{:S(2)}) collective-permute-start(f32[256,512]{1,0:T(8,128)S(1)} %relay.7.refs_4_.refs_10_), channel_id=1, source_target_pairs={{2,3},{5,6},{10,11},{13,14},{18,19},{21,22},{26,27},{29,30}} | collective-permute-start | bytes 1572872 | tf_op jit(solution)/shard_map/ppermute | solution.py:483
  15.2 19.6 %collective-permute-start.4 = (f32[256,512]{1,0:T(8,128)S(1)}, f32[256,512]{1,0:T(8,128)S(1)}, u32[]{:S(2)}, u32[]{:S(2)}) collective-permute-start(f32[256,512]{1,0:T(8,128)S(1)} %get-tuple-element.50), channel_id=1, source_target_pairs={{1,0},{2,1},{3,2},{9,8},{10,9},{11,10},{17,16},{18,17},{19,18},{25... | collective-permute-start | bytes 1572872 | tf_op jit(solution)/shard_map/ppermute | solution.py:547
  16.7 0.7 copy-start.3
  16.7 21.4 %collective-permute-start.3 = (f32[256,512]{1,0:T(8,128)S(1)}, f32[256,512]{1,0:T(8,128)S(1)}, u32[]{:S(2)}, u32[]{:S(2)}) collective-permute-start(f32[256,512]{1,0:T(8,128)S(1)} %get-tuple-element.49.refs_5_.refs_11_.refs_2_), channel_id=1, source_target_pairs={{3,2},{6,7},{11,10},{14,15},{19,18},{22,23},{27,26},{30,31}} | collective-permute-start | bytes 1572872 | tf_op jit(solution)/shard_map/ppermute | solution.py:483
  17.4 0.7 copy-start.1
  17.4 0.7 copy-start.2
  38.1 0.7 collective-permute-start.5
  39.1 30.2 %collective-permute-start.6 = (f32[256,512]{1,0:T(8,128)S(1)}, f32[256,512]{1,0:T(8,128)S(1)}, u32[]{:S(2)}, u32[]{:S(2)}) collective-permute-start(f32[256,512]{1,0:T(8,128)S(1)} %relay.10.refs_4_), channel_id=1, source_target_pairs={{1,0},{6,5},{9,8},{14,13},{17,16},{22,21},{25,24},{30,29}} | collective-permute-start | bytes 1572872 | tf_op jit(solution)/shard_map/ppermute | solution.py:483
  69.2 0.7 collective-permute-start.7
  71.0 9.1 %collective-permute-start.10 = (f32[64,512]{1,0:T(8,128)S(1)}, f32[64,512]{1,0:T(8,128)S(1)}, u32[]{:S(2)}, u32[]{:S(2)}) collective-permute-start(f32[64,512]{1,0:T(8,128)S(1)} %get-tuple-element.64), channel_id=1, source_target_pairs={{0,24},{4,28},{8,16},{12,20},{16,8},{20,12},{24,0},{28,4},{1,25},{... | collective-permute-start | bytes 393224 | tf_op jit(solution)/shard_map/ppermute | solution.py:589
  75.0 5.2 %collective-permute-start.16 = (f32[64,512]{1,0:T(8,128)S(1)}, f32[64,512]{1,0:T(8,128)S(1)}, u32[]{:S(2)}, u32[]{:S(2)}) collective-permute-start(f32[64,512]{1,0:T(8,128)S(1)} %get-tuple-element.73), channel_id=1, source_target_pairs={{0,8},{4,12},{8,0},{12,4},{16,24},{20,28},{24,16},{28,20},{1,9},{5... | collective-permute-start | bytes 393224 | tf_op jit(solution)/shard_map/ppermute | solution.py:589
  75.5 5.0 %collective-permute-start.17 = (f32[64,512]{1,0:T(8,128)S(1)}, f32[64,512]{1,0:T(8,128)S(1)}, u32[]{:S(2)}, u32[]{:S(2)}) collective-permute-start(f32[64,512]{1,0:T(8,128)S(1)} %get-tuple-element.74), channel_id=1, source_target_pairs={{0,16},{4,20},{8,24},{12,28},{16,0},{20,4},{24,8},{28,12},{1,17},{... | collective-permute-start | bytes 393224 | tf_op jit(solution)/shard_map/ppermute | solution.py:589
  76.7 10.8 %collective-permute-start.8 = (f32[64,512]{1,0:T(8,128)S(1)}, f32[64,512]{1,0:T(8,128)S(1)}, u32[]{:S(2)}, u32[]{:S(2)}) collective-permute-start(f32[64,512]{1,0:T(8,128)S(1)} %get-tuple-element.61), channel_id=1, source_target_pairs={{0,24},{4,28},{8,16},{12,20},{16,8},{20,12},{24,0},{28,4},{1,25},{... | collective-permute-start | bytes 393224 | tf_op jit(solution)/shard_map/ppermute | solution.py:589
  79.6 7.9 %collective-permute-start.9 = (f32[64,512]{1,0:T(8,128)S(1)}, f32[64,512]{1,0:T(8,128)S(1)}, u32[]{:S(2)}, u32[]{:S(2)}) collective-permute-start(f32[64,512]{1,0:T(8,128)S(1)} %get-tuple-element.62), channel_id=1, source_target_pairs={{0,8},{4,12},{8,0},{12,4},{16,24},{20,28},{24,16},{28,20},{1,9},{5... | collective-permute-start | bytes 393224 | tf_op jit(solution)/shard_map/ppermute | solution.py:589
  80.1 7.4 %collective-permute-start.11 = (f32[64,512]{1,0:T(8,128)S(1)}, f32[64,512]{1,0:T(8,128)S(1)}, u32[]{:S(2)}, u32[]{:S(2)}) collective-permute-start(f32[64,512]{1,0:T(8,128)S(1)} %get-tuple-element.65), channel_id=1, source_target_pairs={{0,16},{4,20},{8,24},{12,28},{16,0},{20,4},{24,8},{28,12},{1,17},{... | collective-permute-start | bytes 393224 | tf_op jit(solution)/shard_map/ppermute | solution.py:589
  80.7 9.6 %collective-permute-start.18 = (f32[4,64,512]{2,1,0:T(8,128)S(1)}, f32[4,64,512]{2,1,0:T(8,128)S(1)}, u32[]{:S(2)}, u32[]{:S(2)}) collective-permute-start(f32[4,64,512]{2,1,0:T(8,128)S(1)} %get-tuple-element.77), channel_id=1, source_target_pairs={{0,4},{4,0},{8,12},{12,8},{16,20},{20,16},{24,28},{28,24},{1,5},{5... | collective-permute-start | bytes 1572872 | tf_op jit(solution)/shard_map/ppermute | solution.py:608
  87.7 6.2 %collective-permute-start.12 = (f32[4,64,512]{2,1,0:T(8,128)S(1)}, f32[4,64,512]{2,1,0:T(8,128)S(1)}, u32[]{:S(2)}, u32[]{:S(2)}) collective-permute-start(f32[4,64,512]{2,1,0:T(8,128)S(1)} %get-tuple-element.68), channel_id=1, source_target_pairs={{0,4},{4,0},{8,12},{12,8},{16,20},{20,16},{24,28},{28,24},{1,5},{5... | collective-permute-start | bytes 1572872 | tf_op jit(solution)/shard_map/ppermute | solution.py:608
  90.3 7.3 %collective-permute-start.19 = (f32[64,512]{1,0:T(8,128)S(1)}, f32[64,512]{1,0:T(8,128)S(1)}, u32[]{:S(2)}, u32[]{:S(2)}) collective-permute-start(f32[64,512]{1,0:T(8,128)S(1)} %get-tuple-element.78), channel_id=1, source_target_pairs={{0,24},{4,28},{8,16},{12,20},{16,8},{20,12},{24,0},{28,4},{1,25},{... | collective-permute-start | bytes 393224 | tf_op jit(solution)/shard_map/ppermute | solution.py:589
  92.7 7.7 %collective-permute-start.20 = (f32[64,512]{1,0:T(8,128)S(1)}, f32[64,512]{1,0:T(8,128)S(1)}, u32[]{:S(2)}, u32[]{:S(2)}) collective-permute-start(f32[64,512]{1,0:T(8,128)S(1)} %get-tuple-element.79), channel_id=1, source_target_pairs={{0,8},{4,12},{8,0},{12,4},{16,24},{20,28},{24,16},{28,20},{1,9},{5... | collective-permute-start | bytes 393224 | tf_op jit(solution)/shard_map/ppermute | solution.py:589
  93.2 9.3 %collective-permute-start.21 = (f32[64,512]{1,0:T(8,128)S(1)}, f32[64,512]{1,0:T(8,128)S(1)}, u32[]{:S(2)}, u32[]{:S(2)}) collective-permute-start(f32[64,512]{1,0:T(8,128)S(1)} %get-tuple-element.80), channel_id=1, source_target_pairs={{0,16},{4,20},{8,24},{12,28},{16,0},{20,4},{24,8},{28,12},{1,17},{... | collective-permute-start | bytes 393224 | tf_op jit(solution)/shard_map/ppermute | solution.py:589
  94.0 9.4 %collective-permute-start.13 = (f32[64,512]{1,0:T(8,128)S(1)}, f32[64,512]{1,0:T(8,128)S(1)}, u32[]{:S(2)}, u32[]{:S(2)}) collective-permute-start(f32[64,512]{1,0:T(8,128)S(1)} %get-tuple-element.69), channel_id=1, source_target_pairs={{0,24},{4,28},{8,16},{12,20},{16,8},{20,12},{24,0},{28,4},{1,25},{... | collective-permute-start | bytes 393224 | tf_op jit(solution)/shard_map/ppermute | solution.py:589
  96.3 8.8 %collective-permute-start.14 = (f32[64,512]{1,0:T(8,128)S(1)}, f32[64,512]{1,0:T(8,128)S(1)}, u32[]{:S(2)}, u32[]{:S(2)}) collective-permute-start(f32[64,512]{1,0:T(8,128)S(1)} %get-tuple-element.70), channel_id=1, source_target_pairs={{0,8},{4,12},{8,0},{12,4},{16,24},{20,28},{24,16},{28,20},{1,9},{5... | collective-permute-start | bytes 393224 | tf_op jit(solution)/shard_map/ppermute | solution.py:589
  97.7 7.5 %collective-permute-start.15 = (f32[64,512]{1,0:T(8,128)S(1)}, f32[64,512]{1,0:T(8,128)S(1)}, u32[]{:S(2)}, u32[]{:S(2)}) collective-permute-start(f32[64,512]{1,0:T(8,128)S(1)} %get-tuple-element.71), channel_id=1, source_target_pairs={{0,16},{4,20},{8,24},{12,28},{16,0},{20,4},{24,8},{28,12},{1,17},{... | collective-permute-start | bytes 393224 | tf_op jit(solution)/shard_map/ppermute | solution.py:589

commit v15 on v14

--- a/solution.py
+++ b/solution.py
@@ -155,18 +155,18 @@
     first = loads.green(0)
     put(m_b, first)
     put(m_a, loads.sigma(0))
+    coupler = loads.coupler(1)
+    put(m_c, coupler, True)
+    if coupler_out is not None:
+        coupler_out[...] = coupler
     made = first + times(times(first, m_a), m_b)
     if source is not None:
         source[...] = made
+    sigma, second = loads.sigma(1), loads.green(1)
     put(m_a, made)
-    coupler = loads.coupler(1)
-    if coupler_out is not None:
-        coupler_out[...] = coupler
-    put(m_c, coupler, True)
-    inner = loads.sigma(1) + times(times(coupler, m_a), m_c, True)
+    put(m_b, second)
+    inner = sigma + times(times(coupler, m_a), m_c, True)
     put(m_a, inner)
-    second = loads.green(1)
-    put(m_b, second)
     whole[...] = second + times(times(second, m_a), m_b)
     return first, second
 

time: 107 us -> 106 us (level)
  no operation moved by 1% of the time
where the time goes in v15:
time: 106 us
  waiting for transfers between devices  52.2 us (49%)
  starting transfers between devices  32.6 us (31%)
  Pallas kernels  18.7 us (18%)
  local copies, waits for them, and re-layouts  1.36 us (1%)
  between operations  1.11 us (1%)
    ppermute x7, waiting for transfers between devices, relay(): lax.ppermute(value, ('energy', 'slab'), relay_pairs(step, energies, count))  30.9 us
    pallas_call x19, Pallas kernels, call(): pl.pallas_call(kernel, out_shape=outs, in_specs=specs or [VMEM] * len(arg...  18.7 us
    ppermute x12, starting transfers between devices, exchange(): sent[mask] = lax.ppermute(values[mask], 'energy', pairs)  16 us
    ppermute x1, waiting for transfers between devices, shards(): following = lax.ppermute(opening, ('energy', 'slab'), down)  15.9 us
    ppermute x2, starting transfers between devices, shards(): other = lax.ppermute(other, 'energy', [(i, i ^ 1) for i in range(energies)])  9.29 us
    ppermute x7, starting transfers between devices, relay(): lax.ppermute(value, ('energy', 'slab'), relay_pairs(step, energies, count))  6.07 us
    ppermute x12, waiting for transfers between devices, exchange(): sent[mask] = lax.ppermute(values[mask], 'energy', pairs)  5.31 us
  transfers between devices with their start and end apart: 22, of which 9 were waited for; matrix products, arithmetic and copies ran while one was open for 0% of the time, Pallas kernels for 12%

profile of v15, /device:TPU:0, one launch (start us, length us, event | category | flops | bytes accessed | tf_op | source)
XLA Modules:
  0.0 106.1 jit_solution(4484039812889214589)
XLA Ops:
  0.6 0.7 copy-done
  1.3 4.2 %source.1 = f32[256,512]{1,0:T(8,128)S(1)} custom-call(f32[2,2,256,256]{3,2,1,0:T(8,128)} %bitcast.6, f32[2,2,256,256]{3,2,1,0:T(8,128)} %bitcast.8, f32[2,2,256,256]{3,2,1,0:T(8,128)} %coupling.3, s32[2,16,16]{2,1,0:T(8,128)S(1)} %copy-done), custom_call_target="tpu_custom_call" | custom-call | flops 2415919104 | bytes 1048576 | tf_op jit(solution)/shard_map/source/pallas_call | solution.py:101
  5.6 1.3 %collective-permute-start = (f32[256,512]{1,0:T(8,128)S(1)}, f32[256,512]{1,0:T(8,128)S(1)}, u32[]{:S(2)}, u32[]{:S(2)}) collective-permute-start(f32[256,512]{1,0:T(8,128)S(1)} %source.1), channel_id=1, source_target_pairs={{0,1},{5,4},{6,5},{7,6},{8,9},{13,12},{14,13},{15,14},{16,17},{21,... | collective-permute-start | bytes 1572872 | tf_op jit(solution)/shard_map/ppermute | solution.py:483
  6.9 4.6 %left_maps.1 = (f32[256,512]{1,0:T(8,128)S(1)}, f32[256,512]{1,0:T(8,128)S(1)}, f32[256,512]{1,0:T(8,128)S(1)}, f32[256,512]{1,0:T(8,128)S(1)}, bf16[3,512,256]{...) custom-call(f32[2,2,256,256]{3,2,1,0:T(8,128)} %bitcast.7, ...), custom_call_target="tpu_custom_call" | custom-call | flops 4831838208 | bytes 1048576 | tf_op jit(solution)/shard_map/left_maps/pallas_call | solution.py:101
  11.5 2.0 %collective-permute-done.refs_0_.refs_12_ = f32[256,512]{1,0:T(8,128)S(1)} collective-permute-done((f32[256,512]{1,0:T(8,128)S(1)}, f32[256,512]{1,0:T(8,128)S(1)}, u32[]{:S(2)}, u32[]{:S(2)}) %collective-permute-start) | collective-permute-done | bytes 524320 | tf_op jit(solution)/shard_map/ppermute | solution.py:483
  13.6 0.7 collective-permute-start.1
  14.4 0.7 collective-permute-start.2
  15.1 1.3 %collective-permute-start.4 = (f32[256,512]{1,0:T(8,128)S(1)}, f32[256,512]{1,0:T(8,128)S(1)}, u32[]{:S(2)}, u32[]{:S(2)}) collective-permute-start(f32[256,512]{1,0:T(8,128)S(1)} %get-tuple-element.50), channel_id=1, source_target_pairs={{1,0},{2,1},{3,2},{9,8},{10,9},{11,10},{17,16},{18,17},{19,18},{25... | collective-permute-start | bytes 1572872 | tf_op jit(solution)/shard_map/ppermute | solution.py:547
  16.4 0.0 collective-permute-done.2.refs_0_.refs_2_
  16.4 0.2 relay.8
  16.6 0.0 copy-start.3
  16.6 0.7 collective-permute-start.3
  17.3 0.0 copy-start.1
  17.3 0.0 copy-start.2
  17.4 0.6 copy-done.1
  18.0 0.0 copy-done.2
  18.0 0.1 add_reduce_fusion.weights
  18.1 0.7 weights.1.refs_13_.tiles
  18.7 15.9 %collective-permute-done.4.refs_11_ = f32[256,512]{1,0:T(8,128)S(1)} collective-permute-done((f32[256,512]{1,0:T(8,128)S(1)}, f32[256,512]{1,0:T(8,128)S(1)}, u32[]{:S(2)}, u32[]{:S(2)}) %collective-permute-start.4) | collective-permute-done | bytes 524320 | tf_op jit(solution)/shard_map/ppermute | solution.py:547
  34.7 3.3 %right_maps.1 = (bf16[3,512,256]{2,1,0:T(8,128)(2,1)S(1)}, bf16[3,512,256]{2,1,0:T(8,128)(2,1)S(1)}, f32[256,512]{1,0:T(8,128)S(1)}, bf16[3,512,256]{2,1,0:T(8,128)(2,1)S(1)}, bf16[3,512,256]{2,1,0:T(8,128)(2,1)S(1)}) custom-call(f32[256,512]{1,0:T(8,128)S(1)} %collective-permute-done.refs_0_.refs_12_, ...), custom_call_target="tpu_custom_call" | custom-call | flops 4026531840 | bytes 1048576 | tf_op jit(solution)/shard_map/right_maps/pallas_call | solution.py:101
  38.0 0.0 collective-permute-done.3.refs_0_
  38.0 0.7 collective-permute-start.5
  38.7 0.0 collective-permute-done.5.refs_0_.refs_1_
  38.7 0.2 relay.10.refs_4_
  39.0 1.3 %collective-permute-start.6 = (f32[256,512]{1,0:T(8,128)S(1)}, f32[256,512]{1,0:T(8,128)S(1)}, u32[]{:S(2)}, u32[]{:S(2)}) collective-permute-start(f32[256,512]{1,0:T(8,128)S(1)} %relay.10.refs_4_), channel_id=1, source_target_pairs={{1,0},{6,5},{9,8},{14,13},{17,16},{22,21},{25,24},{30,29}} | collective-permute-start | bytes 1572872 | tf_op jit(solution)/shard_map/ppermute | solution.py:483
  40.3 28.9 %collective-permute-done.6.refs_0_.refs_2_ = f32[256,512]{1,0:T(8,128)S(1)} collective-permute-done((f32[256,512]{1,0:T(8,128)S(1)}, f32[256,512]{1,0:T(8,128)S(1)}, u32[]{:S(2)}, u32[]{:S(2)}) %collective-permute-start.6) | collective-permute-done | bytes 524320 | tf_op jit(solution)/shard_map/ppermute | solution.py:483
  69.1 0.7 collective-permute-start.7
  69.8 1.1 %second_slab.1 = (f32[256,512]{1,0:T(8,128)S(1)}, f32[64,512]{1,0:T(8,128)S(1)}, f32[64,512]{1,0:T(8,128)S(1)}, f32[64,512]{1,0:T(8,128)S(1)}, f32[64,512]{1,0:T(8,128)S(1)}) custom-call(f32[256,512]{1,0:T(8,128)S(1)} %collective-permute-done.3.refs_0_, f32[256,512]{1,0:T(8,128)S(1)} %collective-permute-done.5.refs_0_.refs_1_, ...), custom_call_target="tpu_custom_call" | custom-call | flops 805306368 | bytes 1048576 | tf_op jit(solution)/shard_map/second_slab/pallas_call | solution.py:101
  70.9 4.0 %collective-permute-start.10 = (f32[64,512]{1,0:T(8,128)S(1)}, f32[64,512]{1,0:T(8,128)S(1)}, u32[]{:S(2)}, u32[]{:S(2)}) collective-permute-start(f32[64,512]{1,0:T(8,128)S(1)} %get-tuple-element.64), channel_id=1, source_target_pairs={{0,24},{4,28},{8,16},{12,20},{16,8},{20,12},{24,0},{28,4},{1,25},{... | collective-permute-start | bytes 393224 | tf_op jit(solution)/shard_map/ppermute | solution.py:589
  74.9 0.5 collective-permute-start.16
  75.4 0.1 collective-permute-start.17
  75.5 1.0 first_slab.1
  76.6 2.9 %collective-permute-start.8 = (f32[64,512]{1,0:T(8,128)S(1)}, f32[64,512]{1,0:T(8,128)S(1)}, u32[]{:S(2)}, u32[]{:S(2)}) collective-permute-start(f32[64,512]{1,0:T(8,128)S(1)} %get-tuple-element.61), channel_id=1, source_target_pairs={{0,24},{4,28},{8,16},{12,20},{16,8},{20,12},{24,0},{28,4},{1,25},{... | collective-permute-start | bytes 393224 | tf_op jit(solution)/shard_map/ppermute | solution.py:589
  79.5 0.5 collective-permute-start.9
  80.0 0.0 collective-permute-done.10.refs_0_
  80.0 0.1 collective-permute-start.11
  80.1 0.0 collective-permute-done.16.refs_1_
  80.1 0.3 collective-permute-done.17.refs_2_
  80.4 0.2 mix.3
  80.6 6.8 %collective-permute-start.18 = (f32[4,64,512]{2,1,0:T(8,128)S(1)}, f32[4,64,512]{2,1,0:T(8,128)S(1)}, u32[]{:S(2)}, u32[]{:S(2)}) collective-permute-start(f32[4,64,512]{2,1,0:T(8,128)S(1)} %get-tuple-element.77), channel_id=1, source_target_pairs={{0,4},{4,0},{8,12},{12,8},{16,20},{20,16},{24,28},{28,24},{1,5},{5... | collective-permute-start | bytes 1572872 | tf_op jit(solution)/shard_map/ppermute | solution.py:608
  87.4 0.0 collective-permute-done.8.refs_0_
  87.4 0.0 collective-permute-done.9.refs_1_
  87.4 0.0 collective-permute-done.11.refs_2_
  87.4 0.2 mix.2
  87.7 2.5 %collective-permute-start.12 = (f32[4,64,512]{2,1,0:T(8,128)S(1)}, f32[4,64,512]{2,1,0:T(8,128)S(1)}, u32[]{:S(2)}, u32[]{:S(2)}) collective-permute-start(f32[4,64,512]{2,1,0:T(8,128)S(1)} %get-tuple-element.68), channel_id=1, source_target_pairs={{0,4},{4,0},{8,12},{12,8},{16,20},{20,16},{24,28},{28,24},{1,5},{5... | collective-permute-start | bytes 1572872 | tf_op jit(solution)/shard_map/ppermute | solution.py:608
  90.2 0.0 collective-permute-done.18.other
  90.2 0.1 sum.3
  90.3 2.4 %collective-permute-start.19 = (f32[64,512]{1,0:T(8,128)S(1)}, f32[64,512]{1,0:T(8,128)S(1)}, u32[]{:S(2)}, u32[]{:S(2)}) collective-permute-start(f32[64,512]{1,0:T(8,128)S(1)} %get-tuple-element.78), channel_id=1, source_target_pairs={{0,24},{4,28},{8,16},{12,20},{16,8},{20,12},{24,0},{28,4},{1,25},{... | collective-permute-start | bytes 393224 | tf_op jit(solution)/shard_map/ppermute | solution.py:589
  92.6 0.5 collective-permute-start.20
  93.2 0.7 collective-permute-start.21
  93.8 0.0 collective-permute-done.12.other
  93.8 0.1 sum.2
  93.9 2.4 %collective-permute-start.13 = (f32[64,512]{1,0:T(8,128)S(1)}, f32[64,512]{1,0:T(8,128)S(1)}, u32[]{:S(2)}, u32[]{:S(2)}) collective-permute-start(f32[64,512]{1,0:T(8,128)S(1)} %get-tuple-element.69), channel_id=1, source_target_pairs={{0,24},{4,28},{8,16},{12,20},{16,8},{20,12},{24,0},{28,4},{1,25},{... | collective-permute-start | bytes 393224 | tf_op jit(solution)/shard_map/ppermute | solution.py:589
  96.2 0.5 collective-permute-start.14
  96.8 0.8 collective-permute-done.19.refs_0_
  97.6 1.4 %collective-permute-start.15 = (f32[64,512]{1,0:T(8,128)S(1)}, f32[64,512]{1,0:T(8,128)S(1)}, u32[]{:S(2)}, u32[]{:S(2)}) collective-permute-start(f32[64,512]{1,0:T(8,128)S(1)} %get-tuple-element.71), channel_id=1, source_target_pairs={{0,16},{4,20},{8,24},{12,28},{16,0},{20,4},{24,8},{28,12},{1,17},{... | collective-permute-start | bytes 393224 | tf_op jit(solution)/shard_map/ppermute | solution.py:589
  98.9 1.0 retarded.1
  100.0 0.3 collective-permute-done.20.refs_1_
  100.3 2.1 %collective-permute-done.21.refs_2_ = f32[64,512]{1,0:T(8,128)S(1)} collective-permute-done((f32[64,512]{1,0:T(8,128)S(1)}, f32[64,512]{1,0:T(8,128)S(1)}, u32[]{:S(2)}, u32[]{:S(2)}) %collective-permute-start.21) | collective-permute-done | bytes 131104 | tf_op jit(solution)/shard_map/ppermute | solution.py:589
  102.4 0.8 scattering.2.refs_4_
  103.3 0.0 collective-permute-done.13.refs_0_
  103.3 1.7 %collective-permute-done.14.refs_1_ = f32[64,512]{1,0:T(8,128)S(1)} collective-permute-done((f32[64,512]{1,0:T(8,128)S(1)}, f32[64,512]{1,0:T(8,128)S(1)}, u32[]{:S(2)}, u32[]{:S(2)}) %collective-permute-start.14) | collective-permute-done | bytes 131104 | tf_op jit(solution)/shard_map/ppermute | solution.py:589
  105.0 0.1 collective-permute-done.15.refs_2_
  105.1 0.8 scattering.3
  (10 shorter events, 0.1 us)
Async XLA Ops:
  0.6 0.7 copy-start
  5.6 8.0 %collective-permute-start = (f32[256,512]{1,0:T(8,128)S(1)}, f32[256,512]{1,0:T(8,128)S(1)}, u32[]{:S(2)}, u32[]{:S(2)}) collective-permute-start(f32[256,512]{1,0:T(8,128)S(1)} %source.1), channel_id=1, source_target_pairs={{0,1},{5,4},{6,5},{7,6},{8,9},{13,12},{14,13},{15,14},{16,17},{21,... | collective-permute-start | bytes 1572872 | tf_op jit(solution)/shard_map/ppermute | solution.py:483
  13.6 0.7 collective-permute-start.1
  14.4 2.0 %collective-permute-start.2 = (f32[256,512]{1,0:T(8,128)S(1)}, f32[256,512]{1,0:T(8,128)S(1)}, u32[]{:S(2)}, u32[]{:S(2)}) collective-permute-start(f32[256,512]{1,0:T(8,128)S(1)} %relay.7.refs_4_.refs_10_), channel_id=1, source_target_pairs={{2,3},{5,6},{10,11},{13,14},{18,19},{21,22},{26,27},{29,30}} | collective-permute-start | bytes 1572872 | tf_op jit(solution)/shard_map/ppermute | solution.py:483
  15.1 19.6 %collective-permute-start.4 = (f32[256,512]{1,0:T(8,128)S(1)}, f32[256,512]{1,0:T(8,128)S(1)}, u32[]{:S(2)}, u32[]{:S(2)}) collective-permute-start(f32[256,512]{1,0:T(8,128)S(1)} %get-tuple-element.50), channel_id=1, source_target_pairs={{1,0},{2,1},{3,2},{9,8},{10,9},{11,10},{17,16},{18,17},{19,18},{25... | collective-permute-start | bytes 1572872 | tf_op jit(solution)/shard_map/ppermute | solution.py:547
  16.6 0.7 copy-start.3
  16.6 21.4 %collective-permute-start.3 = (f32[256,512]{1,0:T(8,128)S(1)}, f32[256,512]{1,0:T(8,128)S(1)}, u32[]{:S(2)}, u32[]{:S(2)}) collective-permute-start(f32[256,512]{1,0:T(8,128)S(1)} %get-tuple-element.49.refs_5_.refs_11_.refs_2_), channel_id=1, source_target_pairs={{3,2},{6,7},{11,10},{14,15},{19,18},{22,23},{27,26},{30,31}} | collective-permute-start | bytes 1572872 | tf_op jit(solution)/shard_map/ppermute | solution.py:483
  17.3 0.7 copy-start.1
  17.3 0.7 copy-start.2
  38.0 0.7 collective-permute-start.5
  39.0 30.2 %collective-permute-start.6 = (f32[256,512]{1,0:T(8,128)S(1)}, f32[256,512]{1,0:T(8,128)S(1)}, u32[]{:S(2)}, u32[]{:S(2)}) collective-permute-start(f32[256,512]{1,0:T(8,128)S(1)} %relay.10.refs_4_), channel_id=1, source_target_pairs={{1,0},{6,5},{9,8},{14,13},{17,16},{22,21},{25,24},{30,29}} | collective-permute-start | bytes 1572872 | tf_op jit(solution)/shard_map/ppermute | solution.py:483
  69.1 0.7 collective-permute-start.7
  70.9 9.1 %collective-permute-start.10 = (f32[64,512]{1,0:T(8,128)S(1)}, f32[64,512]{1,0:T(8,128)S(1)}, u32[]{:S(2)}, u32[]{:S(2)}) collective-permute-start(f32[64,512]{1,0:T(8,128)S(1)} %get-tuple-element.64), channel_id=1, source_target_pairs={{0,24},{4,28},{8,16},{12,20},{16,8},{20,12},{24,0},{28,4},{1,25},{... | collective-permute-start | bytes 393224 | tf_op jit(solution)/shard_map/ppermute | solution.py:589
  74.9 5.2 %collective-permute-start.16 = (f32[64,512]{1,0:T(8,128)S(1)}, f32[64,512]{1,0:T(8,128)S(1)}, u32[]{:S(2)}, u32[]{:S(2)}) collective-permute-start(f32[64,512]{1,0:T(8,128)S(1)} %get-tuple-element.73), channel_id=1, source_target_pairs={{0,8},{4,12},{8,0},{12,4},{16,24},{20,28},{24,16},{28,20},{1,9},{5... | collective-permute-start | bytes 393224 | tf_op jit(solution)/shard_map/ppermute | solution.py:589
  75.4 5.0 %collective-permute-start.17 = (f32[64,512]{1,0:T(8,128)S(1)}, f32[64,512]{1,0:T(8,128)S(1)}, u32[]{:S(2)}, u32[]{:S(2)}) collective-permute-start(f32[64,512]{1,0:T(8,128)S(1)} %get-tuple-element.74), channel_id=1, source_target_pairs={{0,16},{4,20},{8,24},{12,28},{16,0},{20,4},{24,8},{28,12},{1,17},{... | collective-permute-start | bytes 393224 | tf_op jit(solution)/shard_map/ppermute | solution.py:589
  76.6 10.8 %collective-permute-start.8 = (f32[64,512]{1,0:T(8,128)S(1)}, f32[64,512]{1,0:T(8,128)S(1)}, u32[]{:S(2)}, u32[]{:S(2)}) collective-permute-start(f32[64,512]{1,0:T(8,128)S(1)} %get-tuple-element.61), channel_id=1, source_target_pairs={{0,24},{4,28},{8,16},{12,20},{16,8},{20,12},{24,0},{28,4},{1,25},{... | collective-permute-start | bytes 393224 | tf_op jit(solution)/shard_map/ppermute | solution.py:589
  79.5 7.9 %collective-permute-start.9 = (f32[64,512]{1,0:T(8,128)S(1)}, f32[64,512]{1,0:T(8,128)S(1)}, u32[]{:S(2)}, u32[]{:S(2)}) collective-permute-start(f32[64,512]{1,0:T(8,128)S(1)} %get-tuple-element.62), channel_id=1, source_target_pairs={{0,8},{4,12},{8,0},{12,4},{16,24},{20,28},{24,16},{28,20},{1,9},{5... | collective-permute-start | bytes 393224 | tf_op jit(solution)/shard_map/ppermute | solution.py:589
  80.0 7.4 %collective-permute-start.11 = (f32[64,512]{1,0:T(8,128)S(1)}, f32[64,512]{1,0:T(8,128)S(1)}, u32[]{:S(2)}, u32[]{:S(2)}) collective-permute-start(f32[64,512]{1,0:T(8,128)S(1)} %get-tuple-element.65), channel_id=1, source_target_pairs={{0,16},{4,20},{8,24},{12,28},{16,0},{20,4},{24,8},{28,12},{1,17},{... | collective-permute-start | bytes 393224 | tf_op jit(solution)/shard_map/ppermute | solution.py:589
  80.6 9.6 %collective-permute-start.18 = (f32[4,64,512]{2,1,0:T(8,128)S(1)}, f32[4,64,512]{2,1,0:T(8,128)S(1)}, u32[]{:S(2)}, u32[]{:S(2)}) collective-permute-start(f32[4,64,512]{2,1,0:T(8,128)S(1)} %get-tuple-element.77), channel_id=1, source_target_pairs={{0,4},{4,0},{8,12},{12,8},{16,20},{20,16},{24,28},{28,24},{1,5},{5... | collective-permute-start | bytes 1572872 | tf_op jit(solution)/shard_map/ppermute | solution.py:608
  87.7 6.1 %collective-permute-start.12 = (f32[4,64,512]{2,1,0:T(8,128)S(1)}, f32[4,64,512]{2,1,0:T(8,128)S(1)}, u32[]{:S(2)}, u32[]{:S(2)}) collective-permute-start(f32[4,64,512]{2,1,0:T(8,128)S(1)} %get-tuple-element.68), channel_id=1, source_target_pairs={{0,4},{4,0},{8,12},{12,8},{16,20},{20,16},{24,28},{28,24},{1,5},{5... | collective-permute-start | bytes 1572872 | tf_op jit(solution)/shard_map/ppermute | solution.py:608
  90.3 7.3 %collective-permute-start.19 = (f32[64,512]{1,0:T(8,128)S(1)}, f32[64,512]{1,0:T(8,128)S(1)}, u32[]{:S(2)}, u32[]{:S(2)}) collective-permute-start(f32[64,512]{1,0:T(8,128)S(1)} %get-tuple-element.78), channel_id=1, source_target_pairs={{0,24},{4,28},{8,16},{12,20},{16,8},{20,12},{24,0},{28,4},{1,25},{... | collective-permute-start | bytes 393224 | tf_op jit(solution)/shard_map/ppermute | solution.py:589
  92.6 7.7 %collective-permute-start.20 = (f32[64,512]{1,0:T(8,128)S(1)}, f32[64,512]{1,0:T(8,128)S(1)}, u32[]{:S(2)}, u32[]{:S(2)}) collective-permute-start(f32[64,512]{1,0:T(8,128)S(1)} %get-tuple-element.79), channel_id=1, source_target_pairs={{0,8},{4,12},{8,0},{12,4},{16,24},{20,28},{24,16},{28,20},{1,9},{5... | collective-permute-start | bytes 393224 | tf_op jit(solution)/shard_map/ppermute | solution.py:589
  93.2 9.3 %collective-permute-start.21 = (f32[64,512]{1,0:T(8,128)S(1)}, f32[64,512]{1,0:T(8,128)S(1)}, u32[]{:S(2)}, u32[]{:S(2)}) collective-permute-start(f32[64,512]{1,0:T(8,128)S(1)} %get-tuple-element.80), channel_id=1, source_target_pairs={{0,16},{4,20},{8,24},{12,28},{16,0},{20,4},{24,8},{28,12},{1,17},{... | collective-permute-start | bytes 393224 | tf_op jit(solution)/shard_map/ppermute | solution.py:589
  93.9 9.4 %collective-permute-start.13 = (f32[64,512]{1,0:T(8,128)S(1)}, f32[64,512]{1,0:T(8,128)S(1)}, u32[]{:S(2)}, u32[]{:S(2)}) collective-permute-start(f32[64,512]{1,0:T(8,128)S(1)} %get-tuple-element.69), channel_id=1, source_target_pairs={{0,24},{4,28},{8,16},{12,20},{16,8},{20,12},{24,0},{28,4},{1,25},{... | collective-permute-start | bytes 393224 | tf_op jit(solution)/shard_map/ppermute | solution.py:589
  96.2 8.8 %collective-permute-start.14 = (f32[64,512]{1,0:T(8,128)S(1)}, f32[64,512]{1,0:T(8,128)S(1)}, u32[]{:S(2)}, u32[]{:S(2)}) collective-permute-start(f32[64,512]{1,0:T(8,128)S(1)} %get-tuple-element.70), channel_id=1, source_target_pairs={{0,8},{4,12},{8,0},{12,4},{16,24},{20,28},{24,16},{28,20},{1,9},{5... | collective-permute-start | bytes 393224 | tf_op jit(solution)/shard_map/ppermute | solution.py:589
  97.6 7.5 %collective-permute-start.15 = (f32[64,512]{1,0:T(8,128)S(1)}, f32[64,512]{1,0:T(8,128)S(1)}, u32[]{:S(2)}, u32[]{:S(2)}) collective-permute-start(f32[64,512]{1,0:T(8,128)S(1)} %get-tuple-element.71), channel_id=1, source_target_pairs={{0,16},{4,20},{8,24},{12,28},{16,0},{20,4},{24,8},{28,12},{1,17},{... | collective-permute-start | bytes 393224 | tf_op jit(solution)/shard_map/ppermute | solution.py:589

commit v16 on v15

--- a/solution.py
+++ b/solution.py
@@ -114,7 +114,7 @@
 
 class Loads:
     def __init__(self, args, targets, sems, couplers=(0, 1), blocks=True):
-        order = [(0, 0), (1, 0), (3, 1), (2, 1), (1, 1), (0, 1), (3, 0), (2, 0)]
+        order = [(3, 1), (0, 0), (1, 0), (2, 1), (1, 1), (0, 1), (3, 0), (2, 0)]
         self.copies = {
             (which, slab): pltpu.make_async_copy(
                 args[which].at[slab], targets[which].at[slab], sems.at[index]

time: 106 us -> 106 us (level)
  no operation moved by 1% of the time
where the time goes in v16:
time: 106 us
  waiting for transfers between devices  52.2 us (49%)
  starting transfers between devices  32.6 us (31%)
  Pallas kernels  18.7 us (18%)
  local copies, waits for them, and re-layouts  1.36 us (1%)
  between operations  1.11 us (1%)
    ppermute x7, waiting for transfers between devices, relay(): lax.ppermute(value, ('energy', 'slab'), relay_pairs(step, energies, count))  30.9 us
    pallas_call x19, Pallas kernels, call(): pl.pallas_call(kernel, out_shape=outs, in_specs=specs or [VMEM] * len(arg...  18.7 us
    ppermute x12, starting transfers between devices, exchange(): sent[mask] = lax.ppermute(values[mask], 'energy', pairs)  16 us
    ppermute x1, waiting for transfers between devices, shards(): following = lax.ppermute(opening, ('energy', 'slab'), down)  15.9 us
    ppermute x2, starting transfers between devices, shards(): other = lax.ppermute(other, 'energy', [(i, i ^ 1) for i in range(energies)])  9.29 us
    ppermute x7, starting transfers between devices, relay(): lax.ppermute(value, ('energy', 'slab'), relay_pairs(step, energies, count))  6.07 us
    ppermute x12, waiting for transfers between devices, exchange(): sent[mask] = lax.ppermute(values[mask], 'energy', pairs)  5.31 us
  transfers between devices with their start and end apart: 22, of which 9 were waited for; matrix products, arithmetic and copies ran while one was open for 0% of the time, Pallas kernels for 12%

profile of v16, /device:TPU:0, one launch (start us, length us, event | category | flops | bytes accessed | tf_op | source)
XLA Modules:
  0.0 106.1 jit_solution(10637363550919241751)
XLA Ops:
  0.6 0.7 copy-done
  1.3 4.2 %source.1 = f32[256,512]{1,0:T(8,128)S(1)} custom-call(f32[2,2,256,256]{3,2,1,0:T(8,128)} %bitcast.6, f32[2,2,256,256]{3,2,1,0:T(8,128)} %bitcast.8, f32[2,2,256,256]{3,2,1,0:T(8,128)} %coupling.3, s32[2,16,16]{2,1,0:T(8,128)S(1)} %copy-done), custom_call_target="tpu_custom_call" | custom-call | flops 2415919104 | bytes 1048576 | tf_op jit(solution)/shard_map/source/pallas_call | solution.py:101
  5.6 1.3 %collective-permute-start = (f32[256,512]{1,0:T(8,128)S(1)}, f32[256,512]{1,0:T(8,128)S(1)}, u32[]{:S(2)}, u32[]{:S(2)}) collective-permute-start(f32[256,512]{1,0:T(8,128)S(1)} %source.1), channel_id=1, source_target_pairs={{0,1},{5,4},{6,5},{7,6},{8,9},{13,12},{14,13},{15,14},{16,17},{21,... | collective-permute-start | bytes 1572872 | tf_op jit(solution)/shard_map/ppermute | solution.py:483
  6.9 4.6 %left_maps.1 = (f32[256,512]{1,0:T(8,128)S(1)}, f32[256,512]{1,0:T(8,128)S(1)}, f32[256,512]{1,0:T(8,128)S(1)}, f32[256,512]{1,0:T(8,128)S(1)}, bf16[3,512,256]{...) custom-call(f32[2,2,256,256]{3,2,1,0:T(8,128)} %bitcast.7, ...), custom_call_target="tpu_custom_call" | custom-call | flops 4831838208 | bytes 1048576 | tf_op jit(solution)/shard_map/left_maps/pallas_call | solution.py:101
  11.6 2.0 %collective-permute-done.refs_0_.refs_12_ = f32[256,512]{1,0:T(8,128)S(1)} collective-permute-done((f32[256,512]{1,0:T(8,128)S(1)}, f32[256,512]{1,0:T(8,128)S(1)}, u32[]{:S(2)}, u32[]{:S(2)}) %collective-permute-start) | collective-permute-done | bytes 524320 | tf_op jit(solution)/shard_map/ppermute | solution.py:483
  13.6 0.7 collective-permute-start.1
  14.3 0.0 collective-permute-done.1.refs_0_.refs_1_
  14.4 0.7 collective-permute-start.2
  15.1 1.3 %collective-permute-start.4 = (f32[256,512]{1,0:T(8,128)S(1)}, f32[256,512]{1,0:T(8,128)S(1)}, u32[]{:S(2)}, u32[]{:S(2)}) collective-permute-start(f32[256,512]{1,0:T(8,128)S(1)} %get-tuple-element.50), channel_id=1, source_target_pairs={{1,0},{2,1},{3,2},{9,8},{10,9},{11,10},{17,16},{18,17},{19,18},{25... | collective-permute-start | bytes 1572872 | tf_op jit(solution)/shard_map/ppermute | solution.py:547
  16.4 0.0 collective-permute-done.2.refs_0_.refs_2_
  16.4 0.2 relay.8
  16.6 0.0 copy-start.3
  16.6 0.7 collective-permute-start.3
  17.3 0.0 copy-start.1
  17.3 0.0 copy-start.2
  17.4 0.6 copy-done.1
  18.0 0.0 copy-done.2
  18.0 0.1 add_reduce_fusion.weights
  18.1 0.7 weights.1.refs_13_.tiles
  18.7 15.9 %collective-permute-done.4.refs_11_ = f32[256,512]{1,0:T(8,128)S(1)} collective-permute-done((f32[256,512]{1,0:T(8,128)S(1)}, f32[256,512]{1,0:T(8,128)S(1)}, u32[]{:S(2)}, u32[]{:S(2)}) %collective-permute-start.4) | collective-permute-done | bytes 524320 | tf_op jit(solution)/shard_map/ppermute | solution.py:547
  34.7 3.3 %right_maps.1 = (bf16[3,512,256]{2,1,0:T(8,128)(2,1)S(1)}, bf16[3,512,256]{2,1,0:T(8,128)(2,1)S(1)}, f32[256,512]{1,0:T(8,128)S(1)}, bf16[3,512,256]{2,1,0:T(8,128)(2,1)S(1)}, bf16[3,512,256]{2,1,0:T(8,128)(2,1)S(1)}) custom-call(f32[256,512]{1,0:T(8,128)S(1)} %collective-permute-done.refs_0_.refs_12_, ...), custom_call_target="tpu_custom_call" | custom-call | flops 4026531840 | bytes 1048576 | tf_op jit(solution)/shard_map/right_maps/pallas_call | solution.py:101
  38.0 0.0 collective-permute-done.3.refs_0_
  38.0 0.7 collective-permute-start.5
  38.7 0.0 collective-permute-done.5.refs_0_.refs_1_
  38.7 0.2 relay.10.refs_4_
  39.0 1.3 %collective-permute-start.6 = (f32[256,512]{1,0:T(8,128)S(1)}, f32[256,512]{1,0:T(8,128)S(1)}, u32[]{:S(2)}, u32[]{:S(2)}) collective-permute-start(f32[256,512]{1,0:T(8,128)S(1)} %relay.10.refs_4_), channel_id=1, source_target_pairs={{1,0},{6,5},{9,8},{14,13},{17,16},{22,21},{25,24},{30,29}} | collective-permute-start | bytes 1572872 | tf_op jit(solution)/shard_map/ppermute | solution.py:483
  40.3 28.9 %collective-permute-done.6.refs_0_.refs_2_ = f32[256,512]{1,0:T(8,128)S(1)} collective-permute-done((f32[256,512]{1,0:T(8,128)S(1)}, f32[256,512]{1,0:T(8,128)S(1)}, u32[]{:S(2)}, u32[]{:S(2)}) %collective-permute-start.6) | collective-permute-done | bytes 524320 | tf_op jit(solution)/shard_map/ppermute | solution.py:483
  69.1 0.7 collective-permute-start.7
  69.8 1.1 %second_slab.1 = (f32[256,512]{1,0:T(8,128)S(1)}, f32[64,512]{1,0:T(8,128)S(1)}, f32[64,512]{1,0:T(8,128)S(1)}, f32[64,512]{1,0:T(8,128)S(1)}, f32[64,512]{1,0:T(8,128)S(1)}) custom-call(f32[256,512]{1,0:T(8,128)S(1)} %collective-permute-done.3.refs_0_, f32[256,512]{1,0:T(8,128)S(1)} %collective-permute-done.5.refs_0_.refs_1_, ...), custom_call_target="tpu_custom_call" | custom-call | flops 805306368 | bytes 1048576 | tf_op jit(solution)/shard_map/second_slab/pallas_call | solution.py:101
  70.9 4.0 %collective-permute-start.10 = (f32[64,512]{1,0:T(8,128)S(1)}, f32[64,512]{1,0:T(8,128)S(1)}, u32[]{:S(2)}, u32[]{:S(2)}) collective-permute-start(f32[64,512]{1,0:T(8,128)S(1)} %get-tuple-element.64), channel_id=1, source_target_pairs={{0,24},{4,28},{8,16},{12,20},{16,8},{20,12},{24,0},{28,4},{1,25},{... | collective-permute-start | bytes 393224 | tf_op jit(solution)/shard_map/ppermute | solution.py:589
  74.9 0.5 collective-permute-start.16
  75.4 0.1 collective-permute-start.17
  75.5 1.0 first_slab.1
  76.6 2.9 %collective-permute-start.8 = (f32[64,512]{1,0:T(8,128)S(1)}, f32[64,512]{1,0:T(8,128)S(1)}, u32[]{:S(2)}, u32[]{:S(2)}) collective-permute-start(f32[64,512]{1,0:T(8,128)S(1)} %get-tuple-element.61), channel_id=1, source_target_pairs={{0,24},{4,28},{8,16},{12,20},{16,8},{20,12},{24,0},{28,4},{1,25},{... | collective-permute-start | bytes 393224 | tf_op jit(solution)/shard_map/ppermute | solution.py:589
  79.5 0.5 collective-permute-start.9
  80.0 0.0 collective-permute-done.10.refs_0_
  80.0 0.1 collective-permute-start.11
  80.1 0.3 collective-permute-done.17.refs_2_
  80.4 0.2 mix.3
  80.6 6.8 %collective-permute-start.18 = (f32[4,64,512]{2,1,0:T(8,128)S(1)}, f32[4,64,512]{2,1,0:T(8,128)S(1)}, u32[]{:S(2)}, u32[]{:S(2)}) collective-permute-start(f32[4,64,512]{2,1,0:T(8,128)S(1)} %get-tuple-element.77), channel_id=1, source_target_pairs={{0,4},{4,0},{8,12},{12,8},{16,20},{20,16},{24,28},{28,24},{1,5},{5... | collective-permute-start | bytes 1572872 | tf_op jit(solution)/shard_map/ppermute | solution.py:608
  87.4 0.0 collective-permute-done.8.refs_0_
  87.4 0.0 collective-permute-done.9.refs_1_
  87.4 0.0 collective-permute-done.11.refs_2_
  87.4 0.2 mix.2
  87.7 2.5 %collective-permute-start.12 = (f32[4,64,512]{2,1,0:T(8,128)S(1)}, f32[4,64,512]{2,1,0:T(8,128)S(1)}, u32[]{:S(2)}, u32[]{:S(2)}) collective-permute-start(f32[4,64,512]{2,1,0:T(8,128)S(1)} %get-tuple-element.68), channel_id=1, source_target_pairs={{0,4},{4,0},{8,12},{12,8},{16,20},{20,16},{24,28},{28,24},{1,5},{5... | collective-permute-start | bytes 1572872 | tf_op jit(solution)/shard_map/ppermute | solution.py:608
  90.2 0.0 collective-permute-done.18.other
  90.2 0.1 sum.3
  90.3 2.4 %collective-permute-start.19 = (f32[64,512]{1,0:T(8,128)S(1)}, f32[64,512]{1,0:T(8,128)S(1)}, u32[]{:S(2)}, u32[]{:S(2)}) collective-permute-start(f32[64,512]{1,0:T(8,128)S(1)} %get-tuple-element.78), channel_id=1, source_target_pairs={{0,24},{4,28},{8,16},{12,20},{16,8},{20,12},{24,0},{28,4},{1,25},{... | collective-permute-start | bytes 393224 | tf_op jit(solution)/shard_map/ppermute | solution.py:589
  92.6 0.5 collective-permute-start.20
  93.2 0.7 collective-permute-start.21
  93.8 0.0 collective-permute-done.12.other
  93.8 0.1 sum.2
  93.9 2.4 %collective-permute-start.13 = (f32[64,512]{1,0:T(8,128)S(1)}, f32[64,512]{1,0:T(8,128)S(1)}, u32[]{:S(2)}, u32[]{:S(2)}) collective-permute-start(f32[64,512]{1,0:T(8,128)S(1)} %get-tuple-element.69), channel_id=1, source_target_pairs={{0,24},{4,28},{8,16},{12,20},{16,8},{20,12},{24,0},{28,4},{1,25},{... | collective-permute-start | bytes 393224 | tf_op jit(solution)/shard_map/ppermute | solution.py:589
  96.2 0.5 collective-permute-start.14
  96.8 0.8 collective-permute-done.19.refs_0_
  97.6 1.4 %collective-permute-start.15 = (f32[64,512]{1,0:T(8,128)S(1)}, f32[64,512]{1,0:T(8,128)S(1)}, u32[]{:S(2)}, u32[]{:S(2)}) collective-permute-start(f32[64,512]{1,0:T(8,128)S(1)} %get-tuple-element.71), channel_id=1, source_target_pairs={{0,16},{4,20},{8,24},{12,28},{16,0},{20,4},{24,8},{28,12},{1,17},{... | collective-permute-start | bytes 393224 | tf_op jit(solution)/shard_map/ppermute | solution.py:589
  99.0 1.0 retarded.1
  100.0 0.3 collective-permute-done.20.refs_1_
  100.3 2.1 %collective-permute-done.21.refs_2_ = f32[64,512]{1,0:T(8,128)S(1)} collective-permute-done((f32[64,512]{1,0:T(8,128)S(1)}, f32[64,512]{1,0:T(8,128)S(1)}, u32[]{:S(2)}, u32[]{:S(2)}) %collective-permute-start.21) | collective-permute-done | bytes 131104 | tf_op jit(solution)/shard_map/ppermute | solution.py:589
  102.4 0.8 scattering.2.refs_4_
  103.3 0.0 collective-permute-done.13.refs_0_
  103.3 1.7 %collective-permute-done.14.refs_1_ = f32[64,512]{1,0:T(8,128)S(1)} collective-permute-done((f32[64,512]{1,0:T(8,128)S(1)}, f32[64,512]{1,0:T(8,128)S(1)}, u32[]{:S(2)}, u32[]{:S(2)}) %collective-permute-start.14) | collective-permute-done | bytes 131104 | tf_op jit(solution)/shard_map/ppermute | solution.py:589
  105.0 0.1 collective-permute-done.15.refs_2_
  105.1 0.8 scattering.3
  (10 shorter events, 0.1 us)
Async XLA Ops:
  0.6 0.7 copy-start
  5.6 8.0 %collective-permute-start = (f32[256,512]{1,0:T(8,128)S(1)}, f32[256,512]{1,0:T(8,128)S(1)}, u32[]{:S(2)}, u32[]{:S(2)}) collective-permute-start(f32[256,512]{1,0:T(8,128)S(1)} %source.1), channel_id=1, source_target_pairs={{0,1},{5,4},{6,5},{7,6},{8,9},{13,12},{14,13},{15,14},{16,17},{21,... | collective-permute-start | bytes 1572872 | tf_op jit(solution)/shard_map/ppermute | solution.py:483
  13.6 0.7 collective-permute-start.1
  14.4 2.0 %collective-permute-start.2 = (f32[256,512]{1,0:T(8,128)S(1)}, f32[256,512]{1,0:T(8,128)S(1)}, u32[]{:S(2)}, u32[]{:S(2)}) collective-permute-start(f32[256,512]{1,0:T(8,128)S(1)} %relay.7.refs_4_.refs_10_), channel_id=1, source_target_pairs={{2,3},{5,6},{10,11},{13,14},{18,19},{21,22},{26,27},{29,30}} | collective-permute-start | bytes 1572872 | tf_op jit(solution)/shard_map/ppermute | solution.py:483
  15.1 19.6 %collective-permute-start.4 = (f32[256,512]{1,0:T(8,128)S(1)}, f32[256,512]{1,0:T(8,128)S(1)}, u32[]{:S(2)}, u32[]{:S(2)}) collective-permute-start(f32[256,512]{1,0:T(8,128)S(1)} %get-tuple-element.50), channel_id=1, source_target_pairs={{1,0},{2,1},{3,2},{9,8},{10,9},{11,10},{17,16},{18,17},{19,18},{25... | collective-permute-start | bytes 1572872 | tf_op jit(solution)/shard_map/ppermute | solution.py:547
  16.6 0.7 copy-start.3
  16.6 21.4 %collective-permute-start.3 = (f32[256,512]{1,0:T(8,128)S(1)}, f32[256,512]{1,0:T(8,128)S(1)}, u32[]{:S(2)}, u32[]{:S(2)}) collective-permute-start(f32[256,512]{1,0:T(8,128)S(1)} %get-tuple-element.49.refs_5_.refs_11_.refs_2_), channel_id=1, source_target_pairs={{3,2},{6,7},{11,10},{14,15},{19,18},{22,23},{27,26},{30,31}} | collective-permute-start | bytes 1572872 | tf_op jit(solution)/shard_map/ppermute | solution.py:483
  17.3 0.7 copy-start.1
  17.3 0.7 copy-start.2
  38.0 0.7 collective-permute-start.5
  39.0 30.2 %collective-permute-start.6 = (f32[256,512]{1,0:T(8,128)S(1)}, f32[256,512]{1,0:T(8,128)S(1)}, u32[]{:S(2)}, u32[]{:S(2)}) collective-permute-start(f32[256,512]{1,0:T(8,128)S(1)} %relay.10.refs_4_), channel_id=1, source_target_pairs={{1,0},{6,5},{9,8},{14,13},{17,16},{22,21},{25,24},{30,29}} | collective-permute-start | bytes 1572872 | tf_op jit(solution)/shard_map/ppermute | solution.py:483
  69.1 0.7 collective-permute-start.7
  70.9 9.1 %collective-permute-start.10 = (f32[64,512]{1,0:T(8,128)S(1)}, f32[64,512]{1,0:T(8,128)S(1)}, u32[]{:S(2)}, u32[]{:S(2)}) collective-permute-start(f32[64,512]{1,0:T(8,128)S(1)} %get-tuple-element.64), channel_id=1, source_target_pairs={{0,24},{4,28},{8,16},{12,20},{16,8},{20,12},{24,0},{28,4},{1,25},{... | collective-permute-start | bytes 393224 | tf_op jit(solution)/shard_map/ppermute | solution.py:589
  74.9 5.2 %collective-permute-start.16 = (f32[64,512]{1,0:T(8,128)S(1)}, f32[64,512]{1,0:T(8,128)S(1)}, u32[]{:S(2)}, u32[]{:S(2)}) collective-permute-start(f32[64,512]{1,0:T(8,128)S(1)} %get-tuple-element.73), channel_id=1, source_target_pairs={{0,8},{4,12},{8,0},{12,4},{16,24},{20,28},{24,16},{28,20},{1,9},{5... | collective-permute-start | bytes 393224 | tf_op jit(solution)/shard_map/ppermute | solution.py:589
  75.4 5.0 %collective-permute-start.17 = (f32[64,512]{1,0:T(8,128)S(1)}, f32[64,512]{1,0:T(8,128)S(1)}, u32[]{:S(2)}, u32[]{:S(2)}) collective-permute-start(f32[64,512]{1,0:T(8,128)S(1)} %get-tuple-element.74), channel_id=1, source_target_pairs={{0,16},{4,20},{8,24},{12,28},{16,0},{20,4},{24,8},{28,12},{1,17},{... | collective-permute-start | bytes 393224 | tf_op jit(solution)/shard_map/ppermute | solution.py:589
  76.6 10.9 %collective-permute-start.8 = (f32[64,512]{1,0:T(8,128)S(1)}, f32[64,512]{1,0:T(8,128)S(1)}, u32[]{:S(2)}, u32[]{:S(2)}) collective-permute-start(f32[64,512]{1,0:T(8,128)S(1)} %get-tuple-element.61), channel_id=1, source_target_pairs={{0,24},{4,28},{8,16},{12,20},{16,8},{20,12},{24,0},{28,4},{1,25},{... | collective-permute-start | bytes 393224 | tf_op jit(solution)/shard_map/ppermute | solution.py:589
  79.5 7.9 %collective-permute-start.9 = (f32[64,512]{1,0:T(8,128)S(1)}, f32[64,512]{1,0:T(8,128)S(1)}, u32[]{:S(2)}, u32[]{:S(2)}) collective-permute-start(f32[64,512]{1,0:T(8,128)S(1)} %get-tuple-element.62), channel_id=1, source_target_pairs={{0,8},{4,12},{8,0},{12,4},{16,24},{20,28},{24,16},{28,20},{1,9},{5... | collective-permute-start | bytes 393224 | tf_op jit(solution)/shard_map/ppermute | solution.py:589
  80.0 7.4 %collective-permute-start.11 = (f32[64,512]{1,0:T(8,128)S(1)}, f32[64,512]{1,0:T(8,128)S(1)}, u32[]{:S(2)}, u32[]{:S(2)}) collective-permute-start(f32[64,512]{1,0:T(8,128)S(1)} %get-tuple-element.65), channel_id=1, source_target_pairs={{0,16},{4,20},{8,24},{12,28},{16,0},{20,4},{24,8},{28,12},{1,17},{... | collective-permute-start | bytes 393224 | tf_op jit(solution)/shard_map/ppermute | solution.py:589
  80.6 9.6 %collective-permute-start.18 = (f32[4,64,512]{2,1,0:T(8,128)S(1)}, f32[4,64,512]{2,1,0:T(8,128)S(1)}, u32[]{:S(2)}, u32[]{:S(2)}) collective-permute-start(f32[4,64,512]{2,1,0:T(8,128)S(1)} %get-tuple-element.77), channel_id=1, source_target_pairs={{0,4},{4,0},{8,12},{12,8},{16,20},{20,16},{24,28},{28,24},{1,5},{5... | collective-permute-start | bytes 1572872 | tf_op jit(solution)/shard_map/ppermute | solution.py:608
  87.7 6.1 %collective-permute-start.12 = (f32[4,64,512]{2,1,0:T(8,128)S(1)}, f32[4,64,512]{2,1,0:T(8,128)S(1)}, u32[]{:S(2)}, u32[]{:S(2)}) collective-permute-start(f32[4,64,512]{2,1,0:T(8,128)S(1)} %get-tuple-element.68), channel_id=1, source_target_pairs={{0,4},{4,0},{8,12},{12,8},{16,20},{20,16},{24,28},{28,24},{1,5},{5... | collective-permute-start | bytes 1572872 | tf_op jit(solution)/shard_map/ppermute | solution.py:608
  90.3 7.3 %collective-permute-start.19 = (f32[64,512]{1,0:T(8,128)S(1)}, f32[64,512]{1,0:T(8,128)S(1)}, u32[]{:S(2)}, u32[]{:S(2)}) collective-permute-start(f32[64,512]{1,0:T(8,128)S(1)} %get-tuple-element.78), channel_id=1, source_target_pairs={{0,24},{4,28},{8,16},{12,20},{16,8},{20,12},{24,0},{28,4},{1,25},{... | collective-permute-start | bytes 393224 | tf_op jit(solution)/shard_map/ppermute | solution.py:589
  92.6 7.7 %collective-permute-start.20 = (f32[64,512]{1,0:T(8,128)S(1)}, f32[64,512]{1,0:T(8,128)S(1)}, u32[]{:S(2)}, u32[]{:S(2)}) collective-permute-start(f32[64,512]{1,0:T(8,128)S(1)} %get-tuple-element.79), channel_id=1, source_target_pairs={{0,8},{4,12},{8,0},{12,4},{16,24},{20,28},{24,16},{28,20},{1,9},{5... | collective-permute-start | bytes 393224 | tf_op jit(solution)/shard_map/ppermute | solution.py:589
  93.2 9.3 %collective-permute-start.21 = (f32[64,512]{1,0:T(8,128)S(1)}, f32[64,512]{1,0:T(8,128)S(1)}, u32[]{:S(2)}, u32[]{:S(2)}) collective-permute-start(f32[64,512]{1,0:T(8,128)S(1)} %get-tuple-element.80), channel_id=1, source_target_pairs={{0,16},{4,20},{8,24},{12,28},{16,0},{20,4},{24,8},{28,12},{1,17},{... | collective-permute-start | bytes 393224 | tf_op jit(solution)/shard_map/ppermute | solution.py:589
  93.9 9.4 %collective-permute-start.13 = (f32[64,512]{1,0:T(8,128)S(1)}, f32[64,512]{1,0:T(8,128)S(1)}, u32[]{:S(2)}, u32[]{:S(2)}) collective-permute-start(f32[64,512]{1,0:T(8,128)S(1)} %get-tuple-element.69), channel_id=1, source_target_pairs={{0,24},{4,28},{8,16},{12,20},{16,8},{20,12},{24,0},{28,4},{1,25},{... | collective-permute-start | bytes 393224 | tf_op jit(solution)/shard_map/ppermute | solution.py:589
  96.2 8.8 %collective-permute-start.14 = (f32[64,512]{1,0:T(8,128)S(1)}, f32[64,512]{1,0:T(8,128)S(1)}, u32[]{:S(2)}, u32[]{:S(2)}) collective-permute-start(f32[64,512]{1,0:T(8,128)S(1)} %get-tuple-element.70), channel_id=1, source_target_pairs={{0,8},{4,12},{8,0},{12,4},{16,24},{20,28},{24,16},{28,20},{1,9},{5... | collective-permute-start | bytes 393224 | tf_op jit(solution)/shard_map/ppermute | solution.py:589
  97.6 7.5 %collective-permute-start.15 = (f32[64,512]{1,0:T(8,128)S(1)}, f32[64,512]{1,0:T(8,128)S(1)}, u32[]{:S(2)}, u32[]{:S(2)}) collective-permute-start(f32[64,512]{1,0:T(8,128)S(1)} %get-tuple-element.71), channel_id=1, source_target_pairs={{0,16},{4,20},{8,24},{12,28},{16,0},{20,4},{24,8},{28,12},{1,17},{... | collective-permute-start | bytes 393224 | tf_op jit(solution)/shard_map/ppermute | solution.py:589
